TPU v7x, 32 devices: a whole 2x2x4 slice. The times are simulated.
32 devices in a mesh: coef: 1, pair: 32 (over z, y, x, core).
Axes of the slice: x: 2, y: 2, z: 4, core: 2. Of those that a mesh axis runs over, the one named last changes fastest.
Arguments:
- integrals: bfloat16 [128, 32, 8192], P(('coef', 'pair')), may hold values from -66 to 66
- coefficients: bfloat16 [2, 8192, 384], P(None, ('coef', 'pair')), may hold values from -0.0625 to 0.0625
- shell_starts: int32 [8], replicated, may hold values from 0 to 8188, as said below
- pair_ids: int32 [1, 128], P('coef'), may hold values from 0 to 127, each once within a row
Outputs:
- half_ints: bfloat16 [2, 384, 384, 128], P(None, 'pair', None, 'coef')
Inputs may be any that keep to these rules, and one draw needn't show every extreme that they name: `shell_starts`: distinct multiples of 4.
All inputs are finite; a program needn't handle non-finite values.
Results may differ from a plain program's by a relative error of at most 0.0049.
Values may be sent and summed in bfloat16 or wider, within the bound.
No kernel may reach another device: no remote copies, remote signals or barrier semaphores. Data moves between devices by JAX's collectives and lax.ppermute only.
A program may use at most 64 MiB of HBM per device.

v0:
```python
import jax
import jax.numpy as jnp
from jax import lax
from jax.sharding import PartitionSpec as P

SHW = 4


def on_device(integrals, coefficients, shell_starts, pair_ids):
    slot_count, batch_rows, ao_width = integrals.shape
    occupied = coefficients.shape[2]
    flat_ints = integrals.reshape(slot_count * batch_rows, ao_width)
    offsets = jnp.arange(SHW, dtype=jnp.int32)
    batch_index = (shell_starts[:, None] + offsets[None, :]).reshape(-1)
    panel_piece = lax.all_gather(coefficients, ("coef", "pair"), axis=1, tiled=True)
    products = jnp.einsum("rn,cnj->crj", flat_ints, panel_piece, preferred_element_type=jnp.float32)
    row_count = panel_piece.shape[1]
    inside_mask = (batch_index >= 0) & (batch_index < row_count)
    safe_index = jnp.clip(batch_index, 0, row_count - 1)
    chosen = jnp.take(panel_piece, safe_index, axis=1).astype(jnp.float32)
    picked = jnp.where(inside_mask[None, :, None], chosen, 0.0)
    half_done, picked = (products, picked)
    batch_coef = picked.astype(jnp.bfloat16)
    half_done = half_done.astype(jnp.bfloat16).reshape(2, slot_count, batch_rows, occupied)
    real_part = jnp.einsum(
        "mi,kmj->kij", batch_coef[0], half_done[0], preferred_element_type=jnp.float32
    ) + jnp.einsum("mi,kmj->kij", batch_coef[1], half_done[1], preferred_element_type=jnp.float32)
    imag_part = jnp.einsum(
        "mi,kmj->kij", batch_coef[0], half_done[1], preferred_element_type=jnp.float32
    ) - jnp.einsum("mi,kmj->kij", batch_coef[1], half_done[0], preferred_element_type=jnp.float32)
    local_block = jnp.stack([real_part, imag_part]).astype(jnp.bfloat16)
    arrived = lax.all_to_all(local_block, "pair", split_axis=2, concat_axis=1, tiled=True)
    pair_order = pair_ids.reshape(-1)
    columns = jnp.arange(pair_order.shape[0], dtype=jnp.int32)
    selector = (pair_order[:, None] == columns[None, :]).astype(jnp.bfloat16)
    result = jnp.einsum("csij,sq->cijq", arrived, selector, preferred_element_type=jnp.float32)
    return result.astype(jnp.bfloat16)


def solution(mesh):
    return jax.shard_map(
        on_device,
        mesh=mesh,
        in_specs=(
            P(("coef", "pair"), None, None),
            P(None, ("coef", "pair"), None),
            P(),
            P("coef", None),
        ),
        out_specs=P(None, "pair", None, "coef"),
        check_vma=False,
    )
```

profile of v0, /device:TPU:0, one launch (start us, length us, event | category | flops | bytes accessed | tf_op | source)
XLA Modules:
  0.0 318.9 jit_solution(11575807264792634785)
XLA Ops:
  6.5 0.0 copy-start
  6.5 0.0 all-gather.2.cloned.1.call-start
  6.5 0.7 all-gather.2.cloned.1.call-update
  7.3 0.7 fusion.14
  8.0 0.1 min.18
  8.1 0.1 min.16
  8.1 0.7 fusion.17
  8.9 0.1 and.18
  9.0 99.9 %all-gather.2.cloned.1.call-done = bf16[2,8192,384]{2,1,0:T(8,128)(2,1)} async-done(((bf16[2,256,384]{2,1,0:T(8,128)(2,1)}), bf16[2,8192,384]{2,1,0:T(8,128)(2,1)}) %all-gather.2.cloned.1.call-update) | async-done | bytes 12582928 | tf_op jit(solution)/shard_map/all_gather | solution.py:15
  108.9 0.0 copy-done
  109.0 0.0 copy-start.1
  109.0 6.5 %fusion.7 = bf16[2,128,384]{2,1,0:T(8,128)(2,1)S(1)} fusion(bf16[128,8192,1]{1,0,2:T(8,128)(2,1)S(1)} %bitcast.45, bf16[2,8192,384]{2,1,0:T(8,128)(2,1)} %all-gather.2.cloned.1.call-done), kind=kOutput, calls=%fused_computation.10 | convolution fusion | flops 1610711040 | bytes 14876672 | tf_op jit(solution)/shard_map/rn,cnj->crj/dot_general | solution.py:16
  115.5 1.6 copy-done.1
  117.1 117.8 %copy.11 = bf16[2,8192,384]{2,0,1:T(2,128)(2,1)} copy(bf16[2,8192,384]{2,1,0:T(8,128)(2,1)S(1)} %copy-done.1) | data formatting | bytes 25165824 | tf_op jit(solution)/shard_map/all_gather | solution.py:15
  234.9 5.2 %gather_fusion = bf16[32,2,384]{2,1,0:T(2,128)(2,1)S(1)} fusion(bf16[2,8192,384]{2,0,1:T(2,128)(2,1)} %copy.11, s32[1024]{0:T(1024)S(1)} %pad_clamp_fusion), kind=kCustom, calls=%fused_computation | custom fusion | bytes 98432 | tf_op jit(solution)/shard_map/jit(_take)/gather | solution.py:20
  240.1 0.1 fusion.10
  240.2 0.5 fusion.13
  240.7 0.5 fusion.12
  241.2 0.5 fusion.5
  241.8 0.5 fusion.6
  242.3 1.7 pad_maximum_fusion
  243.9 5.4 %copy.13 = bf16[2,4,384,384]{3,1,0,2:T(4,128)(2,1)} copy(bf16[2,4,384,384]{2,3,1,0:T(8,128)(2,1)} %pad_maximum_fusion) | data formatting | bytes 4718592 | tf_op jit(solution)/shard_map/stack | solution.py:31
  249.3 58.6 %all_to_all.18 = bf16[2,4,384,384]{3,1,0,2:T(4,128)(2,1)S(1)} all-to-all(bf16[2,4,384,384]{3,1,0,2:T(4,128)(2,1)} %copy.13), channel_id=1, replica_groups=mesh['coef'=1,'pair'=32] {'pair'}, dimensions={2} | all-to-all | bytes 4718592 | tf_op jit(solution)/shard_map/all_to_all | solution.py:32
  307.9 0.0 copy-start.2
  307.9 1.8 copy.15
  309.7 0.0 copy-done.2
  309.7 2.3 fusion.2
  (4 shorter events, 0.0 us)
Async XLA Ops:
  6.5 102.4 %copy-start = (bf16[4,32,8192]{2,1,0:T(8,128)(2,1)S(1)}, bf16[4,32,8192]{2,1,0:T(8,128)(2,1)}, u32[]{:S(2)}) copy-start(bf16[4,32,8192]{2,1,0:T(8,128)(2,1)} %param.4) | copy-start | bytes 6291460
  6.5 102.4 %all-gather.2.cloned.1.call-start = ((), (), s32[]{:S(2)}) async-start(), calls=%async_computation.1 | async-start | bytes 12976128 | tf_op jit(solution)/shard_map/all_gather | solution.py:15
  109.0 8.2 %copy-start.1 = (bf16[2,8192,384]{2,1,0:T(8,128)(2,1)S(1)}, bf16[2,8192,384]{2,1,0:T(8,128)(2,1)}, u32[]{:S(2)}) copy-start(bf16[2,8192,384]{2,1,0:T(8,128)(2,1)} %all-gather.2.cloned.1.call-done) | copy-start | bytes 37748740
  307.9 1.8 copy-start.2
Sparse Core Ops, SparseCore 0:
  10.2 98.7 all-gather.1
where the time goes:
time: 319 us
  local copies, waits for them, and re-layouts  132 us (41%)
  waiting for transfers between devices  101 us (32%)
  blocking collectives  58.6 us (18%)
  between operations  13.5 us (4%)
  matrix products  10.8 us (3%)
  other arithmetic  3.23 us (1%)
    all_gather x1, local copies, waits for them, and re-layouts, on_device(): lax.all_gather(coefficients, ('coef', 'pair'), axis=1, tiled=True)  118 us
    all_gather x1, waiting for transfers between devices, on_device(): lax.all_gather(coefficients, ('coef', 'pair'), axis=1, tiled=True)  99.9 us
    all_to_all x1, blocking collectives, on_device(): lax.all_to_all(local_block, 'pair', split_axis=2, concat_axis=1, tiled=True)  58.6 us
    dot_general x1, matrix products, on_device(): jnp.einsum('rn,cnj->crj', flat_ints, panel_piece, preferred_element_type=...  6.54 us
  transfers between devices with their start and end apart: 1, of which 1 were waited for; matrix products, arithmetic and copies ran while one was open for 1% of the time, Pallas kernels for 0%

commit v1 on v0

v1 whole, which is shorter than its diff:
```python
import functools

import jax
import jax.numpy as jnp
from jax import lax
from jax.experimental import pallas as pl
from jax.experimental.pallas import tpu as pltpu
from jax.sharding import PartitionSpec as P

SHW = 4
LANES = 128
F32, BF16 = jnp.float32, jnp.bfloat16
VMEM_LIMIT = 40 * 1024 * 1024


class Grid:
    def __init__(self, n_pair):
        assert n_pair % 8 == 0
        self.nz = n_pair // 8
        self.ring = 2 * self.nz

    def device(self, q, y, c):
        turned = q >= self.nz
        z = jnp.where(turned, self.ring - 1 - q, q)
        x = turned.astype(jnp.int32)
        return ((z * 2 + y) * 2 + x) * 2 + c

    def number(self, q, y, c):
        z, x = (q, 0) if q < self.nz else (self.ring - 1 - q, 1)
        return ((z * 2 + y) * 2 + x) * 2 + c

    def moves(self, target):
        return [
            (self.number(q, y, c), self.number(*target(q, y, c)))
            for q in range(self.ring)
            for y in range(2)
            for c in range(2)
        ]

    def around(self, way):
        return self.moves(lambda q, y, c: ((q + (way if c == 0 else -way)) % self.ring, y, c))

    def across_y(self):
        return self.moves(lambda q, y, c: (q, 1 - y, c))

    def across_core(self):
        return self.moves(lambda q, y, c: (q, y, 1 - c))

    def offsets(self):
        found = [0]
        for step in range(1, self.nz):
            found += [-step, step]
        return found + [-self.nz]


def gather_chips(grid, first, later):
    send = functools.partial(lax.ppermute, axis_name="pair")
    around = {-1: grid.around(1), 1: grid.around(-1)}
    over_y = grid.across_y()
    pairs = {0: jnp.concatenate([first, send(first, perm=over_y)], axis=0)}
    singles = {0: later}
    for step in range(1, grid.nz + 1):
        for side in (-1, 1):
            if side == 1 and step == grid.nz:
                continue
            offset = side * step
            singles[offset] = send(singles[offset - side], perm=around[side])
            pairs[offset] = send(pairs[offset - side], perm=around[side])
    mirrored = {offset: send(block, perm=over_y) for offset, block in singles.items()}
    return pairs, singles, mirrored


def vmem(count):
    return [pl.BlockSpec(memory_space=pltpu.VMEM)] * count


PARAMS = pltpu.CompilerParams(vmem_limit_bytes=VMEM_LIMIT)


def first_product(source, own_ints, other_ints, batch_column, total, parts, last):
    width = parts[0][0].shape[1]
    rows = own_ints.shape[0]
    batch_rows = batch_column.shape[0]
    depth = min(block.shape[0] // len(slots) for block, slots in parts)
    begins = total is None

    def body(source_ref, own_ref, other_ref, batch_ref, *refs):
        refs = list(refs)
        total_ref = None if begins else refs.pop(0)
        block_refs, out_refs = refs[: len(parts)], refs[len(parts):]
        running = None if begins else total_ref[...]
        for ref, (_, slots) in zip(block_refs, parts):
            for place, slot in enumerate(slots):
                start = pl.multiple_of(source_ref[slot] * depth, depth)
                columns = pl.ds(start, depth)
                position = lax.broadcasted_iota(jnp.int32, (batch_rows, depth), 1) + start
                picks = (batch_ref[...] == position).astype(F32).astype(BF16)
                left = jnp.concatenate([own_ref[:, columns], other_ref[:, columns], picks], axis=0)
                term = jnp.dot(left, ref[place * depth:(place + 1) * depth, :], preferred_element_type=F32)
                running = term if running is None else running + term
        if last:
            out_refs[0][...] = running[:rows].astype(BF16)
            out_refs[1][...] = running[rows:].astype(BF16)
        else:
            out_refs[0][...] = running

    high = 2 * rows + batch_rows
    if last:
        shapes = [jax.ShapeDtypeStruct((rows, width), BF16), jax.ShapeDtypeStruct((high - rows, width), BF16)]
    else:
        shapes = [jax.ShapeDtypeStruct((high, width), F32)]
    operands = ([] if begins else [total]) + [block for block, _ in parts]
    return pl.pallas_call(
        body,
        out_shape=shapes,
        in_specs=[pl.BlockSpec(memory_space=pltpu.SMEM)] + vmem(3 + len(operands)),
        out_specs=vmem(len(shapes)),
        compiler_params=PARAMS,
        name="first_product",
    )(source, own_ints, other_ints, batch_column, *operands)


def weights(where, own_batch, other_batch, slots, share):
    batch_rows, width = own_batch.shape
    high = 2 * slots * 2 * share

    def body(where_ref, own_ref, other_ref, own_out, other_out):
        me = where_ref[0]
        core = lax.rem(me, 2)
        row = lax.broadcasted_iota(jnp.int32, (high, width), 0)
        column = lax.broadcasted_iota(jnp.int32, (high, width), 1)
        half = lax.div(row, high // 2)
        wanted = (me - core + lax.rem(core + half, 2)) * share + lax.rem(row, share)
        chosen = (column == wanted).astype(F32).astype(BF16)
        deep = slots * batch_rows
        repeat = (
            lax.broadcasted_iota(jnp.int32, (batch_rows, deep), 0)
            == lax.rem(lax.broadcasted_iota(jnp.int32, (batch_rows, deep), 1), batch_rows)
        ).astype(F32).astype(BF16)

        def spread(ref):
            picked = lax.dot_general(chosen, ref[...], (((1,), (1,)), ((), ())), preferred_element_type=F32)
            return jnp.dot(picked.astype(BF16), repeat, preferred_element_type=F32)

        row = lax.broadcasted_iota(jnp.int32, (high, deep), 0)
        column = lax.broadcasted_iota(jnp.int32, (high, deep), 1)
        keep = lax.rem(lax.div(row, 2 * share), slots) == lax.div(column, batch_rows)
        real = lax.rem(lax.div(row, share), 2) == 0
        own, other = spread(own_ref), spread(other_ref)
        sign = (2 * core - 1).astype(F32)
        own_out[...] = jnp.where(keep, jnp.where(real, own, sign * other), 0.0).astype(BF16)
        other_out[...] = jnp.where(keep, jnp.where(real, other, -sign * own), 0.0).astype(BF16)

    shape = jax.ShapeDtypeStruct((high, slots * batch_rows), BF16)
    return pl.pallas_call(
        body,
        out_shape=[shape, shape],
        in_specs=[pl.BlockSpec(memory_space=pltpu.SMEM)] + vmem(2),
        out_specs=vmem(2),
        compiler_params=PARAMS,
        name="weights",
    )(where, own_batch, other_batch)


def second_product(own_weights, other_weights, blocks):
    high, rows = own_weights.shape
    half = high // 2
    width = blocks[0][0].shape[1]
    flat = []
    for pair_block, _, single in blocks:
        flat += [pair_block, single]

    def body(own_ref, other_ref, *refs):
        block_refs, (mine, theirs) = refs[: len(flat)], refs[len(flat):]
        for number, (_, place, _) in enumerate(blocks):
            first, later = block_refs[2 * number], block_refs[2 * number + 1]
            both = jnp.dot(
                own_ref[...], first[place * rows:(place + 1) * rows, :], preferred_element_type=F32
            ) + jnp.dot(other_ref[...], later[...], preferred_element_type=F32)
            both = both.astype(BF16)
            mine[number * half:(number + 1) * half, :] = both[:half]
            theirs[number * half:(number + 1) * half, :] = both[half:]

    shape = jax.ShapeDtypeStruct((len(blocks) * half, width), BF16)
    return pl.pallas_call(
        body,
        out_shape=[shape, shape],
        in_specs=vmem(2 + len(flat)),
        out_specs=vmem(2),
        compiler_params=PARAMS,
        name="second_product",
    )(own_weights, other_weights, *flat)


def place_pairs(order, pair_column, pieces, share):
    width = pieces[0].shape[1]
    slots = order.shape[0]
    each = 2 * share

    def body(order_ref, pair_ref, *refs):
        piece_refs, out_ref, held = refs[: len(pieces)], refs[-2], refs[-1]
        start = 0
        for ref in piece_refs:
            for tile in range(width // LANES):
                held[tile, start:start + ref.shape[0], :] = ref[:, tile * LANES:(tile + 1) * LANES].astype(F32)
            start += ref.shape[0]
        lane = lax.broadcasted_iota(jnp.int32, (slots, slots), 1)
        ordered = (order_ref[...] == lane).astype(F32).astype(BF16)
        paired = (pair_ref[...] == lane).astype(F32).astype(BF16)
        place = jnp.dot(ordered, paired, preferred_element_type=F32).astype(BF16)
        for number in range(each):
            for tile in range(width // LANES):
                rows = held[tile, pl.ds(number, slots, stride=each), :].astype(BF16)
                placed = lax.dot_general(rows, place, (((0,), (0,)), ((), ())), preferred_element_type=F32)
                lanes = pl.ds(tile * LANES, LANES)
                out_ref[number // share, number % share, lanes, :] = placed.astype(BF16)

    return pl.pallas_call(
        body,
        out_shape=jax.ShapeDtypeStruct((2, share, width, slots), BF16),
        in_specs=vmem(2 + len(pieces)),
        out_specs=pl.BlockSpec(memory_space=pltpu.VMEM),
        scratch_shapes=[pltpu.VMEM((width // LANES, slots * each, LANES), F32)],
        compiler_params=PARAMS,
        name="place_pairs",
    )(order, pair_column, *pieces)


def on_device(n_coef, n_pair, integrals, coefficients, shell_starts, pair_ids):
    grid = Grid(n_pair)
    swap = functools.partial(lax.ppermute, axis_name="pair", perm=grid.across_core())
    slots, batch_rows, ao_width = integrals.shape
    occupied = coefficients.shape[2]
    share = occupied // n_pair
    rows = slots * batch_rows
    depth = ao_width // n_pair
    piece = depth // n_coef

    me = lax.axis_index("pair")
    core, x, y, z = me % 2, me // 2 % 2, me // 4 % 2, me // 8
    q = jnp.where(x == 0, z, grid.ring - 1 - z)

    def source_of(offset, flip, on_core, rows_core):
        spot = (q + jnp.where(on_core == 0, offset, -offset) + grid.ring) % grid.ring
        return grid.device(spot, (y + flip) % 2, rows_core)

    batch_index = (shell_starts[:, None] + jnp.arange(SHW, dtype=jnp.int32)[None, :]).reshape(-1)
    flat_ints = integrals.reshape(rows, ao_width)
    if n_coef > 1:
        coefficients = lax.all_gather(coefficients, "coef", axis=1, tiled=True)
        flat_ints = flat_ints.reshape(rows, n_coef, n_pair, piece).transpose(0, 2, 1, 3).reshape(rows, ao_width)
        batch_index = (
            batch_index // piece % n_pair * depth + batch_index // (n_pair * piece) * piece + batch_index % piece
        )
    batch_column = batch_index[:, None]

    own_rows = lax.dynamic_index_in_dim(coefficients, core, 0, keepdims=False)
    other_rows = swap(lax.dynamic_index_in_dim(coefficients, 1 - core, 0, keepdims=False))
    other_ints = swap(flat_ints)
    offsets = grid.offsets()
    groups = [offsets[:3], offsets[3:5], offsets[5:]] if len(offsets) > 5 else [offsets]

    pairs, singles, mirrored = gather_chips(grid, own_rows, other_rows)
    sources, total = [], None
    for number, group in enumerate(groups):
        parts = []
        for offset in group:
            for block, ids in (
                (pairs[offset], [(0, core), (1, core)]),
                (singles[offset], [(0, 1 - core)]),
                (mirrored[offset], [(1, 1 - core)]),
            ):
                named = [len(sources) + k for k in range(len(ids))]
                sources += [source_of(offset, flip, core, rows_core) for flip, rows_core in ids]
                parts.append((block, named))
        last = number == len(groups) - 1
        total = (total, parts, last)
        groups[number] = (group, parts, last)
    source = jnp.stack(sources).astype(jnp.int32)
    total = None
    for group, parts, last in groups:
        result = first_product(source, flat_ints, other_ints, batch_column, total, parts, last)
        total = result[0]
    half_own, leaving = result
    arrived = swap(leaving)
    half_other, other_batch = arrived[:rows], arrived[rows:]
    own_batch = leaving[rows:]

    own_weights, other_weights = weights(me[None].astype(jnp.int32), own_batch, other_batch, slots, share)
    pairs, singles, mirrored = gather_chips(grid, half_own, half_other)
    mine, theirs, mine_order, their_order = [], [], [], []
    within = jnp.arange(slots, dtype=jnp.int32)
    for group, _, _ in groups:
        blocks = []
        for offset in group:
            blocks += [(pairs[offset], 0, singles[offset]), (pairs[offset], 1, mirrored[offset])]
            for flip in range(2):
                mine_order.append(source_of(offset, flip, core, core) * slots + within)
                their_order.append(source_of(offset, flip, 1 - core, 1 - core) * slots + within)
        stay, leave = second_product(own_weights, other_weights, blocks)
        mine.append(stay)
        theirs.append(swap(leave))
    order = jnp.concatenate(mine_order + their_order)[:, None]
    return place_pairs(order, pair_ids.reshape(-1)[:, None], mine + theirs, share)


def solution(mesh):
    return jax.shard_map(
        functools.partial(on_device, mesh.shape["coef"], mesh.shape["pair"]),
        mesh=mesh,
        in_specs=(
            P(("coef", "pair"), None, None),
            P(None, ("coef", "pair"), None),
            P(),
            P("coef", None),
        ),
        out_specs=P(None, "pair", None, "coef"),
        check_vma=False,
    )
```

time: 319 us -> 133 us (0.42)
  local copies, waits for them, and re-layouts: 132 us -> 8.08 us
  blocking collectives: 58.6 us -> 0 us
  starting transfers between devices: 0.01 us -> 54.1 us
  waiting for transfers between devices: 101 us -> 56.5 us
  Pallas kernels: 0 us -> 14 us
  between operations: 13.5 us -> 0.3 us
  matrix products: 10.8 us -> 0 us
    all_gather x1 -> x0, local copies, waits for them, and re-layouts: 118 us -> none  [on_device(): lax.all_gather(coefficients, ('coef', 'pair'), axis=1, tiled=True)]
    all_gather x1 -> x0, waiting for transfers between devices: 99.9 us -> none  [on_device(): lax.all_gather(coefficients, ('coef', 'pair'), axis=1, tiled=True)]
    all_to_all x1 -> x0, blocking collectives: 58.6 us -> none  [on_device(): lax.all_to_all(local_block, 'pair', split_axis=2, concat_axis=1, tiled=True)]
    ppermute x0 -> x52, waiting for transfers between devices: none -> 56.5 us  [the longest x14 27.4 us: gather_chips(): singles[offset] = send(singles[offset - side], perm=around[side])]
    ppermute x0 -> x52, starting transfers between devices: none -> 54.1 us  [the longest x14 17.1 us: gather_chips(): singles[offset] = send(singles[offset - side], perm=around[side])]
    pallas_call x0 -> x8, Pallas kernels: none -> 14 us  [the longest x3 8.34 us: first_product(): pl.pallas_call(body, out_shape=shapes, in_specs=[pl.BlockSpec(memory_spac...]
    dot_general x6 -> x0, matrix products: 10.8 us -> none  [the longest x1 6.54 us: on_device(): jnp.einsum('rn,cnj->crj', flat_ints, panel_piece, preferred_element_type=...]
    gather x1 -> x0, local copies, waits for them, and re-layouts: 5.24 us -> none  [on_device(): chosen = jnp.take(panel_piece, safe_index, axis=1).astype(jnp.float32)]
  transfers between devices with their start and end apart: 1 -> 52, of which waited for: 1 -> 18; matrix products, arithmetic and copies ran while one was open for 1% -> 1% of each run, Pallas kernels for 0% -> 6%
where the time goes in v1:
time: 133 us
  waiting for transfers between devices  56.5 us (42%)
  starting transfers between devices  54.1 us (41%)
  Pallas kernels  14 us (11%)
  local copies, waits for them, and re-layouts  8.08 us (6%)
    ppermute x14, waiting for transfers between devices, gather_chips(): singles[offset] = send(singles[offset - side], perm=around[side])  27.4 us
    ppermute x14, starting transfers between devices, gather_chips(): singles[offset] = send(singles[offset - side], perm=around[side])  17.1 us
    ppermute x16, starting transfers between devices, gather_chips(): send(block, perm=over_y)  16.5 us
    ppermute x14, starting transfers between devices, gather_chips(): pairs[offset] = send(pairs[offset - side], perm=around[side])  16.4 us
    ppermute x16, waiting for transfers between devices, gather_chips(): send(block, perm=over_y)  13.1 us
    ppermute x2, waiting for transfers between devices, gather_chips(): pairs = {0: jnp.concatenate([first, send(first, perm=over_y)], axis=0)}  9.31 us
    pallas_call x3, Pallas kernels, first_product(): pl.pallas_call(body, out_shape=shapes, in_specs=[pl.BlockSpec(memory_spac...  8.34 us
    unnamed x23, local copies, waits for them, and re-layouts  6.47 us
  transfers between devices with their start and end apart: 52, of which 18 were waited for; matrix products, arithmetic and copies ran while one was open for 1% of the time, Pallas kernels for 6%

profile of v1, /device:TPU:0, one launch (start us, length us, event | category | flops | bytes accessed | tf_op | source)
XLA Modules:
  0.0 133.2 jit_solution(15895774001308891741)
XLA Ops:
  0.5 1.1 dynamic-slice_bitcast_fusion
  1.5 2.8 %collective-permute-start.1 = (bf16[256,384]{1,0:T(8,128)(2,1)S(1)}, bf16[256,384]{1,0:T(8,128)(2,1)S(1)}, u32[]{:S(2)}, u32[]{:S(2)}) collective-permute-start(bf16[256,384]{1,0:T(8,128)(2,1)S(1)} %get-tuple-element.26), channel_id=1, source_target_pairs={{0,4},{1,5},{4,0},{5,1},{8,12},{9,13},{12,8},{13,9},{16,20},{17,21... | collective-permute-start | bytes 589832 | tf_op jit(solution)/shard_map/ppermute | solution.py:60
  4.3 5.3 %collective-permute-done.1 = bf16[256,384]{1,0:T(8,128)(2,1)S(1)} collective-permute-done((bf16[256,384]{1,0:T(8,128)(2,1)S(1)}, bf16[256,384]{1,0:T(8,128)(2,1)S(1)}, u32[]{:S(2)}, u32[]{:S(2)}) %collective-permute-start.1) | collective-permute-done | bytes 196640 | tf_op jit(solution)/shard_map/ppermute | solution.py:60
  9.7 1.8 %collective-permute-start.4 = (bf16[512,384]{1,0:T(8,128)(2,1)S(1)}, bf16[512,384]{1,0:T(8,128)(2,1)S(1)}, u32[]{:S(2)}, u32[]{:S(2)}) collective-permute-start(bf16[512,384]{1,0:T(8,128)(2,1)S(1)} %pad_maximum_fusion.refs_0_), channel_id=1, source_target_pairs={{0,8},{1,3},{4,12},{5,7},{8,16},{9,1},{12,20},{13,5},{16,24},{17,9... | collective-permute-start | bytes 1179656 | tf_op jit(solution)/shard_map/ppermute | solution.py:68
  11.6 1.6 %collective-permute-start.5 = (bf16[256,384]{1,0:T(8,128)(2,1)S(1)}, bf16[256,384]{1,0:T(8,128)(2,1)S(1)}, u32[]{:S(2)}, u32[]{:S(2)}) collective-permute-start(bf16[256,384]{1,0:T(8,128)(2,1)S(1)} %collective-permute-done.2.refs_1_), channel_id=1, source_target_pairs={{0,8},{1,3},{4,12},{5,7},{8,16},{9,1},{12,20},{13,5},{16,24},{17,9... | collective-permute-start | bytes 589832 | tf_op jit(solution)/shard_map/ppermute | solution.py:67
  13.8 11.4 %collective-permute-done.5.refs_4_ = bf16[256,384]{1,0:T(8,128)(2,1)S(1)} collective-permute-done((bf16[256,384]{1,0:T(8,128)(2,1)S(1)}, bf16[256,384]{1,0:T(8,128)(2,1)S(1)}, u32[]{:S(2)}, u32[]{:S(2)}) %collective-permute-start.5) | collective-permute-done | bytes 196640 | tf_op jit(solution)/shard_map/ppermute | solution.py:67
  25.3 1.5 %collective-permute-start.3 = (bf16[256,384]{1,0:T(8,128)(2,1)S(1)}, bf16[256,384]{1,0:T(8,128)(2,1)S(1)}, u32[]{:S(2)}, u32[]{:S(2)}) collective-permute-start(bf16[256,384]{1,0:T(8,128)(2,1)S(1)} %collective-permute-done.2.refs_1_), channel_id=1, source_target_pairs={{0,4},{1,5},{4,0},{5,1},{8,12},{9,13},{12,8},{13,9},{16,20},{17,21... | collective-permute-start | bytes 589832 | tf_op jit(solution)/shard_map/ppermute | solution.py:69
  26.8 2.5 %collective-permute-start.10 = (bf16[512,384]{1,0:T(8,128)(2,1)S(1)}, bf16[512,384]{1,0:T(8,128)(2,1)}, u32[]{:S(2)}, u32[]{:S(2)}) collective-permute-start(bf16[512,384]{1,0:T(8,128)(2,1)S(1)} %collective-permute-done.4.refs_3_), channel_id=1, source_target_pairs={{0,8},{1,3},{4,12},{5,7},{8,16},{9,1},{12,20},{13,5},{16,24},{17,9... | collective-permute-start | bytes 1179656 | tf_op jit(solution)/shard_map/ppermute | solution.py:68
  29.8 3.3 %collective-permute-done.3.refs_2_ = bf16[256,384]{1,0:T(8,128)(2,1)S(1)} collective-permute-done((bf16[256,384]{1,0:T(8,128)(2,1)S(1)}, bf16[256,384]{1,0:T(8,128)(2,1)S(1)}, u32[]{:S(2)}, u32[]{:S(2)}) %collective-permute-start.3) | collective-permute-done | bytes 196640 | tf_op jit(solution)/shard_map/ppermute | solution.py:69
  33.0 0.7 copy-done.3
  33.7 2.4 %collective-permute-start.11 = (bf16[256,384]{1,0:T(8,128)(2,1)S(1)}, bf16[256,384]{1,0:T(8,128)(2,1)}, u32[]{:S(2)}, u32[]{:S(2)}) collective-permute-start(bf16[256,384]{1,0:T(8,128)(2,1)S(1)} %collective-permute-done.5.refs_4_), channel_id=1, source_target_pairs={{0,8},{1,3},{4,12},{5,7},{8,16},{9,1},{12,20},{13,5},{16,24},{17,9... | collective-permute-start | bytes 589832 | tf_op jit(solution)/shard_map/ppermute | solution.py:67
  36.2 0.7 copy-done.1
  36.9 1.5 %collective-permute-start.9 = (bf16[256,384]{1,0:T(8,128)(2,1)}, bf16[256,384]{1,0:T(8,128)(2,1)S(1)}, u32[]{:S(2)}, u32[]{:S(2)}) collective-permute-start(bf16[256,384]{1,0:T(8,128)(2,1)} %collective-permute-done.8.refs_7_), channel_id=1, source_target_pairs={{0,4},{1,5},{4,0},{5,1},{8,12},{9,13},{12,8},{13,9},{16,20},{17,21... | collective-permute-start | bytes 589832 | tf_op jit(solution)/shard_map/ppermute | solution.py:69
  38.4 0.7 copy-done.5
  39.1 2.2 %collective-permute-done.11.refs_2_ = bf16[256,384]{1,0:T(8,128)(2,1)} collective-permute-done((bf16[256,384]{1,0:T(8,128)(2,1)S(1)}, bf16[256,384]{1,0:T(8,128)(2,1)}, u32[]{:S(2)}, u32[]{:S(2)}) %collective-permute-start.11) | collective-permute-done | bytes 196640 | tf_op jit(solution)/shard_map/ppermute | solution.py:67
  41.2 1.7 %collective-permute-start.12 = (bf16[256,384]{1,0:T(8,128)(2,1)}, bf16[256,384]{1,0:T(8,128)(2,1)}, u32[]{:S(2)}, u32[]{:S(2)}) collective-permute-start(bf16[256,384]{1,0:T(8,128)(2,1)} %collective-permute-done.11.refs_2_), channel_id=1, source_target_pairs={{0,4},{1,5},{4,0},{5,1},{8,12},{9,13},{12,8},{13,9},{16,20},{17,21... | collective-permute-start | bytes 589832 | tf_op jit(solution)/shard_map/ppermute | solution.py:69
  42.9 0.7 copy-done.7
  43.6 1.3 collective-permute-start.13
  44.9 0.7 collective-permute-start.16
  45.6 1.6 %collective-permute-done.14.refs_5_ = bf16[256,384]{1,0:T(8,128)(2,1)} collective-permute-done((bf16[256,384]{1,0:T(8,128)(2,1)}, bf16[256,384]{1,0:T(8,128)(2,1)}, u32[]{:S(2)}, u32[]{:S(2)}) %collective-permute-start.14) | collective-permute-done | bytes 196640 | tf_op jit(solution)/shard_map/ppermute | solution.py:67
  47.2 1.3 collective-permute-start.17
  49.1 1.5 %collective-permute-start.15 = (bf16[256,384]{1,0:T(8,128)(2,1)}, bf16[256,384]{1,0:T(8,128)(2,1)}, u32[]{:S(2)}, u32[]{:S(2)}) collective-permute-start(bf16[256,384]{1,0:T(8,128)(2,1)} %collective-permute-done.14.refs_5_), channel_id=1, source_target_pairs={{0,4},{1,5},{4,0},{5,1},{8,12},{9,13},{12,8},{13,9},{16,20},{17,21... | collective-permute-start | bytes 589832 | tf_op jit(solution)/shard_map/ppermute | solution.py:69
  50.9 4.2 %collective-permute-done.15.refs_6_ = bf16[256,384]{1,0:T(8,128)(2,1)} collective-permute-done((bf16[256,384]{1,0:T(8,128)(2,1)}, bf16[256,384]{1,0:T(8,128)(2,1)}, u32[]{:S(2)}, u32[]{:S(2)}) %collective-permute-start.15) | collective-permute-done | bytes 196640 | tf_op jit(solution)/shard_map/ppermute | solution.py:69
  55.1 1.3 collective-permute-start.20
  56.4 1.8 %collective-permute-done.17.refs_2_ = bf16[256,384]{1,0:T(8,128)(2,1)} collective-permute-done((bf16[256,384]{1,0:T(8,128)(2,1)}, bf16[256,384]{1,0:T(8,128)(2,1)}, u32[]{:S(2)}, u32[]{:S(2)}) %collective-permute-start.17) | collective-permute-done | bytes 196640 | tf_op jit(solution)/shard_map/ppermute | solution.py:67
  58.2 0.7 collective-permute-start.23
  58.9 1.5 %collective-permute-start.19 = (bf16[512,384]{1,0:T(8,128)(2,1)}, bf16[512,384]{1,0:T(8,128)(2,1)S(1)}, u32[]{:S(2)}, u32[]{:S(2)}) collective-permute-start(bf16[512,384]{1,0:T(8,128)(2,1)} %collective-permute-done.13.refs_4_), channel_id=1, source_target_pairs={{0,2},{1,9},{4,6},{5,13},{8,0},{9,17},{12,4},{13,21},{16,8},{17,25... | collective-permute-start | bytes 1179656 | tf_op jit(solution)/shard_map/ppermute | solution.py:68
  60.9 2.2 %collective-permute-done.20.refs_5_ = bf16[256,384]{1,0:T(8,128)(2,1)S(1)} collective-permute-done((bf16[256,384]{1,0:T(8,128)(2,1)}, bf16[256,384]{1,0:T(8,128)(2,1)S(1)}, u32[]{:S(2)}, u32[]{:S(2)}) %collective-permute-start.20) | collective-permute-done | bytes 196640 | tf_op jit(solution)/shard_map/ppermute | solution.py:67
  63.2 1.5 %collective-permute-start.18 = (bf16[256,384]{1,0:T(8,128)(2,1)}, bf16[256,384]{1,0:T(8,128)(2,1)S(1)}, u32[]{:S(2)}, u32[]{:S(2)}) collective-permute-start(bf16[256,384]{1,0:T(8,128)(2,1)} %collective-permute-done.17.refs_2_), channel_id=1, source_target_pairs={{0,4},{1,5},{4,0},{5,1},{8,12},{9,13},{12,8},{13,9},{16,20},{17,21... | collective-permute-start | bytes 589832 | tf_op jit(solution)/shard_map/ppermute | solution.py:69
  64.7 0.6 collective-permute-start.21
  65.3 1.4 %collective-permute-start.24 = (bf16[256,384]{1,0:T(8,128)(2,1)S(1)}, bf16[256,384]{1,0:T(8,128)(2,1)S(1)}, u32[]{:S(2)}, u32[]{:S(2)}) collective-permute-start(bf16[256,384]{1,0:T(8,128)(2,1)S(1)} %collective-permute-done.23.refs_8_), channel_id=1, source_target_pairs={{0,4},{1,5},{4,0},{5,1},{8,12},{9,13},{12,8},{13,9},{16,20},{17,21... | collective-permute-start | bytes 589832 | tf_op jit(solution)/shard_map/ppermute | solution.py:69
  66.7 0.9 copy-done.2
  67.7 0.9 copy-done.4
  68.6 0.9 copy-done.6
  69.5 0.9 copy-done.8
  70.4 2.7 %first_product.3.refs_0_ = f32[288,384]{1,0:T(8,128)S(1)} custom-call(s32[32]{0:T(128)S(1)} %stack.131.source_ref, bf16[128,8192]{1,0:T(8,128)(2,1)S(1)} %bitcast.41, bf16[128,8192]{1,0:T(8,128)(2,1)} %collective-permute-done.other_ref, s32[32,1]{1,0:T(8,128)S(1)} %add.1248.batch_ref, bf16[512,384]{1,0:T(8,128)(2,1)S(1)} %pad_maximum_fusion.refs_0_, ...), custom_call_target="tpu_custom_call" | custom-call | tf_op jit(solution)/shard_map/first_product/pallas_call | solution.py:113
  73.1 2.8 %first_product.4.refs_0_ = f32[288,384]{1,0:T(8,128)S(1)} custom-call(s32[32]{0:T(128)S(1)} %stack.131.source_ref, bf16[128,8192]{1,0:T(8,128)(2,1)S(1)} %bitcast.42, bf16[128,8192]{1,0:T(8,128)(2,1)} %collective-permute-done.other_ref, s32[32,1]{1,0:T(8,128)S(1)} %add.1248.batch_ref, f32[288,384]{1,0:T(8,128)S(1)} %first_product.3.refs_0_, ...), custom_call_target="tpu_custom_call" | custom-call | tf_op jit(solution)/shard_map/first_product/pallas_call | solution.py:113
  76.0 2.8 %first_product.5 = (bf16[128,384]{1,0:T(8,128)(2,1)S(1)}, bf16[160,384]{1,0:T(8,128)(2,1)S(1)}) custom-call(s32[32]{0:T(128)S(1)} %stack.131.source_ref, bf16[128,8192]{1,0:T(8,128)(2,1)S(1)} %bitcast.43, bf16[128,8192]{1,0:T(8,128)(2,1)} %collective-permute-done.other_ref, s32[32,1]{1,0:T(8,128)S(1)} %add.1248.batch_ref, ...), custom_call_target="tpu_custom_call" | custom-call | tf_op jit(solution)/shard_map/first_product/pallas_call | solution.py:113
  78.9 0.7 collective-permute-start.26
  79.6 4.0 %collective-permute-done.26 = bf16[128,384]{1,0:T(8,128)(2,1)S(1)} collective-permute-done((bf16[128,384]{1,0:T(8,128)(2,1)S(1)}, bf16[128,384]{1,0:T(8,128)(2,1)S(1)}, u32[]{:S(2)}, u32[]{:S(2)}) %collective-permute-start.26) | collective-permute-done | bytes 98336 | tf_op jit(solution)/shard_map/ppermute | solution.py:60
  83.6 1.0 collective-permute-start.28
  84.6 1.1 collective-permute-start.31
  85.8 5.2 %collective-permute-done.28.refs_4_.refs_6_ = bf16[256,384]{1,0:T(8,128)(2,1)S(1)} collective-permute-done((bf16[256,384]{1,0:T(8,128)(2,1)S(1)}, bf16[256,384]{1,0:T(8,128)(2,1)S(1)}, u32[]{:S(2)}, u32[]{:S(2)}) %collective-permute-start.28) | collective-permute-done | bytes 196640 | tf_op jit(solution)/shard_map/ppermute | solution.py:68
  91.0 1.4 %collective-permute-start.34 = (bf16[256,384]{1,0:T(8,128)(2,1)S(1)}, bf16[256,384]{1,0:T(8,128)(2,1)S(1)}, u32[]{:S(2)}, u32[]{:S(2)}) collective-permute-start(bf16[256,384]{1,0:T(8,128)(2,1)S(1)} %collective-permute-done.28.refs_4_.refs_6_), channel_id=1, source_target_pairs={{0,8},{1,3},{4,12},{5,7},{8,16},{9,1},{12,20},{13,5},{16,24},{17,9... | collective-permute-start | bytes 589832 | tf_op jit(solution)/shard_map/ppermute | solution.py:68
  92.4 2.0 %collective-permute-start.32 = (bf16[128,384]{1,0:T(8,128)(2,1)S(1)}, bf16[128,384]{1,0:T(8,128)(2,1)S(1)}, u32[]{:S(2)}, u32[]{:S(2)}) collective-permute-start(bf16[128,384]{1,0:T(8,128)(2,1)S(1)} %slice.13.refs_1_), channel_id=1, source_target_pairs={{0,2},{1,9},{4,6},{5,13},{8,0},{9,17},{12,4},{13,21},{16,8},{17,25... | collective-permute-start | bytes 294920 | tf_op jit(solution)/shard_map/ppermute | solution.py:67
  94.7 3.9 %collective-permute-done.29.refs_5_ = bf16[128,384]{1,0:T(8,128)(2,1)S(1)} collective-permute-done((bf16[128,384]{1,0:T(8,128)(2,1)S(1)}, bf16[128,384]{1,0:T(8,128)(2,1)S(1)}, u32[]{:S(2)}, u32[]{:S(2)}) %collective-permute-start.29) | collective-permute-done | bytes 98336 | tf_op jit(solution)/shard_map/ppermute | solution.py:67
  98.6 2.3 %collective-permute-start.35 = (bf16[128,384]{1,0:T(8,128)(2,1)S(1)}, bf16[128,384]{1,0:T(8,128)(2,1)S(1)}, u32[]{:S(2)}, u32[]{:S(2)}) collective-permute-start(bf16[128,384]{1,0:T(8,128)(2,1)S(1)} %collective-permute-done.29.refs_5_), channel_id=1, source_target_pairs={{0,8},{1,3},{4,12},{5,7},{8,16},{9,1},{12,20},{13,5},{16,24},{17,9... | collective-permute-start | bytes 294920 | tf_op jit(solution)/shard_map/ppermute | solution.py:67
  101.4 1.5 %collective-permute-start.40 = (bf16[256,384]{1,0:T(8,128)(2,1)S(1)}, bf16[256,384]{1,0:T(8,128)(2,1)S(1)}, u32[]{:S(2)}, u32[]{:S(2)}) collective-permute-start(bf16[256,384]{1,0:T(8,128)(2,1)S(1)} %collective-permute-done.34.refs_0_.refs_2_), channel_id=1, source_target_pairs={{0,8},{1,3},{4,12},{5,7},{8,16},{9,1},{12,20},{13,5},{16,24},{17,9... | collective-permute-start | bytes 589832 | tf_op jit(solution)/shard_map/ppermute | solution.py:68
  103.2 0.9 collective-permute-start.38
  104.1 2.3 %collective-permute-start.41 = (bf16[128,384]{1,0:T(8,128)(2,1)S(1)}, bf16[128,384]{1,0:T(8,128)(2,1)S(1)}, u32[]{:S(2)}, u32[]{:S(2)}) collective-permute-start(bf16[128,384]{1,0:T(8,128)(2,1)S(1)} %collective-permute-done.35.refs_1_), channel_id=1, source_target_pairs={{0,8},{1,3},{4,12},{5,7},{8,16},{9,1},{12,20},{13,5},{16,24},{17,9... | collective-permute-start | bytes 294920 | tf_op jit(solution)/shard_map/ppermute | solution.py:67
  106.4 4.3 %collective-permute-done.38.refs_5_ = bf16[128,384]{1,0:T(8,128)(2,1)S(1)} collective-permute-done((bf16[128,384]{1,0:T(8,128)(2,1)S(1)}, bf16[128,384]{1,0:T(8,128)(2,1)S(1)}, u32[]{:S(2)}, u32[]{:S(2)}) %collective-permute-start.38) | collective-permute-done | bytes 98336 | tf_op jit(solution)/shard_map/ppermute | solution.py:67
  111.3 1.4 %collective-permute-start.47 = (bf16[128,384]{1,0:T(8,128)(2,1)S(1)}, bf16[128,384]{1,0:T(8,128)(2,1)S(1)}, u32[]{:S(2)}, u32[]{:S(2)}) collective-permute-start(bf16[128,384]{1,0:T(8,128)(2,1)S(1)} %collective-permute-done.41.refs_1_), channel_id=1, source_target_pairs={{0,8},{1,3},{4,12},{5,7},{8,16},{9,1},{12,20},{13,5},{16,24},{17,9... | collective-permute-start | bytes 294920 | tf_op jit(solution)/shard_map/ppermute | solution.py:67
  112.8 0.6 collective-permute-start.43
  113.4 1.4 %collective-permute-start.46 = (bf16[256,384]{1,0:T(8,128)(2,1)S(1)}, bf16[256,384]{1,0:T(8,128)(2,1)S(1)}, u32[]{:S(2)}, u32[]{:S(2)}) collective-permute-start(bf16[256,384]{1,0:T(8,128)(2,1)S(1)} %collective-permute-done.40.refs_0_.refs_2_), channel_id=1, source_target_pairs={{0,8},{1,3},{4,12},{5,7},{8,16},{9,1},{12,20},{13,5},{16,24},{17,9... | collective-permute-start | bytes 589832 | tf_op jit(solution)/shard_map/ppermute | solution.py:68
  115.3 1.5 %collective-permute-start.42 = (bf16[128,384]{1,0:T(8,128)(2,1)S(1)}, bf16[128,384]{1,0:T(8,128)(2,1)S(1)}, u32[]{:S(2)}, u32[]{:S(2)}) collective-permute-start(bf16[128,384]{1,0:T(8,128)(2,1)S(1)} %collective-permute-done.41.refs_1_), channel_id=1, source_target_pairs={{0,4},{1,5},{4,0},{5,1},{8,12},{9,13},{12,8},{13,9},{16,20},{17,21... | collective-permute-start | bytes 294920 | tf_op jit(solution)/shard_map/ppermute | solution.py:69
  117.3 1.5 %collective-permute-start.48 = (bf16[128,384]{1,0:T(8,128)(2,1)S(1)}, bf16[128,384]{1,0:T(8,128)(2,1)S(1)}, u32[]{:S(2)}, u32[]{:S(2)}) collective-permute-start(bf16[128,384]{1,0:T(8,128)(2,1)S(1)} %collective-permute-done.47.refs_9_), channel_id=1, source_target_pairs={{0,4},{1,5},{4,0},{5,1},{8,12},{9,13},{12,8},{13,9},{16,20},{17,21... | collective-permute-start | bytes 294920 | tf_op jit(solution)/shard_map/ppermute | solution.py:69
  120.1 1.4 %collective-permute-done.45.refs_7_ = bf16[128,384]{1,0:T(8,128)(2,1)S(1)} collective-permute-done((bf16[128,384]{1,0:T(8,128)(2,1)S(1)}, bf16[128,384]{1,0:T(8,128)(2,1)S(1)}, u32[]{:S(2)}, u32[]{:S(2)}) %collective-permute-start.45) | collective-permute-done | bytes 98336 | tf_op jit(solution)/shard_map/ppermute | solution.py:69
  121.4 1.0 collective-permute-start.36
  122.5 1.0 collective-permute-start.39
  124.2 2.1 %collective-permute-done.36.refs_3_ = bf16[128,384]{1,0:T(8,128)(2,1)S(1)} collective-permute-done((bf16[128,384]{1,0:T(8,128)(2,1)S(1)}, bf16[128,384]{1,0:T(8,128)(2,1)S(1)}, u32[]{:S(2)}, u32[]{:S(2)}) %collective-permute-start.36) | collective-permute-done | bytes 98336 | tf_op jit(solution)/shard_map/ppermute | solution.py:69
  126.3 1.1 collective-permute-done.39.refs_7_
  127.4 1.2 second_product.4
  128.9 1.4 %collective-permute-done.50.refs_4_ = bf16[384,384]{1,0:T(8,128)(2,1)S(1)} collective-permute-done((bf16[384,384]{1,0:T(8,128)(2,1)}, bf16[384,384]{1,0:T(8,128)(2,1)S(1)}, u32[]{:S(2)}, u32[]{:S(2)}) %collective-permute-start.50) | collective-permute-done | bytes 294944 | tf_op jit(solution)/shard_map/ppermute | solution.py:302
  130.4 2.8 %place_pairs.1 = bf16[2,12,384,128]{3,2,1,0:T(8,128)(2,1)} custom-call(s32[128,1]{1,0:T(8,128)S(1)} %copy.13.order_ref, s32[128,1]{1,0:T(8,128)S(1)} %copy.14.pair_ref, bf16[576,384]{1,0:T(8,128)(2,1)S(1)} %get-tuple-element.19.refs_0_, bf16[384,384]{1,0:T(8,128)(2,1)S(1)} %get-tuple-element.20.refs_1_, bf16[576,384]{1,0:T(8,128)(2,1)S(1)} %get-tuple-element.21.refs_2_, ...), custom_call_target="tpu_custom_call" | custom-call | tf_op jit(solution)/shard_map/place_pairs/pallas_call | solution.py:218
  (99 shorter events, 8.4 us)
Async XLA Ops:
  0.0 66.7 %copy-start = (bf16[4,32,8192]{2,1,0:T(8,128)(2,1)S(1)}, bf16[4,32,8192]{2,1,0:T(8,128)(2,1)}, u32[]{:S(2)}) copy-start(bf16[4,32,8192]{2,1,0:T(8,128)(2,1)} %param.4) | copy-start | bytes 6291460
  0.0 50.7 %copy-start.10 = (s32[8]{0:T(128)S(1)}, s32[8]{0:T(128)}, u32[]{:S(2)}) copy-start(s32[8]{0:T(128)} %param.6) | copy-start | bytes 100
  0.0 65.3 %collective-permute-start = (bf16[128,8192]{1,0:T(8,128)(2,1)}, bf16[128,8192]{1,0:T(8,128)(2,1)}, u32[]{:S(2)}, u32[]{:S(2)}) collective-permute-start(bf16[128,8192]{1,0:T(8,128)(2,1)} %bitcast.40), channel_id=1, source_target_pairs={{0,1},{1,0},{4,5},{5,4},{8,9},{9,8},{12,13},{13,12},{16,17},{17,16... | collective-permute-start | bytes 6291464 | tf_op jit(solution)/shard_map/ppermute | solution.py:259
  1.5 8.2 %collective-permute-start.1 = (bf16[256,384]{1,0:T(8,128)(2,1)S(1)}, bf16[256,384]{1,0:T(8,128)(2,1)S(1)}, u32[]{:S(2)}, u32[]{:S(2)}) collective-permute-start(bf16[256,384]{1,0:T(8,128)(2,1)S(1)} %get-tuple-element.26), channel_id=1, source_target_pairs={{0,4},{1,5},{4,0},{5,1},{8,12},{9,13},{12,8},{13,9},{16,20},{17,21... | collective-permute-start | bytes 589832 | tf_op jit(solution)/shard_map/ppermute | solution.py:60
  4.3 7.3 %collective-permute-start.2 = (bf16[256,384]{1,0:T(8,128)(2,1)S(1)}, bf16[256,384]{1,0:T(8,128)(2,1)S(1)}, u32[]{:S(2)}, u32[]{:S(2)}) collective-permute-start(bf16[256,384]{1,0:T(8,128)(2,1)S(1)} %get-tuple-element.25), channel_id=1, source_target_pairs={{0,1},{1,0},{4,5},{5,4},{8,9},{9,8},{12,13},{13,12},{16,17},{17,16... | collective-permute-start | bytes 589832 | tf_op jit(solution)/shard_map/ppermute | solution.py:258
  9.7 17.1 %collective-permute-start.4 = (bf16[512,384]{1,0:T(8,128)(2,1)S(1)}, bf16[512,384]{1,0:T(8,128)(2,1)S(1)}, u32[]{:S(2)}, u32[]{:S(2)}) collective-permute-start(bf16[512,384]{1,0:T(8,128)(2,1)S(1)} %pad_maximum_fusion.refs_0_), channel_id=1, source_target_pairs={{0,8},{1,3},{4,12},{5,7},{8,16},{9,1},{12,20},{13,5},{16,24},{17,9... | collective-permute-start | bytes 1179656 | tf_op jit(solution)/shard_map/ppermute | solution.py:68
  11.6 13.7 %collective-permute-start.5 = (bf16[256,384]{1,0:T(8,128)(2,1)S(1)}, bf16[256,384]{1,0:T(8,128)(2,1)S(1)}, u32[]{:S(2)}, u32[]{:S(2)}) collective-permute-start(bf16[256,384]{1,0:T(8,128)(2,1)S(1)} %collective-permute-done.2.refs_1_), channel_id=1, source_target_pairs={{0,8},{1,3},{4,12},{5,7},{8,16},{9,1},{12,20},{13,5},{16,24},{17,9... | collective-permute-start | bytes 589832 | tf_op jit(solution)/shard_map/ppermute | solution.py:67
  13.2 23.7 %collective-permute-start.7 = (bf16[512,384]{1,0:T(8,128)(2,1)S(1)}, bf16[512,384]{1,0:T(8,128)(2,1)S(1)}, u32[]{:S(2)}, u32[]{:S(2)}) collective-permute-start(bf16[512,384]{1,0:T(8,128)(2,1)S(1)} %pad_maximum_fusion.refs_0_), channel_id=1, source_target_pairs={{0,2},{1,9},{4,6},{5,13},{8,0},{9,17},{12,4},{13,21},{16,8},{17,25... | collective-permute-start | bytes 1179656 | tf_op jit(solution)/shard_map/ppermute | solution.py:68
  13.6 15.6 %collective-permute-start.8 = (bf16[256,384]{1,0:T(8,128)(2,1)S(1)}, bf16[256,384]{1,0:T(8,128)(2,1)}, u32[]{:S(2)}, u32[]{:S(2)}) collective-permute-start(bf16[256,384]{1,0:T(8,128)(2,1)S(1)} %collective-permute-done.2.refs_1_), channel_id=1, source_target_pairs={{0,2},{1,9},{4,6},{5,13},{8,0},{9,17},{12,4},{13,21},{16,8},{17,25... | collective-permute-start | bytes 589832 | tf_op jit(solution)/shard_map/ppermute | solution.py:67
  25.3 7.8 %collective-permute-start.3 = (bf16[256,384]{1,0:T(8,128)(2,1)S(1)}, bf16[256,384]{1,0:T(8,128)(2,1)S(1)}, u32[]{:S(2)}, u32[]{:S(2)}) collective-permute-start(bf16[256,384]{1,0:T(8,128)(2,1)S(1)} %collective-permute-done.2.refs_1_), channel_id=1, source_target_pairs={{0,4},{1,5},{4,0},{5,1},{8,12},{9,13},{12,8},{13,9},{16,20},{17,21... | collective-permute-start | bytes 589832 | tf_op jit(solution)/shard_map/ppermute | solution.py:69
  26.8 18.1 %collective-permute-start.10 = (bf16[512,384]{1,0:T(8,128)(2,1)S(1)}, bf16[512,384]{1,0:T(8,128)(2,1)}, u32[]{:S(2)}, u32[]{:S(2)}) collective-permute-start(bf16[512,384]{1,0:T(8,128)(2,1)S(1)} %collective-permute-done.4.refs_3_), channel_id=1, source_target_pairs={{0,8},{1,3},{4,12},{5,7},{8,16},{9,1},{12,20},{13,5},{16,24},{17,9... | collective-permute-start | bytes 1179656 | tf_op jit(solution)/shard_map/ppermute | solution.py:68
  29.2 9.1 %collective-permute-start.6 = (bf16[256,384]{1,0:T(8,128)(2,1)S(1)}, bf16[256,384]{1,0:T(8,128)(2,1)S(1)}, u32[]{:S(2)}, u32[]{:S(2)}) collective-permute-start(bf16[256,384]{1,0:T(8,128)(2,1)S(1)} %collective-permute-done.5.refs_4_), channel_id=1, source_target_pairs={{0,4},{1,5},{4,0},{5,1},{8,12},{9,13},{12,8},{13,9},{16,20},{17,21... | collective-permute-start | bytes 589832 | tf_op jit(solution)/shard_map/ppermute | solution.py:69
  33.0 0.7 copy-start.3
  33.7 7.5 %collective-permute-start.11 = (bf16[256,384]{1,0:T(8,128)(2,1)S(1)}, bf16[256,384]{1,0:T(8,128)(2,1)}, u32[]{:S(2)}, u32[]{:S(2)}) collective-permute-start(bf16[256,384]{1,0:T(8,128)(2,1)S(1)} %collective-permute-done.5.refs_4_), channel_id=1, source_target_pairs={{0,8},{1,3},{4,12},{5,7},{8,16},{9,1},{12,20},{13,5},{16,24},{17,9... | collective-permute-start | bytes 589832 | tf_op jit(solution)/shard_map/ppermute | solution.py:67
  36.2 0.7 copy-start.1
  36.9 6.1 %collective-permute-start.9 = (bf16[256,384]{1,0:T(8,128)(2,1)}, bf16[256,384]{1,0:T(8,128)(2,1)S(1)}, u32[]{:S(2)}, u32[]{:S(2)}) collective-permute-start(bf16[256,384]{1,0:T(8,128)(2,1)} %collective-permute-done.8.refs_7_), channel_id=1, source_target_pairs={{0,4},{1,5},{4,0},{5,1},{8,12},{9,13},{12,8},{13,9},{16,20},{17,21... | collective-permute-start | bytes 589832 | tf_op jit(solution)/shard_map/ppermute | solution.py:69
  38.4 0.7 copy-start.5
  39.1 8.2 %collective-permute-start.14 = (bf16[256,384]{1,0:T(8,128)(2,1)}, bf16[256,384]{1,0:T(8,128)(2,1)}, u32[]{:S(2)}, u32[]{:S(2)}) collective-permute-start(bf16[256,384]{1,0:T(8,128)(2,1)} %collective-permute-done.8.refs_7_), channel_id=1, source_target_pairs={{0,2},{1,9},{4,6},{5,13},{8,0},{9,17},{12,4},{13,21},{16,8},{17,25... | collective-permute-start | bytes 589832 | tf_op jit(solution)/shard_map/ppermute | solution.py:67
  41.2 7.9 %collective-permute-start.12 = (bf16[256,384]{1,0:T(8,128)(2,1)}, bf16[256,384]{1,0:T(8,128)(2,1)}, u32[]{:S(2)}, u32[]{:S(2)}) collective-permute-start(bf16[256,384]{1,0:T(8,128)(2,1)} %collective-permute-done.11.refs_2_), channel_id=1, source_target_pairs={{0,4},{1,5},{4,0},{5,1},{8,12},{9,13},{12,8},{13,9},{16,20},{17,21... | collective-permute-start | bytes 589832 | tf_op jit(solution)/shard_map/ppermute | solution.py:69
  42.9 0.7 copy-start.7
  43.6 15.3 %collective-permute-start.13 = (bf16[512,384]{1,0:T(8,128)(2,1)S(1)}, bf16[512,384]{1,0:T(8,128)(2,1)}, u32[]{:S(2)}, u32[]{:S(2)}) collective-permute-start(bf16[512,384]{1,0:T(8,128)(2,1)S(1)} %collective-permute-done.7.refs_6_), channel_id=1, source_target_pairs={{0,2},{1,9},{4,6},{5,13},{8,0},{9,17},{12,4},{13,21},{16,8},{17,25... | collective-permute-start | bytes 1179656 | tf_op jit(solution)/shard_map/ppermute | solution.py:68
  44.9 15.5 %collective-permute-start.16 = (bf16[512,384]{1,0:T(8,128)(2,1)}, bf16[512,384]{1,0:T(8,128)(2,1)}, u32[]{:S(2)}, u32[]{:S(2)}) collective-permute-start(bf16[512,384]{1,0:T(8,128)(2,1)} %collective-permute-done.10.refs_1_), channel_id=1, source_target_pairs={{0,8},{1,3},{4,12},{5,7},{8,16},{9,1},{12,20},{13,5},{16,24},{17,9... | collective-permute-start | bytes 1179656 | tf_op jit(solution)/shard_map/ppermute | solution.py:68
  47.2 11.0 %collective-permute-start.17 = (bf16[256,384]{1,0:T(8,128)(2,1)}, bf16[256,384]{1,0:T(8,128)(2,1)}, u32[]{:S(2)}, u32[]{:S(2)}) collective-permute-start(bf16[256,384]{1,0:T(8,128)(2,1)} %collective-permute-done.11.refs_2_), channel_id=1, source_target_pairs={{0,8},{1,3},{4,12},{5,7},{8,16},{9,1},{12,20},{13,5},{16,24},{17,9... | collective-permute-start | bytes 589832 | tf_op jit(solution)/shard_map/ppermute | solution.py:67
  49.1 6.0 %collective-permute-start.15 = (bf16[256,384]{1,0:T(8,128)(2,1)}, bf16[256,384]{1,0:T(8,128)(2,1)}, u32[]{:S(2)}, u32[]{:S(2)}) collective-permute-start(bf16[256,384]{1,0:T(8,128)(2,1)} %collective-permute-done.14.refs_5_), channel_id=1, source_target_pairs={{0,4},{1,5},{4,0},{5,1},{8,12},{9,13},{12,8},{13,9},{16,20},{17,21... | collective-permute-start | bytes 589832 | tf_op jit(solution)/shard_map/ppermute | solution.py:69
  55.1 8.0 %collective-permute-start.20 = (bf16[256,384]{1,0:T(8,128)(2,1)}, bf16[256,384]{1,0:T(8,128)(2,1)S(1)}, u32[]{:S(2)}, u32[]{:S(2)}) collective-permute-start(bf16[256,384]{1,0:T(8,128)(2,1)} %collective-permute-done.14.refs_5_), channel_id=1, source_target_pairs={{0,2},{1,9},{4,6},{5,13},{8,0},{9,17},{12,4},{13,21},{16,8},{17,25... | collective-permute-start | bytes 589832 | tf_op jit(solution)/shard_map/ppermute | solution.py:67
  58.2 6.5 %collective-permute-start.23 = (bf16[256,384]{1,0:T(8,128)(2,1)}, bf16[256,384]{1,0:T(8,128)(2,1)S(1)}, u32[]{:S(2)}, u32[]{:S(2)}) collective-permute-start(bf16[256,384]{1,0:T(8,128)(2,1)} %collective-permute-done.17.refs_2_), channel_id=1, source_target_pairs={{0,8},{1,3},{4,12},{5,7},{8,16},{9,1},{12,20},{13,5},{16,24},{17,9... | collective-permute-start | bytes 589832 | tf_op jit(solution)/shard_map/ppermute | solution.py:67
  58.9 17.1 %collective-permute-start.19 = (bf16[512,384]{1,0:T(8,128)(2,1)}, bf16[512,384]{1,0:T(8,128)(2,1)S(1)}, u32[]{:S(2)}, u32[]{:S(2)}) collective-permute-start(bf16[512,384]{1,0:T(8,128)(2,1)} %collective-permute-done.13.refs_4_), channel_id=1, source_target_pairs={{0,2},{1,9},{4,6},{5,13},{8,0},{9,17},{12,4},{13,21},{16,8},{17,25... | collective-permute-start | bytes 1179656 | tf_op jit(solution)/shard_map/ppermute | solution.py:68
  60.4 15.6 %collective-permute-start.22 = (bf16[512,384]{1,0:T(8,128)(2,1)}, bf16[512,384]{1,0:T(8,128)(2,1)S(1)}, u32[]{:S(2)}, u32[]{:S(2)}) collective-permute-start(bf16[512,384]{1,0:T(8,128)(2,1)} %collective-permute-done.16.refs_1_), channel_id=1, source_target_pairs={{0,8},{1,3},{4,12},{5,7},{8,16},{9,1},{12,20},{13,5},{16,24},{17,9... | collective-permute-start | bytes 1179656 | tf_op jit(solution)/shard_map/ppermute | solution.py:68
  63.2 12.8 %collective-permute-start.18 = (bf16[256,384]{1,0:T(8,128)(2,1)}, bf16[256,384]{1,0:T(8,128)(2,1)S(1)}, u32[]{:S(2)}, u32[]{:S(2)}) collective-permute-start(bf16[256,384]{1,0:T(8,128)(2,1)} %collective-permute-done.17.refs_2_), channel_id=1, source_target_pairs={{0,4},{1,5},{4,0},{5,1},{8,12},{9,13},{12,8},{13,9},{16,20},{17,21... | collective-permute-start | bytes 589832 | tf_op jit(solution)/shard_map/ppermute | solution.py:69
  64.7 11.3 %collective-permute-start.21 = (bf16[256,384]{1,0:T(8,128)(2,1)S(1)}, bf16[256,384]{1,0:T(8,128)(2,1)S(1)}, u32[]{:S(2)}, u32[]{:S(2)}) collective-permute-start(bf16[256,384]{1,0:T(8,128)(2,1)S(1)} %collective-permute-done.20.refs_5_), channel_id=1, source_target_pairs={{0,4},{1,5},{4,0},{5,1},{8,12},{9,13},{12,8},{13,9},{16,20},{17,21... | collective-permute-start | bytes 589832 | tf_op jit(solution)/shard_map/ppermute | solution.py:69
  65.3 10.6 %collective-permute-start.24 = (bf16[256,384]{1,0:T(8,128)(2,1)S(1)}, bf16[256,384]{1,0:T(8,128)(2,1)S(1)}, u32[]{:S(2)}, u32[]{:S(2)}) collective-permute-start(bf16[256,384]{1,0:T(8,128)(2,1)S(1)} %collective-permute-done.23.refs_8_), channel_id=1, source_target_pairs={{0,4},{1,5},{4,0},{5,1},{8,12},{9,13},{12,8},{13,9},{16,20},{17,21... | collective-permute-start | bytes 589832 | tf_op jit(solution)/shard_map/ppermute | solution.py:69
  66.7 0.9 copy-start.2
  67.7 0.9 copy-start.4
  68.6 0.9 copy-start.6
  69.5 0.9 copy-start.8
  78.9 4.7 %collective-permute-start.26 = (bf16[128,384]{1,0:T(8,128)(2,1)S(1)}, bf16[128,384]{1,0:T(8,128)(2,1)S(1)}, u32[]{:S(2)}, u32[]{:S(2)}) collective-permute-start(bf16[128,384]{1,0:T(8,128)(2,1)S(1)} %get-tuple-element.18), channel_id=1, source_target_pairs={{0,4},{1,5},{4,0},{5,1},{8,12},{9,13},{12,8},{13,9},{16,20},{17,21... | collective-permute-start | bytes 294920 | tf_op jit(solution)/shard_map/ppermute | solution.py:60
  83.6 7.4 %collective-permute-start.28 = (bf16[256,384]{1,0:T(8,128)(2,1)S(1)}, bf16[256,384]{1,0:T(8,128)(2,1)S(1)}, u32[]{:S(2)}, u32[]{:S(2)}) collective-permute-start(bf16[256,384]{1,0:T(8,128)(2,1)S(1)} %constant_dynamic-update-slice_fusion.refs_0_.refs_2_), channel_id=1, source_target_pairs={{0,8},{1,3},{4,12},{5,7},{8,16},{9,1},{12,20},{13,5},{16,24},{17,9... | collective-permute-start | bytes 589832 | tf_op jit(solution)/shard_map/ppermute | solution.py:68
  84.6 7.8 %collective-permute-start.25 = (bf16[160,384]{1,0:T(8,128)(2,1)S(1)}, bf16[160,384]{1,0:T(8,128)(2,1)S(1)}, u32[]{:S(2)}, u32[]{:S(2)}) collective-permute-start(bf16[160,384]{1,0:T(8,128)(2,1)S(1)} %get-tuple-element.15), channel_id=1, source_target_pairs={{0,1},{1,0},{4,5},{5,4},{8,9},{9,8},{12,13},{13,12},{16,17},{17,16... | collective-permute-start | bytes 368648 | tf_op jit(solution)/shard_map/ppermute | solution.py:285
  84.6 16.3 %collective-permute-start.31 = (bf16[256,384]{1,0:T(8,128)(2,1)S(1)}, bf16[256,384]{1,0:T(8,128)(2,1)S(1)}, u32[]{:S(2)}, u32[]{:S(2)}) collective-permute-start(bf16[256,384]{1,0:T(8,128)(2,1)S(1)} %constant_dynamic-update-slice_fusion.refs_0_.refs_2_), channel_id=1, source_target_pairs={{0,2},{1,9},{4,6},{5,13},{8,0},{9,17},{12,4},{13,21},{16,8},{17,25... | collective-permute-start | bytes 589832 | tf_op jit(solution)/shard_map/ppermute | solution.py:68
  91.0 10.4 %collective-permute-start.34 = (bf16[256,384]{1,0:T(8,128)(2,1)S(1)}, bf16[256,384]{1,0:T(8,128)(2,1)S(1)}, u32[]{:S(2)}, u32[]{:S(2)}) collective-permute-start(bf16[256,384]{1,0:T(8,128)(2,1)S(1)} %collective-permute-done.28.refs_4_.refs_6_), channel_id=1, source_target_pairs={{0,8},{1,3},{4,12},{5,7},{8,16},{9,1},{12,20},{13,5},{16,24},{17,9... | collective-permute-start | bytes 589832 | tf_op jit(solution)/shard_map/ppermute | solution.py:68
  92.4 6.2 %collective-permute-start.29 = (bf16[128,384]{1,0:T(8,128)(2,1)S(1)}, bf16[128,384]{1,0:T(8,128)(2,1)S(1)}, u32[]{:S(2)}, u32[]{:S(2)}) collective-permute-start(bf16[128,384]{1,0:T(8,128)(2,1)S(1)} %slice.13.refs_1_), channel_id=1, source_target_pairs={{0,8},{1,3},{4,12},{5,7},{8,16},{9,1},{12,20},{13,5},{16,24},{17,9... | collective-permute-start | bytes 294920 | tf_op jit(solution)/shard_map/ppermute | solution.py:67
  92.4 10.5 %collective-permute-start.32 = (bf16[128,384]{1,0:T(8,128)(2,1)S(1)}, bf16[128,384]{1,0:T(8,128)(2,1)S(1)}, u32[]{:S(2)}, u32[]{:S(2)}) collective-permute-start(bf16[128,384]{1,0:T(8,128)(2,1)S(1)} %slice.13.refs_1_), channel_id=1, source_target_pairs={{0,2},{1,9},{4,6},{5,13},{8,0},{9,17},{12,4},{13,21},{16,8},{17,25... | collective-permute-start | bytes 294920 | tf_op jit(solution)/shard_map/ppermute | solution.py:67
  94.4 8.8 %collective-permute-start.27 = (bf16[128,384]{1,0:T(8,128)(2,1)S(1)}, bf16[128,384]{1,0:T(8,128)(2,1)S(1)}, u32[]{:S(2)}, u32[]{:S(2)}) collective-permute-start(bf16[128,384]{1,0:T(8,128)(2,1)S(1)} %slice.13.refs_1_), channel_id=1, source_target_pairs={{0,4},{1,5},{4,0},{5,1},{8,12},{9,13},{12,8},{13,9},{16,20},{17,21... | collective-permute-start | bytes 294920 | tf_op jit(solution)/shard_map/ppermute | solution.py:69
  98.6 5.5 %collective-permute-start.35 = (bf16[128,384]{1,0:T(8,128)(2,1)S(1)}, bf16[128,384]{1,0:T(8,128)(2,1)S(1)}, u32[]{:S(2)}, u32[]{:S(2)}) collective-permute-start(bf16[128,384]{1,0:T(8,128)(2,1)S(1)} %collective-permute-done.29.refs_5_), channel_id=1, source_target_pairs={{0,8},{1,3},{4,12},{5,7},{8,16},{9,1},{12,20},{13,5},{16,24},{17,9... | collective-permute-start | bytes 294920 | tf_op jit(solution)/shard_map/ppermute | solution.py:67
  100.9 11.8 %collective-permute-start.37 = (bf16[256,384]{1,0:T(8,128)(2,1)S(1)}, bf16[256,384]{1,0:T(8,128)(2,1)S(1)}, u32[]{:S(2)}, u32[]{:S(2)}) collective-permute-start(bf16[256,384]{1,0:T(8,128)(2,1)S(1)} %collective-permute-done.31.refs_8_.refs_10_), channel_id=1, source_target_pairs={{0,2},{1,9},{4,6},{5,13},{8,0},{9,17},{12,4},{13,21},{16,8},{17,25... | collective-permute-start | bytes 589832 | tf_op jit(solution)/shard_map/ppermute | solution.py:68
  101.4 12.0 %collective-permute-start.40 = (bf16[256,384]{1,0:T(8,128)(2,1)S(1)}, bf16[256,384]{1,0:T(8,128)(2,1)S(1)}, u32[]{:S(2)}, u32[]{:S(2)}) collective-permute-start(bf16[256,384]{1,0:T(8,128)(2,1)S(1)} %collective-permute-done.34.refs_0_.refs_2_), channel_id=1, source_target_pairs={{0,8},{1,3},{4,12},{5,7},{8,16},{9,1},{12,20},{13,5},{16,24},{17,9... | collective-permute-start | bytes 589832 | tf_op jit(solution)/shard_map/ppermute | solution.py:68
  103.0 7.8 %collective-permute-start.30 = (bf16[128,384]{1,0:T(8,128)(2,1)S(1)}, bf16[128,384]{1,0:T(8,128)(2,1)S(1)}, u32[]{:S(2)}, u32[]{:S(2)}) collective-permute-start(bf16[128,384]{1,0:T(8,128)(2,1)S(1)} %collective-permute-done.29.refs_5_), channel_id=1, source_target_pairs={{0,4},{1,5},{4,0},{5,1},{8,12},{9,13},{12,8},{13,9},{16,20},{17,21... | collective-permute-start | bytes 294920 | tf_op jit(solution)/shard_map/ppermute | solution.py:69
  103.2 7.4 %collective-permute-start.38 = (bf16[128,384]{1,0:T(8,128)(2,1)S(1)}, bf16[128,384]{1,0:T(8,128)(2,1)S(1)}, u32[]{:S(2)}, u32[]{:S(2)}) collective-permute-start(bf16[128,384]{1,0:T(8,128)(2,1)S(1)} %collective-permute-done.32.refs_9_), channel_id=1, source_target_pairs={{0,2},{1,9},{4,6},{5,13},{8,0},{9,17},{12,4},{13,21},{16,8},{17,25... | collective-permute-start | bytes 294920 | tf_op jit(solution)/shard_map/ppermute | solution.py:67
  104.1 7.2 %collective-permute-start.41 = (bf16[128,384]{1,0:T(8,128)(2,1)S(1)}, bf16[128,384]{1,0:T(8,128)(2,1)S(1)}, u32[]{:S(2)}, u32[]{:S(2)}) collective-permute-start(bf16[128,384]{1,0:T(8,128)(2,1)S(1)} %collective-permute-done.35.refs_1_), channel_id=1, source_target_pairs={{0,8},{1,3},{4,12},{5,7},{8,16},{9,1},{12,20},{13,5},{16,24},{17,9... | collective-permute-start | bytes 294920 | tf_op jit(solution)/shard_map/ppermute | solution.py:67
  110.7 4.6 %collective-permute-start.33 = (bf16[128,384]{1,0:T(8,128)(2,1)S(1)}, bf16[128,384]{1,0:T(8,128)(2,1)S(1)}, u32[]{:S(2)}, u32[]{:S(2)}) collective-permute-start(bf16[128,384]{1,0:T(8,128)(2,1)S(1)} %collective-permute-done.32.refs_9_), channel_id=1, source_target_pairs={{0,4},{1,5},{4,0},{5,1},{8,12},{9,13},{12,8},{13,9},{16,20},{17,21... | collective-permute-start | bytes 294920 | tf_op jit(solution)/shard_map/ppermute | solution.py:69
  110.7 6.1 %collective-permute-start.44 = (bf16[128,384]{1,0:T(8,128)(2,1)S(1)}, bf16[128,384]{1,0:T(8,128)(2,1)S(1)}, u32[]{:S(2)}, u32[]{:S(2)}) collective-permute-start(bf16[128,384]{1,0:T(8,128)(2,1)S(1)} %collective-permute-done.38.refs_5_), channel_id=1, source_target_pairs={{0,2},{1,9},{4,6},{5,13},{8,0},{9,17},{12,4},{13,21},{16,8},{17,25... | collective-permute-start | bytes 294920 | tf_op jit(solution)/shard_map/ppermute | solution.py:67
  111.3 6.0 %collective-permute-start.47 = (bf16[128,384]{1,0:T(8,128)(2,1)S(1)}, bf16[128,384]{1,0:T(8,128)(2,1)S(1)}, u32[]{:S(2)}, u32[]{:S(2)}) collective-permute-start(bf16[128,384]{1,0:T(8,128)(2,1)S(1)} %collective-permute-done.41.refs_1_), channel_id=1, source_target_pairs={{0,8},{1,3},{4,12},{5,7},{8,16},{9,1},{12,20},{13,5},{16,24},{17,9... | collective-permute-start | bytes 294920 | tf_op jit(solution)/shard_map/ppermute | solution.py:67
  112.8 10.8 %collective-permute-start.43 = (bf16[256,384]{1,0:T(8,128)(2,1)S(1)}, bf16[256,384]{1,0:T(8,128)(2,1)S(1)}, u32[]{:S(2)}, u32[]{:S(2)}) collective-permute-start(bf16[256,384]{1,0:T(8,128)(2,1)S(1)} %collective-permute-done.37.refs_4_.refs_6_), channel_id=1, source_target_pairs={{0,2},{1,9},{4,6},{5,13},{8,0},{9,17},{12,4},{13,21},{16,8},{17,25... | collective-permute-start | bytes 589832 | tf_op jit(solution)/shard_map/ppermute | solution.py:68
  113.4 10.1 %collective-permute-start.46 = (bf16[256,384]{1,0:T(8,128)(2,1)S(1)}, bf16[256,384]{1,0:T(8,128)(2,1)S(1)}, u32[]{:S(2)}, u32[]{:S(2)}) collective-permute-start(bf16[256,384]{1,0:T(8,128)(2,1)S(1)} %collective-permute-done.40.refs_0_.refs_2_), channel_id=1, source_target_pairs={{0,8},{1,3},{4,12},{5,7},{8,16},{9,1},{12,20},{13,5},{16,24},{17,9... | collective-permute-start | bytes 589832 | tf_op jit(solution)/shard_map/ppermute | solution.py:68
  115.3 4.7 %collective-permute-start.42 = (bf16[128,384]{1,0:T(8,128)(2,1)S(1)}, bf16[128,384]{1,0:T(8,128)(2,1)S(1)}, u32[]{:S(2)}, u32[]{:S(2)}) collective-permute-start(bf16[128,384]{1,0:T(8,128)(2,1)S(1)} %collective-permute-done.41.refs_1_), channel_id=1, source_target_pairs={{0,4},{1,5},{4,0},{5,1},{8,12},{9,13},{12,8},{13,9},{16,20},{17,21... | collective-permute-start | bytes 294920 | tf_op jit(solution)/shard_map/ppermute | solution.py:69
  116.8 4.6 %collective-permute-start.45 = (bf16[128,384]{1,0:T(8,128)(2,1)S(1)}, bf16[128,384]{1,0:T(8,128)(2,1)S(1)}, u32[]{:S(2)}, u32[]{:S(2)}) collective-permute-start(bf16[128,384]{1,0:T(8,128)(2,1)S(1)} %collective-permute-done.44.refs_5_), channel_id=1, source_target_pairs={{0,4},{1,5},{4,0},{5,1},{8,12},{9,13},{12,8},{13,9},{16,20},{17,21... | collective-permute-start | bytes 294920 | tf_op jit(solution)/shard_map/ppermute | solution.py:69
  117.3 5.1 %collective-permute-start.48 = (bf16[128,384]{1,0:T(8,128)(2,1)S(1)}, bf16[128,384]{1,0:T(8,128)(2,1)S(1)}, u32[]{:S(2)}, u32[]{:S(2)}) collective-permute-start(bf16[128,384]{1,0:T(8,128)(2,1)S(1)} %collective-permute-done.47.refs_9_), channel_id=1, source_target_pairs={{0,4},{1,5},{4,0},{5,1},{8,12},{9,13},{12,8},{13,9},{16,20},{17,21... | collective-permute-start | bytes 294920 | tf_op jit(solution)/shard_map/ppermute | solution.py:69
  120.0 8.9 %copy-start.9 = (s32[1,128]{1,0:T(1,128)S(1)}, s32[1,128]{1,0:T(1,128)}, u32[]{:S(2)}) copy-start(s32[1,128]{1,0:T(1,128)} %param.7) | copy-start | bytes 1540
  120.0 9.0 %collective-permute-start.49 = (bf16[576,384]{1,0:T(8,128)(2,1)S(1)}, bf16[576,384]{1,0:T(8,128)(2,1)S(1)}, u32[]{:S(2)}, u32[]{:S(2)}) collective-permute-start(bf16[576,384]{1,0:T(8,128)(2,1)S(1)} %get-tuple-element.22), channel_id=1, source_target_pairs={{0,1},{1,0},{4,5},{5,4},{8,9},{9,8},{12,13},{13,12},{16,17},{17,16... | collective-permute-start | bytes 1327112 | tf_op jit(solution)/shard_map/ppermute | solution.py:302
  121.4 4.9 %collective-permute-start.36 = (bf16[128,384]{1,0:T(8,128)(2,1)S(1)}, bf16[128,384]{1,0:T(8,128)(2,1)S(1)}, u32[]{:S(2)}, u32[]{:S(2)}) collective-permute-start(bf16[128,384]{1,0:T(8,128)(2,1)S(1)} %collective-permute-done.35.refs_1_), channel_id=1, source_target_pairs={{0,4},{1,5},{4,0},{5,1},{8,12},{9,13},{12,8},{13,9},{16,20},{17,21... | collective-permute-start | bytes 294920 | tf_op jit(solution)/shard_map/ppermute | solution.py:69
  122.5 4.9 %collective-permute-start.39 = (bf16[128,384]{1,0:T(8,128)(2,1)S(1)}, bf16[128,384]{1,0:T(8,128)(2,1)S(1)}, u32[]{:S(2)}, u32[]{:S(2)}) collective-permute-start(bf16[128,384]{1,0:T(8,128)(2,1)S(1)} %collective-permute-done.38.refs_5_), channel_id=1, source_target_pairs={{0,4},{1,5},{4,0},{5,1},{8,12},{9,13},{12,8},{13,9},{16,20},{17,21... | collective-permute-start | bytes 294920 | tf_op jit(solution)/shard_map/ppermute | solution.py:69
  124.1 6.2 %collective-permute-start.51 = (bf16[576,384]{1,0:T(8,128)(2,1)S(1)}, bf16[576,384]{1,0:T(8,128)(2,1)S(1)}, u32[]{:S(2)}, u32[]{:S(2)}) collective-permute-start(bf16[576,384]{1,0:T(8,128)(2,1)S(1)} %get-tuple-element.24), channel_id=1, source_target_pairs={{0,1},{1,0},{4,5},{5,4},{8,9},{9,8},{12,13},{13,12},{16,17},{17,16... | collective-permute-start | bytes 1327112 | tf_op jit(solution)/shard_map/ppermute | solution.py:302
  128.6 1.8 %collective-permute-start.50 = (bf16[384,384]{1,0:T(8,128)(2,1)}, bf16[384,384]{1,0:T(8,128)(2,1)S(1)}, u32[]{:S(2)}, u32[]{:S(2)}) collective-permute-start(bf16[384,384]{1,0:T(8,128)(2,1)} %get-tuple-element.23), channel_id=1, source_target_pairs={{0,1},{1,0},{4,5},{5,4},{8,9},{9,8},{12,13},{13,12},{16,17},{17,16... | collective-permute-start | bytes 884744 | tf_op jit(solution)/shard_map/ppermute | solution.py:302

commit v2 on v1

v2 whole, which is shorter than its diff:
```python
import functools

import jax
import jax.numpy as jnp
from jax import lax
from jax.experimental import pallas as pl
from jax.experimental.pallas import tpu as pltpu
from jax.sharding import PartitionSpec as P

SHW = 4
LANES = 128
F32, BF16 = jnp.float32, jnp.bfloat16
VMEM_LIMIT = 40 * 1024 * 1024


class Grid:
    def __init__(self, n_pair):
        assert n_pair % 8 == 0
        self.nz = n_pair // 8
        self.ring = 2 * self.nz

    def device(self, spot, side, core):
        turned = (spot >= self.nz) * 1
        z = spot + turned * (self.ring - 1 - 2 * spot)
        x = turned + core * (side - turned)
        y = side + core * (turned - side)
        return ((z * 2 + y) * 2 + x) * 2 + core

    def place(self, device):
        core, x, y, z = device % 2, device // 2 % 2, device // 4 % 2, device // 8
        turned = x + core * (y - x)
        side = y + core * (x - y)
        return z + turned * (self.ring - 1 - 2 * z), side, core

    def moves(self, target):
        every = range(self.ring * 4)
        return [(device, int(self.device(*target(*self.place(device))))) for device in every]

    def around(self, way):
        return self.moves(lambda spot, side, core: ((spot + way * (1 - 2 * core)) % self.ring, side, core))

    def across(self):
        return self.moves(lambda spot, side, core: (spot, 1 - side, core))

    def across_core(self):
        return [(device, device ^ 1) for device in range(self.ring * 4)]

    def source(self, me, offset, flip):
        spot, side, core = self.place(me)
        spot = (spot + offset * (1 - 2 * core) + self.ring) % self.ring
        return self.device(spot, (side + flip) % 2, core)

    def groups(self):
        steps = [[-step, step] for step in range(1, self.nz)]
        return [[0] + steps[0]] + steps[1:] + [[-self.nz]] if steps else [[0, -self.nz]]


def gather_chips(grid, own):
    send = functools.partial(lax.ppermute, axis_name="pair")
    around = {-1: grid.around(1), 1: grid.around(-1)}
    across = grid.across()
    held = {0: own}
    for step in range(1, grid.nz + 1):
        for way in (-1, 1):
            if way == -1 or step < grid.nz:
                held[way * step] = send(held[way * (step - 1)], perm=around[way])
    return {offset: (block, send(block, perm=across)) for offset, block in held.items()}


def vmem(count):
    return [pl.BlockSpec(memory_space=pltpu.VMEM)] * count


PARAMS = pltpu.CompilerParams(vmem_limit_bytes=VMEM_LIMIT)


def first_product(source, own_ints, other_ints, batch_column, total, blocks):
    parts, depth, width = blocks[0].shape
    batch_rows = batch_column.shape[0]
    high = own_ints.shape[0] + other_ints.shape[0] + batch_rows
    begins = total is None

    def body(source_ref, own_ref, other_ref, batch_ref, *refs):
        block_refs, out_ref = refs[-1 - len(blocks):-1], refs[-1]
        for number, ref in enumerate(block_refs):
            start = pl.multiple_of(source_ref[number] * depth, depth)
            columns = pl.ds(start, depth)
            position = lax.broadcasted_iota(jnp.int32, (batch_rows, depth), 1) + start
            picks = (batch_ref[...] == position).astype(F32).astype(BF16)
            left = jnp.concatenate([own_ref[:, columns], other_ref[:, columns], picks], axis=0)
            for part in range(parts):
                term = jnp.dot(left, ref[part], preferred_element_type=F32)
                lanes = pl.ds(part * width, width)
                if number > 0:
                    out_ref[:, lanes] += term
                elif begins:
                    out_ref[:, lanes] = term
                else:
                    out_ref[:, lanes] = refs[0][:, lanes] + term

    operands = ([] if begins else [total]) + blocks
    return pl.pallas_call(
        body,
        out_shape=jax.ShapeDtypeStruct((high, parts * width), F32),
        in_specs=[pl.BlockSpec(memory_space=pltpu.SMEM)] + vmem(3 + len(operands)),
        out_specs=pl.BlockSpec(memory_space=pltpu.VMEM),
        compiler_params=PARAMS,
        name="first_product",
    )(source, own_ints, other_ints, batch_column, *operands)


def add_halves(kept, arrived, rows, width):
    batch_rows = kept.shape[0] - rows

    def body(kept_ref, arrived_ref, half_ref, batch_ref):
        for part in range(2):
            lanes = pl.ds(part * width, width)
            both = (kept_ref[:, lanes] + arrived_ref[:, lanes]).astype(BF16)
            half_ref[part * rows:(part + 1) * rows, :] = both[:rows]
            batch_ref[part * batch_rows:(part + 1) * batch_rows, :] = both[rows:]

    return pl.pallas_call(
        body,
        out_shape=[jax.ShapeDtypeStruct((2 * n, width), BF16) for n in (rows, batch_rows)],
        in_specs=vmem(2),
        out_specs=vmem(2),
        compiler_params=PARAMS,
        name="add_halves",
    )(kept, arrived)


def weights(where, batch, slots, share):
    batch_rows, width = batch.shape[0] // 2, batch.shape[1]
    high = 2 * slots * 2 * share
    deep = slots * batch_rows

    def body(where_ref, batch_ref, out_ref):
        me = where_ref[0]
        core = lax.rem(me, 2)
        row = lax.broadcasted_iota(jnp.int32, (high, width), 0)
        column = lax.broadcasted_iota(jnp.int32, (high, width), 1)
        half = lax.div(row, high // 2)
        wanted = (me - core + lax.rem(core + half, 2)) * share + lax.rem(row, share)
        chosen = (column == wanted).astype(F32).astype(BF16)
        repeat = (
            lax.broadcasted_iota(jnp.int32, (batch_rows, deep), 0)
            == lax.rem(lax.broadcasted_iota(jnp.int32, (batch_rows, deep), 1), batch_rows)
        ).astype(F32).astype(BF16)

        def spread(part):
            rows = batch_ref[part * batch_rows:(part + 1) * batch_rows, :]
            picked = lax.dot_general(chosen, rows, (((1,), (1,)), ((), ())), preferred_element_type=F32)
            return jnp.dot(picked.astype(BF16), repeat, preferred_element_type=F32)

        row = lax.broadcasted_iota(jnp.int32, (high, deep), 0)
        column = lax.broadcasted_iota(jnp.int32, (high, deep), 1)
        keep = lax.rem(lax.div(row, 2 * share), slots) == lax.div(column, batch_rows)
        real = lax.rem(lax.div(row, share), 2) == 0
        re, im = spread(0), spread(1)
        out_ref[:, :deep] = jnp.where(keep, jnp.where(real, re, -im), 0.0).astype(BF16)
        out_ref[:, deep:] = jnp.where(keep, jnp.where(real, im, re), 0.0).astype(BF16)

    return pl.pallas_call(
        body,
        out_shape=jax.ShapeDtypeStruct((high, 2 * deep), BF16),
        in_specs=[pl.BlockSpec(memory_space=pltpu.SMEM)] + vmem(1),
        out_specs=pl.BlockSpec(memory_space=pltpu.VMEM),
        compiler_params=PARAMS,
        name="weights",
    )(where, batch)


def second_product(matrix, blocks):
    half = matrix.shape[0] // 2
    width = blocks[0].shape[1]

    def body(matrix_ref, *refs):
        block_refs, (mine, theirs) = refs[: len(blocks)], refs[len(blocks):]
        for number, ref in enumerate(block_refs):
            both = jnp.dot(matrix_ref[...], ref[...], preferred_element_type=F32).astype(BF16)
            mine[number * half:(number + 1) * half, :] = both[:half]
            theirs[number * half:(number + 1) * half, :] = both[half:]

    shape = jax.ShapeDtypeStruct((len(blocks) * half, width), BF16)
    return pl.pallas_call(
        body,
        out_shape=[shape, shape],
        in_specs=vmem(1 + len(blocks)),
        out_specs=vmem(2),
        compiler_params=PARAMS,
        name="second_product",
    )(matrix, *blocks)


def place_pairs(order, pair_column, pieces, share):
    width = pieces[0].shape[1]
    slots = order.shape[0]
    each = 2 * share

    def body(order_ref, pair_ref, *refs):
        piece_refs, out_ref, held = refs[: len(pieces)], refs[-2], refs[-1]
        start = 0
        for ref in piece_refs:
            for tile in range(width // LANES):
                held[tile, start:start + ref.shape[0], :] = ref[:, tile * LANES:(tile + 1) * LANES].astype(F32)
            start += ref.shape[0]
        lane = lax.broadcasted_iota(jnp.int32, (slots, slots), 1)
        ordered = (order_ref[...] == lane).astype(F32).astype(BF16)
        paired = (pair_ref[...] == lane).astype(F32).astype(BF16)
        place = jnp.dot(ordered, paired, preferred_element_type=F32).astype(BF16)
        for number in range(each):
            for tile in range(width // LANES):
                rows = held[tile, pl.ds(number, slots, stride=each), :].astype(BF16)
                placed = lax.dot_general(rows, place, (((0,), (0,)), ((), ())), preferred_element_type=F32)
                lanes = pl.ds(tile * LANES, LANES)
                out_ref[number // share, number % share, lanes, :] = placed.astype(BF16)

    return pl.pallas_call(
        body,
        out_shape=jax.ShapeDtypeStruct((2, share, width, slots), BF16),
        in_specs=vmem(2 + len(pieces)),
        out_specs=pl.BlockSpec(memory_space=pltpu.VMEM),
        scratch_shapes=[pltpu.VMEM((width // LANES, slots * each, LANES), F32)],
        compiler_params=PARAMS,
        name="place_pairs",
    )(order, pair_column, *pieces)


def on_device(n_coef, n_pair, integrals, coefficients, shell_starts, pair_ids):
    grid = Grid(n_pair)
    swap = functools.partial(lax.ppermute, axis_name="pair", perm=grid.across_core())
    slots, batch_rows, ao_width = integrals.shape
    occupied = coefficients.shape[2]
    share = occupied // n_pair
    rows = slots * batch_rows
    depth = ao_width // n_pair
    piece = depth // n_coef
    me = lax.axis_index("pair").astype(jnp.int32)

    batch_index = (shell_starts[:, None] + jnp.arange(SHW, dtype=jnp.int32)[None, :]).reshape(-1)
    flat_ints = integrals.reshape(rows, ao_width)
    if n_coef > 1:
        coefficients = lax.all_gather(coefficients, "coef", axis=1, tiled=True)
        flat_ints = flat_ints.reshape(rows, n_coef, n_pair, piece).transpose(0, 2, 1, 3).reshape(rows, ao_width)
        batch_index = (
            batch_index // piece % n_pair * depth + batch_index // (n_pair * piece) * piece + batch_index % piece
        )
    batch_column = batch_index[:, None]

    other_ints = swap(flat_ints)
    gathered = gather_chips(grid, coefficients)
    total = None
    for group in grid.groups():
        blocks = [block for offset in group for block in gathered[offset]]
        source = jnp.stack([grid.source(me, offset, flip) for offset in group for flip in range(2)])
        total = first_product(source, flat_ints, other_ints, batch_column, total, blocks)
    kept = jnp.concatenate([total[:rows], total[2 * rows:]], axis=0)
    half, batch = add_halves(kept, swap(total[rows:]), rows, occupied)
    matrix = weights(me[None], batch, slots, share)

    gathered = gather_chips(grid, half)
    mine, theirs, mine_order, their_order = [], [], [], []
    within = jnp.arange(slots, dtype=jnp.int32)
    for group in grid.groups():
        stay, leave = second_product(matrix, [block for offset in group for block in gathered[offset]])
        mine.append(stay)
        theirs.append(swap(leave))
        for offset in group:
            for flip in range(2):
                mine_order.append(grid.source(me, offset, flip) * slots + within)
                their_order.append(grid.source(me ^ 1, offset, flip) * slots + within)
    order = jnp.concatenate(mine_order + their_order)[:, None]
    return place_pairs(order, pair_ids.reshape(-1)[:, None], mine + theirs, share)


def solution(mesh):
    return jax.shard_map(
        functools.partial(on_device, mesh.shape["coef"], mesh.shape["pair"]),
        mesh=mesh,
        in_specs=(
            P(("coef", "pair"), None, None),
            P(None, ("coef", "pair"), None),
            P(),
            P("coef", None),
        ),
        out_specs=P(None, "pair", None, "coef"),
        check_vma=False,
    )
```

time: 133 us -> 108 us (0.81)
  starting transfers between devices: 54.1 us -> 33 us
  waiting for transfers between devices: 56.5 us -> 51 us
    ppermute x48 -> x31, starting transfers between devices: 53.5 us -> 32.4 us  [the longest x14 16.7 us: gather_chips(): held[way * step] = send(held[way * (step - 1)], perm=around[way])]
    ppermute x48 -> x31, waiting for transfers between devices: 55.1 us -> 49.8 us  [the longest x14 42.3 us: gather_chips(): held[way * step] = send(held[way * (step - 1)], perm=around[way])]
    unnamed x23 -> x24, local copies, waits for them, and re-layouts: 6.47 us -> 8.85 us
    pallas_call x7 -> x10, Pallas kernels: 11.2 us -> 10 us  [the longest x4 7.39 us: first_product(): pl.pallas_call(body, out_shape=jax.ShapeDtypeStruct((high, parts * width)...]
  transfers between devices with their start and end apart: 52 -> 36, of which waited for: 18 -> 13; matrix products, arithmetic and copies ran while one was open for 1% -> 1% of each run, Pallas kernels for 6% -> 8%
where the time goes in v2:
time: 108 us
  waiting for transfers between devices  51 us (47%)
  starting transfers between devices  33 us (31%)
  Pallas kernels  12.8 us (12%)
  local copies, waits for them, and re-layouts  9.4 us (9%)
    ppermute x14, waiting for transfers between devices, gather_chips(): held[way * step] = send(held[way * (step - 1)], perm=around[way])  42.3 us
    ppermute x14, starting transfers between devices, gather_chips(): held[way * step] = send(held[way * (step - 1)], perm=around[way])  16.7 us
    ppermute x16, starting transfers between devices, gather_chips(): send(block, perm=across)  15.6 us
    unnamed x24, local copies, waits for them, and re-layouts  8.85 us
    pallas_call x4, Pallas kernels, first_product(): pl.pallas_call(body, out_shape=jax.ShapeDtypeStruct((high, parts * width)...  7.39 us
    ppermute x16, waiting for transfers between devices, gather_chips(): send(block, perm=across)  6.12 us
    pallas_call x1, Pallas kernels, place_pairs(): pl.pallas_call(body, out_shape=jax.ShapeDtypeStruct((2, share, width, slo...  2.8 us
  transfers between devices with their start and end apart: 36, of which 13 were waited for; matrix products, arithmetic and copies ran while one was open for 1% of the time, Pallas kernels for 8%

profile of v2, /device:TPU:0, one launch (start us, length us, event | category | flops | bytes accessed | tf_op | source)
XLA Modules:
  0.0 107.9 jit_solution(16785794231624893964)
XLA Ops:
  0.0 0.5 collective-permute-start
  0.5 2.6 %collective-permute-start.2 = (bf16[2,256,384]{2,1,0:T(8,128)(2,1)}, bf16[2,256,384]{2,1,0:T(8,128)(2,1)S(1)}, u32[]{:S(2)}, u32[]{:S(2)}) collective-permute-start(bf16[2,256,384]{2,1,0:T(8,128)(2,1)} %refs_0_.1), channel_id=1, source_target_pairs={{0,8},{1,5},{2,0},{3,7},{4,12},{5,13},{6,4},{7,15},{8,16},{9,1},{1... | collective-permute-start | bytes 1179656 | tf_op jit(solution)/shard_map/ppermute | solution.py:66
  3.0 9.4 %collective-permute-done.2.refs_2_ = bf16[2,256,384]{2,1,0:T(8,128)(2,1)S(1)} collective-permute-done((bf16[2,256,384]{2,1,0:T(8,128)(2,1)}, bf16[2,256,384]{2,1,0:T(8,128)(2,1)S(1)}, u32[]{:S(2)}, u32[]{:S(2)}) %collective-permute-start.2) | collective-permute-done | bytes 393248 | tf_op jit(solution)/shard_map/ppermute | solution.py:66
  12.4 2.4 %collective-permute-start.6 = (bf16[2,256,384]{2,1,0:T(8,128)(2,1)S(1)}, bf16[2,256,384]{2,1,0:T(8,128)(2,1)S(1)}, u32[]{:S(2)}, u32[]{:S(2)}) collective-permute-start(bf16[2,256,384]{2,1,0:T(8,128)(2,1)S(1)} %collective-permute-done.2.refs_2_), channel_id=1, source_target_pairs={{0,8},{1,5},{2,0},{3,7},{4,12},{5,13},{6,4},{7,15},{8,16},{9,1},{1... | collective-permute-start | bytes 1179656 | tf_op jit(solution)/shard_map/ppermute | solution.py:66
  14.8 1.5 %collective-permute-start.1 = (bf16[2,256,384]{2,1,0:T(8,128)(2,1)}, bf16[2,256,384]{2,1,0:T(8,128)(2,1)S(1)}, u32[]{:S(2)}, u32[]{:S(2)}) collective-permute-start(bf16[2,256,384]{2,1,0:T(8,128)(2,1)} %refs_0_.1), channel_id=1, source_target_pairs={{0,4},{1,3},{2,6},{3,1},{4,0},{5,7},{6,2},{7,5},{8,12},{9,11},{10,... | collective-permute-start | bytes 1179656 | tf_op jit(solution)/shard_map/ppermute | solution.py:67
  16.3 8.3 %collective-permute-done.6.refs_1_ = bf16[2,256,384]{2,1,0:T(8,128)(2,1)S(1)} collective-permute-done((bf16[2,256,384]{2,1,0:T(8,128)(2,1)S(1)}, bf16[2,256,384]{2,1,0:T(8,128)(2,1)S(1)}, u32[]{:S(2)}, u32[]{:S(2)}) %collective-permute-start.6) | collective-permute-done | bytes 393248 | tf_op jit(solution)/shard_map/ppermute | solution.py:66
  24.6 2.1 %collective-permute-start.10 = (bf16[2,256,384]{2,1,0:T(8,128)(2,1)S(1)}, bf16[2,256,384]{2,1,0:T(8,128)(2,1)}, u32[]{:S(2)}, u32[]{:S(2)}) collective-permute-start(bf16[2,256,384]{2,1,0:T(8,128)(2,1)S(1)} %collective-permute-done.6.refs_1_), channel_id=1, source_target_pairs={{0,8},{1,5},{2,0},{3,7},{4,12},{5,13},{6,4},{7,15},{8,16},{9,1},{1... | collective-permute-start | bytes 1179656 | tf_op jit(solution)/shard_map/ppermute | solution.py:66
  26.6 0.4 collective-permute-start.3
  27.0 0.7 copy-done.5
  27.8 1.6 %collective-permute-start.5 = (bf16[2,256,384]{2,1,0:T(8,128)(2,1)S(1)}, bf16[2,256,384]{2,1,0:T(8,128)(2,1)S(1)}, u32[]{:S(2)}, u32[]{:S(2)}) collective-permute-start(bf16[2,256,384]{2,1,0:T(8,128)(2,1)S(1)} %collective-permute-done.4.refs_4_), channel_id=1, source_target_pairs={{0,4},{1,3},{2,6},{3,1},{4,0},{5,7},{6,2},{7,5},{8,12},{9,11},{10,... | collective-permute-start | bytes 1179656 | tf_op jit(solution)/shard_map/ppermute | solution.py:67
  29.4 7.3 %collective-permute-done.10.refs_1_ = bf16[2,256,384]{2,1,0:T(8,128)(2,1)} collective-permute-done((bf16[2,256,384]{2,1,0:T(8,128)(2,1)S(1)}, bf16[2,256,384]{2,1,0:T(8,128)(2,1)}, u32[]{:S(2)}, u32[]{:S(2)}) %collective-permute-start.10) | collective-permute-done | bytes 393248 | tf_op jit(solution)/shard_map/ppermute | solution.py:66
  36.7 1.6 %collective-permute-start.14 = (bf16[2,256,384]{2,1,0:T(8,128)(2,1)}, bf16[2,256,384]{2,1,0:T(8,128)(2,1)}, u32[]{:S(2)}, u32[]{:S(2)}) collective-permute-start(bf16[2,256,384]{2,1,0:T(8,128)(2,1)} %collective-permute-done.10.refs_1_), channel_id=1, source_target_pairs={{0,8},{1,5},{2,0},{3,7},{4,12},{5,13},{6,4},{7,15},{8,16},{9,1},{1... | collective-permute-start | bytes 1179656 | tf_op jit(solution)/shard_map/ppermute | solution.py:66
  38.3 0.7 copy-done.7
  39.1 2.5 %collective-permute-done.5.refs_5_ = bf16[2,256,384]{2,1,0:T(8,128)(2,1)S(1)} collective-permute-done((bf16[2,256,384]{2,1,0:T(8,128)(2,1)S(1)}, bf16[2,256,384]{2,1,0:T(8,128)(2,1)S(1)}, u32[]{:S(2)}, u32[]{:S(2)}) %collective-permute-start.5) | collective-permute-done | bytes 393248 | tf_op jit(solution)/shard_map/ppermute | solution.py:67
  41.6 0.8 copy-done.9
  42.4 1.0 collective-permute-start.9
  43.4 1.0 collective-permute-start.11
  44.4 4.7 %collective-permute-done.14.refs_1_ = bf16[2,256,384]{2,1,0:T(8,128)(2,1)} collective-permute-done((bf16[2,256,384]{2,1,0:T(8,128)(2,1)}, bf16[2,256,384]{2,1,0:T(8,128)(2,1)}, u32[]{:S(2)}, u32[]{:S(2)}) %collective-permute-start.14) | collective-permute-done | bytes 393248 | tf_op jit(solution)/shard_map/ppermute | solution.py:66
  49.1 0.5 collective-permute-start.13
  49.6 1.6 %collective-permute-start.15 = (bf16[2,256,384]{2,1,0:T(8,128)(2,1)}, bf16[2,256,384]{2,1,0:T(8,128)(2,1)}, u32[]{:S(2)}, u32[]{:S(2)}) collective-permute-start(bf16[2,256,384]{2,1,0:T(8,128)(2,1)} %collective-permute-done.14.refs_1_), channel_id=1, source_target_pairs={{0,4},{1,3},{2,6},{3,1},{4,0},{5,7},{6,2},{7,5},{8,12},{9,11},{10,... | collective-permute-start | bytes 1179656 | tf_op jit(solution)/shard_map/ppermute | solution.py:67
  51.1 0.7 iota_add_fusion
  51.9 0.1 add.1796.batch_ref
  51.9 0.1 stack.79.source_ref
  52.0 0.1 pad_add_fusion.source_ref
  52.1 0.1 pad_add_fusion.2.source_ref
  52.2 0.1 pad_add_fusion.1.source_ref
  52.3 1.6 %copy-done = bf16[4,32,8192]{2,1,0:T(8,128)(2,1)S(1)} copy-done((bf16[4,32,8192]{2,1,0:T(8,128)(2,1)S(1)}, bf16[4,32,8192]{2,1,0:T(8,128)(2,1)}, u32[]{:S(2)}) %copy-start) | copy-done | bytes 2097176
  53.9 1.0 copy-done.2
  54.9 1.0 copy-done.4
  55.9 1.0 copy-done.6
  56.9 1.0 copy-done.8
  57.8 1.0 copy-done.10
  58.8 1.6 %first_product.4.refs_0_ = f32[288,768]{1,0:T(8,128)S(1)} custom-call(s32[6]{0:T(128)S(1)} %stack.79.source_ref, bf16[128,8192]{1,0:T(8,128)(2,1)S(1)} %bitcast.21, bf16[128,8192]{1,0:T(8,128)(2,1)S(1)} %collective-permute-done.other_ref, s32[32,1]{1,0:T(8,128)S(1)} %add.1796.batch_ref, bf16[2,256,384]{2,1,0:T(8,128)(2,1)S(1)} %copy-done.2, ...), custom_call_target="tpu_custom_call" | custom-call | tf_op jit(solution)/shard_map/first_product/pallas_call | solution.py:102
  60.5 2.0 %first_product.5.refs_0_ = f32[288,768]{1,0:T(8,128)S(1)} custom-call(s32[4]{0:T(128)S(1)} %pad_add_fusion.2.source_ref, bf16[128,8192]{1,0:T(8,128)(2,1)S(1)} %bitcast.22, bf16[128,8192]{1,0:T(8,128)(2,1)S(1)} %collective-permute-done.other_ref, s32[32,1]{1,0:T(8,128)S(1)} %add.1796.batch_ref, f32[288,768]{1,0:T(8,128)S(1)} %first_product.4.refs_0_, ...), custom_call_target="tpu_custom_call" | custom-call | tf_op jit(solution)/shard_map/first_product/pallas_call | solution.py:102
  62.6 2.1 %first_product.6.refs_0_ = f32[288,768]{1,0:T(8,128)S(1)} custom-call(s32[4]{0:T(128)S(1)} %pad_add_fusion.1.source_ref, bf16[128,8192]{1,0:T(8,128)(2,1)S(1)} %bitcast.23, bf16[128,8192]{1,0:T(8,128)(2,1)S(1)} %collective-permute-done.other_ref, s32[32,1]{1,0:T(8,128)S(1)} %add.1796.batch_ref, f32[288,768]{1,0:T(8,128)S(1)} %first_product.5.refs_0_, ...), custom_call_target="tpu_custom_call" | custom-call | tf_op jit(solution)/shard_map/first_product/pallas_call | solution.py:102
  64.7 1.6 %first_product.7 = f32[288,768]{1,0:T(8,128)S(1)} custom-call(s32[2]{0:T(128)S(1)} %pad_add_fusion.source_ref, bf16[128,8192]{1,0:T(8,128)(2,1)S(1)} %bitcast.24, bf16[128,8192]{1,0:T(8,128)(2,1)S(1)} %collective-permute-done.other_ref, s32[32,1]{1,0:T(8,128)S(1)} %add.1796.batch_ref, f32[288,768]{1,0:T(8,128)S(1)} %first_product.6.refs_0_, ...), custom_call_target="tpu_custom_call" | custom-call | tf_op jit(solution)/shard_map/first_product/pallas_call | solution.py:102
  66.9 1.4 %collective-permute-done.16.arrived_ref = f32[160,768]{1,0:T(8,128)S(1)} collective-permute-done((f32[160,768]{1,0:T(8,128)S(1)}, f32[160,768]{1,0:T(8,128)S(1)}, u32[]{:S(2)}, u32[]{:S(2)}) %collective-permute-start.16) | collective-permute-done | bytes 491552 | tf_op jit(solution)/shard_map/ppermute | solution.py:258
  68.4 0.7 collective-permute-start.18
  69.1 1.4 %collective-permute-start.20 = (bf16[256,384]{1,0:T(8,128)(2,1)S(1)}, bf16[256,384]{1,0:T(8,128)(2,1)S(1)}, u32[]{:S(2)}, u32[]{:S(2)}) collective-permute-start(bf16[256,384]{1,0:T(8,128)(2,1)S(1)} %get-tuple-element.16.refs_0_), channel_id=1, source_target_pairs={{0,2},{1,9},{2,10},{3,11},{4,6},{5,1},{6,14},{7,3},{8,0},{9,17},{1... | collective-permute-start | bytes 589832 | tf_op jit(solution)/shard_map/ppermute | solution.py:66
  70.4 3.7 %collective-permute-done.18.refs_2_ = bf16[256,384]{1,0:T(8,128)(2,1)S(1)} collective-permute-done((bf16[256,384]{1,0:T(8,128)(2,1)S(1)}, bf16[256,384]{1,0:T(8,128)(2,1)S(1)}, u32[]{:S(2)}, u32[]{:S(2)}) %collective-permute-start.18) | collective-permute-done | bytes 196640 | tf_op jit(solution)/shard_map/ppermute | solution.py:66
  74.1 2.5 %collective-permute-start.22 = (bf16[256,384]{1,0:T(8,128)(2,1)S(1)}, bf16[256,384]{1,0:T(8,128)(2,1)S(1)}, u32[]{:S(2)}, u32[]{:S(2)}) collective-permute-start(bf16[256,384]{1,0:T(8,128)(2,1)S(1)} %collective-permute-done.18.refs_2_), channel_id=1, source_target_pairs={{0,8},{1,5},{2,0},{3,7},{4,12},{5,13},{6,4},{7,15},{8,16},{9,1},{1... | collective-permute-start | bytes 589832 | tf_op jit(solution)/shard_map/ppermute | solution.py:66
  76.6 0.5 collective-permute-start.17
  77.2 4.1 %collective-permute-done.22.refs_0_ = bf16[256,384]{1,0:T(8,128)(2,1)S(1)} collective-permute-done((bf16[256,384]{1,0:T(8,128)(2,1)S(1)}, bf16[256,384]{1,0:T(8,128)(2,1)S(1)}, u32[]{:S(2)}, u32[]{:S(2)}) %collective-permute-start.22) | collective-permute-done | bytes 196640 | tf_op jit(solution)/shard_map/ppermute | solution.py:66
  81.3 2.5 %collective-permute-start.26 = (bf16[256,384]{1,0:T(8,128)(2,1)S(1)}, bf16[256,384]{1,0:T(8,128)(2,1)S(1)}, u32[]{:S(2)}, u32[]{:S(2)}) collective-permute-start(bf16[256,384]{1,0:T(8,128)(2,1)S(1)} %collective-permute-done.22.refs_0_), channel_id=1, source_target_pairs={{0,8},{1,5},{2,0},{3,7},{4,12},{5,13},{6,4},{7,15},{8,16},{9,1},{1... | collective-permute-start | bytes 589832 | tf_op jit(solution)/shard_map/ppermute | solution.py:66
  83.8 2.0 %collective-permute-start.21 = (bf16[256,384]{1,0:T(8,128)(2,1)S(1)}, bf16[256,384]{1,0:T(8,128)(2,1)S(1)}, u32[]{:S(2)}, u32[]{:S(2)}) collective-permute-start(bf16[256,384]{1,0:T(8,128)(2,1)S(1)} %collective-permute-done.20.refs_4_), channel_id=1, source_target_pairs={{0,4},{1,3},{2,6},{3,1},{4,0},{5,7},{6,2},{7,5},{8,12},{9,11},{10,... | collective-permute-start | bytes 589832 | tf_op jit(solution)/shard_map/ppermute | solution.py:67
  85.8 0.8 collective-permute-start.23
  86.6 2.5 %collective-permute-done.26.refs_0_ = bf16[256,384]{1,0:T(8,128)(2,1)S(1)} collective-permute-done((bf16[256,384]{1,0:T(8,128)(2,1)S(1)}, bf16[256,384]{1,0:T(8,128)(2,1)S(1)}, u32[]{:S(2)}, u32[]{:S(2)}) %collective-permute-start.26) | collective-permute-done | bytes 196640 | tf_op jit(solution)/shard_map/ppermute | solution.py:66
  89.1 1.0 collective-permute-start.30
  90.1 1.4 %collective-permute-start.25 = (bf16[256,384]{1,0:T(8,128)(2,1)S(1)}, bf16[256,384]{1,0:T(8,128)(2,1)S(1)}, u32[]{:S(2)}, u32[]{:S(2)}) collective-permute-start(bf16[256,384]{1,0:T(8,128)(2,1)S(1)} %collective-permute-done.24.refs_2_), channel_id=1, source_target_pairs={{0,4},{1,3},{2,6},{3,1},{4,0},{5,7},{6,2},{7,5},{8,12},{9,11},{10,... | collective-permute-start | bytes 589832 | tf_op jit(solution)/shard_map/ppermute | solution.py:67
  91.6 2.1 %collective-permute-start.27 = (bf16[256,384]{1,0:T(8,128)(2,1)S(1)}, bf16[256,384]{1,0:T(8,128)(2,1)S(1)}, u32[]{:S(2)}, u32[]{:S(2)}) collective-permute-start(bf16[256,384]{1,0:T(8,128)(2,1)S(1)} %collective-permute-done.26.refs_0_), channel_id=1, source_target_pairs={{0,4},{1,3},{2,6},{3,1},{4,0},{5,7},{6,2},{7,5},{8,12},{9,11},{10,... | collective-permute-start | bytes 589832 | tf_op jit(solution)/shard_map/ppermute | solution.py:67
  93.7 0.5 weights.1.matrix_ref
  94.2 0.5 second_product.4
  94.7 2.2 %collective-permute-done.30.refs_0_ = bf16[256,384]{1,0:T(8,128)(2,1)S(1)} collective-permute-done((bf16[256,384]{1,0:T(8,128)(2,1)S(1)}, bf16[256,384]{1,0:T(8,128)(2,1)S(1)}, u32[]{:S(2)}, u32[]{:S(2)}) %collective-permute-start.30) | collective-permute-done | bytes 196640 | tf_op jit(solution)/shard_map/ppermute | solution.py:66
  97.0 1.2 %collective-permute-start.31 = (bf16[256,384]{1,0:T(8,128)(2,1)S(1)}, bf16[256,384]{1,0:T(8,128)(2,1)S(1)}, u32[]{:S(2)}, u32[]{:S(2)}) collective-permute-start(bf16[256,384]{1,0:T(8,128)(2,1)S(1)} %collective-permute-done.30.refs_0_), channel_id=1, source_target_pairs={{0,4},{1,3},{2,6},{3,1},{4,0},{5,7},{6,2},{7,5},{8,12},{9,11},{10,... | collective-permute-start | bytes 589832 | tf_op jit(solution)/shard_map/ppermute | solution.py:67
  98.2 0.4 second_product.5
  98.7 1.4 %collective-permute-done.29.refs_3_ = bf16[256,384]{1,0:T(8,128)(2,1)S(1)} collective-permute-done((bf16[256,384]{1,0:T(8,128)(2,1)S(1)}, bf16[256,384]{1,0:T(8,128)(2,1)S(1)}, u32[]{:S(2)}, u32[]{:S(2)}) %collective-permute-start.29) | collective-permute-done | bytes 196640 | tf_op jit(solution)/shard_map/ppermute | solution.py:67
  100.0 0.4 second_product.6
  100.5 2.2 %collective-permute-done.31.refs_1_ = bf16[256,384]{1,0:T(8,128)(2,1)S(1)} collective-permute-done((bf16[256,384]{1,0:T(8,128)(2,1)S(1)}, bf16[256,384]{1,0:T(8,128)(2,1)S(1)}, u32[]{:S(2)}, u32[]{:S(2)}) %collective-permute-start.31) | collective-permute-done | bytes 196640 | tf_op jit(solution)/shard_map/ppermute | solution.py:67
  102.6 0.9 second_product.7
  103.6 0.1 concatenate.6
  103.7 0.1 copy.15.order_ref
  103.8 0.1 copy.16.pair_ref
  103.9 1.2 %collective-permute-done.35.refs_7_ = bf16[192,384]{1,0:T(8,128)(2,1)S(1)} collective-permute-done((bf16[192,384]{1,0:T(8,128)(2,1)}, bf16[192,384]{1,0:T(8,128)(2,1)S(1)}, u32[]{:S(2)}, u32[]{:S(2)}) %collective-permute-start.35) | collective-permute-done | bytes 147488 | tf_op jit(solution)/shard_map/ppermute | solution.py:267
  105.1 2.8 %place_pairs.1 = bf16[2,12,384,128]{3,2,1,0:T(8,128)(2,1)} custom-call(s32[128,1]{1,0:T(8,128)S(1)} %copy.15.order_ref, s32[128,1]{1,0:T(8,128)S(1)} %copy.16.pair_ref, bf16[576,384]{1,0:T(8,128)(2,1)S(1)} %get-tuple-element.17.refs_0_, bf16[384,384]{1,0:T(8,128)(2,1)S(1)} %get-tuple-element.18.refs_1_, bf16[384,384]{1,0:T(8,128)(2,1)S(1)} %get-tuple-element.19.refs_2_, ...), custom_call_target="tpu_custom_call" | custom-call | tf_op jit(solution)/shard_map/place_pairs/pallas_call | solution.py:218
  (72 shorter events, 0.7 us)
Async XLA Ops:
  0.0 49.6 %collective-permute-start = (bf16[128,8192]{1,0:T(8,128)(2,1)}, bf16[128,8192]{1,0:T(8,128)(2,1)S(1)}, u32[]{:S(2)}, u32[]{:S(2)}) collective-permute-start(bf16[128,8192]{1,0:T(8,128)(2,1)} %bitcast.20), channel_id=1, source_target_pairs={{0,1},{1,0},{2,3},{3,2},{4,5},{5,4},{6,7},{7,6},{8,9},{9,8},{10,11... | collective-permute-start | bytes 6291464 | tf_op jit(solution)/shard_map/ppermute | solution.py:250
  0.5 12.0 %collective-permute-start.2 = (bf16[2,256,384]{2,1,0:T(8,128)(2,1)}, bf16[2,256,384]{2,1,0:T(8,128)(2,1)S(1)}, u32[]{:S(2)}, u32[]{:S(2)}) collective-permute-start(bf16[2,256,384]{2,1,0:T(8,128)(2,1)} %refs_0_.1), channel_id=1, source_target_pairs={{0,8},{1,5},{2,0},{3,7},{4,12},{5,13},{6,4},{7,15},{8,16},{9,1},{1... | collective-permute-start | bytes 1179656 | tf_op jit(solution)/shard_map/ppermute | solution.py:66
  3.0 13.3 %collective-permute-start.4 = (bf16[2,256,384]{2,1,0:T(8,128)(2,1)}, bf16[2,256,384]{2,1,0:T(8,128)(2,1)S(1)}, u32[]{:S(2)}, u32[]{:S(2)}) collective-permute-start(bf16[2,256,384]{2,1,0:T(8,128)(2,1)} %refs_0_.1), channel_id=1, source_target_pairs={{0,2},{1,9},{2,10},{3,11},{4,6},{5,1},{6,14},{7,3},{8,0},{9,17},{1... | collective-permute-start | bytes 1179656 | tf_op jit(solution)/shard_map/ppermute | solution.py:66
  12.4 12.2 %collective-permute-start.6 = (bf16[2,256,384]{2,1,0:T(8,128)(2,1)S(1)}, bf16[2,256,384]{2,1,0:T(8,128)(2,1)S(1)}, u32[]{:S(2)}, u32[]{:S(2)}) collective-permute-start(bf16[2,256,384]{2,1,0:T(8,128)(2,1)S(1)} %collective-permute-done.2.refs_2_), channel_id=1, source_target_pairs={{0,8},{1,5},{2,0},{3,7},{4,12},{5,13},{6,4},{7,15},{8,16},{9,1},{1... | collective-permute-start | bytes 1179656 | tf_op jit(solution)/shard_map/ppermute | solution.py:66
  14.8 12.3 %collective-permute-start.1 = (bf16[2,256,384]{2,1,0:T(8,128)(2,1)}, bf16[2,256,384]{2,1,0:T(8,128)(2,1)S(1)}, u32[]{:S(2)}, u32[]{:S(2)}) collective-permute-start(bf16[2,256,384]{2,1,0:T(8,128)(2,1)} %refs_0_.1), channel_id=1, source_target_pairs={{0,4},{1,3},{2,6},{3,1},{4,0},{5,7},{6,2},{7,5},{8,12},{9,11},{10,... | collective-permute-start | bytes 1179656 | tf_op jit(solution)/shard_map/ppermute | solution.py:67
  16.3 35.9 %copy-start.3 = (bf16[2,256,384]{2,1,0:T(8,128)(2,1)}, bf16[2,256,384]{2,1,0:T(8,128)(2,1)S(1)}, u32[]{:S(2)}) copy-start(bf16[2,256,384]{2,1,0:T(8,128)(2,1)S(1)} %collective-permute-done.4.refs_4_) | copy-start | bytes 1179652
  16.3 13.1 %collective-permute-start.8 = (bf16[2,256,384]{2,1,0:T(8,128)(2,1)S(1)}, bf16[2,256,384]{2,1,0:T(8,128)(2,1)}, u32[]{:S(2)}, u32[]{:S(2)}) collective-permute-start(bf16[2,256,384]{2,1,0:T(8,128)(2,1)S(1)} %collective-permute-done.4.refs_4_), channel_id=1, source_target_pairs={{0,2},{1,9},{2,10},{3,11},{4,6},{5,1},{6,14},{7,3},{8,0},{9,17},{1... | collective-permute-start | bytes 1179656 | tf_op jit(solution)/shard_map/ppermute | solution.py:66
  24.6 12.2 %collective-permute-start.10 = (bf16[2,256,384]{2,1,0:T(8,128)(2,1)S(1)}, bf16[2,256,384]{2,1,0:T(8,128)(2,1)}, u32[]{:S(2)}, u32[]{:S(2)}) collective-permute-start(bf16[2,256,384]{2,1,0:T(8,128)(2,1)S(1)} %collective-permute-done.6.refs_1_), channel_id=1, source_target_pairs={{0,8},{1,5},{2,0},{3,7},{4,12},{5,13},{6,4},{7,15},{8,16},{9,1},{1... | collective-permute-start | bytes 1179656 | tf_op jit(solution)/shard_map/ppermute | solution.py:66
  26.6 11.7 %collective-permute-start.3 = (bf16[2,256,384]{2,1,0:T(8,128)(2,1)S(1)}, bf16[2,256,384]{2,1,0:T(8,128)(2,1)S(1)}, u32[]{:S(2)}, u32[]{:S(2)}) collective-permute-start(bf16[2,256,384]{2,1,0:T(8,128)(2,1)S(1)} %collective-permute-done.2.refs_2_), channel_id=1, source_target_pairs={{0,4},{1,3},{2,6},{3,1},{4,0},{5,7},{6,2},{7,5},{8,12},{9,11},{10,... | collective-permute-start | bytes 1179656 | tf_op jit(solution)/shard_map/ppermute | solution.py:67
  27.0 0.7 copy-start.5
  27.8 13.8 %collective-permute-start.5 = (bf16[2,256,384]{2,1,0:T(8,128)(2,1)S(1)}, bf16[2,256,384]{2,1,0:T(8,128)(2,1)S(1)}, u32[]{:S(2)}, u32[]{:S(2)}) collective-permute-start(bf16[2,256,384]{2,1,0:T(8,128)(2,1)S(1)} %collective-permute-done.4.refs_4_), channel_id=1, source_target_pairs={{0,4},{1,3},{2,6},{3,1},{4,0},{5,7},{6,2},{7,5},{8,12},{9,11},{10,... | collective-permute-start | bytes 1179656 | tf_op jit(solution)/shard_map/ppermute | solution.py:67
  29.4 14.0 %collective-permute-start.12 = (bf16[2,256,384]{2,1,0:T(8,128)(2,1)}, bf16[2,256,384]{2,1,0:T(8,128)(2,1)}, u32[]{:S(2)}, u32[]{:S(2)}) collective-permute-start(bf16[2,256,384]{2,1,0:T(8,128)(2,1)} %collective-permute-done.8.refs_3_), channel_id=1, source_target_pairs={{0,2},{1,9},{2,10},{3,11},{4,6},{5,1},{6,14},{7,3},{8,0},{9,17},{1... | collective-permute-start | bytes 1179656 | tf_op jit(solution)/shard_map/ppermute | solution.py:66
  36.7 12.4 %collective-permute-start.14 = (bf16[2,256,384]{2,1,0:T(8,128)(2,1)}, bf16[2,256,384]{2,1,0:T(8,128)(2,1)}, u32[]{:S(2)}, u32[]{:S(2)}) collective-permute-start(bf16[2,256,384]{2,1,0:T(8,128)(2,1)} %collective-permute-done.10.refs_1_), channel_id=1, source_target_pairs={{0,8},{1,5},{2,0},{3,7},{4,12},{5,13},{6,4},{7,15},{8,16},{9,1},{1... | collective-permute-start | bytes 1179656 | tf_op jit(solution)/shard_map/ppermute | solution.py:66
  38.3 0.7 copy-start.7
  39.1 21.4 %collective-permute-start.7 = (bf16[2,256,384]{2,1,0:T(8,128)(2,1)S(1)}, bf16[2,256,384]{2,1,0:T(8,128)(2,1)}, u32[]{:S(2)}, u32[]{:S(2)}) collective-permute-start(bf16[2,256,384]{2,1,0:T(8,128)(2,1)S(1)} %collective-permute-done.6.refs_1_), channel_id=1, source_target_pairs={{0,4},{1,3},{2,6},{3,1},{4,0},{5,7},{6,2},{7,5},{8,12},{9,11},{10,... | collective-permute-start | bytes 1179656 | tf_op jit(solution)/shard_map/ppermute | solution.py:67
  41.6 0.8 copy-start.9
  42.4 18.1 %collective-permute-start.9 = (bf16[2,256,384]{2,1,0:T(8,128)(2,1)}, bf16[2,256,384]{2,1,0:T(8,128)(2,1)}, u32[]{:S(2)}, u32[]{:S(2)}) collective-permute-start(bf16[2,256,384]{2,1,0:T(8,128)(2,1)} %collective-permute-done.8.refs_3_), channel_id=1, source_target_pairs={{0,4},{1,3},{2,6},{3,1},{4,0},{5,7},{6,2},{7,5},{8,12},{9,11},{10,... | collective-permute-start | bytes 1179656 | tf_op jit(solution)/shard_map/ppermute | solution.py:67
  43.4 19.1 %collective-permute-start.11 = (bf16[2,256,384]{2,1,0:T(8,128)(2,1)}, bf16[2,256,384]{2,1,0:T(8,128)(2,1)}, u32[]{:S(2)}, u32[]{:S(2)}) collective-permute-start(bf16[2,256,384]{2,1,0:T(8,128)(2,1)} %collective-permute-done.10.refs_1_), channel_id=1, source_target_pairs={{0,4},{1,3},{2,6},{3,1},{4,0},{5,7},{6,2},{7,5},{8,12},{9,11},{10,... | collective-permute-start | bytes 1179656 | tf_op jit(solution)/shard_map/ppermute | solution.py:67
  49.1 13.4 %collective-permute-start.13 = (bf16[2,256,384]{2,1,0:T(8,128)(2,1)}, bf16[2,256,384]{2,1,0:T(8,128)(2,1)}, u32[]{:S(2)}, u32[]{:S(2)}) collective-permute-start(bf16[2,256,384]{2,1,0:T(8,128)(2,1)} %collective-permute-done.12.refs_3_), channel_id=1, source_target_pairs={{0,4},{1,3},{2,6},{3,1},{4,0},{5,7},{6,2},{7,5},{8,12},{9,11},{10,... | collective-permute-start | bytes 1179656 | tf_op jit(solution)/shard_map/ppermute | solution.py:67
  49.6 15.1 %collective-permute-start.15 = (bf16[2,256,384]{2,1,0:T(8,128)(2,1)}, bf16[2,256,384]{2,1,0:T(8,128)(2,1)}, u32[]{:S(2)}, u32[]{:S(2)}) collective-permute-start(bf16[2,256,384]{2,1,0:T(8,128)(2,1)} %collective-permute-done.14.refs_1_), channel_id=1, source_target_pairs={{0,4},{1,3},{2,6},{3,1},{4,0},{5,7},{6,2},{7,5},{8,12},{9,11},{10,... | collective-permute-start | bytes 1179656 | tf_op jit(solution)/shard_map/ppermute | solution.py:67
  52.3 1.6 %copy-start = (bf16[4,32,8192]{2,1,0:T(8,128)(2,1)S(1)}, bf16[4,32,8192]{2,1,0:T(8,128)(2,1)}, u32[]{:S(2)}) copy-start(bf16[4,32,8192]{2,1,0:T(8,128)(2,1)} %param.4) | copy-start | bytes 6291460
  53.9 1.0 copy-start.2
  54.9 1.0 copy-start.4
  55.9 1.0 copy-start.6
  56.9 1.0 copy-start.8
  57.8 1.0 copy-start.10
  58.8 1.7 %copy-start.1 = (bf16[4,32,8192]{2,1,0:T(8,128)(2,1)S(1)}, bf16[4,32,8192]{2,1,0:T(8,128)(2,1)}, u32[]{:S(2)}) copy-start(bf16[4,32,8192]{2,1,0:T(8,128)(2,1)} %param.4) | copy-start | bytes 6291460
  66.4 1.9 %collective-permute-start.16 = (f32[160,768]{1,0:T(8,128)S(1)}, f32[160,768]{1,0:T(8,128)S(1)}, u32[]{:S(2)}, u32[]{:S(2)}) collective-permute-start(f32[160,768]{1,0:T(8,128)S(1)} %slice.14), channel_id=1, source_target_pairs={{0,1},{1,0},{2,3},{3,2},{4,5},{5,4},{6,7},{7,6},{8,9},{9,8},{10,11... | collective-permute-start | bytes 1474568 | tf_op jit(solution)/shard_map/ppermute | solution.py:258
  68.3 35.5 %copy-start.11 = (s32[1,128]{1,0:T(1,128)S(1)}, s32[1,128]{1,0:T(1,128)}, u32[]{:S(2)}) copy-start(s32[1,128]{1,0:T(1,128)} %param.7) | copy-start | bytes 1540
  68.4 5.8 %collective-permute-start.18 = (bf16[256,384]{1,0:T(8,128)(2,1)S(1)}, bf16[256,384]{1,0:T(8,128)(2,1)S(1)}, u32[]{:S(2)}, u32[]{:S(2)}) collective-permute-start(bf16[256,384]{1,0:T(8,128)(2,1)S(1)} %get-tuple-element.16.refs_0_), channel_id=1, source_target_pairs={{0,8},{1,5},{2,0},{3,7},{4,12},{5,13},{6,4},{7,15},{8,16},{9,1},{1... | collective-permute-start | bytes 589832 | tf_op jit(solution)/shard_map/ppermute | solution.py:66
  69.1 7.5 %collective-permute-start.20 = (bf16[256,384]{1,0:T(8,128)(2,1)S(1)}, bf16[256,384]{1,0:T(8,128)(2,1)S(1)}, u32[]{:S(2)}, u32[]{:S(2)}) collective-permute-start(bf16[256,384]{1,0:T(8,128)(2,1)S(1)} %get-tuple-element.16.refs_0_), channel_id=1, source_target_pairs={{0,2},{1,9},{2,10},{3,11},{4,6},{5,1},{6,14},{7,3},{8,0},{9,17},{1... | collective-permute-start | bytes 589832 | tf_op jit(solution)/shard_map/ppermute | solution.py:66
  74.1 7.2 %collective-permute-start.22 = (bf16[256,384]{1,0:T(8,128)(2,1)S(1)}, bf16[256,384]{1,0:T(8,128)(2,1)S(1)}, u32[]{:S(2)}, u32[]{:S(2)}) collective-permute-start(bf16[256,384]{1,0:T(8,128)(2,1)S(1)} %collective-permute-done.18.refs_2_), channel_id=1, source_target_pairs={{0,8},{1,5},{2,0},{3,7},{4,12},{5,13},{6,4},{7,15},{8,16},{9,1},{1... | collective-permute-start | bytes 589832 | tf_op jit(solution)/shard_map/ppermute | solution.py:66
  76.6 9.2 %collective-permute-start.24 = (bf16[256,384]{1,0:T(8,128)(2,1)S(1)}, bf16[256,384]{1,0:T(8,128)(2,1)S(1)}, u32[]{:S(2)}, u32[]{:S(2)}) collective-permute-start(bf16[256,384]{1,0:T(8,128)(2,1)S(1)} %collective-permute-done.20.refs_4_), channel_id=1, source_target_pairs={{0,2},{1,9},{2,10},{3,11},{4,6},{5,1},{6,14},{7,3},{8,0},{9,17},{1... | collective-permute-start | bytes 589832 | tf_op jit(solution)/shard_map/ppermute | solution.py:66
  76.6 9.2 %collective-permute-start.17 = (bf16[256,384]{1,0:T(8,128)(2,1)S(1)}, bf16[256,384]{1,0:T(8,128)(2,1)S(1)}, u32[]{:S(2)}, u32[]{:S(2)}) collective-permute-start(bf16[256,384]{1,0:T(8,128)(2,1)S(1)} %get-tuple-element.16.refs_0_), channel_id=1, source_target_pairs={{0,4},{1,3},{2,6},{3,1},{4,0},{5,7},{6,2},{7,5},{8,12},{9,11},{10,... | collective-permute-start | bytes 589832 | tf_op jit(solution)/shard_map/ppermute | solution.py:67
  81.3 7.8 %collective-permute-start.26 = (bf16[256,384]{1,0:T(8,128)(2,1)S(1)}, bf16[256,384]{1,0:T(8,128)(2,1)S(1)}, u32[]{:S(2)}, u32[]{:S(2)}) collective-permute-start(bf16[256,384]{1,0:T(8,128)(2,1)S(1)} %collective-permute-done.22.refs_0_), channel_id=1, source_target_pairs={{0,8},{1,5},{2,0},{3,7},{4,12},{5,13},{6,4},{7,15},{8,16},{9,1},{1... | collective-permute-start | bytes 589832 | tf_op jit(solution)/shard_map/ppermute | solution.py:66
  83.8 6.4 %collective-permute-start.19 = (bf16[256,384]{1,0:T(8,128)(2,1)S(1)}, bf16[256,384]{1,0:T(8,128)(2,1)S(1)}, u32[]{:S(2)}, u32[]{:S(2)}) collective-permute-start(bf16[256,384]{1,0:T(8,128)(2,1)S(1)} %collective-permute-done.18.refs_2_), channel_id=1, source_target_pairs={{0,4},{1,3},{2,6},{3,1},{4,0},{5,7},{6,2},{7,5},{8,12},{9,11},{10,... | collective-permute-start | bytes 589832 | tf_op jit(solution)/shard_map/ppermute | solution.py:67
  83.8 7.8 %collective-permute-start.21 = (bf16[256,384]{1,0:T(8,128)(2,1)S(1)}, bf16[256,384]{1,0:T(8,128)(2,1)S(1)}, u32[]{:S(2)}, u32[]{:S(2)}) collective-permute-start(bf16[256,384]{1,0:T(8,128)(2,1)S(1)} %collective-permute-done.20.refs_4_), channel_id=1, source_target_pairs={{0,4},{1,3},{2,6},{3,1},{4,0},{5,7},{6,2},{7,5},{8,12},{9,11},{10,... | collective-permute-start | bytes 589832 | tf_op jit(solution)/shard_map/ppermute | solution.py:67
  85.8 7.9 %collective-permute-start.28 = (bf16[256,384]{1,0:T(8,128)(2,1)S(1)}, bf16[256,384]{1,0:T(8,128)(2,1)S(1)}, u32[]{:S(2)}, u32[]{:S(2)}) collective-permute-start(bf16[256,384]{1,0:T(8,128)(2,1)S(1)} %collective-permute-done.24.refs_2_), channel_id=1, source_target_pairs={{0,2},{1,9},{2,10},{3,11},{4,6},{5,1},{6,14},{7,3},{8,0},{9,17},{1... | collective-permute-start | bytes 589832 | tf_op jit(solution)/shard_map/ppermute | solution.py:66
  85.8 8.8 %collective-permute-start.23 = (bf16[256,384]{1,0:T(8,128)(2,1)S(1)}, bf16[256,384]{1,0:T(8,128)(2,1)S(1)}, u32[]{:S(2)}, u32[]{:S(2)}) collective-permute-start(bf16[256,384]{1,0:T(8,128)(2,1)S(1)} %collective-permute-done.22.refs_0_), channel_id=1, source_target_pairs={{0,4},{1,3},{2,6},{3,1},{4,0},{5,7},{6,2},{7,5},{8,12},{9,11},{10,... | collective-permute-start | bytes 589832 | tf_op jit(solution)/shard_map/ppermute | solution.py:67
  89.1 7.8 %collective-permute-start.30 = (bf16[256,384]{1,0:T(8,128)(2,1)S(1)}, bf16[256,384]{1,0:T(8,128)(2,1)S(1)}, u32[]{:S(2)}, u32[]{:S(2)}) collective-permute-start(bf16[256,384]{1,0:T(8,128)(2,1)S(1)} %collective-permute-done.26.refs_0_), channel_id=1, source_target_pairs={{0,8},{1,5},{2,0},{3,7},{4,12},{5,13},{6,4},{7,15},{8,16},{9,1},{1... | collective-permute-start | bytes 589832 | tf_op jit(solution)/shard_map/ppermute | solution.py:66
  90.1 8.1 %collective-permute-start.25 = (bf16[256,384]{1,0:T(8,128)(2,1)S(1)}, bf16[256,384]{1,0:T(8,128)(2,1)S(1)}, u32[]{:S(2)}, u32[]{:S(2)}) collective-permute-start(bf16[256,384]{1,0:T(8,128)(2,1)S(1)} %collective-permute-done.24.refs_2_), channel_id=1, source_target_pairs={{0,4},{1,3},{2,6},{3,1},{4,0},{5,7},{6,2},{7,5},{8,12},{9,11},{10,... | collective-permute-start | bytes 589832 | tf_op jit(solution)/shard_map/ppermute | solution.py:67
  91.6 7.1 %collective-permute-start.27 = (bf16[256,384]{1,0:T(8,128)(2,1)S(1)}, bf16[256,384]{1,0:T(8,128)(2,1)S(1)}, u32[]{:S(2)}, u32[]{:S(2)}) collective-permute-start(bf16[256,384]{1,0:T(8,128)(2,1)S(1)} %collective-permute-done.26.refs_0_), channel_id=1, source_target_pairs={{0,4},{1,3},{2,6},{3,1},{4,0},{5,7},{6,2},{7,5},{8,12},{9,11},{10,... | collective-permute-start | bytes 589832 | tf_op jit(solution)/shard_map/ppermute | solution.py:67
  93.7 6.4 %collective-permute-start.29 = (bf16[256,384]{1,0:T(8,128)(2,1)S(1)}, bf16[256,384]{1,0:T(8,128)(2,1)S(1)}, u32[]{:S(2)}, u32[]{:S(2)}) collective-permute-start(bf16[256,384]{1,0:T(8,128)(2,1)S(1)} %collective-permute-done.28.refs_2_), channel_id=1, source_target_pairs={{0,4},{1,3},{2,6},{3,1},{4,0},{5,7},{6,2},{7,5},{8,12},{9,11},{10,... | collective-permute-start | bytes 589832 | tf_op jit(solution)/shard_map/ppermute | solution.py:67
  94.7 9.2 %collective-permute-start.32 = (bf16[576,384]{1,0:T(8,128)(2,1)S(1)}, bf16[576,384]{1,0:T(8,128)(2,1)S(1)}, u32[]{:S(2)}, u32[]{:S(2)}) collective-permute-start(bf16[576,384]{1,0:T(8,128)(2,1)S(1)} %get-tuple-element.21), channel_id=1, source_target_pairs={{0,1},{1,0},{2,3},{3,2},{4,5},{5,4},{6,7},{7,6},{8,9},{9,8},{10,11... | collective-permute-start | bytes 1327112 | tf_op jit(solution)/shard_map/ppermute | solution.py:267
  97.0 5.7 %collective-permute-start.31 = (bf16[256,384]{1,0:T(8,128)(2,1)S(1)}, bf16[256,384]{1,0:T(8,128)(2,1)S(1)}, u32[]{:S(2)}, u32[]{:S(2)}) collective-permute-start(bf16[256,384]{1,0:T(8,128)(2,1)S(1)} %collective-permute-done.30.refs_0_), channel_id=1, source_target_pairs={{0,4},{1,3},{2,6},{3,1},{4,0},{5,7},{6,2},{7,5},{8,12},{9,11},{10,... | collective-permute-start | bytes 589832 | tf_op jit(solution)/shard_map/ppermute | solution.py:67
  98.6 5.4 %collective-permute-start.33 = (bf16[384,384]{1,0:T(8,128)(2,1)S(1)}, bf16[384,384]{1,0:T(8,128)(2,1)S(1)}, u32[]{:S(2)}, u32[]{:S(2)}) collective-permute-start(bf16[384,384]{1,0:T(8,128)(2,1)S(1)} %get-tuple-element.22), channel_id=1, source_target_pairs={{0,1},{1,0},{2,3},{3,2},{4,5},{5,4},{6,7},{7,6},{8,9},{9,8},{10,11... | collective-permute-start | bytes 884744 | tf_op jit(solution)/shard_map/ppermute | solution.py:267
  100.4 3.5 %collective-permute-start.34 = (bf16[384,384]{1,0:T(8,128)(2,1)S(1)}, bf16[384,384]{1,0:T(8,128)(2,1)S(1)}, u32[]{:S(2)}, u32[]{:S(2)}) collective-permute-start(bf16[384,384]{1,0:T(8,128)(2,1)S(1)} %get-tuple-element.23), channel_id=1, source_target_pairs={{0,1},{1,0},{2,3},{3,2},{4,5},{5,4},{6,7},{7,6},{8,9},{9,8},{10,11... | collective-permute-start | bytes 884744 | tf_op jit(solution)/shard_map/ppermute | solution.py:267
  103.6 1.6 %collective-permute-start.35 = (bf16[192,384]{1,0:T(8,128)(2,1)}, bf16[192,384]{1,0:T(8,128)(2,1)S(1)}, u32[]{:S(2)}, u32[]{:S(2)}) collective-permute-start(bf16[192,384]{1,0:T(8,128)(2,1)} %get-tuple-element.24), channel_id=1, source_target_pairs={{0,1},{1,0},{2,3},{3,2},{4,5},{5,4},{6,7},{7,6},{8,9},{9,8},{10,11... | collective-permute-start | bytes 442376 | tf_op jit(solution)/shard_map/ppermute | solution.py:267

commit v3 on v2

v3 whole, which is shorter than its diff:
```python
import functools

import jax
import jax.numpy as jnp
from jax import lax
from jax.experimental import pallas as pl
from jax.experimental.pallas import tpu as pltpu
from jax.sharding import PartitionSpec as P

SHW = 4
LANES = 128
F32, BF16 = jnp.float32, jnp.bfloat16
VMEM_LIMIT = 16 * 1024 * 1024


class Grid:
    def __init__(self, n_pair):
        assert n_pair % 8 == 0
        self.nz = n_pair // 8
        self.ring = 2 * self.nz

    def device(self, spot, side, core):
        turned = (spot >= self.nz) * 1
        z = spot + turned * (self.ring - 1 - 2 * spot)
        x = turned + core * (side - turned)
        y = side + core * (turned - side)
        return ((z * 2 + y) * 2 + x) * 2 + core

    def place(self, device):
        core, x, y, z = device % 2, device // 2 % 2, device // 4 % 2, device // 8
        turned = x + core * (y - x)
        side = y + core * (x - y)
        return z + turned * (self.ring - 1 - 2 * z), side, core

    def moves(self, target):
        every = range(self.ring * 4)
        return [(device, int(self.device(*target(*self.place(device))))) for device in every]

    def around(self, way):
        return self.moves(lambda spot, side, core: ((spot + way * (1 - 2 * core)) % self.ring, side, core))

    def mate(self, device):
        return device + 1 - 2 * (device % 2)

    def opposite(self, device):
        spot, side, core = self.place(device)
        return self.device(spot, 1 - side, core)

    def helpers(self, device):
        return [device, self.mate(device), self.opposite(device), self.opposite(self.mate(device))]

    def helped(self, device):
        return [device, self.mate(device), self.opposite(device), self.mate(self.opposite(device))]

    def exchange(self, blocks, partners):
        every = range(self.ring * 4)
        return [
            lax.ppermute(block, "pair", [(device, int(partners(device)[k])) for device in every])
            for k, block in zip((1, 2, 3), blocks)
        ]

    def spot(self, device, offset):
        spot, _, core = self.place(device)
        return (spot + offset * (1 - 2 * core) + self.ring) % self.ring

    def source_at(self, device, spot):
        _, side, core = self.place(device)
        return self.device(spot, side, core)

    def source(self, device, offset):
        _, side, core = self.place(device)
        return self.device(self.spot(device, offset), side, core)


def gather_ring(grid, own):
    around = {-1: grid.around(1), 1: grid.around(-1)}
    held, groups = {0: own}, [[0]]
    for step in range(1, grid.nz + 1):
        ways = (-1, 1) if step < grid.nz else (-1,)
        for way in ways:
            held[way * step] = lax.ppermute(held[way * (step - 1)], "pair", around[way])
        groups.append([way * step for way in ways])
    return held, [groups[0] + groups[1]] + groups[2:]


def vmem(count):
    return [pl.BlockSpec(memory_space=pltpu.VMEM)] * count


PARAMS = pltpu.CompilerParams(vmem_limit_bytes=VMEM_LIMIT)


def share_integrals(columns, integrals, depth):
    rows = integrals.shape[0]
    partners, ring = columns.shape

    def body(columns_ref, ints_ref, *refs):
        outs, moved = refs[:-1], refs[-1]
        copies = []
        for k, out in enumerate(outs):
            for spot in range(ring):
                start = pl.multiple_of(columns_ref[k, spot] * depth, depth)
                copies.append(
                    pltpu.make_async_copy(
                        ints_ref.at[:, pl.ds(start, depth)], out.at[:, pl.ds(spot * depth, depth)], moved.at[k, spot]
                    )
                )
        for copy in copies:
            copy.start()
        for copy in copies:
            copy.wait()

    return pl.pallas_call(
        body,
        out_shape=[jax.ShapeDtypeStruct((rows, ring * depth), BF16)] * partners,
        in_specs=[pl.BlockSpec(memory_space=pltpu.SMEM), pl.BlockSpec(memory_space=pl.ANY)],
        out_specs=vmem(partners),
        scratch_shapes=[pltpu.SemaphoreType.DMA((partners, ring))],
        compiler_params=PARAMS,
        name="share_integrals",
    )(columns, integrals)


def first_product(spots, source, ints, batch_column, total, blocks, last):
    parts, depth, width = blocks[0].shape
    rows, batch_rows = ints[0].shape[0], batch_column.shape[0]
    high = len(ints) * rows + batch_rows
    begins = total is None

    def body(spots_ref, source_ref, batch_ref, *refs):
        ints_refs, refs = refs[: len(ints)], refs[len(ints):]
        total_ref, refs = (None, refs) if begins else (refs[0], refs[1:])
        block_refs, outs = refs[: len(blocks)], refs[len(blocks):]
        sum_ref = outs[-1]
        for number, ref in enumerate(block_refs):
            columns = pl.ds(pl.multiple_of(spots_ref[number] * depth, depth), depth)
            position = lax.broadcasted_iota(jnp.int32, (batch_rows, depth), 1) + source_ref[number] * depth
            picks = (batch_ref[...] == position).astype(F32).astype(BF16)
            left = jnp.concatenate([ints_ref[:, columns] for ints_ref in ints_refs] + [picks], axis=0)
            for part in range(parts):
                term = jnp.dot(left, ref[part], preferred_element_type=F32)
                lanes = pl.ds(part * width, width)
                if number > 0:
                    sum_ref[:, lanes] += term
                elif begins:
                    sum_ref[:, lanes] = term
                else:
                    sum_ref[:, lanes] = total_ref[:, lanes] + term
        if last:
            for k, out in enumerate(outs[:-1]):
                out[:rows, :] = sum_ref[k * rows:(k + 1) * rows, :].astype(out.dtype)
                out[rows:, :] = sum_ref[len(ints) * rows:, :].astype(out.dtype)

    totals = [] if begins else [total]
    whole = jax.ShapeDtypeStruct((high, parts * width), F32)
    kinds = (F32, F32, BF16, BF16)
    shapes = [jax.ShapeDtypeStruct((rows + batch_rows, parts * width), kind) for kind in kinds] if last else [whole]
    return pl.pallas_call(
        body,
        out_shape=shapes,
        in_specs=[pl.BlockSpec(memory_space=pltpu.SMEM)] * 2 + vmem(1 + len(ints) + len(totals) + len(blocks)),
        out_specs=vmem(len(shapes)),
        scratch_shapes=[pltpu.VMEM(whole.shape, F32)] if last else [],
        compiler_params=PARAMS,
        cost_estimate=pl.CostEstimate(
            flops=10 * high * depth * width * parts * len(blocks), bytes_accessed=0, transcendentals=0
        ),
        name="first_product",
    )(spots, source, batch_column, *ints, *totals, *blocks)


def add_partners(sums, rows, width):
    batch_rows = sums[0].shape[0] - rows

    def body(*refs):
        half_ref, batch_ref = refs[-2:]
        for part in range(2):
            lanes = pl.ds(part * width, width)
            both = sum(ref[:, lanes].astype(F32) for ref in refs[:-2]).astype(BF16)
            half_ref[part * rows:(part + 1) * rows, :] = both[:rows]
            batch_ref[part * batch_rows:(part + 1) * batch_rows, :] = both[rows:]

    return pl.pallas_call(
        body,
        out_shape=[jax.ShapeDtypeStruct((2 * n, width), BF16) for n in (rows, batch_rows)],
        in_specs=vmem(len(sums)),
        out_specs=vmem(2),
        compiler_params=PARAMS,
        name="add_partners",
    )(*sums)


def weights(devices, batch, slots, share):
    batch_rows, width = batch.shape[0] // 2, batch.shape[1]
    partners = devices.shape[0]
    each = slots * 2 * share
    deep = slots * batch_rows

    def body(devices_ref, batch_ref, out_ref):
        repeat = (
            lax.broadcasted_iota(jnp.int32, (batch_rows, deep), 0)
            == lax.rem(lax.broadcasted_iota(jnp.int32, (batch_rows, deep), 1), batch_rows)
        ).astype(F32).astype(BF16)
        row = lax.broadcasted_iota(jnp.int32, (each, deep), 0)
        keep = lax.rem(lax.div(row, 2 * share), slots) == lax.div(
            lax.broadcasted_iota(jnp.int32, (each, deep), 1), batch_rows
        )
        real = lax.rem(lax.div(row, share), 2) == 0
        row = lax.broadcasted_iota(jnp.int32, (each, width), 0)
        column = lax.broadcasted_iota(jnp.int32, (each, width), 1)
        for k in range(partners):
            chosen = (column == devices_ref[k] * share + lax.rem(row, share)).astype(F32).astype(BF16)

            def spread(part):
                rows = batch_ref[part * batch_rows:(part + 1) * batch_rows, :]
                picked = lax.dot_general(chosen, rows, (((1,), (1,)), ((), ())), preferred_element_type=F32)
                return jnp.dot(picked.astype(BF16), repeat, preferred_element_type=F32)

            re, im = spread(0), spread(1)
            here = pl.ds(k * each, each)
            out_ref[here, :deep] = jnp.where(keep, jnp.where(real, re, -im), 0.0).astype(BF16)
            out_ref[here, deep:] = jnp.where(keep, jnp.where(real, im, re), 0.0).astype(BF16)

    return pl.pallas_call(
        body,
        out_shape=jax.ShapeDtypeStruct((partners * each, 2 * deep), BF16),
        in_specs=[pl.BlockSpec(memory_space=pltpu.SMEM)] + vmem(1),
        out_specs=pl.BlockSpec(memory_space=pltpu.VMEM),
        compiler_params=PARAMS,
        name="weights",
    )(devices, batch)


def second_product(matrix, blocks, partners):
    each = matrix.shape[0] // partners
    width = blocks[0].shape[1]

    def body(matrix_ref, *refs):
        block_refs, outs = refs[: len(blocks)], refs[len(blocks):]
        for number, ref in enumerate(block_refs):
            every = jnp.dot(matrix_ref[...], ref[...], preferred_element_type=F32).astype(BF16)
            for k, out in enumerate(outs):
                out[number * each:(number + 1) * each, :] = every[k * each:(k + 1) * each]

    return pl.pallas_call(
        body,
        out_shape=[jax.ShapeDtypeStruct((len(blocks) * each, width), BF16)] * partners,
        in_specs=vmem(1 + len(blocks)),
        out_specs=vmem(partners),
        compiler_params=PARAMS,
        name="second_product",
    )(matrix, *blocks)


def place_pairs(order, pair_column, pieces, share):
    width = pieces[0].shape[1]
    slots = order.shape[0]
    each = 2 * share

    def body(order_ref, pair_ref, *refs):
        piece_refs, out_ref, held = refs[: len(pieces)], refs[-2], refs[-1]
        start = 0
        for ref in piece_refs:
            for tile in range(width // LANES):
                held[tile, start:start + ref.shape[0], :] = ref[:, tile * LANES:(tile + 1) * LANES].astype(F32)
            start += ref.shape[0]
        lane = lax.broadcasted_iota(jnp.int32, (slots, slots), 1)
        ordered = (order_ref[...] == lane).astype(F32).astype(BF16)
        paired = (pair_ref[...] == lane).astype(F32).astype(BF16)
        place = jnp.dot(ordered, paired, preferred_element_type=F32).astype(BF16)
        for number in range(each):
            for tile in range(width // LANES):
                rows = held[tile, pl.ds(number, slots, stride=each), :].astype(BF16)
                placed = lax.dot_general(rows, place, (((0,), (0,)), ((), ())), preferred_element_type=F32)
                lanes = pl.ds(tile * LANES, LANES)
                out_ref[number // share, number % share, lanes, :] = placed.astype(BF16)

    return pl.pallas_call(
        body,
        out_shape=jax.ShapeDtypeStruct((2, share, width, slots), BF16),
        in_specs=vmem(2 + len(pieces)),
        out_specs=pl.BlockSpec(memory_space=pltpu.VMEM),
        scratch_shapes=[pltpu.VMEM((width // LANES, slots * each, LANES), F32)],
        compiler_params=PARAMS,
        name="place_pairs",
    )(order, pair_column, *pieces)


def on_device(n_coef, n_pair, integrals, coefficients, shell_starts, pair_ids):
    grid = Grid(n_pair)
    slots, batch_rows, ao_width = integrals.shape
    occupied = coefficients.shape[2]
    share = occupied // n_pair
    rows = slots * batch_rows
    depth = ao_width // n_pair
    piece = depth // n_coef
    me = lax.axis_index("pair").astype(jnp.int32)

    batch_index = (shell_starts[:, None] + jnp.arange(SHW, dtype=jnp.int32)[None, :]).reshape(-1)
    flat_ints = integrals.reshape(rows, ao_width)
    if n_coef > 1:
        coefficients = lax.all_gather(coefficients, "coef", axis=1, tiled=True)
        flat_ints = flat_ints.reshape(rows, n_coef, n_pair, piece).transpose(0, 2, 1, 3).reshape(rows, ao_width)
        batch_index = (
            batch_index // piece % n_pair * depth + batch_index // (n_pair * piece) * piece + batch_index % piece
        )
    batch_column = batch_index[:, None]

    helpers, helped = grid.helpers(me), grid.helped(me)
    columns = jnp.stack([grid.source_at(device, jnp.arange(grid.ring, dtype=jnp.int32)) for device in helpers])
    kept, *leaving = share_integrals(columns, flat_ints, depth)
    ints = [kept, *grid.exchange(leaving, grid.helpers)]
    held, groups = gather_ring(grid, coefficients)
    total = None
    for number, group in enumerate(groups):
        spots = jnp.stack([grid.spot(me, offset) for offset in group])
        source = jnp.stack([grid.source(me, offset) for offset in group])
        last = number == len(groups) - 1
        blocks = [held[offset] for offset in group]
        result = first_product(spots, source, ints, batch_column, total, blocks, last)
        total = result[0]
    kept, *leaving = result
    half, batch = add_partners([kept, *grid.exchange(leaving, grid.helped)], rows, occupied)
    matrix = weights(jnp.stack(helped), batch, slots, share)

    held, groups = gather_ring(grid, half)
    pieces, order = [], []
    within = jnp.arange(slots, dtype=jnp.int32)
    for group in groups:
        kept, *leaving = second_product(matrix, [held[offset] for offset in group], len(helped))
        pieces += [kept, *grid.exchange(leaving, grid.helped)]
        order += [grid.source(device, offset) * slots + within for device in helpers for offset in group]
    return place_pairs(jnp.concatenate(order)[:, None], pair_ids.reshape(-1)[:, None], pieces, share)


def solution(mesh):
    return jax.shard_map(
        functools.partial(on_device, mesh.shape["coef"], mesh.shape["pair"]),
        mesh=mesh,
        in_specs=(
            P(("coef", "pair"), None, None),
            P(None, ("coef", "pair"), None),
            P(),
            P("coef", None),
        ),
        out_specs=P(None, "pair", None, "coef"),
        check_vma=False,
    )
```

time: 108 us -> 97.8 us (0.906)
  waiting for transfers between devices: 51 us -> 37.7 us
  local copies, waits for them, and re-layouts: 9.4 us -> 4.06 us
  other arithmetic: 1.06 us -> 5.64 us
  Pallas kernels: 12.8 us -> 14.8 us
  starting transfers between devices: 33 us -> 35 us
    ppermute x36 -> x32, waiting for transfers between devices: 51 us -> 37.7 us  [the longest x14 28.8 us: gather_ring(): held[way * step] = lax.ppermute(held[way * (step - 1)], 'pair', around[way])]
    unnamed x24 -> x8, local copies, waits for them, and re-layouts: 8.85 us -> 2.28 us
    add x16 -> x19, other arithmetic: 0.08 us -> 5.25 us  [the longest x17 5.22 us: on_device(): grid.source(device, offset) * slots + within]
    pallas_call x10 -> x11, Pallas kernels: 10 us -> 12 us  [the longest x4 5.11 us: first_product(): pl.pallas_call(body, out_shape=shapes, in_specs=[pl.BlockSpec(memory_spac...]
    ppermute x36 -> x32, starting transfers between devices: 33 us -> 35 us  [the longest x14 19.2 us: gather_ring(): held[way * step] = lax.ppermute(held[way * (step - 1)], 'pair', around[way])]
  transfers between devices with their start and end apart: 36 -> 32, of which waited for: 13 -> 12; matrix products, arithmetic and copies ran while one was open for 1% -> 8% of each run, Pallas kernels for 8% -> 12%
where the time goes in v3:
time: 97.8 us; the launch traced here: 97.5 us
  waiting for transfers between devices  37.7 us (39%)
  starting transfers between devices  35 us (36%)
  Pallas kernels  14.8 us (15%)
  other arithmetic  5.64 us (6%)
  local copies, waits for them, and re-layouts  4.06 us (4%)
    ppermute x14, waiting for transfers between devices, gather_ring(): held[way * step] = lax.ppermute(held[way * (step - 1)], 'pair', around[way])  28.8 us
    ppermute x14, starting transfers between devices, gather_ring(): held[way * step] = lax.ppermute(held[way * (step - 1)], 'pair', around[way])  19.2 us
    ppermute x18, starting transfers between devices, exchange(): lax.ppermute(block, 'pair', [(device, int(partners(device)[k])) for devic...  15.8 us
    ppermute x18, waiting for transfers between devices, exchange(): lax.ppermute(block, 'pair', [(device, int(partners(device)[k])) for devic...  8.9 us
    add x17, other arithmetic, on_device(): grid.source(device, offset) * slots + within  5.22 us
    pallas_call x4, Pallas kernels, first_product(): pl.pallas_call(body, out_shape=shapes, in_specs=[pl.BlockSpec(memory_spac...  5.11 us
    pallas_call x1, Pallas kernels, place_pairs(): pl.pallas_call(body, out_shape=jax.ShapeDtypeStruct((2, share, width, slo...  2.81 us
    pallas_call x4, Pallas kernels, second_product(): pl.pallas_call(body, out_shape=[jax.ShapeDtypeStruct((len(blocks) * each,...  2.68 us
  transfers between devices with their start and end apart: 32, of which 12 were waited for; matrix products, arithmetic and copies ran while one was open for 8% of the time, Pallas kernels for 12%

profile of v3, /device:TPU:0, one launch (start us, length us, event | category | flops | bytes accessed | tf_op | source)
XLA Modules:
  0.0 97.5 jit_solution(7213887244098327458)
XLA Ops:
  0.0 3.0 %collective-permute-start.3 = (bf16[2,256,384]{2,1,0:T(8,128)(2,1)}, bf16[2,256,384]{2,1,0:T(8,128)(2,1)S(1)}, u32[]{:S(2)}, u32[]{:S(2)}) collective-permute-start(bf16[2,256,384]{2,1,0:T(8,128)(2,1)} %refs_4_.1), channel_id=1, source_target_pairs={{0,8},{1,5},{2,0},{3,7},{4,12},{5,13},{6,4},{7,15},{8,16},{9,1},{1... | collective-permute-start | bytes 1179656 | tf_op jit(solution)/shard_map/ppermute | solution.py:81
  3.2 1.6 %copy-done = bf16[4,32,8192]{2,1,0:T(8,128)(2,1)S(1)} copy-done((bf16[4,32,8192]{2,1,0:T(8,128)(2,1)S(1)}, bf16[4,32,8192]{2,1,0:T(8,128)(2,1)}, u32[]{:S(2)}) %copy-start) | copy-done | bytes 2097176
  4.7 2.3 %share_integrals.1 = (bf16[128,2048]{1,0:T(8,128)(2,1)S(1)}, bf16[128,2048]{1,0:T(8,128)(2,1)}, bf16[128,2048]{1,0:T(8,128)(2,1)}, bf16[128,2048]{1,0:T(8,128)(2,1)S(1)}) custom-call(s32[4,8]{1,0:T(4,128)S(1)} %pad_add_fusion.columns_ref, bf16[128,8192]{1,0:T(8,128)(2,1)S(1)} %bitcast.23), custom_call_target="tpu_custom_call" | custom-call | tf_op jit(solution)/shard_map/share_integrals/pallas_call | solution.py:113
  7.2 2.0 %collective-permute-start.1 = (bf16[128,2048]{1,0:T(8,128)(2,1)}, bf16[128,2048]{1,0:T(8,128)(2,1)S(1)}, u32[]{:S(2)}, u32[]{:S(2)}) collective-permute-start(bf16[128,2048]{1,0:T(8,128)(2,1)} %get-tuple-element.33), channel_id=1, source_target_pairs={{0,4},{1,3},{2,6},{3,1},{4,0},{5,7},{6,2},{7,5},{8,12},{9,11},{10,... | collective-permute-start | bytes 1572872 | tf_op jit(solution)/shard_map/ppermute | solution.py:58
  9.5 2.2 %collective-permute-done.3.refs_5_ = bf16[2,256,384]{2,1,0:T(8,128)(2,1)S(1)} collective-permute-done((bf16[2,256,384]{2,1,0:T(8,128)(2,1)}, bf16[2,256,384]{2,1,0:T(8,128)(2,1)S(1)}, u32[]{:S(2)}, u32[]{:S(2)}) %collective-permute-start.3) | collective-permute-done | bytes 393248 | tf_op jit(solution)/shard_map/ppermute | solution.py:81
  11.7 2.4 %collective-permute-start.5 = (bf16[2,256,384]{2,1,0:T(8,128)(2,1)S(1)}, bf16[2,256,384]{2,1,0:T(8,128)(2,1)S(1)}, u32[]{:S(2)}, u32[]{:S(2)}) collective-permute-start(bf16[2,256,384]{2,1,0:T(8,128)(2,1)S(1)} %collective-permute-done.3.refs_5_), channel_id=1, source_target_pairs={{0,8},{1,5},{2,0},{3,7},{4,12},{5,13},{6,4},{7,15},{8,16},{9,1},{1... | collective-permute-start | bytes 1179656 | tf_op jit(solution)/shard_map/ppermute | solution.py:81
  14.1 0.1 pad_add_fusion.4
  14.2 0.1 pad_add_fusion.2
  14.3 11.8 %collective-permute-done.5.refs_5_ = bf16[2,256,384]{2,1,0:T(8,128)(2,1)S(1)} collective-permute-done((bf16[2,256,384]{2,1,0:T(8,128)(2,1)S(1)}, bf16[2,256,384]{2,1,0:T(8,128)(2,1)S(1)}, u32[]{:S(2)}, u32[]{:S(2)}) %collective-permute-start.5) | collective-permute-done | bytes 393248 | tf_op jit(solution)/shard_map/ppermute | solution.py:81
  26.1 0.1 pad_add_fusion.6
  26.2 2.0 %collective-permute-start.8 = (bf16[2,256,384]{2,1,0:T(8,128)(2,1)S(1)}, bf16[2,256,384]{2,1,0:T(8,128)(2,1)S(1)}, u32[]{:S(2)}, u32[]{:S(2)}) collective-permute-start(bf16[2,256,384]{2,1,0:T(8,128)(2,1)S(1)} %collective-permute-done.6.refs_6_), channel_id=1, source_target_pairs={{0,2},{1,9},{2,10},{3,11},{4,6},{5,1},{6,14},{7,3},{8,0},{9,17},{1... | collective-permute-start | bytes 1179656 | tf_op jit(solution)/shard_map/ppermute | solution.py:81
  28.2 2.0 %first_product.4.refs_4_ = f32[544,768]{1,0:T(8,128)S(1)} custom-call(s32[3]{0:T(128)S(1)} %get-tuple-element.91.spots_ref, s32[3]{0:T(128)S(1)} %get-tuple-element.92.source_ref, s32[32,1]{1,0:T(8,128)S(1)} %add.2384.batch_ref, bf16[128,2048]{1,0:T(8,128)(2,1)S(1)} %get-tuple-element.31.refs_0_, bf16[128,2048]{1,0:T(8,128)(2,1)S(1)} %collective-permute-done.refs_1_, ...), custom_call_target="tpu_custom_call" | custom-call | flops 3208642560 | tf_op jit(solution)/shard_map/first_product/pallas_call | solution.py:158
  30.3 4.5 %collective-permute-done.7.refs_5_ = bf16[2,256,384]{2,1,0:T(8,128)(2,1)S(1)} collective-permute-done((bf16[2,256,384]{2,1,0:T(8,128)(2,1)S(1)}, bf16[2,256,384]{2,1,0:T(8,128)(2,1)S(1)}, u32[]{:S(2)}, u32[]{:S(2)}) %collective-permute-start.7) | collective-permute-done | bytes 393248 | tf_op jit(solution)/shard_map/ppermute | solution.py:81
  34.8 2.5 %collective-permute-start.9 = (bf16[2,256,384]{2,1,0:T(8,128)(2,1)S(1)}, bf16[2,256,384]{2,1,0:T(8,128)(2,1)S(1)}, u32[]{:S(2)}, u32[]{:S(2)}) collective-permute-start(bf16[2,256,384]{2,1,0:T(8,128)(2,1)S(1)} %collective-permute-done.7.refs_5_), channel_id=1, source_target_pairs={{0,8},{1,5},{2,0},{3,7},{4,12},{5,13},{6,4},{7,15},{8,16},{9,1},{1... | collective-permute-start | bytes 1179656 | tf_op jit(solution)/shard_map/ppermute | solution.py:81
  37.3 1.3 %first_product.5.refs_4_ = f32[544,768]{1,0:T(8,128)S(1)} custom-call(s32[2]{0:T(128)S(1)} %get-tuple-element.93.spots_ref, s32[2]{0:T(128)S(1)} %get-tuple-element.94.source_ref, s32[32,1]{1,0:T(8,128)S(1)} %add.2384.batch_ref, bf16[128,2048]{1,0:T(8,128)(2,1)S(1)} %get-tuple-element.31.refs_0_, bf16[128,2048]{1,0:T(8,128)(2,1)S(1)} %collective-permute-done.refs_1_, ...), custom_call_target="tpu_custom_call" | custom-call | flops 2139095040 | tf_op jit(solution)/shard_map/first_product/pallas_call | solution.py:158
  38.6 1.3 %first_product.6.refs_4_ = f32[544,768]{1,0:T(8,128)S(1)} custom-call(s32[2]{0:T(128)S(1)} %get-tuple-element.95.spots_ref, s32[2]{0:T(128)S(1)} %get-tuple-element.96.source_ref, s32[32,1]{1,0:T(8,128)S(1)} %add.2384.batch_ref, bf16[128,2048]{1,0:T(8,128)(2,1)S(1)} %get-tuple-element.31.refs_0_, bf16[128,2048]{1,0:T(8,128)(2,1)S(1)} %collective-permute-done.refs_1_, ...), custom_call_target="tpu_custom_call" | custom-call | flops 2139095040 | tf_op jit(solution)/shard_map/first_product/pallas_call | solution.py:158
  39.9 2.9 %collective-permute-done.9.refs_5_ = bf16[2,256,384]{2,1,0:T(8,128)(2,1)S(1)} collective-permute-done((bf16[2,256,384]{2,1,0:T(8,128)(2,1)S(1)}, bf16[2,256,384]{2,1,0:T(8,128)(2,1)S(1)}, u32[]{:S(2)}, u32[]{:S(2)}) %collective-permute-start.9) | collective-permute-done | bytes 393248 | tf_op jit(solution)/shard_map/ppermute | solution.py:81
  42.8 0.5 first_product.7
  43.3 0.7 copy-done.2
  44.0 0.6 iota_add_fusion.13
  44.6 4.2 %collective-permute-start.11 = (bf16[160,768]{1,0:T(8,128)(2,1)}, bf16[160,768]{1,0:T(8,128)(2,1)S(1)}, u32[]{:S(2)}, u32[]{:S(2)}) collective-permute-start(bf16[160,768]{1,0:T(8,128)(2,1)} %copy-done.2), channel_id=1, source_target_pairs={{0,4},{1,3},{2,6},{3,1},{4,0},{5,7},{6,2},{7,5},{8,12},{9,11},{10,... | collective-permute-start | bytes 737288 | tf_op jit(solution)/shard_map/ppermute | solution.py:58
  48.8 0.1 collective-permute-start.12
  48.9 0.6 iota_add_fusion.15
  49.5 0.6 iota_add_fusion.17
  50.1 3.1 %collective-permute-done.11.refs_2_ = bf16[160,768]{1,0:T(8,128)(2,1)S(1)} collective-permute-done((bf16[160,768]{1,0:T(8,128)(2,1)}, bf16[160,768]{1,0:T(8,128)(2,1)S(1)}, u32[]{:S(2)}, u32[]{:S(2)}) %collective-permute-start.11) | collective-permute-done | bytes 245792 | tf_op jit(solution)/shard_map/ppermute | solution.py:58
  53.2 3.9 %collective-permute-done.12.refs_3_ = bf16[160,768]{1,0:T(8,128)(2,1)S(1)} collective-permute-done((bf16[160,768]{1,0:T(8,128)(2,1)S(1)}, bf16[160,768]{1,0:T(8,128)(2,1)S(1)}, u32[]{:S(2)}, u32[]{:S(2)}) %collective-permute-start.12) | collective-permute-done | bytes 245792 | tf_op jit(solution)/shard_map/ppermute | solution.py:58
  57.1 0.1 add_partners.1
  57.2 2.8 %collective-permute-start.13 = (bf16[256,384]{1,0:T(8,128)(2,1)S(1)}, bf16[256,384]{1,0:T(8,128)(2,1)S(1)}, u32[]{:S(2)}, u32[]{:S(2)}) collective-permute-start(bf16[256,384]{1,0:T(8,128)(2,1)S(1)} %get-tuple-element.40.refs_0_), channel_id=1, source_target_pairs={{0,8},{1,5},{2,0},{3,7},{4,12},{5,13},{6,4},{7,15},{8,16},{9,1},{1... | collective-permute-start | bytes 589832 | tf_op jit(solution)/shard_map/ppermute | solution.py:81
  60.0 0.5 iota_add_fusion.19
  60.6 0.6 iota_add_fusion.21
  61.2 2.6 %collective-permute-done.13.refs_1_ = bf16[256,384]{1,0:T(8,128)(2,1)S(1)} collective-permute-done((bf16[256,384]{1,0:T(8,128)(2,1)S(1)}, bf16[256,384]{1,0:T(8,128)(2,1)S(1)}, u32[]{:S(2)}, u32[]{:S(2)}) %collective-permute-start.13) | collective-permute-done | bytes 196640 | tf_op jit(solution)/shard_map/ppermute | solution.py:81
  63.8 2.5 %collective-permute-start.18 = (bf16[256,384]{1,0:T(8,128)(2,1)S(1)}, bf16[256,384]{1,0:T(8,128)(2,1)S(1)}, u32[]{:S(2)}, u32[]{:S(2)}) collective-permute-start(bf16[256,384]{1,0:T(8,128)(2,1)S(1)} %collective-permute-done.13.refs_1_), channel_id=1, source_target_pairs={{0,8},{1,5},{2,0},{3,7},{4,12},{5,13},{6,4},{7,15},{8,16},{9,1},{1... | collective-permute-start | bytes 589832 | tf_op jit(solution)/shard_map/ppermute | solution.py:81
  66.3 0.9 collective-permute-start.19
  67.1 0.6 iota_add_fusion.23
  67.7 0.5 iota_add_fusion.25
  68.3 2.5 %collective-permute-done.18.refs_0_ = bf16[256,384]{1,0:T(8,128)(2,1)S(1)} collective-permute-done((bf16[256,384]{1,0:T(8,128)(2,1)S(1)}, bf16[256,384]{1,0:T(8,128)(2,1)S(1)}, u32[]{:S(2)}, u32[]{:S(2)}) %collective-permute-start.18) | collective-permute-done | bytes 196640 | tf_op jit(solution)/shard_map/ppermute | solution.py:81
  70.8 1.2 %collective-permute-start.23 = (bf16[256,384]{1,0:T(8,128)(2,1)S(1)}, bf16[256,384]{1,0:T(8,128)(2,1)S(1)}, u32[]{:S(2)}, u32[]{:S(2)}) collective-permute-start(bf16[256,384]{1,0:T(8,128)(2,1)S(1)} %collective-permute-done.18.refs_0_), channel_id=1, source_target_pairs={{0,8},{1,5},{2,0},{3,7},{4,12},{5,13},{6,4},{7,15},{8,16},{9,1},{1... | collective-permute-start | bytes 589832 | tf_op jit(solution)/shard_map/ppermute | solution.py:81
  71.9 1.8 %collective-permute-done.19.refs_1_ = bf16[256,384]{1,0:T(8,128)(2,1)S(1)} collective-permute-done((bf16[256,384]{1,0:T(8,128)(2,1)S(1)}, bf16[256,384]{1,0:T(8,128)(2,1)S(1)}, u32[]{:S(2)}, u32[]{:S(2)}) %collective-permute-start.19) | collective-permute-done | bytes 196640 | tf_op jit(solution)/shard_map/ppermute | solution.py:81
  73.8 0.1 pad_add_fusion.1.devices_ref
  73.8 1.8 %weights.1.matrix_ref = bf16[384,256]{1,0:T(8,128)(2,1)S(1)} custom-call(s32[4]{0:T(128)S(1)} %pad_add_fusion.1.devices_ref, bf16[64,384]{1,0:T(8,128)(2,1)S(1)} %get-tuple-element.39.batch_ref), custom_call_target="tpu_custom_call" | custom-call | tf_op jit(solution)/shard_map/weights/pallas_call | solution.py:224
  75.6 0.5 second_product.4
  76.2 0.7 collective-permute-start.16
  76.8 1.8 %collective-permute-start.17 = (bf16[288,384]{1,0:T(8,128)(2,1)S(1)}, bf16[288,384]{1,0:T(8,128)(2,1)S(1)}, u32[]{:S(2)}, u32[]{:S(2)}) collective-permute-start(bf16[288,384]{1,0:T(8,128)(2,1)S(1)} %get-tuple-element.44), channel_id=1, source_target_pairs={{0,5},{1,2},{2,7},{3,0},{4,1},{5,6},{6,3},{7,4},{8,13},{9,10},{10,... | collective-permute-start | bytes 663560 | tf_op jit(solution)/shard_map/ppermute | solution.py:58
  78.6 0.6 iota_add_fusion.27
  79.2 1.0 %second_product.5 = (bf16[192,384]{1,0:T(8,128)(2,1)S(1)}, bf16[192,384]{1,0:T(8,128)(2,1)}, bf16[192,384]{1,0:T(8,128)(2,1)S(1)}, bf16[192,384]{1,0:T(8,128)(2,1)S(1)}) custom-call(bf16[384,256]{1,0:T(8,128)(2,1)S(1)} %weights.1.matrix_ref, bf16[256,384]{1,0:T(8,128)(2,1)S(1)} %collective-permute-done.18.refs_0_, ...), custom_call_target="tpu_custom_call" | custom-call | tf_op jit(solution)/shard_map/second_product/pallas_call | solution.py:245
  80.2 0.4 collective-permute-start.20
  80.5 1.9 %collective-permute-start.28 = (bf16[256,384]{1,0:T(8,128)(2,1)S(1)}, bf16[256,384]{1,0:T(8,128)(2,1)S(1)}, u32[]{:S(2)}, u32[]{:S(2)}) collective-permute-start(bf16[256,384]{1,0:T(8,128)(2,1)S(1)} %collective-permute-done.23.refs_0_), channel_id=1, source_target_pairs={{0,8},{1,5},{2,0},{3,7},{4,12},{5,13},{6,4},{7,15},{8,16},{9,1},{1... | collective-permute-start | bytes 589832 | tf_op jit(solution)/shard_map/ppermute | solution.py:81
  82.5 0.6 iota_add_fusion.29
  83.0 1.0 second_product.6
  84.0 0.9 collective-permute-start.21
  84.9 0.7 collective-permute-start.25
  85.6 0.6 collective-permute-start.26
  86.3 0.4 collective-permute-done.28.refs_0_
  86.7 1.8 %collective-permute-start.27 = (bf16[192,384]{1,0:T(8,128)(2,1)S(1)}, bf16[192,384]{1,0:T(8,128)(2,1)S(1)}, u32[]{:S(2)}, u32[]{:S(2)}) collective-permute-start(bf16[192,384]{1,0:T(8,128)(2,1)S(1)} %get-tuple-element.52), channel_id=1, source_target_pairs={{0,5},{1,2},{2,7},{3,0},{4,1},{5,6},{6,3},{7,4},{8,13},{9,10},{10,... | collective-permute-start | bytes 442376 | tf_op jit(solution)/shard_map/ppermute | solution.py:58
  88.5 0.3 second_product.7
  88.7 0.4 collective-permute-done.21.refs_6_
  89.2 0.4 collective-permute-start.29
  89.5 1.2 %collective-permute-start.30 = (bf16[96,384]{1,0:T(8,128)(2,1)S(1)}, bf16[96,384]{1,0:T(8,128)(2,1)S(1)}, u32[]{:S(2)}, u32[]{:S(2)}) collective-permute-start(bf16[96,384]{1,0:T(8,128)(2,1)S(1)} %get-tuple-element.55), channel_id=1, source_target_pairs={{0,4},{1,3},{2,6},{3,1},{4,0},{5,7},{6,2},{7,5},{8,12},{9,11},{10,... | collective-permute-start | bytes 221192 | tf_op jit(solution)/shard_map/ppermute | solution.py:58
  90.8 0.8 collective-permute-start.31
  91.6 0.8 concatenate.3
  92.4 0.1 copy.15.order_ref
  92.5 0.8 copy.16.pair_ref
  93.3 1.4 %collective-permute-done.30.refs_14_ = bf16[96,384]{1,0:T(8,128)(2,1)S(1)} collective-permute-done((bf16[96,384]{1,0:T(8,128)(2,1)S(1)}, bf16[96,384]{1,0:T(8,128)(2,1)S(1)}, u32[]{:S(2)}, u32[]{:S(2)}) %collective-permute-start.30) | collective-permute-done | bytes 73760 | tf_op jit(solution)/shard_map/ppermute | solution.py:58
  94.7 2.8 %place_pairs.1 = bf16[2,12,384,128]{3,2,1,0:T(8,128)(2,1)} custom-call(s32[128,1]{1,0:T(8,128)S(1)} %copy.15.order_ref, s32[128,1]{1,0:T(8,128)S(1)} %copy.16.pair_ref, bf16[288,384]{1,0:T(8,128)(2,1)S(1)} %get-tuple-element.41.refs_0_, bf16[288,384]{1,0:T(8,128)(2,1)S(1)} %collective-permute-done.15.refs_1_, ...), custom_call_target="tpu_custom_call" | custom-call | tf_op jit(solution)/shard_map/place_pairs/pallas_call | solution.py:278
  (49 shorter events, 0.5 us)
Async XLA Ops:
  0.0 11.7 %collective-permute-start.3 = (bf16[2,256,384]{2,1,0:T(8,128)(2,1)}, bf16[2,256,384]{2,1,0:T(8,128)(2,1)S(1)}, u32[]{:S(2)}, u32[]{:S(2)}) collective-permute-start(bf16[2,256,384]{2,1,0:T(8,128)(2,1)} %refs_4_.1), channel_id=1, source_target_pairs={{0,8},{1,5},{2,0},{3,7},{4,12},{5,13},{6,4},{7,15},{8,16},{9,1},{1... | collective-permute-start | bytes 1179656 | tf_op jit(solution)/shard_map/ppermute | solution.py:81
  3.0 11.1 %collective-permute-start.4 = (bf16[2,256,384]{2,1,0:T(8,128)(2,1)}, bf16[2,256,384]{2,1,0:T(8,128)(2,1)}, u32[]{:S(2)}, u32[]{:S(2)}) collective-permute-start(bf16[2,256,384]{2,1,0:T(8,128)(2,1)} %refs_4_.1), channel_id=1, source_target_pairs={{0,2},{1,9},{2,10},{3,11},{4,6},{5,1},{6,14},{7,3},{8,0},{9,17},{1... | collective-permute-start | bytes 1179656 | tf_op jit(solution)/shard_map/ppermute | solution.py:81
  3.0 6.2 %copy-start.3 = (s32[8]{0:T(128)S(1)}, s32[8]{0:T(128)}, u32[]{:S(2)}) copy-start(s32[8]{0:T(128)} %param.6) | copy-start | bytes 100
  3.1 1.6 %copy-start = (bf16[4,32,8192]{2,1,0:T(8,128)(2,1)S(1)}, bf16[4,32,8192]{2,1,0:T(8,128)(2,1)}, u32[]{:S(2)}) copy-start(bf16[4,32,8192]{2,1,0:T(8,128)(2,1)} %param.4) | copy-start | bytes 6291460
  4.7 23.5 %copy-start.1 = (bf16[2,256,384]{2,1,0:T(8,128)(2,1)S(1)}, bf16[2,256,384]{2,1,0:T(8,128)(2,1)}, u32[]{:S(2)}) copy-start(bf16[2,256,384]{2,1,0:T(8,128)(2,1)} %refs_4_.1) | copy-start | bytes 1179652
  7.1 21.1 %collective-permute-start = (bf16[128,2048]{1,0:T(8,128)(2,1)}, bf16[128,2048]{1,0:T(8,128)(2,1)S(1)}, u32[]{:S(2)}, u32[]{:S(2)}) collective-permute-start(bf16[128,2048]{1,0:T(8,128)(2,1)} %get-tuple-element.32), channel_id=1, source_target_pairs={{0,1},{1,0},{2,3},{3,2},{4,5},{5,4},{6,7},{7,6},{8,9},{9,8},{10,11... | collective-permute-start | bytes 1572872 | tf_op jit(solution)/shard_map/ppermute | solution.py:58
  7.2 21.1 %collective-permute-start.1 = (bf16[128,2048]{1,0:T(8,128)(2,1)}, bf16[128,2048]{1,0:T(8,128)(2,1)S(1)}, u32[]{:S(2)}, u32[]{:S(2)}) collective-permute-start(bf16[128,2048]{1,0:T(8,128)(2,1)} %get-tuple-element.33), channel_id=1, source_target_pairs={{0,4},{1,3},{2,6},{3,1},{4,0},{5,7},{6,2},{7,5},{8,12},{9,11},{10,... | collective-permute-start | bytes 1572872 | tf_op jit(solution)/shard_map/ppermute | solution.py:58
  9.2 19.0 %collective-permute-start.2 = (bf16[128,2048]{1,0:T(8,128)(2,1)S(1)}, bf16[128,2048]{1,0:T(8,128)(2,1)S(1)}, u32[]{:S(2)}, u32[]{:S(2)}) collective-permute-start(bf16[128,2048]{1,0:T(8,128)(2,1)S(1)} %get-tuple-element.34), channel_id=1, source_target_pairs={{0,3},{1,4},{2,1},{3,6},{4,7},{5,0},{6,5},{7,2},{8,11},{9,12},{10,... | collective-permute-start | bytes 1572872 | tf_op jit(solution)/shard_map/ppermute | solution.py:58
  11.7 14.4 %collective-permute-start.5 = (bf16[2,256,384]{2,1,0:T(8,128)(2,1)S(1)}, bf16[2,256,384]{2,1,0:T(8,128)(2,1)S(1)}, u32[]{:S(2)}, u32[]{:S(2)}) collective-permute-start(bf16[2,256,384]{2,1,0:T(8,128)(2,1)S(1)} %collective-permute-done.3.refs_5_), channel_id=1, source_target_pairs={{0,8},{1,5},{2,0},{3,7},{4,12},{5,13},{6,4},{7,15},{8,16},{9,1},{1... | collective-permute-start | bytes 1179656 | tf_op jit(solution)/shard_map/ppermute | solution.py:81
  14.1 12.1 %collective-permute-start.6 = (bf16[2,256,384]{2,1,0:T(8,128)(2,1)}, bf16[2,256,384]{2,1,0:T(8,128)(2,1)S(1)}, u32[]{:S(2)}, u32[]{:S(2)}) collective-permute-start(bf16[2,256,384]{2,1,0:T(8,128)(2,1)} %collective-permute-done.4.refs_6_), channel_id=1, source_target_pairs={{0,2},{1,9},{2,10},{3,11},{4,6},{5,1},{6,14},{7,3},{8,0},{9,17},{1... | collective-permute-start | bytes 1179656 | tf_op jit(solution)/shard_map/ppermute | solution.py:81
  26.1 8.7 %collective-permute-start.7 = (bf16[2,256,384]{2,1,0:T(8,128)(2,1)S(1)}, bf16[2,256,384]{2,1,0:T(8,128)(2,1)S(1)}, u32[]{:S(2)}, u32[]{:S(2)}) collective-permute-start(bf16[2,256,384]{2,1,0:T(8,128)(2,1)S(1)} %collective-permute-done.5.refs_5_), channel_id=1, source_target_pairs={{0,8},{1,5},{2,0},{3,7},{4,12},{5,13},{6,4},{7,15},{8,16},{9,1},{1... | collective-permute-start | bytes 1179656 | tf_op jit(solution)/shard_map/ppermute | solution.py:81
  26.2 12.4 %collective-permute-start.8 = (bf16[2,256,384]{2,1,0:T(8,128)(2,1)S(1)}, bf16[2,256,384]{2,1,0:T(8,128)(2,1)S(1)}, u32[]{:S(2)}, u32[]{:S(2)}) collective-permute-start(bf16[2,256,384]{2,1,0:T(8,128)(2,1)S(1)} %collective-permute-done.6.refs_6_), channel_id=1, source_target_pairs={{0,2},{1,9},{2,10},{3,11},{4,6},{5,1},{6,14},{7,3},{8,0},{9,17},{1... | collective-permute-start | bytes 1179656 | tf_op jit(solution)/shard_map/ppermute | solution.py:81
  34.8 8.0 %collective-permute-start.9 = (bf16[2,256,384]{2,1,0:T(8,128)(2,1)S(1)}, bf16[2,256,384]{2,1,0:T(8,128)(2,1)S(1)}, u32[]{:S(2)}, u32[]{:S(2)}) collective-permute-start(bf16[2,256,384]{2,1,0:T(8,128)(2,1)S(1)} %collective-permute-done.7.refs_5_), channel_id=1, source_target_pairs={{0,8},{1,5},{2,0},{3,7},{4,12},{5,13},{6,4},{7,15},{8,16},{9,1},{1... | collective-permute-start | bytes 1179656 | tf_op jit(solution)/shard_map/ppermute | solution.py:81
  43.3 0.7 copy-start.2
  44.0 13.1 %collective-permute-start.10 = (f32[160,768]{1,0:T(8,128)S(1)}, f32[160,768]{1,0:T(8,128)S(1)}, u32[]{:S(2)}, u32[]{:S(2)}) collective-permute-start(f32[160,768]{1,0:T(8,128)S(1)} %get-tuple-element.36), channel_id=1, source_target_pairs={{0,1},{1,0},{2,3},{3,2},{4,5},{5,4},{6,7},{7,6},{8,9},{9,8},{10,11... | collective-permute-start | bytes 1474568 | tf_op jit(solution)/shard_map/ppermute | solution.py:58
  44.6 8.6 %collective-permute-start.11 = (bf16[160,768]{1,0:T(8,128)(2,1)}, bf16[160,768]{1,0:T(8,128)(2,1)S(1)}, u32[]{:S(2)}, u32[]{:S(2)}) collective-permute-start(bf16[160,768]{1,0:T(8,128)(2,1)} %copy-done.2), channel_id=1, source_target_pairs={{0,4},{1,3},{2,6},{3,1},{4,0},{5,7},{6,2},{7,5},{8,12},{9,11},{10,... | collective-permute-start | bytes 737288 | tf_op jit(solution)/shard_map/ppermute | solution.py:58
  48.8 8.3 %collective-permute-start.12 = (bf16[160,768]{1,0:T(8,128)(2,1)S(1)}, bf16[160,768]{1,0:T(8,128)(2,1)S(1)}, u32[]{:S(2)}, u32[]{:S(2)}) collective-permute-start(bf16[160,768]{1,0:T(8,128)(2,1)S(1)} %get-tuple-element.38), channel_id=1, source_target_pairs={{0,5},{1,2},{2,7},{3,0},{4,1},{5,6},{6,3},{7,4},{8,13},{9,10},{10,... | collective-permute-start | bytes 737288 | tf_op jit(solution)/shard_map/ppermute | solution.py:58
  57.2 6.6 %collective-permute-start.13 = (bf16[256,384]{1,0:T(8,128)(2,1)S(1)}, bf16[256,384]{1,0:T(8,128)(2,1)S(1)}, u32[]{:S(2)}, u32[]{:S(2)}) collective-permute-start(bf16[256,384]{1,0:T(8,128)(2,1)S(1)} %get-tuple-element.40.refs_0_), channel_id=1, source_target_pairs={{0,8},{1,5},{2,0},{3,7},{4,12},{5,13},{6,4},{7,15},{8,16},{9,1},{1... | collective-permute-start | bytes 589832 | tf_op jit(solution)/shard_map/ppermute | solution.py:81
  60.0 6.3 %collective-permute-start.14 = (bf16[256,384]{1,0:T(8,128)(2,1)S(1)}, bf16[256,384]{1,0:T(8,128)(2,1)S(1)}, u32[]{:S(2)}, u32[]{:S(2)}) collective-permute-start(bf16[256,384]{1,0:T(8,128)(2,1)S(1)} %get-tuple-element.40.refs_0_), channel_id=1, source_target_pairs={{0,2},{1,9},{2,10},{3,11},{4,6},{5,1},{6,14},{7,3},{8,0},{9,17},{1... | collective-permute-start | bytes 589832 | tf_op jit(solution)/shard_map/ppermute | solution.py:81
  63.8 7.0 %collective-permute-start.18 = (bf16[256,384]{1,0:T(8,128)(2,1)S(1)}, bf16[256,384]{1,0:T(8,128)(2,1)S(1)}, u32[]{:S(2)}, u32[]{:S(2)}) collective-permute-start(bf16[256,384]{1,0:T(8,128)(2,1)S(1)} %collective-permute-done.13.refs_1_), channel_id=1, source_target_pairs={{0,8},{1,5},{2,0},{3,7},{4,12},{5,13},{6,4},{7,15},{8,16},{9,1},{1... | collective-permute-start | bytes 589832 | tf_op jit(solution)/shard_map/ppermute | solution.py:81
  66.3 7.5 %collective-permute-start.19 = (bf16[256,384]{1,0:T(8,128)(2,1)S(1)}, bf16[256,384]{1,0:T(8,128)(2,1)S(1)}, u32[]{:S(2)}, u32[]{:S(2)}) collective-permute-start(bf16[256,384]{1,0:T(8,128)(2,1)S(1)} %collective-permute-done.14.refs_2_), channel_id=1, source_target_pairs={{0,2},{1,9},{2,10},{3,11},{4,6},{5,1},{6,14},{7,3},{8,0},{9,17},{1... | collective-permute-start | bytes 589832 | tf_op jit(solution)/shard_map/ppermute | solution.py:81
  70.8 9.4 %collective-permute-start.23 = (bf16[256,384]{1,0:T(8,128)(2,1)S(1)}, bf16[256,384]{1,0:T(8,128)(2,1)S(1)}, u32[]{:S(2)}, u32[]{:S(2)}) collective-permute-start(bf16[256,384]{1,0:T(8,128)(2,1)S(1)} %collective-permute-done.18.refs_0_), channel_id=1, source_target_pairs={{0,8},{1,5},{2,0},{3,7},{4,12},{5,13},{6,4},{7,15},{8,16},{9,1},{1... | collective-permute-start | bytes 589832 | tf_op jit(solution)/shard_map/ppermute | solution.py:81
  73.8 6.8 %collective-permute-start.24 = (bf16[256,384]{1,0:T(8,128)(2,1)S(1)}, bf16[256,384]{1,0:T(8,128)(2,1)S(1)}, u32[]{:S(2)}, u32[]{:S(2)}) collective-permute-start(bf16[256,384]{1,0:T(8,128)(2,1)S(1)} %collective-permute-done.19.refs_1_), channel_id=1, source_target_pairs={{0,2},{1,9},{2,10},{3,11},{4,6},{5,1},{6,14},{7,3},{8,0},{9,17},{1... | collective-permute-start | bytes 589832 | tf_op jit(solution)/shard_map/ppermute | solution.py:81
  76.1 7.9 %collective-permute-start.15 = (bf16[288,384]{1,0:T(8,128)(2,1)S(1)}, bf16[288,384]{1,0:T(8,128)(2,1)S(1)}, u32[]{:S(2)}, u32[]{:S(2)}) collective-permute-start(bf16[288,384]{1,0:T(8,128)(2,1)S(1)} %get-tuple-element.42), channel_id=1, source_target_pairs={{0,1},{1,0},{2,3},{3,2},{4,5},{5,4},{6,7},{7,6},{8,9},{9,8},{10,11... | collective-permute-start | bytes 663560 | tf_op jit(solution)/shard_map/ppermute | solution.py:58
  76.2 8.8 %collective-permute-start.16 = (bf16[288,384]{1,0:T(8,128)(2,1)S(1)}, bf16[288,384]{1,0:T(8,128)(2,1)S(1)}, u32[]{:S(2)}, u32[]{:S(2)}) collective-permute-start(bf16[288,384]{1,0:T(8,128)(2,1)S(1)} %get-tuple-element.43), channel_id=1, source_target_pairs={{0,4},{1,3},{2,6},{3,1},{4,0},{5,7},{6,2},{7,5},{8,12},{9,11},{10,... | collective-permute-start | bytes 663560 | tf_op jit(solution)/shard_map/ppermute | solution.py:58
  76.8 8.1 %collective-permute-start.17 = (bf16[288,384]{1,0:T(8,128)(2,1)S(1)}, bf16[288,384]{1,0:T(8,128)(2,1)S(1)}, u32[]{:S(2)}, u32[]{:S(2)}) collective-permute-start(bf16[288,384]{1,0:T(8,128)(2,1)S(1)} %get-tuple-element.44), channel_id=1, source_target_pairs={{0,5},{1,2},{2,7},{3,0},{4,1},{5,6},{6,3},{7,4},{8,13},{9,10},{10,... | collective-permute-start | bytes 663560 | tf_op jit(solution)/shard_map/ppermute | solution.py:58
  80.2 5.5 %collective-permute-start.20 = (bf16[192,384]{1,0:T(8,128)(2,1)}, bf16[192,384]{1,0:T(8,128)(2,1)S(1)}, u32[]{:S(2)}, u32[]{:S(2)}) collective-permute-start(bf16[192,384]{1,0:T(8,128)(2,1)} %get-tuple-element.46), channel_id=1, source_target_pairs={{0,1},{1,0},{2,3},{3,2},{4,5},{5,4},{6,7},{7,6},{8,9},{9,8},{10,11... | collective-permute-start | bytes 442376 | tf_op jit(solution)/shard_map/ppermute | solution.py:58
  80.5 6.2 %collective-permute-start.28 = (bf16[256,384]{1,0:T(8,128)(2,1)S(1)}, bf16[256,384]{1,0:T(8,128)(2,1)S(1)}, u32[]{:S(2)}, u32[]{:S(2)}) collective-permute-start(bf16[256,384]{1,0:T(8,128)(2,1)S(1)} %collective-permute-done.23.refs_0_), channel_id=1, source_target_pairs={{0,8},{1,5},{2,0},{3,7},{4,12},{5,13},{6,4},{7,15},{8,16},{9,1},{1... | collective-permute-start | bytes 589832 | tf_op jit(solution)/shard_map/ppermute | solution.py:81
  84.0 5.1 %collective-permute-start.21 = (bf16[192,384]{1,0:T(8,128)(2,1)S(1)}, bf16[192,384]{1,0:T(8,128)(2,1)S(1)}, u32[]{:S(2)}, u32[]{:S(2)}) collective-permute-start(bf16[192,384]{1,0:T(8,128)(2,1)S(1)} %get-tuple-element.47), channel_id=1, source_target_pairs={{0,4},{1,3},{2,6},{3,1},{4,0},{5,7},{6,2},{7,5},{8,12},{9,11},{10,... | collective-permute-start | bytes 442376 | tf_op jit(solution)/shard_map/ppermute | solution.py:58
  84.9 4.6 %collective-permute-start.22 = (bf16[192,384]{1,0:T(8,128)(2,1)S(1)}, bf16[192,384]{1,0:T(8,128)(2,1)S(1)}, u32[]{:S(2)}, u32[]{:S(2)}) collective-permute-start(bf16[192,384]{1,0:T(8,128)(2,1)S(1)} %get-tuple-element.48), channel_id=1, source_target_pairs={{0,5},{1,2},{2,7},{3,0},{4,1},{5,6},{6,3},{7,4},{8,13},{9,10},{10,... | collective-permute-start | bytes 442376 | tf_op jit(solution)/shard_map/ppermute | solution.py:58
  84.9 5.8 %collective-permute-start.25 = (bf16[192,384]{1,0:T(8,128)(2,1)}, bf16[192,384]{1,0:T(8,128)(2,1)S(1)}, u32[]{:S(2)}, u32[]{:S(2)}) collective-permute-start(bf16[192,384]{1,0:T(8,128)(2,1)} %get-tuple-element.50), channel_id=1, source_target_pairs={{0,1},{1,0},{2,3},{3,2},{4,5},{5,4},{6,7},{7,6},{8,9},{9,8},{10,11... | collective-permute-start | bytes 442376 | tf_op jit(solution)/shard_map/ppermute | solution.py:58
  85.6 7.6 %collective-permute-start.26 = (bf16[192,384]{1,0:T(8,128)(2,1)S(1)}, bf16[192,384]{1,0:T(8,128)(2,1)S(1)}, u32[]{:S(2)}, u32[]{:S(2)}) collective-permute-start(bf16[192,384]{1,0:T(8,128)(2,1)S(1)} %get-tuple-element.51), channel_id=1, source_target_pairs={{0,4},{1,3},{2,6},{3,1},{4,0},{5,7},{6,2},{7,5},{8,12},{9,11},{10,... | collective-permute-start | bytes 442376 | tf_op jit(solution)/shard_map/ppermute | solution.py:58
  86.7 6.6 %collective-permute-start.27 = (bf16[192,384]{1,0:T(8,128)(2,1)S(1)}, bf16[192,384]{1,0:T(8,128)(2,1)S(1)}, u32[]{:S(2)}, u32[]{:S(2)}) collective-permute-start(bf16[192,384]{1,0:T(8,128)(2,1)S(1)} %get-tuple-element.52), channel_id=1, source_target_pairs={{0,5},{1,2},{2,7},{3,0},{4,1},{5,6},{6,3},{7,4},{8,13},{9,10},{10,... | collective-permute-start | bytes 442376 | tf_op jit(solution)/shard_map/ppermute | solution.py:58
  89.2 4.1 %collective-permute-start.29 = (bf16[96,384]{1,0:T(8,128)(2,1)S(1)}, bf16[96,384]{1,0:T(8,128)(2,1)S(1)}, u32[]{:S(2)}, u32[]{:S(2)}) collective-permute-start(bf16[96,384]{1,0:T(8,128)(2,1)S(1)} %get-tuple-element.54), channel_id=1, source_target_pairs={{0,1},{1,0},{2,3},{3,2},{4,5},{5,4},{6,7},{7,6},{8,9},{9,8},{10,11... | collective-permute-start | bytes 221192 | tf_op jit(solution)/shard_map/ppermute | solution.py:58
  89.5 5.2 %collective-permute-start.30 = (bf16[96,384]{1,0:T(8,128)(2,1)S(1)}, bf16[96,384]{1,0:T(8,128)(2,1)S(1)}, u32[]{:S(2)}, u32[]{:S(2)}) collective-permute-start(bf16[96,384]{1,0:T(8,128)(2,1)S(1)} %get-tuple-element.55), channel_id=1, source_target_pairs={{0,4},{1,3},{2,6},{3,1},{4,0},{5,7},{6,2},{7,5},{8,12},{9,11},{10,... | collective-permute-start | bytes 221192 | tf_op jit(solution)/shard_map/ppermute | solution.py:58
  90.8 4.0 %collective-permute-start.31 = (bf16[96,384]{1,0:T(8,128)(2,1)S(1)}, bf16[96,384]{1,0:T(8,128)(2,1)S(1)}, u32[]{:S(2)}, u32[]{:S(2)}) collective-permute-start(bf16[96,384]{1,0:T(8,128)(2,1)S(1)} %get-tuple-element.56), channel_id=1, source_target_pairs={{0,5},{1,2},{2,7},{3,0},{4,1},{5,6},{6,3},{7,4},{8,13},{9,10},{10,... | collective-permute-start | bytes 221192 | tf_op jit(solution)/shard_map/ppermute | solution.py:58

commit v4 on v3

v4 whole, which is shorter than its diff:
```python
import functools

import jax
import jax.numpy as jnp
from jax import lax
from jax.experimental import pallas as pl
from jax.experimental.pallas import tpu as pltpu
from jax.sharding import PartitionSpec as P

SHW = 4
LANES = 128
F32, BF16 = jnp.float32, jnp.bfloat16
VMEM_LIMIT = 16 * 1024 * 1024


class Grid:
    def __init__(self, n_pair):
        assert n_pair % 8 == 0
        self.nz = n_pair // 8
        self.ring = 2 * self.nz

    def device(self, spot, side, core):
        turned = (spot >= self.nz) * 1
        z = spot + turned * (self.ring - 1 - 2 * spot)
        x = turned + core * (side - turned)
        y = side + core * (turned - side)
        return ((z * 2 + y) * 2 + x) * 2 + core

    def place(self, device):
        core, x, y, z = device % 2, device // 2 % 2, device // 4 % 2, device // 8
        turned = x + core * (y - x)
        side = y + core * (x - y)
        return z + turned * (self.ring - 1 - 2 * z), side, core

    def moves(self, target):
        every = range(self.ring * 4)
        return [(device, int(self.device(*target(*self.place(device))))) for device in every]

    def around(self, way):
        return self.moves(lambda spot, side, core: ((spot + way * (1 - 2 * core)) % self.ring, side, core))

    def mate(self, device):
        return device + 1 - 2 * (device % 2)

    def opposite(self, device):
        spot, side, core = self.place(device)
        return self.device(spot, 1 - side, core)

    def helpers(self, device):
        return [device, self.mate(device), self.opposite(device), self.opposite(self.mate(device))]

    def helped(self, device):
        return [device, self.mate(device), self.opposite(device), self.mate(self.opposite(device))]

    def send(self, block, target):
        return lax.ppermute(block, "pair", [(device, int(target(device))) for device in range(self.ring * 4)])

    def exchange(self, blocks, partners):
        return [self.send(block, lambda device: partners(device)[k]) for k, block in zip((1, 2, 3), blocks)]

    def spot(self, device, offset):
        spot, _, core = self.place(device)
        return (spot + offset * (1 - 2 * core) + self.ring) % self.ring

    def source_at(self, device, spot):
        _, side, core = self.place(device)
        return self.device(spot, side, core)

    def source(self, device, offset):
        _, side, core = self.place(device)
        return self.device(self.spot(device, offset), side, core)


def after(value, *done):
    return lax.optimization_barrier((value, *done))[0] if done else value


def gather_ring(grid, own, meanwhile):
    around = {-1: grid.around(1), 1: grid.around(-1)}
    held, gates = {0: own}, [[]]
    for step in range(1, grid.nz + 1):
        ways = (-1, 1) if step < grid.nz else (-1,)
        for way in ways:
            block = after(held[way * (step - 1)], *gates[step - 1])
            held[way * step] = lax.ppermute(block, "pair", around[way])
        gates.append(meanwhile(held, [0] if step == 1 else [1 - step, step - 1]))
    meanwhile(held, [-grid.nz])
    return held


def vmem(count):
    return [pl.BlockSpec(memory_space=pltpu.VMEM)] * count


PARAMS = pltpu.CompilerParams(vmem_limit_bytes=VMEM_LIMIT)


def in_hbm(array):
    return pltpu.with_memory_space_constraint(array, pltpu.HBM)


def share_integrals(grid, where, integrals, depth):
    rows = integrals.shape[0]

    def body(where_ref, ints_ref, *refs):
        outs, moved = refs[:-1], refs[-1]
        copies = []
        for k, (out, helper) in enumerate(zip(outs, grid.helpers(where_ref[0]))):
            for spot in range(grid.ring):
                start = pl.multiple_of(grid.source_at(helper, spot) * depth, depth)
                copies.append(
                    pltpu.make_async_copy(
                        ints_ref.at[:, pl.ds(start, depth)], out.at[:, pl.ds(spot * depth, depth)], moved.at[k, spot]
                    )
                )
        for copy in copies:
            copy.start()
        for copy in copies:
            copy.wait()

    return pl.pallas_call(
        body,
        out_shape=[jax.ShapeDtypeStruct((rows, grid.ring * depth), BF16)] * 4,
        in_specs=[pl.BlockSpec(memory_space=pltpu.SMEM), pl.BlockSpec(memory_space=pl.ANY)],
        out_specs=vmem(4),
        scratch_shapes=[pltpu.SemaphoreType.DMA((4, grid.ring))],
        compiler_params=PARAMS,
        name="share_integrals",
    )(where, in_hbm(integrals))


def first_product(grid, where, offsets, ints, batch_column, total, blocks, last):
    parts, depth, width = blocks[0].shape
    rows, batch_rows = ints[0].shape[0], batch_column.shape[0]
    high = len(ints) * rows + batch_rows
    begins = total is None

    def body(where_ref, batch_ref, *refs):
        ints_refs, refs = refs[: len(ints)], refs[len(ints):]
        total_ref, refs = (None, refs) if begins else (refs[0], refs[1:])
        block_refs, outs = refs[: len(blocks)], refs[len(blocks):]
        sum_ref = outs[-1]
        me = where_ref[0]
        for number, (offset, ref) in enumerate(zip(offsets, block_refs)):
            columns = pl.ds(pl.multiple_of(grid.spot(me, offset) * depth, depth), depth)
            position = lax.broadcasted_iota(jnp.int32, (batch_rows, depth), 1) + grid.source(me, offset) * depth
            picks = (batch_ref[...] == position).astype(F32).astype(BF16)
            left = jnp.concatenate([ints_ref[:, columns] for ints_ref in ints_refs] + [picks], axis=0)
            for part in range(parts):
                term = jnp.dot(left, ref[part], preferred_element_type=F32)
                lanes = pl.ds(part * width, width)
                if number > 0:
                    sum_ref[:, lanes] += term
                elif begins:
                    sum_ref[:, lanes] = term
                else:
                    sum_ref[:, lanes] = total_ref[:, lanes] + term
        if last:
            for k, out in enumerate(outs[:-1]):
                out[:rows, :] = sum_ref[k * rows:(k + 1) * rows, :].astype(out.dtype)
                out[rows:, :] = sum_ref[len(ints) * rows:, :].astype(out.dtype)

    totals = [] if begins else [total]
    whole = jax.ShapeDtypeStruct((high, parts * width), F32)
    kinds = (F32, F32, BF16, BF16)
    shapes = [jax.ShapeDtypeStruct((rows + batch_rows, parts * width), kind) for kind in kinds] if last else [whole]
    return pl.pallas_call(
        body,
        out_shape=shapes,
        in_specs=[pl.BlockSpec(memory_space=pltpu.SMEM)] + vmem(1 + len(ints) + len(totals) + len(blocks)),
        out_specs=vmem(len(shapes)),
        scratch_shapes=[pltpu.VMEM(whole.shape, F32)] if last else [],
        compiler_params=PARAMS,
        cost_estimate=pl.CostEstimate(
            flops=10 * high * depth * width * parts * len(blocks), bytes_accessed=0, transcendentals=0
        ),
        name="first_product",
    )(where, batch_column, *ints, *totals, *blocks)


def add_partners(sums, rows, width):
    batch_rows = sums[0].shape[0] - rows

    def body(*refs):
        half_ref, batch_ref = refs[-2:]
        for part in range(2):
            lanes = pl.ds(part * width, width)
            both = sum(ref[:, lanes].astype(F32) for ref in refs[:-2]).astype(BF16)
            half_ref[part * rows:(part + 1) * rows, :] = both[:rows]
            batch_ref[part * batch_rows:(part + 1) * batch_rows, :] = both[rows:]

    return pl.pallas_call(
        body,
        out_shape=[jax.ShapeDtypeStruct((2 * n, width), BF16) for n in (rows, batch_rows)],
        in_specs=vmem(len(sums)),
        out_specs=vmem(2),
        compiler_params=PARAMS,
        name="add_partners",
    )(*sums)


def weights(grid, where, batch, slots, share):
    batch_rows, width = batch.shape[0] // 2, batch.shape[1]
    each = slots * 2 * share
    deep = slots * batch_rows

    def body(where_ref, batch_ref, out_ref):
        repeat = (
            lax.broadcasted_iota(jnp.int32, (batch_rows, deep), 0)
            == lax.rem(lax.broadcasted_iota(jnp.int32, (batch_rows, deep), 1), batch_rows)
        ).astype(F32).astype(BF16)
        row = lax.broadcasted_iota(jnp.int32, (each, deep), 0)
        keep = lax.rem(lax.div(row, 2 * share), slots) == lax.div(
            lax.broadcasted_iota(jnp.int32, (each, deep), 1), batch_rows
        )
        real = lax.rem(lax.div(row, share), 2) == 0
        row = lax.broadcasted_iota(jnp.int32, (each, width), 0)
        column = lax.broadcasted_iota(jnp.int32, (each, width), 1)
        for k, device in enumerate(grid.helped(where_ref[0])):
            chosen = (column == device * share + lax.rem(row, share)).astype(F32).astype(BF16)

            def spread(part):
                rows = batch_ref[part * batch_rows:(part + 1) * batch_rows, :]
                picked = lax.dot_general(chosen, rows, (((1,), (1,)), ((), ())), preferred_element_type=F32)
                return jnp.dot(picked.astype(BF16), repeat, preferred_element_type=F32)

            re, im = spread(0), spread(1)
            here = pl.ds(k * each, each)
            out_ref[here, :deep] = jnp.where(keep, jnp.where(real, re, -im), 0.0).astype(BF16)
            out_ref[here, deep:] = jnp.where(keep, jnp.where(real, im, re), 0.0).astype(BF16)

    return pl.pallas_call(
        body,
        out_shape=jax.ShapeDtypeStruct((4 * each, 2 * deep), BF16),
        in_specs=[pl.BlockSpec(memory_space=pltpu.SMEM)] + vmem(1),
        out_specs=pl.BlockSpec(memory_space=pltpu.VMEM),
        compiler_params=PARAMS,
        name="weights",
    )(where, batch)


def second_product(matrix, blocks):
    each = matrix.shape[0] // 4
    width = blocks[0].shape[1]

    def body(matrix_ref, *refs):
        block_refs, outs = refs[: len(blocks)], refs[len(blocks):]
        high = len(blocks) * each
        for number, ref in enumerate(block_refs):
            every = jnp.dot(matrix_ref[...], ref[...], preferred_element_type=F32).astype(BF16)
            for k, (out, start) in enumerate(zip((outs[0], outs[1], outs[2], outs[2]), (0, 0, 0, high))):
                start += number * each
                out[start:start + each, :] = every[k * each:(k + 1) * each]

    return pl.pallas_call(
        body,
        out_shape=[jax.ShapeDtypeStruct((n * len(blocks) * each, width), BF16) for n in (1, 1, 2)],
        in_specs=vmem(1 + len(blocks)),
        out_specs=vmem(3),
        compiler_params=PARAMS,
        name="second_product",
    )(matrix, *blocks)


def place_pairs(grid, where, groups, pair_row, pieces, share):
    width = pieces[0].shape[1]
    pairs = pair_row.shape[1]
    each = 2 * share
    slots = pairs // (4 * grid.ring)

    def body(where_ref, pair_ref, *refs):
        piece_refs, (out_ref, held, ready, leaves) = refs[: len(pieces)], refs[-4:]
        start = 0
        for number, ref in enumerate(piece_refs):
            rows = len(groups[number // 4]) * slots * each
            for tile in range(width // LANES):
                held[tile, start:start + rows, :] = ref[:rows, tile * LANES:(tile + 1) * LANES].astype(F32)
            start += rows
        row = lax.broadcasted_iota(jnp.int32, (pairs, pairs), 0)
        lane = lax.broadcasted_iota(jnp.int32, (pairs, pairs), 1)
        helpers = grid.helpers(where_ref[0])
        sources = [grid.source(helper, offset) for group in groups for helper in helpers for offset in group]
        order = lax.rem(row, slots)
        for number, source in enumerate(sources):
            order += jnp.where(lax.div(row, slots) == number, source * slots, 0)
        ordered = (order == lane).astype(F32).astype(BF16)
        paired = (pair_ref[...] == row).astype(F32).astype(BF16)
        place = lax.dot_general(ordered, paired, (((1,), (1,)), ((), ())), preferred_element_type=F32).astype(BF16)
        copies = []
        for number in range(each):
            for tile in range(width // LANES):
                rows = held[tile, pl.ds(number, pairs, stride=each), :].astype(BF16)
                placed = lax.dot_general(rows, place, (((0,), (0,)), ((), ())), preferred_element_type=F32)
                ready[number, tile * LANES:(tile + 1) * LANES, :] = placed.astype(BF16)
            copies.append(
                pltpu.make_async_copy(ready.at[number], out_ref.at[number // share, number % share], leaves.at[number])
            )
            copies[-1].start()
        for copy in copies:
            copy.wait()

    return pl.pallas_call(
        body,
        out_shape=jax.ShapeDtypeStruct((2, share, width, pairs), BF16),
        in_specs=[pl.BlockSpec(memory_space=pltpu.SMEM)] + vmem(1 + len(pieces)),
        out_specs=pl.BlockSpec(memory_space=pl.ANY),
        scratch_shapes=[
            pltpu.VMEM((width // LANES, pairs * each, LANES), F32),
            pltpu.VMEM((each, width, pairs), BF16),
            pltpu.SemaphoreType.DMA((each,)),
        ],
        compiler_params=PARAMS,
        name="place_pairs",
    )(where, pair_row, *pieces)


def on_device(n_coef, n_pair, integrals, coefficients, shell_starts, pair_ids):
    grid = Grid(n_pair)
    slots, batch_rows, ao_width = integrals.shape
    occupied = coefficients.shape[2]
    share = occupied // n_pair
    rows = slots * batch_rows
    depth = ao_width // n_pair
    piece = depth // n_coef
    where = lax.axis_index("pair").astype(jnp.int32)[None]

    batch_index = (shell_starts[:, None] + jnp.arange(SHW, dtype=jnp.int32)[None, :]).reshape(-1)
    flat_ints = integrals.reshape(rows, ao_width)
    if n_coef > 1:
        coefficients = lax.all_gather(coefficients, "coef", axis=1, tiled=True)
        flat_ints = flat_ints.reshape(rows, n_coef, n_pair, piece).transpose(0, 2, 1, 3).reshape(rows, ao_width)
        batch_index = (
            batch_index // piece % n_pair * depth + batch_index // (n_pair * piece) * piece + batch_index % piece
        )
    batch_column = batch_index[:, None]

    kept, *leaving = share_integrals(grid, where, flat_ints, depth)
    ints = [kept, *grid.exchange(leaving, grid.helpers)]
    result = [None]

    def multiply(held, offsets):
        nonlocal result
        if offsets == [0] and grid.nz > 1:
            return [kept]
        group = [0, *offsets] if offsets == [-1, 1] else offsets
        blocks = [held[offset] for offset in group]
        last = offsets == [-grid.nz]
        result = first_product(grid, where, group, ints, batch_column, result[0], blocks, last)
        return ints if offsets == [-1, 1] else []

    gather_ring(grid, coefficients, multiply)
    kept, *leaving = result
    half, batch = add_partners([kept, *grid.exchange(leaving, grid.helped)], rows, occupied)
    matrix = weights(grid, where, batch, slots, share)
    pieces, groups = [], []
    before = []

    def transform(held, group):
        kept, aside, across = second_product(matrix, [held[offset] for offset in group])
        across = grid.send(across, grid.opposite)
        passed_on = across[kept.shape[0]:]
        arrived = [kept, grid.send(aside, grid.mate), across, grid.send(passed_on, grid.mate)]
        pieces.extend(arrived)
        groups.append(group)
        nonlocal before
        before, ready = arrived, before
        return [kept,*ready[:3]]

    gather_ring(grid, half, transform)
    return place_pairs(grid, where, groups, pair_ids, pieces, share)


def solution(mesh):
    return jax.shard_map(
        functools.partial(on_device, mesh.shape["coef"], mesh.shape["pair"]),
        mesh=mesh,
        in_specs=(
            P(("coef", "pair"), None, None),
            P(None, ("coef", "pair"), None),
            P(),
            P("coef", None),
        ),
        out_specs=P(None, "pair", None, "coef"),
        check_vma=False,
    )
```

time: 97.8 us -> 93.2 us (0.953)
  waiting for transfers between devices: 37.7 us -> 44.6 us
  other arithmetic: 5.64 us -> 0.07 us
  local copies, waits for them, and re-layouts: 4.06 us -> 0.15 us
  Pallas kernels: 14.8 us -> 12.5 us
    ppermute x32 -> x35, waiting for transfers between devices: 37.7 us -> 44.6 us  [the longest x14 24.2 us: gather_ring(): held[way * step] = lax.ppermute(block, 'pair', around[way])]
    add x19 -> x0, other arithmetic: 5.25 us -> none  [the longest x17 5.22 us: on_device(): grid.source(device, offset) * slots + within]
    pallas_call x7 -> x8, Pallas kernels: 9.56 us -> 7.27 us  [the longest x1 2.54 us: place_pairs(): pl.pallas_call(body, out_shape=jax.ShapeDtypeStruct((2, share, width, pai...]
    unnamed x8 -> x6, local copies, waits for them, and re-layouts: 2.28 us -> 0.01 us
    ppermute x32 -> x35, starting transfers between devices: 35 us -> 35.4 us  [the longest x14 18.8 us: gather_ring(): held[way * step] = lax.ppermute(block, 'pair', around[way])]
  transfers between devices with their start and end apart: 32 -> 35, of which waited for: 12 -> 17; matrix products, arithmetic and copies ran while one was open for 8% -> 0% of each run, Pallas kernels for 12% -> 10%
where the time goes in v4:
time: 93.2 us; the launch traced here: 92.9 us
  waiting for transfers between devices  44.6 us (48%)
  starting transfers between devices  35.4 us (38%)
  Pallas kernels  12.5 us (13%)
    ppermute x14, waiting for transfers between devices, gather_ring(): held[way * step] = lax.ppermute(block, 'pair', around[way])  24.2 us
    ppermute x21, waiting for transfers between devices, send(): lax.ppermute(block, 'pair', [(device, int(target(device))) for device in...  20.5 us
    ppermute x14, starting transfers between devices, gather_ring(): held[way * step] = lax.ppermute(block, 'pair', around[way])  18.8 us
    ppermute x21, starting transfers between devices, send(): lax.ppermute(block, 'pair', [(device, int(target(device))) for device in...  16.6 us
    pallas_call x4, Pallas kernels, first_product(): pl.pallas_call(body, out_shape=shapes, in_specs=[pl.BlockSpec(memory_spac...  5.1 us
    pallas_call x1, Pallas kernels, place_pairs(): pl.pallas_call(body, out_shape=jax.ShapeDtypeStruct((2, share, width, pai...  2.54 us
    pallas_call x1, Pallas kernels, share_integrals(): pl.pallas_call(body, out_shape=[jax.ShapeDtypeStruct((rows, grid.ring * d...  1.88 us
  transfers between devices with their start and end apart: 35, of which 17 were waited for; matrix products, arithmetic and copies ran while one was open for 0% of the time, Pallas kernels for 10%

profile of v4, /device:TPU:0, one launch (start us, length us, event | category | flops | bytes accessed | tf_op | source)
XLA Modules:
  0.0 92.9 jit_solution(16116599528739632906)
XLA Ops:
  0.0 3.0 %collective-permute-start.3 = (bf16[2,256,384]{2,1,0:T(8,128)(2,1)}, bf16[2,256,384]{2,1,0:T(8,128)(2,1)S(1)}, u32[]{:S(2)}, u32[]{:S(2)}) collective-permute-start(bf16[2,256,384]{2,1,0:T(8,128)(2,1)} %refs_4_.1), channel_id=1, source_target_pairs={{0,8},{1,5},{2,0},{3,7},{4,12},{5,13},{6,4},{7,15},{8,16},{9,1},{1... | collective-permute-start | bytes 1179656 | tf_op jit(solution)/shard_map/ppermute | solution.py:85
  3.0 0.0 collective-permute-start.4
  3.0 1.9 %share_integrals.1 = (bf16[128,2048]{1,0:T(8,128)(2,1)S(1)}, bf16[128,2048]{1,0:T(8,128)(2,1)S(1)}, bf16[128,2048]{1,0:T(8,128)(2,1)S(1)}, bf16[128,2048]{1,0:T(8,128)(2,1)S(1)}) custom-call(s32[1]{0:T(128)} %bitcast.where_ref, bf16[128,8192]{1,0:T(8,128)(2,1)} %bitcast.2), custom_call_target="tpu_custom_call" | custom-call | tf_op jit(solution)/shard_map/share_integrals/pallas_call | solution.py:121
  4.9 0.1 collective-permute-start
  5.0 2.0 %collective-permute-start.1 = (bf16[128,2048]{1,0:T(8,128)(2,1)S(1)}, bf16[128,2048]{1,0:T(8,128)(2,1)S(1)}, u32[]{:S(2)}, u32[]{:S(2)}) collective-permute-start(bf16[128,2048]{1,0:T(8,128)(2,1)S(1)} %get-tuple-element.41), channel_id=1, source_target_pairs={{0,4},{1,3},{2,6},{3,1},{4,0},{5,7},{6,2},{7,5},{8,12},{9,11},{10,... | collective-permute-start | bytes 1572872 | tf_op jit(solution)/shard_map/ppermute | solution.py:56
  7.0 0.0 collective-permute-start.2
  7.1 4.7 %collective-permute-done.3.refs_5_ = bf16[2,256,384]{2,1,0:T(8,128)(2,1)S(1)} collective-permute-done((bf16[2,256,384]{2,1,0:T(8,128)(2,1)}, bf16[2,256,384]{2,1,0:T(8,128)(2,1)S(1)}, u32[]{:S(2)}, u32[]{:S(2)}) %collective-permute-start.3) | collective-permute-done | bytes 393248 | tf_op jit(solution)/shard_map/ppermute | solution.py:85
  11.8 2.4 %collective-permute-start.5 = (bf16[2,256,384]{2,1,0:T(8,128)(2,1)S(1)}, bf16[2,256,384]{2,1,0:T(8,128)(2,1)}, u32[]{:S(2)}, u32[]{:S(2)}) collective-permute-start(bf16[2,256,384]{2,1,0:T(8,128)(2,1)S(1)} %collective-permute-done.3.refs_5_), channel_id=1, source_target_pairs={{0,8},{1,5},{2,0},{3,7},{4,12},{5,13},{6,4},{7,15},{8,16},{9,1},{1... | collective-permute-start | bytes 1179656 | tf_op jit(solution)/shard_map/ppermute | solution.py:85
  14.2 0.0 collective-permute-done.4.refs_6_
  14.2 0.0 collective-permute-start.6
  14.2 5.8 %collective-permute-done.1.refs_2_ = bf16[128,2048]{1,0:T(8,128)(2,1)S(1)} collective-permute-done((bf16[128,2048]{1,0:T(8,128)(2,1)S(1)}, bf16[128,2048]{1,0:T(8,128)(2,1)S(1)}, u32[]{:S(2)}, u32[]{:S(2)}) %collective-permute-start.1) | collective-permute-done | bytes 524320 | tf_op jit(solution)/shard_map/ppermute | solution.py:56
  19.9 0.8 collective-permute-done.2.refs_3_
  20.8 3.8 %collective-permute-done.5.refs_5_ = bf16[2,256,384]{2,1,0:T(8,128)(2,1)} collective-permute-done((bf16[2,256,384]{2,1,0:T(8,128)(2,1)S(1)}, bf16[2,256,384]{2,1,0:T(8,128)(2,1)}, u32[]{:S(2)}, u32[]{:S(2)}) %collective-permute-start.5) | collective-permute-done | bytes 393248 | tf_op jit(solution)/shard_map/ppermute | solution.py:85
  24.5 0.1 iota_add_fusion
  24.6 0.1 add.27.batch_ref
  24.7 2.0 %collective-permute-start.8 = (bf16[2,256,384]{2,1,0:T(8,128)(2,1)}, bf16[2,256,384]{2,1,0:T(8,128)(2,1)S(1)}, u32[]{:S(2)}, u32[]{:S(2)}) collective-permute-start(bf16[2,256,384]{2,1,0:T(8,128)(2,1)} %collective-permute-done.6.refs_6_), channel_id=1, source_target_pairs={{0,2},{1,9},{2,10},{3,11},{4,6},{5,1},{6,14},{7,3},{8,0},{9,17},{1... | collective-permute-start | bytes 1179656 | tf_op jit(solution)/shard_map/ppermute | solution.py:85
  26.7 1.0 %first_product.4.refs_4_ = f32[544,768]{1,0:T(8,128)S(1)} custom-call(s32[1]{0:T(128)} %bitcast.where_ref, s32[32,1]{1,0:T(8,128)S(1)} %add.27.batch_ref, bf16[128,2048]{1,0:T(8,128)(2,1)S(1)} %get-tuple-element.39.refs_0_, bf16[128,2048]{1,0:T(8,128)(2,1)S(1)} %collective-permute-done.refs_1_, bf16[128,2048]{1,0:T(8,128)(2,1)S(1)} %collective-permute-done.1.refs_2_, ...), custom_call_target="tpu_custom_call" | custom-call | flops 3208642560 | tf_op jit(solution)/shard_map/first_product/pallas_call | solution.py:167
  27.7 6.3 %collective-permute-done.7.refs_5_ = bf16[2,256,384]{2,1,0:T(8,128)(2,1)} collective-permute-done((bf16[2,256,384]{2,1,0:T(8,128)(2,1)}, bf16[2,256,384]{2,1,0:T(8,128)(2,1)}, u32[]{:S(2)}, u32[]{:S(2)}) %collective-permute-start.7) | collective-permute-done | bytes 393248 | tf_op jit(solution)/shard_map/ppermute | solution.py:85
  34.0 2.5 %collective-permute-start.9 = (bf16[2,256,384]{2,1,0:T(8,128)(2,1)}, bf16[2,256,384]{2,1,0:T(8,128)(2,1)S(1)}, u32[]{:S(2)}, u32[]{:S(2)}) collective-permute-start(bf16[2,256,384]{2,1,0:T(8,128)(2,1)} %collective-permute-done.7.refs_5_), channel_id=1, source_target_pairs={{0,8},{1,5},{2,0},{3,7},{4,12},{5,13},{6,4},{7,15},{8,16},{9,1},{1... | collective-permute-start | bytes 1179656 | tf_op jit(solution)/shard_map/ppermute | solution.py:85
  36.5 1.9 %first_product.5.refs_4_ = f32[544,768]{1,0:T(8,128)S(1)} custom-call(s32[1]{0:T(128)} %bitcast.where_ref, s32[32,1]{1,0:T(8,128)S(1)} %add.27.batch_ref, bf16[128,2048]{1,0:T(8,128)(2,1)S(1)} %get-tuple-element.39.refs_0_, bf16[128,2048]{1,0:T(8,128)(2,1)S(1)} %collective-permute-done.refs_1_, bf16[128,2048]{1,0:T(8,128)(2,1)S(1)} %collective-permute-done.1.refs_2_, ...), custom_call_target="tpu_custom_call" | custom-call | flops 2139095040 | tf_op jit(solution)/shard_map/first_product/pallas_call | solution.py:167
  38.4 1.7 %first_product.6.refs_4_ = f32[544,768]{1,0:T(8,128)S(1)} custom-call(s32[1]{0:T(128)} %bitcast.where_ref, s32[32,1]{1,0:T(8,128)S(1)} %add.27.batch_ref, bf16[128,2048]{1,0:T(8,128)(2,1)S(1)} %get-tuple-element.39.refs_0_, bf16[128,2048]{1,0:T(8,128)(2,1)S(1)} %collective-permute-done.refs_1_, bf16[128,2048]{1,0:T(8,128)(2,1)S(1)} %collective-permute-done.1.refs_2_, ...), custom_call_target="tpu_custom_call" | custom-call | flops 2139095040 | tf_op jit(solution)/shard_map/first_product/pallas_call | solution.py:167
  40.2 2.2 %collective-permute-done.9.refs_5_ = bf16[2,256,384]{2,1,0:T(8,128)(2,1)S(1)} collective-permute-done((bf16[2,256,384]{2,1,0:T(8,128)(2,1)}, bf16[2,256,384]{2,1,0:T(8,128)(2,1)S(1)}, u32[]{:S(2)}, u32[]{:S(2)}) %collective-permute-start.9) | collective-permute-done | bytes 393248 | tf_op jit(solution)/shard_map/ppermute | solution.py:85
  42.3 0.5 first_product.7
  42.8 0.1 collective-permute-start.10
  42.9 2.9 %collective-permute-start.11 = (bf16[160,768]{1,0:T(8,128)(2,1)S(1)}, bf16[160,768]{1,0:T(8,128)(2,1)S(1)}, u32[]{:S(2)}, u32[]{:S(2)}) collective-permute-start(bf16[160,768]{1,0:T(8,128)(2,1)S(1)} %get-tuple-element.49), channel_id=1, source_target_pairs={{0,4},{1,3},{2,6},{3,1},{4,0},{5,7},{6,2},{7,5},{8,12},{9,11},{10,... | collective-permute-start | bytes 737288 | tf_op jit(solution)/shard_map/ppermute | solution.py:56
  45.8 1.8 %collective-permute-start.12 = (bf16[160,768]{1,0:T(8,128)(2,1)S(1)}, bf16[160,768]{1,0:T(8,128)(2,1)S(1)}, u32[]{:S(2)}, u32[]{:S(2)}) collective-permute-start(bf16[160,768]{1,0:T(8,128)(2,1)S(1)} %get-tuple-element.50), channel_id=1, source_target_pairs={{0,5},{1,2},{2,7},{3,0},{4,1},{5,6},{6,3},{7,4},{8,13},{9,10},{10,... | collective-permute-start | bytes 737288 | tf_op jit(solution)/shard_map/ppermute | solution.py:56
  47.5 2.4 %collective-permute-done.11.refs_2_ = bf16[160,768]{1,0:T(8,128)(2,1)S(1)} collective-permute-done((bf16[160,768]{1,0:T(8,128)(2,1)S(1)}, bf16[160,768]{1,0:T(8,128)(2,1)S(1)}, u32[]{:S(2)}, u32[]{:S(2)}) %collective-permute-start.11) | collective-permute-done | bytes 245792 | tf_op jit(solution)/shard_map/ppermute | solution.py:56
  49.9 4.9 %collective-permute-done.12.refs_3_ = bf16[160,768]{1,0:T(8,128)(2,1)S(1)} collective-permute-done((bf16[160,768]{1,0:T(8,128)(2,1)S(1)}, bf16[160,768]{1,0:T(8,128)(2,1)S(1)}, u32[]{:S(2)}, u32[]{:S(2)}) %collective-permute-start.12) | collective-permute-done | bytes 245792 | tf_op jit(solution)/shard_map/ppermute | solution.py:56
  54.9 0.1 add_partners.1
  55.0 1.6 %collective-permute-start.16 = (bf16[256,384]{1,0:T(8,128)(2,1)S(1)}, bf16[256,384]{1,0:T(8,128)(2,1)S(1)}, u32[]{:S(2)}, u32[]{:S(2)}) collective-permute-start(bf16[256,384]{1,0:T(8,128)(2,1)S(1)} %get-tuple-element.52.refs_0_), channel_id=1, source_target_pairs={{0,8},{1,5},{2,0},{3,7},{4,12},{5,13},{6,4},{7,15},{8,16},{9,1},{1... | collective-permute-start | bytes 589832 | tf_op jit(solution)/shard_map/ppermute | solution.py:85
  56.5 0.5 collective-permute-start.17
  57.1 1.2 %weights.1.matrix_ref = bf16[384,256]{1,0:T(8,128)(2,1)S(1)} custom-call(s32[1]{0:T(128)} %bitcast.where_ref, bf16[64,384]{1,0:T(8,128)(2,1)S(1)} %get-tuple-element.51.batch_ref), custom_call_target="tpu_custom_call" | custom-call | tf_op jit(solution)/shard_map/weights/pallas_call | solution.py:232
  58.3 0.3 second_product.5
  58.6 2.2 %collective-permute-done.16.refs_0_ = bf16[256,384]{1,0:T(8,128)(2,1)S(1)} collective-permute-done((bf16[256,384]{1,0:T(8,128)(2,1)S(1)}, bf16[256,384]{1,0:T(8,128)(2,1)S(1)}, u32[]{:S(2)}, u32[]{:S(2)}) %collective-permute-start.16) | collective-permute-done | bytes 196640 | tf_op jit(solution)/shard_map/ppermute | solution.py:85
  60.7 2.4 %collective-permute-start.21 = (bf16[256,384]{1,0:T(8,128)(2,1)S(1)}, bf16[256,384]{1,0:T(8,128)(2,1)S(1)}, u32[]{:S(2)}, u32[]{:S(2)}) collective-permute-start(bf16[256,384]{1,0:T(8,128)(2,1)S(1)} %collective-permute-done.16.refs_0_), channel_id=1, source_target_pairs={{0,8},{1,5},{2,0},{3,7},{4,12},{5,13},{6,4},{7,15},{8,16},{9,1},{1... | collective-permute-start | bytes 589832 | tf_op jit(solution)/shard_map/ppermute | solution.py:85
  63.1 0.3 collective-permute-start.14
  63.4 0.7 collective-permute-start.22
  64.2 0.4 second_product.6
  64.6 1.9 %collective-permute-start.19 = (bf16[384,384]{1,0:T(8,128)(2,1)S(1)}, bf16[384,384]{1,0:T(8,128)(2,1)S(1)}, u32[]{:S(2)}, u32[]{:S(2)}) collective-permute-start(bf16[384,384]{1,0:T(8,128)(2,1)S(1)} %get-tuple-element.58), channel_id=1, source_target_pairs={{0,4},{1,3},{2,6},{3,1},{4,0},{5,7},{6,2},{7,5},{8,12},{9,11},{10,... | collective-permute-start | bytes 884744 | tf_op jit(solution)/shard_map/ppermute | solution.py:56
  66.4 1.3 %collective-permute-done.13.refs_1_ = bf16[96,384]{1,0:T(8,128)(2,1)S(1)} collective-permute-done((bf16[96,384]{1,0:T(8,128)(2,1)S(1)}, bf16[96,384]{1,0:T(8,128)(2,1)S(1)}, u32[]{:S(2)}, u32[]{:S(2)}) %collective-permute-start.13) | collective-permute-done | bytes 73760 | tf_op jit(solution)/shard_map/ppermute | solution.py:56
  67.7 1.8 %collective-permute-done.14.refs_2_ = bf16[192,384]{1,0:T(8,128)(2,1)S(1)} collective-permute-done((bf16[192,384]{1,0:T(8,128)(2,1)S(1)}, bf16[192,384]{1,0:T(8,128)(2,1)S(1)}, u32[]{:S(2)}, u32[]{:S(2)}) %collective-permute-start.14) | collective-permute-done | bytes 147488 | tf_op jit(solution)/shard_map/ppermute | solution.py:56
  69.5 0.5 collective-permute-start.26
  70.0 1.6 %collective-permute-start.27 = (bf16[256,384]{1,0:T(8,128)(2,1)S(1)}, bf16[256,384]{1,0:T(8,128)(2,1)S(1)}, u32[]{:S(2)}, u32[]{:S(2)}) collective-permute-start(bf16[256,384]{1,0:T(8,128)(2,1)S(1)} %collective-permute-done.22.refs_1_), channel_id=1, source_target_pairs={{0,2},{1,9},{2,10},{3,11},{4,6},{5,1},{6,14},{7,3},{8,0},{9,17},{1... | collective-permute-start | bytes 589832 | tf_op jit(solution)/shard_map/ppermute | solution.py:85
  71.6 0.4 second_product.7
  72.0 2.1 %collective-permute-start.24 = (bf16[384,384]{1,0:T(8,128)(2,1)S(1)}, bf16[384,384]{1,0:T(8,128)(2,1)S(1)}, u32[]{:S(2)}, u32[]{:S(2)}) collective-permute-start(bf16[384,384]{1,0:T(8,128)(2,1)S(1)} %get-tuple-element.63), channel_id=1, source_target_pairs={{0,4},{1,3},{2,6},{3,1},{4,0},{5,7},{6,2},{7,5},{8,12},{9,11},{10,... | collective-permute-start | bytes 884744 | tf_op jit(solution)/shard_map/ppermute | solution.py:56
  74.1 1.3 %collective-permute-done.26.refs_0_ = bf16[256,384]{1,0:T(8,128)(2,1)S(1)} collective-permute-done((bf16[256,384]{1,0:T(8,128)(2,1)S(1)}, bf16[256,384]{1,0:T(8,128)(2,1)S(1)}, u32[]{:S(2)}, u32[]{:S(2)}) %collective-permute-start.26) | collective-permute-done | bytes 196640 | tf_op jit(solution)/shard_map/ppermute | solution.py:85
  75.4 1.6 %collective-permute-start.31 = (bf16[256,384]{1,0:T(8,128)(2,1)S(1)}, bf16[256,384]{1,0:T(8,128)(2,1)S(1)}, u32[]{:S(2)}, u32[]{:S(2)}) collective-permute-start(bf16[256,384]{1,0:T(8,128)(2,1)S(1)} %collective-permute-done.26.refs_0_), channel_id=1, source_target_pairs={{0,8},{1,5},{2,0},{3,7},{4,12},{5,13},{6,4},{7,15},{8,16},{9,1},{1... | collective-permute-start | bytes 589832 | tf_op jit(solution)/shard_map/ppermute | solution.py:85
  76.9 0.4 second_product.8
  77.3 2.0 %collective-permute-start.29 = (bf16[384,384]{1,0:T(8,128)(2,1)S(1)}, bf16[384,384]{1,0:T(8,128)(2,1)S(1)}, u32[]{:S(2)}, u32[]{:S(2)}) collective-permute-start(bf16[384,384]{1,0:T(8,128)(2,1)S(1)} %get-tuple-element.68), channel_id=1, source_target_pairs={{0,4},{1,3},{2,6},{3,1},{4,0},{5,7},{6,2},{7,5},{8,12},{9,11},{10,... | collective-permute-start | bytes 884744 | tf_op jit(solution)/shard_map/ppermute | solution.py:56
  79.3 3.8 %collective-permute-done.31.refs_0_ = bf16[256,384]{1,0:T(8,128)(2,1)S(1)} collective-permute-done((bf16[256,384]{1,0:T(8,128)(2,1)S(1)}, bf16[256,384]{1,0:T(8,128)(2,1)S(1)}, u32[]{:S(2)}, u32[]{:S(2)}) %collective-permute-start.31) | collective-permute-done | bytes 196640 | tf_op jit(solution)/shard_map/ppermute | solution.py:85
  83.1 0.3 second_product.9
  83.3 1.7 %collective-permute-start.33 = (bf16[192,384]{1,0:T(8,128)(2,1)S(1)}, bf16[192,384]{1,0:T(8,128)(2,1)S(1)}, u32[]{:S(2)}, u32[]{:S(2)}) collective-permute-start(bf16[192,384]{1,0:T(8,128)(2,1)S(1)} %get-tuple-element.72), channel_id=1, source_target_pairs={{0,4},{1,3},{2,6},{3,1},{4,0},{5,7},{6,2},{7,5},{8,12},{9,11},{10,... | collective-permute-start | bytes 442376 | tf_op jit(solution)/shard_map/ppermute | solution.py:56
  85.0 0.1 collective-permute-start.15
  85.1 0.5 collective-permute-start.23
  85.6 0.1 collective-permute-start.20
  85.8 0.6 collective-permute-done.15.refs_3_
  86.3 0.2 collective-permute-start.28
  86.5 0.4 collective-permute-start.25
  86.9 1.7 %collective-permute-done.33.refs_18_ = bf16[192,384]{1,0:T(8,128)(2,1)S(1)} collective-permute-done((bf16[192,384]{1,0:T(8,128)(2,1)S(1)}, bf16[192,384]{1,0:T(8,128)(2,1)S(1)}, u32[]{:S(2)}, u32[]{:S(2)}) %collective-permute-start.33) | collective-permute-done | bytes 147488 | tf_op jit(solution)/shard_map/ppermute | solution.py:56
  88.6 0.6 collective-permute-start.32
  89.1 0.1 collective-permute-start.34
  89.2 0.8 collective-permute-done.32.refs_17_
  90.0 0.4 collective-permute-done.34.refs_19_
  90.4 2.5 %place_pairs.1 = bf16[2,12,384,128]{3,2,1,0:T(8,128)(2,1)} custom-call(s32[1]{0:T(128)} %bitcast.where_ref, s32[1,128]{1,0:T(1,128)S(1)} %copy-done, bf16[96,384]{1,0:T(8,128)(2,1)S(1)} %get-tuple-element.53.refs_0_, bf16[96,384]{1,0:T(8,128)(2,1)S(1)} %collective-permute-done.13.refs_1_, bf16[192,384]{1,0:T(8,128)(2,1)S(1)} %collective-permute-done.14.refs_2_, ...), custom_call_target="tpu_custom_call" | custom-call | tf_op jit(solution)/shard_map/place_pairs/pallas_call | solution.py:302
  (32 shorter events, 0.1 us)
Async XLA Ops:
  0.0 26.7 %copy-start.1 = (bf16[2,256,384]{2,1,0:T(8,128)(2,1)S(1)}, bf16[2,256,384]{2,1,0:T(8,128)(2,1)}, u32[]{:S(2)}) copy-start(bf16[2,256,384]{2,1,0:T(8,128)(2,1)} %refs_4_.1) | copy-start | bytes 1179652
  0.0 24.5 %copy-start.2 = (s32[8]{0:T(128)S(1)}, s32[8]{0:T(128)}, u32[]{:S(2)}) copy-start(s32[8]{0:T(128)} %param.6) | copy-start | bytes 100
  0.0 11.8 %collective-permute-start.3 = (bf16[2,256,384]{2,1,0:T(8,128)(2,1)}, bf16[2,256,384]{2,1,0:T(8,128)(2,1)S(1)}, u32[]{:S(2)}, u32[]{:S(2)}) collective-permute-start(bf16[2,256,384]{2,1,0:T(8,128)(2,1)} %refs_4_.1), channel_id=1, source_target_pairs={{0,8},{1,5},{2,0},{3,7},{4,12},{5,13},{6,4},{7,15},{8,16},{9,1},{1... | collective-permute-start | bytes 1179656 | tf_op jit(solution)/shard_map/ppermute | solution.py:85
  3.0 11.1 %collective-permute-start.4 = (bf16[2,256,384]{2,1,0:T(8,128)(2,1)}, bf16[2,256,384]{2,1,0:T(8,128)(2,1)S(1)}, u32[]{:S(2)}, u32[]{:S(2)}) collective-permute-start(bf16[2,256,384]{2,1,0:T(8,128)(2,1)} %refs_4_.1), channel_id=1, source_target_pairs={{0,2},{1,9},{2,10},{3,11},{4,6},{5,1},{6,14},{7,3},{8,0},{9,17},{1... | collective-permute-start | bytes 1179656 | tf_op jit(solution)/shard_map/ppermute | solution.py:85
  4.9 9.2 %collective-permute-start = (bf16[128,2048]{1,0:T(8,128)(2,1)S(1)}, bf16[128,2048]{1,0:T(8,128)(2,1)S(1)}, u32[]{:S(2)}, u32[]{:S(2)}) collective-permute-start(bf16[128,2048]{1,0:T(8,128)(2,1)S(1)} %get-tuple-element.40), channel_id=1, source_target_pairs={{0,1},{1,0},{2,3},{3,2},{4,5},{5,4},{6,7},{7,6},{8,9},{9,8},{10,11... | collective-permute-start | bytes 1572872 | tf_op jit(solution)/shard_map/ppermute | solution.py:56
  5.0 14.9 %collective-permute-start.1 = (bf16[128,2048]{1,0:T(8,128)(2,1)S(1)}, bf16[128,2048]{1,0:T(8,128)(2,1)S(1)}, u32[]{:S(2)}, u32[]{:S(2)}) collective-permute-start(bf16[128,2048]{1,0:T(8,128)(2,1)S(1)} %get-tuple-element.41), channel_id=1, source_target_pairs={{0,4},{1,3},{2,6},{3,1},{4,0},{5,7},{6,2},{7,5},{8,12},{9,11},{10,... | collective-permute-start | bytes 1572872 | tf_op jit(solution)/shard_map/ppermute | solution.py:56
  7.0 13.8 %collective-permute-start.2 = (bf16[128,2048]{1,0:T(8,128)(2,1)S(1)}, bf16[128,2048]{1,0:T(8,128)(2,1)S(1)}, u32[]{:S(2)}, u32[]{:S(2)}) collective-permute-start(bf16[128,2048]{1,0:T(8,128)(2,1)S(1)} %get-tuple-element.42), channel_id=1, source_target_pairs={{0,3},{1,4},{2,1},{3,6},{4,7},{5,0},{6,5},{7,2},{8,11},{9,12},{10,... | collective-permute-start | bytes 1572872 | tf_op jit(solution)/shard_map/ppermute | solution.py:56
  11.8 12.8 %collective-permute-start.5 = (bf16[2,256,384]{2,1,0:T(8,128)(2,1)S(1)}, bf16[2,256,384]{2,1,0:T(8,128)(2,1)}, u32[]{:S(2)}, u32[]{:S(2)}) collective-permute-start(bf16[2,256,384]{2,1,0:T(8,128)(2,1)S(1)} %collective-permute-done.3.refs_5_), channel_id=1, source_target_pairs={{0,8},{1,5},{2,0},{3,7},{4,12},{5,13},{6,4},{7,15},{8,16},{9,1},{1... | collective-permute-start | bytes 1179656 | tf_op jit(solution)/shard_map/ppermute | solution.py:85
  14.2 10.5 %collective-permute-start.6 = (bf16[2,256,384]{2,1,0:T(8,128)(2,1)S(1)}, bf16[2,256,384]{2,1,0:T(8,128)(2,1)}, u32[]{:S(2)}, u32[]{:S(2)}) collective-permute-start(bf16[2,256,384]{2,1,0:T(8,128)(2,1)S(1)} %collective-permute-done.4.refs_6_), channel_id=1, source_target_pairs={{0,2},{1,9},{2,10},{3,11},{4,6},{5,1},{6,14},{7,3},{8,0},{9,17},{1... | collective-permute-start | bytes 1179656 | tf_op jit(solution)/shard_map/ppermute | solution.py:85
  24.5 9.5 %collective-permute-start.7 = (bf16[2,256,384]{2,1,0:T(8,128)(2,1)}, bf16[2,256,384]{2,1,0:T(8,128)(2,1)}, u32[]{:S(2)}, u32[]{:S(2)}) collective-permute-start(bf16[2,256,384]{2,1,0:T(8,128)(2,1)} %collective-permute-done.5.refs_5_), channel_id=1, source_target_pairs={{0,8},{1,5},{2,0},{3,7},{4,12},{5,13},{6,4},{7,15},{8,16},{9,1},{1... | collective-permute-start | bytes 1179656 | tf_op jit(solution)/shard_map/ppermute | solution.py:85
  24.7 13.7 %collective-permute-start.8 = (bf16[2,256,384]{2,1,0:T(8,128)(2,1)}, bf16[2,256,384]{2,1,0:T(8,128)(2,1)S(1)}, u32[]{:S(2)}, u32[]{:S(2)}) collective-permute-start(bf16[2,256,384]{2,1,0:T(8,128)(2,1)} %collective-permute-done.6.refs_6_), channel_id=1, source_target_pairs={{0,2},{1,9},{2,10},{3,11},{4,6},{5,1},{6,14},{7,3},{8,0},{9,17},{1... | collective-permute-start | bytes 1179656 | tf_op jit(solution)/shard_map/ppermute | solution.py:85
  34.0 8.3 %collective-permute-start.9 = (bf16[2,256,384]{2,1,0:T(8,128)(2,1)}, bf16[2,256,384]{2,1,0:T(8,128)(2,1)S(1)}, u32[]{:S(2)}, u32[]{:S(2)}) collective-permute-start(bf16[2,256,384]{2,1,0:T(8,128)(2,1)} %collective-permute-done.7.refs_5_), channel_id=1, source_target_pairs={{0,8},{1,5},{2,0},{3,7},{4,12},{5,13},{6,4},{7,15},{8,16},{9,1},{1... | collective-permute-start | bytes 1179656 | tf_op jit(solution)/shard_map/ppermute | solution.py:85
  42.8 12.1 %collective-permute-start.10 = (f32[160,768]{1,0:T(8,128)S(1)}, f32[160,768]{1,0:T(8,128)S(1)}, u32[]{:S(2)}, u32[]{:S(2)}) collective-permute-start(f32[160,768]{1,0:T(8,128)S(1)} %get-tuple-element.48), channel_id=1, source_target_pairs={{0,1},{1,0},{2,3},{3,2},{4,5},{5,4},{6,7},{7,6},{8,9},{9,8},{10,11... | collective-permute-start | bytes 1474568 | tf_op jit(solution)/shard_map/ppermute | solution.py:56
  42.9 7.0 %collective-permute-start.11 = (bf16[160,768]{1,0:T(8,128)(2,1)S(1)}, bf16[160,768]{1,0:T(8,128)(2,1)S(1)}, u32[]{:S(2)}, u32[]{:S(2)}) collective-permute-start(bf16[160,768]{1,0:T(8,128)(2,1)S(1)} %get-tuple-element.49), channel_id=1, source_target_pairs={{0,4},{1,3},{2,6},{3,1},{4,0},{5,7},{6,2},{7,5},{8,12},{9,11},{10,... | collective-permute-start | bytes 737288 | tf_op jit(solution)/shard_map/ppermute | solution.py:56
  45.8 9.1 %collective-permute-start.12 = (bf16[160,768]{1,0:T(8,128)(2,1)S(1)}, bf16[160,768]{1,0:T(8,128)(2,1)S(1)}, u32[]{:S(2)}, u32[]{:S(2)}) collective-permute-start(bf16[160,768]{1,0:T(8,128)(2,1)S(1)} %get-tuple-element.50), channel_id=1, source_target_pairs={{0,5},{1,2},{2,7},{3,0},{4,1},{5,6},{6,3},{7,4},{8,13},{9,10},{10,... | collective-permute-start | bytes 737288 | tf_op jit(solution)/shard_map/ppermute | solution.py:56
  55.0 5.7 %collective-permute-start.16 = (bf16[256,384]{1,0:T(8,128)(2,1)S(1)}, bf16[256,384]{1,0:T(8,128)(2,1)S(1)}, u32[]{:S(2)}, u32[]{:S(2)}) collective-permute-start(bf16[256,384]{1,0:T(8,128)(2,1)S(1)} %get-tuple-element.52.refs_0_), channel_id=1, source_target_pairs={{0,8},{1,5},{2,0},{3,7},{4,12},{5,13},{6,4},{7,15},{8,16},{9,1},{1... | collective-permute-start | bytes 589832 | tf_op jit(solution)/shard_map/ppermute | solution.py:85
  56.5 6.9 %collective-permute-start.17 = (bf16[256,384]{1,0:T(8,128)(2,1)S(1)}, bf16[256,384]{1,0:T(8,128)(2,1)S(1)}, u32[]{:S(2)}, u32[]{:S(2)}) collective-permute-start(bf16[256,384]{1,0:T(8,128)(2,1)S(1)} %get-tuple-element.52.refs_0_), channel_id=1, source_target_pairs={{0,2},{1,9},{2,10},{3,11},{4,6},{5,1},{6,14},{7,3},{8,0},{9,17},{1... | collective-permute-start | bytes 589832 | tf_op jit(solution)/shard_map/ppermute | solution.py:85
  60.7 8.8 %collective-permute-start.21 = (bf16[256,384]{1,0:T(8,128)(2,1)S(1)}, bf16[256,384]{1,0:T(8,128)(2,1)S(1)}, u32[]{:S(2)}, u32[]{:S(2)}) collective-permute-start(bf16[256,384]{1,0:T(8,128)(2,1)S(1)} %collective-permute-done.16.refs_0_), channel_id=1, source_target_pairs={{0,8},{1,5},{2,0},{3,7},{4,12},{5,13},{6,4},{7,15},{8,16},{9,1},{1... | collective-permute-start | bytes 589832 | tf_op jit(solution)/shard_map/ppermute | solution.py:85
  63.1 27.3 %copy-start = (s32[1,128]{1,0:T(1,128)S(1)}, s32[1,128]{1,0:T(1,128)}, u32[]{:S(2)}) copy-start(s32[1,128]{1,0:T(1,128)} %pair_ref.1) | copy-start | bytes 1540
  63.1 6.4 %collective-permute-start.14 = (bf16[192,384]{1,0:T(8,128)(2,1)S(1)}, bf16[192,384]{1,0:T(8,128)(2,1)S(1)}, u32[]{:S(2)}, u32[]{:S(2)}) collective-permute-start(bf16[192,384]{1,0:T(8,128)(2,1)S(1)} %get-tuple-element.55), channel_id=1, source_target_pairs={{0,4},{1,3},{2,6},{3,1},{4,0},{5,7},{6,2},{7,5},{8,12},{9,11},{10,... | collective-permute-start | bytes 442376 | tf_op jit(solution)/shard_map/ppermute | solution.py:56
  63.4 6.6 %collective-permute-start.22 = (bf16[256,384]{1,0:T(8,128)(2,1)S(1)}, bf16[256,384]{1,0:T(8,128)(2,1)S(1)}, u32[]{:S(2)}, u32[]{:S(2)}) collective-permute-start(bf16[256,384]{1,0:T(8,128)(2,1)S(1)} %collective-permute-done.17.refs_1_), channel_id=1, source_target_pairs={{0,2},{1,9},{2,10},{3,11},{4,6},{5,1},{6,14},{7,3},{8,0},{9,17},{1... | collective-permute-start | bytes 589832 | tf_op jit(solution)/shard_map/ppermute | solution.py:85
  64.6 9.5 %collective-permute-start.19 = (bf16[384,384]{1,0:T(8,128)(2,1)S(1)}, bf16[384,384]{1,0:T(8,128)(2,1)S(1)}, u32[]{:S(2)}, u32[]{:S(2)}) collective-permute-start(bf16[384,384]{1,0:T(8,128)(2,1)S(1)} %get-tuple-element.58), channel_id=1, source_target_pairs={{0,4},{1,3},{2,6},{3,1},{4,0},{5,7},{6,2},{7,5},{8,12},{9,11},{10,... | collective-permute-start | bytes 884744 | tf_op jit(solution)/shard_map/ppermute | solution.py:56
  66.4 1.3 %collective-permute-start.13 = (bf16[96,384]{1,0:T(8,128)(2,1)S(1)}, bf16[96,384]{1,0:T(8,128)(2,1)S(1)}, u32[]{:S(2)}, u32[]{:S(2)}) collective-permute-start(bf16[96,384]{1,0:T(8,128)(2,1)S(1)} %get-tuple-element.54), channel_id=1, source_target_pairs={{0,1},{1,0},{2,3},{3,2},{4,5},{5,4},{6,7},{7,6},{8,9},{9,8},{10,11... | collective-permute-start | bytes 221192 | tf_op jit(solution)/shard_map/ppermute | solution.py:56
  69.5 5.8 %collective-permute-start.26 = (bf16[256,384]{1,0:T(8,128)(2,1)S(1)}, bf16[256,384]{1,0:T(8,128)(2,1)S(1)}, u32[]{:S(2)}, u32[]{:S(2)}) collective-permute-start(bf16[256,384]{1,0:T(8,128)(2,1)S(1)} %collective-permute-done.21.refs_0_), channel_id=1, source_target_pairs={{0,8},{1,5},{2,0},{3,7},{4,12},{5,13},{6,4},{7,15},{8,16},{9,1},{1... | collective-permute-start | bytes 589832 | tf_op jit(solution)/shard_map/ppermute | solution.py:85
  70.0 4.0 %collective-permute-start.18 = (bf16[192,384]{1,0:T(8,128)(2,1)S(1)}, bf16[192,384]{1,0:T(8,128)(2,1)S(1)}, u32[]{:S(2)}, u32[]{:S(2)}) collective-permute-start(bf16[192,384]{1,0:T(8,128)(2,1)S(1)} %get-tuple-element.57), channel_id=1, source_target_pairs={{0,1},{1,0},{2,3},{3,2},{4,5},{5,4},{6,7},{7,6},{8,9},{9,8},{10,11... | collective-permute-start | bytes 442376 | tf_op jit(solution)/shard_map/ppermute | solution.py:56
  70.0 6.9 %collective-permute-start.27 = (bf16[256,384]{1,0:T(8,128)(2,1)S(1)}, bf16[256,384]{1,0:T(8,128)(2,1)S(1)}, u32[]{:S(2)}, u32[]{:S(2)}) collective-permute-start(bf16[256,384]{1,0:T(8,128)(2,1)S(1)} %collective-permute-done.22.refs_1_), channel_id=1, source_target_pairs={{0,2},{1,9},{2,10},{3,11},{4,6},{5,1},{6,14},{7,3},{8,0},{9,17},{1... | collective-permute-start | bytes 589832 | tf_op jit(solution)/shard_map/ppermute | solution.py:85
  72.0 13.6 %collective-permute-start.24 = (bf16[384,384]{1,0:T(8,128)(2,1)S(1)}, bf16[384,384]{1,0:T(8,128)(2,1)S(1)}, u32[]{:S(2)}, u32[]{:S(2)}) collective-permute-start(bf16[384,384]{1,0:T(8,128)(2,1)S(1)} %get-tuple-element.63), channel_id=1, source_target_pairs={{0,4},{1,3},{2,6},{3,1},{4,0},{5,7},{6,2},{7,5},{8,12},{9,11},{10,... | collective-permute-start | bytes 884744 | tf_op jit(solution)/shard_map/ppermute | solution.py:56
  75.4 7.7 %collective-permute-start.31 = (bf16[256,384]{1,0:T(8,128)(2,1)S(1)}, bf16[256,384]{1,0:T(8,128)(2,1)S(1)}, u32[]{:S(2)}, u32[]{:S(2)}) collective-permute-start(bf16[256,384]{1,0:T(8,128)(2,1)S(1)} %collective-permute-done.26.refs_0_), channel_id=1, source_target_pairs={{0,8},{1,5},{2,0},{3,7},{4,12},{5,13},{6,4},{7,15},{8,16},{9,1},{1... | collective-permute-start | bytes 589832 | tf_op jit(solution)/shard_map/ppermute | solution.py:85
  77.3 9.2 %collective-permute-start.29 = (bf16[384,384]{1,0:T(8,128)(2,1)S(1)}, bf16[384,384]{1,0:T(8,128)(2,1)S(1)}, u32[]{:S(2)}, u32[]{:S(2)}) collective-permute-start(bf16[384,384]{1,0:T(8,128)(2,1)S(1)} %get-tuple-element.68), channel_id=1, source_target_pairs={{0,4},{1,3},{2,6},{3,1},{4,0},{5,7},{6,2},{7,5},{8,12},{9,11},{10,... | collective-permute-start | bytes 884744 | tf_op jit(solution)/shard_map/ppermute | solution.py:56
  83.3 5.2 %collective-permute-start.33 = (bf16[192,384]{1,0:T(8,128)(2,1)S(1)}, bf16[192,384]{1,0:T(8,128)(2,1)S(1)}, u32[]{:S(2)}, u32[]{:S(2)}) collective-permute-start(bf16[192,384]{1,0:T(8,128)(2,1)S(1)} %get-tuple-element.72), channel_id=1, source_target_pairs={{0,4},{1,3},{2,6},{3,1},{4,0},{5,7},{6,2},{7,5},{8,12},{9,11},{10,... | collective-permute-start | bytes 442376 | tf_op jit(solution)/shard_map/ppermute | solution.py:56
  85.0 1.3 %collective-permute-start.15 = (bf16[96,384]{1,0:T(8,128)(2,1)S(1)}, bf16[96,384]{1,0:T(8,128)(2,1)S(1)}, u32[]{:S(2)}, u32[]{:S(2)}) collective-permute-start(bf16[96,384]{1,0:T(8,128)(2,1)S(1)} %slice.20), channel_id=1, source_target_pairs={{0,1},{1,0},{2,3},{3,2},{4,5},{5,4},{6,7},{7,6},{8,9},{9,8},{10,11... | collective-permute-start | bytes 221192 | tf_op jit(solution)/shard_map/ppermute | solution.py:56
  85.1 3.5 %collective-permute-start.23 = (bf16[192,384]{1,0:T(8,128)(2,1)S(1)}, bf16[192,384]{1,0:T(8,128)(2,1)S(1)}, u32[]{:S(2)}, u32[]{:S(2)}) collective-permute-start(bf16[192,384]{1,0:T(8,128)(2,1)S(1)} %get-tuple-element.62), channel_id=1, source_target_pairs={{0,1},{1,0},{2,3},{3,2},{4,5},{5,4},{6,7},{7,6},{8,9},{9,8},{10,11... | collective-permute-start | bytes 442376 | tf_op jit(solution)/shard_map/ppermute | solution.py:56
  85.6 3.5 %collective-permute-start.20 = (bf16[192,384]{1,0:T(8,128)(2,1)S(1)}, bf16[192,384]{1,0:T(8,128)(2,1)S(1)}, u32[]{:S(2)}, u32[]{:S(2)}) collective-permute-start(bf16[192,384]{1,0:T(8,128)(2,1)S(1)} %slice.21), channel_id=1, source_target_pairs={{0,1},{1,0},{2,3},{3,2},{4,5},{5,4},{6,7},{7,6},{8,9},{9,8},{10,11... | collective-permute-start | bytes 442376 | tf_op jit(solution)/shard_map/ppermute | solution.py:56
  86.3 2.9 %collective-permute-start.28 = (bf16[192,384]{1,0:T(8,128)(2,1)S(1)}, bf16[192,384]{1,0:T(8,128)(2,1)S(1)}, u32[]{:S(2)}, u32[]{:S(2)}) collective-permute-start(bf16[192,384]{1,0:T(8,128)(2,1)S(1)} %get-tuple-element.67), channel_id=1, source_target_pairs={{0,1},{1,0},{2,3},{3,2},{4,5},{5,4},{6,7},{7,6},{8,9},{9,8},{10,11... | collective-permute-start | bytes 442376 | tf_op jit(solution)/shard_map/ppermute | solution.py:56
  86.5 2.7 %collective-permute-start.25 = (bf16[192,384]{1,0:T(8,128)(2,1)S(1)}, bf16[192,384]{1,0:T(8,128)(2,1)S(1)}, u32[]{:S(2)}, u32[]{:S(2)}) collective-permute-start(bf16[192,384]{1,0:T(8,128)(2,1)S(1)} %slice.22), channel_id=1, source_target_pairs={{0,1},{1,0},{2,3},{3,2},{4,5},{5,4},{6,7},{7,6},{8,9},{9,8},{10,11... | collective-permute-start | bytes 442376 | tf_op jit(solution)/shard_map/ppermute | solution.py:56
  88.5 1.9 %collective-permute-start.30 = (bf16[192,384]{1,0:T(8,128)(2,1)S(1)}, bf16[192,384]{1,0:T(8,128)(2,1)S(1)}, u32[]{:S(2)}, u32[]{:S(2)}) collective-permute-start(bf16[192,384]{1,0:T(8,128)(2,1)S(1)} %slice.23), channel_id=1, source_target_pairs={{0,1},{1,0},{2,3},{3,2},{4,5},{5,4},{6,7},{7,6},{8,9},{9,8},{10,11... | collective-permute-start | bytes 442376 | tf_op jit(solution)/shard_map/ppermute | solution.py:56
  88.6 1.5 %collective-permute-start.32 = (bf16[96,384]{1,0:T(8,128)(2,1)S(1)}, bf16[96,384]{1,0:T(8,128)(2,1)S(1)}, u32[]{:S(2)}, u32[]{:S(2)}) collective-permute-start(bf16[96,384]{1,0:T(8,128)(2,1)S(1)} %get-tuple-element.71), channel_id=1, source_target_pairs={{0,1},{1,0},{2,3},{3,2},{4,5},{5,4},{6,7},{7,6},{8,9},{9,8},{10,11... | collective-permute-start | bytes 221192 | tf_op jit(solution)/shard_map/ppermute | solution.py:56
  89.1 1.3 %collective-permute-start.34 = (bf16[96,384]{1,0:T(8,128)(2,1)S(1)}, bf16[96,384]{1,0:T(8,128)(2,1)S(1)}, u32[]{:S(2)}, u32[]{:S(2)}) collective-permute-start(bf16[96,384]{1,0:T(8,128)(2,1)S(1)} %slice.24), channel_id=1, source_target_pairs={{0,1},{1,0},{2,3},{3,2},{4,5},{5,4},{6,7},{7,6},{8,9},{9,8},{10,11... | collective-permute-start | bytes 221192 | tf_op jit(solution)/shard_map/ppermute | solution.py:56

commit v5 on v4

--- a/solution.py
+++ b/solution.py
@@ -36,8 +36,11 @@
         every = range(self.ring * 4)
         return [(device, int(self.device(*target(*self.place(device))))) for device in every]
 
+    def sense(self, side, core):
+        return (1 - 2 * core) * (1 - 2 * side)
+
     def around(self, way):
-        return self.moves(lambda spot, side, core: ((spot + way * (1 - 2 * core)) % self.ring, side, core))
+        return self.moves(lambda spot, side, core: ((spot + way * self.sense(side, core)) % self.ring, side, core))
 
     def mate(self, device):
         return device + 1 - 2 * (device % 2)
@@ -59,8 +62,8 @@
         return [self.send(block, lambda device: partners(device)[k]) for k, block in zip((1, 2, 3), blocks)]
 
     def spot(self, device, offset):
-        spot, _, core = self.place(device)
-        return (spot + offset * (1 - 2 * core) + self.ring) % self.ring
+        spot, side, core = self.place(device)
+        return (spot + offset * self.sense(side, core) + self.ring) % self.ring
 
     def source_at(self, device, spot):
         _, side, core = self.place(device)
@@ -99,52 +102,57 @@
     return pltpu.with_memory_space_constraint(array, pltpu.HBM)
 
 
-def share_integrals(grid, where, integrals, depth):
+def share_integrals(grid, where, integrals, depth, groups):
     rows = integrals.shape[0]
 
     def body(where_ref, ints_ref, *refs):
         outs, moved = refs[:-1], refs[-1]
         copies = []
-        for k, (out, helper) in enumerate(zip(outs, grid.helpers(where_ref[0]))):
-            for spot in range(grid.ring):
-                start = pl.multiple_of(grid.source_at(helper, spot) * depth, depth)
-                copies.append(
-                    pltpu.make_async_copy(
-                        ints_ref.at[:, pl.ds(start, depth)], out.at[:, pl.ds(spot * depth, depth)], moved.at[k, spot]
+        for k, helper in enumerate(grid.helpers(where_ref[0])):
+            for number, group in enumerate(groups):
+                for place, offset in enumerate(group):
+                    start = pl.multiple_of(grid.source(helper, offset) * depth, depth)
+                    out = outs[4 * number + k].at[:, pl.ds(place * depth, depth)]
+                    copies.append(
+                        pltpu.make_async_copy(ints_ref.at[:, pl.ds(start, depth)], out, moved.at[len(copies)])
                     )
-                )
         for copy in copies:
             copy.start()
         for copy in copies:
             copy.wait()
 
-    return pl.pallas_call(
-        body,
-        out_shape=[jax.ShapeDtypeStruct((rows, grid.ring * depth), BF16)] * 4,
+    outs = pl.pallas_call(
+        body,
+        out_shape=[jax.ShapeDtypeStruct((rows, len(group) * depth), BF16) for group in groups for _ in range(4)],
         in_specs=[pl.BlockSpec(memory_space=pltpu.SMEM), pl.BlockSpec(memory_space=pl.ANY)],
-        out_specs=vmem(4),
-        scratch_shapes=[pltpu.SemaphoreType.DMA((4, grid.ring))],
+        out_specs=vmem(4 * len(groups)),
+        scratch_shapes=[pltpu.SemaphoreType.DMA((4 * grid.ring,))],
         compiler_params=PARAMS,
         name="share_integrals",
     )(where, in_hbm(integrals))
-
-
-def first_product(grid, where, offsets, ints, batch_column, total, blocks, last):
+    return [outs[4 * number:4 * number + 4] for number in range(len(groups))]
+
+
+def first_product(grid, where, offsets, ints, begin, batch_starts, moved_to, total, blocks, last):
     parts, depth, width = blocks[0].shape
-    rows, batch_rows = ints[0].shape[0], batch_column.shape[0]
+    rows, batch_rows = ints[0].shape[0], batch_starts.shape[0] * SHW
     high = len(ints) * rows + batch_rows
     begins = total is None
 
-    def body(where_ref, batch_ref, *refs):
+    def body(where_ref, starts_ref, *refs):
         ints_refs, refs = refs[: len(ints)], refs[len(ints):]
         total_ref, refs = (None, refs) if begins else (refs[0], refs[1:])
         block_refs, outs = refs[: len(blocks)], refs[len(blocks):]
         sum_ref = outs[-1]
         me = where_ref[0]
+        row = lax.broadcasted_iota(jnp.int32, (batch_rows, depth), 0)
+        wanted = row
+        for shell in range(batch_starts.shape[0]):
+            wanted = jnp.where(row >= shell * SHW, row + (moved_to(starts_ref[shell]) - shell * SHW), wanted)
         for number, (offset, ref) in enumerate(zip(offsets, block_refs)):
-            columns = pl.ds(pl.multiple_of(grid.spot(me, offset) * depth, depth), depth)
+            columns = pl.ds((begin + number) * depth, depth)
             position = lax.broadcasted_iota(jnp.int32, (batch_rows, depth), 1) + grid.source(me, offset) * depth
-            picks = (batch_ref[...] == position).astype(F32).astype(BF16)
+            picks = (wanted == position).astype(F32).astype(BF16)
             left = jnp.concatenate([ints_ref[:, columns] for ints_ref in ints_refs] + [picks], axis=0)
             for part in range(parts):
                 term = jnp.dot(left, ref[part], preferred_element_type=F32)
@@ -167,7 +175,7 @@
     return pl.pallas_call(
         body,
         out_shape=shapes,
-        in_specs=[pl.BlockSpec(memory_space=pltpu.SMEM)] + vmem(1 + len(ints) + len(totals) + len(blocks)),
+        in_specs=[pl.BlockSpec(memory_space=pltpu.SMEM)] * 2 + vmem(len(ints) + len(totals) + len(blocks)),
         out_specs=vmem(len(shapes)),
         scratch_shapes=[pltpu.VMEM(whole.shape, F32)] if last else [],
         compiler_params=PARAMS,
@@ -175,7 +183,7 @@
             flops=10 * high * depth * width * parts * len(blocks), bytes_accessed=0, transcendentals=0
         ),
         name="first_product",
-    )(where, batch_column, *ints, *totals, *blocks)
+    )(where, batch_starts, *ints, *totals, *blocks)
 
 
 def add_partners(sums, rows, width):
@@ -322,51 +330,65 @@
     rows = slots * batch_rows
     depth = ao_width // n_pair
     piece = depth // n_coef
+    assert piece % SHW == 0
     where = lax.axis_index("pair").astype(jnp.int32)[None]
 
-    batch_index = (shell_starts[:, None] + jnp.arange(SHW, dtype=jnp.int32)[None, :]).reshape(-1)
     flat_ints = integrals.reshape(rows, ao_width)
     if n_coef > 1:
         coefficients = lax.all_gather(coefficients, "coef", axis=1, tiled=True)
         flat_ints = flat_ints.reshape(rows, n_coef, n_pair, piece).transpose(0, 2, 1, 3).reshape(rows, ao_width)
-        batch_index = (
-            batch_index // piece % n_pair * depth + batch_index // (n_pair * piece) * piece + batch_index % piece
-        )
-    batch_column = batch_index[:, None]
-
-    kept, *leaving = share_integrals(grid, where, flat_ints, depth)
-    ints = [kept, *grid.exchange(leaving, grid.helpers)]
+
+    def moved_to(start):
+        if n_coef == 1:
+            return start
+        return start // piece % n_pair * depth + start // (n_pair * piece) * piece + start % piece
+
+    reach = grid.nz
+    groups = [[0, -1, 1]] + [[-step, step] for step in range(2, reach)]
+    groups[-1].append(-reach)
+    shared = share_integrals(grid, where, flat_ints, depth, groups)
+    ints = []
     result = [None]
 
     def multiply(held, offsets):
         nonlocal result
-        if offsets == [0] and grid.nz > 1:
-            return [kept]
-        group = [0, *offsets] if offsets == [-1, 1] else offsets
-        blocks = [held[offset] for offset in group]
-        last = offsets == [-grid.nz]
-        result = first_product(grid, where, group, ints, batch_column, result[0], blocks, last)
-        return ints if offsets == [-1, 1] else []
+        if offsets == [0]:
+            return [shared[0][0]]
+        if len(ints) < len(groups):
+            kept, *leaving = shared[len(ints)]
+            if ints:
+                leaving = [after(block, held[0]) for block in leaving]
+            ints.append([kept, *grid.exchange(leaving, grid.helpers)])
+        last = offsets == [-reach]
+        offsets = [0, *offsets] if offsets == [-1, 1] else offsets
+        blocks = [held[offset] for offset in offsets]
+        number = [offsets[-1] in group for group in groups].index(True)
+        begin = groups[number].index(offsets[0])
+        result = first_product(grid, where, offsets, ints[number], begin, shell_starts, moved_to, result[0], blocks, last)
+        return ints[-1]
 
     gather_ring(grid, coefficients, multiply)
     kept, *leaving = result
-    half, batch = add_partners([kept, *grid.exchange(leaving, grid.helped)], rows, occupied)
+    half_first, batch = add_partners([kept, *grid.exchange(leaving, grid.helped)], rows, occupied)
     matrix = weights(grid, where, batch, slots, share)
     pieces, groups = [], []
     before = []
 
     def transform(held, group):
         kept, aside, across = second_product(matrix, [held[offset] for offset in group])
-        across = grid.send(across, grid.opposite)
-        passed_on = across[kept.shape[0]:]
-        arrived = [kept, grid.send(aside, grid.mate), across, grid.send(passed_on, grid.mate)]
+        half = kept.shape[0]
+        if group == [-grid.nz]:
+            arrived = [kept, *grid.exchange([aside, across[:half], across[half:]], grid.helped)]
+        else:
+            across = grid.send(across, grid.opposite)
+            arrived = [kept, grid.send(aside, grid.mate), across, grid.send(across[half:], grid.mate)]
         pieces.extend(arrived)
         groups.append(group)
         nonlocal before
         before, ready = arrived, before
-        return [kept,*ready[:3]]
-
-    gather_ring(grid, half, transform)
+        return [[kept,*ready[:3]],[kept,*ready[:3]],[kept,*ready[:3]]][len(groups) - 1] if len(groups) < 4 else []
+
+    gather_ring(grid, half_first, transform)
     return place_pairs(grid, where, groups, pair_ids, pieces, share)
 
 

time: 93.2 us -> 91.9 us (0.986)
  starting transfers between devices: 35.4 us -> 33.8 us
    ppermute x21 -> x27, waiting for transfers between devices: 20.5 us -> 27.3 us  [send(): lax.ppermute(block, 'pair', [(device, int(target(device))) for device in...]
    ppermute x14, waiting for transfers between devices: 24.2 us -> 17.7 us  [gather_ring(): held[way * step] = lax.ppermute(block, 'pair', around[way])]
    ppermute x14, starting transfers between devices: 18.8 us -> 14.5 us  [gather_ring(): held[way * step] = lax.ppermute(block, 'pair', around[way])]
    ppermute x21 -> x27, starting transfers between devices: 16.6 us -> 19.3 us  [send(): lax.ppermute(block, 'pair', [(device, int(target(device))) for device in...]
  transfers between devices with their start and end apart: 35 -> 41, of which waited for: 17 -> 18; matrix products, arithmetic and copies ran while one was open for 0% -> 0% of each run, Pallas kernels for 10% -> 10%
where the time goes in v5:
time: 91.9 us; the launch traced here: 91.6 us
  waiting for transfers between devices  44.9 us (49%)
  starting transfers between devices  33.8 us (37%)
  Pallas kernels  12.6 us (14%)
    ppermute x27, waiting for transfers between devices, send(): lax.ppermute(block, 'pair', [(device, int(target(device))) for device in...  27.3 us
    ppermute x27, starting transfers between devices, send(): lax.ppermute(block, 'pair', [(device, int(target(device))) for device in...  19.3 us
    ppermute x14, waiting for transfers between devices, gather_ring(): held[way * step] = lax.ppermute(block, 'pair', around[way])  17.7 us
    ppermute x14, starting transfers between devices, gather_ring(): held[way * step] = lax.ppermute(block, 'pair', around[way])  14.5 us
    pallas_call x4, Pallas kernels, first_product(): pl.pallas_call(body, out_shape=shapes, in_specs=[pl.BlockSpec(memory_spac...  5.14 us
    pallas_call x1, Pallas kernels, place_pairs(): pl.pallas_call(body, out_shape=jax.ShapeDtypeStruct((2, share, width, pai...  2.56 us
    pallas_call x1, Pallas kernels, share_integrals(): pl.pallas_call(body, out_shape=[jax.ShapeDtypeStruct((rows, len(group) *...  1.92 us
  transfers between devices with their start and end apart: 41, of which 18 were waited for; matrix products, arithmetic and copies ran while one was open for 0% of the time, Pallas kernels for 10%

profile of v5, /device:TPU:0, one launch (start us, length us, event | category | flops | bytes accessed | tf_op | source)
XLA Modules:
  0.0 91.6 jit_solution(13428376423611687498)
XLA Ops:
  0.0 3.0 %collective-permute-start.9 = (bf16[2,256,384]{2,1,0:T(8,128)(2,1)}, bf16[2,256,384]{2,1,0:T(8,128)(2,1)S(1)}, u32[]{:S(2)}, u32[]{:S(2)}) collective-permute-start(bf16[2,256,384]{2,1,0:T(8,128)(2,1)} %refs_4_.1), channel_id=1, source_target_pairs={{0,8},{1,5},{2,0},{3,11},{4,6},{5,13},{6,14},{7,3},{8,16},{9,1},{1... | collective-permute-start | bytes 1179656 | tf_op jit(solution)/shard_map/ppermute | solution.py:88
  3.0 1.9 %share_integrals.1 = (bf16[128,768]{1,0:T(8,128)(2,1)S(1)}, bf16[128,768]{1,0:T(8,128)(2,1)S(1)}, bf16[128,768]{1,0:T(8,128)(2,1)S(1)}, bf16[128,768]{1,0:T(8,12...) custom-call(s32[1]{0:T(128)} %bitcast.where_ref, ...), custom_call_target="tpu_custom_call" | custom-call | tf_op jit(solution)/shard_map/share_integrals/pallas_call | solution.py:124
  5.0 6.8 %collective-permute-done.9.refs_5_ = bf16[2,256,384]{2,1,0:T(8,128)(2,1)S(1)} collective-permute-done((bf16[2,256,384]{2,1,0:T(8,128)(2,1)}, bf16[2,256,384]{2,1,0:T(8,128)(2,1)S(1)}, u32[]{:S(2)}, u32[]{:S(2)}) %collective-permute-start.9) | collective-permute-done | bytes 393248 | tf_op jit(solution)/shard_map/ppermute | solution.py:88
  11.8 2.4 %collective-permute-start.11 = (bf16[2,256,384]{2,1,0:T(8,128)(2,1)S(1)}, bf16[2,256,384]{2,1,0:T(8,128)(2,1)S(1)}, u32[]{:S(2)}, u32[]{:S(2)}) collective-permute-start(bf16[2,256,384]{2,1,0:T(8,128)(2,1)S(1)} %collective-permute-done.9.refs_5_), channel_id=1, source_target_pairs={{0,8},{1,5},{2,0},{3,11},{4,6},{5,13},{6,14},{7,3},{8,16},{9,1},{1... | collective-permute-start | bytes 1179656 | tf_op jit(solution)/shard_map/ppermute | solution.py:88
  14.2 0.8 collective-permute-start.12
  15.0 2.1 %collective-permute-start.7 = (bf16[128,768]{1,0:T(8,128)(2,1)S(1)}, bf16[128,768]{1,0:T(8,128)(2,1)S(1)}, u32[]{:S(2)}, u32[]{:S(2)}) collective-permute-start(bf16[128,768]{1,0:T(8,128)(2,1)S(1)} %get-tuple-element.70), channel_id=1, source_target_pairs={{0,4},{1,3},{2,6},{3,1},{4,0},{5,7},{6,2},{7,5},{8,12},{9,11},{10,... | collective-permute-start | bytes 589832 | tf_op jit(solution)/shard_map/ppermute | solution.py:59
  17.0 0.1 collective-permute-start.8
  17.2 5.7 %collective-permute-done.7.refs_2_ = bf16[128,768]{1,0:T(8,128)(2,1)S(1)} collective-permute-done((bf16[128,768]{1,0:T(8,128)(2,1)S(1)}, bf16[128,768]{1,0:T(8,128)(2,1)S(1)}, u32[]{:S(2)}, u32[]{:S(2)}) %collective-permute-start.7) | collective-permute-done | bytes 196640 | tf_op jit(solution)/shard_map/ppermute | solution.py:59
  22.9 1.6 %collective-permute-done.8.refs_3_ = bf16[128,768]{1,0:T(8,128)(2,1)S(1)} collective-permute-done((bf16[128,768]{1,0:T(8,128)(2,1)S(1)}, bf16[128,768]{1,0:T(8,128)(2,1)S(1)}, u32[]{:S(2)}, u32[]{:S(2)}) %collective-permute-start.8) | collective-permute-done | bytes 196640 | tf_op jit(solution)/shard_map/ppermute | solution.py:59
  24.5 2.3 %collective-permute-start.3 = (bf16[128,512]{1,0:T(8,128)(2,1)S(1)}, bf16[128,512]{1,0:T(8,128)(2,1)S(1)}, u32[]{:S(2)}, u32[]{:S(2)}) collective-permute-start(bf16[128,512]{1,0:T(8,128)(2,1)S(1)} %get-tuple-element.63), channel_id=1, source_target_pairs={{0,1},{1,0},{2,3},{3,2},{4,5},{5,4},{6,7},{7,6},{8,9},{9,8},{10,11... | collective-permute-start | bytes 393224 | tf_op jit(solution)/shard_map/ppermute | solution.py:59
  26.8 0.3 collective-permute-start.4
  27.1 1.1 %collective-permute-start.5 = (bf16[128,512]{1,0:T(8,128)(2,1)S(1)}, bf16[128,512]{1,0:T(8,128)(2,1)S(1)}, u32[]{:S(2)}, u32[]{:S(2)}) collective-permute-start(bf16[128,512]{1,0:T(8,128)(2,1)S(1)} %get-tuple-element.67), channel_id=1, source_target_pairs={{0,3},{1,4},{2,1},{3,6},{4,7},{5,0},{6,5},{7,2},{8,11},{9,12},{10,... | collective-permute-start | bytes 393224 | tf_op jit(solution)/shard_map/ppermute | solution.py:59
  28.1 0.4 collective-permute-start.14
  28.6 1.6 %first_product.4.refs_4_ = f32[544,768]{1,0:T(8,128)S(1)} custom-call(s32[1]{0:T(128)} %bitcast.where_ref, s32[8]{0:T(128)S(1)} %copy-done.2, bf16[128,768]{1,0:T(8,128)(2,1)S(1)} %get-tuple-element.68.refs_0_, bf16[128,768]{1,0:T(8,128)(2,1)S(1)} %collective-permute-done.6.refs_1_, bf16[128,768]{1,0:T(8,128)(2,1)S(1)} %collective-permute-done.7.refs_2_, ...), custom_call_target="tpu_custom_call" | custom-call | flops 3208642560 | tf_op jit(solution)/shard_map/first_product/pallas_call | solution.py:175
  30.1 0.5 collective-permute-start
  30.6 2.6 %collective-permute-done.4.refs_2_ = bf16[128,512]{1,0:T(8,128)(2,1)S(1)} collective-permute-done((bf16[128,512]{1,0:T(8,128)(2,1)S(1)}, bf16[128,512]{1,0:T(8,128)(2,1)S(1)}, u32[]{:S(2)}, u32[]{:S(2)}) %collective-permute-start.4) | collective-permute-done | bytes 131104 | tf_op jit(solution)/shard_map/ppermute | solution.py:59
  33.2 0.3 collective-permute-start.1
  33.4 0.3 collective-permute-start.2
  33.7 0.7 collective-permute-start.15
  34.4 1.3 %first_product.5.refs_4_ = f32[544,768]{1,0:T(8,128)S(1)} custom-call(s32[1]{0:T(128)} %bitcast.where_ref, s32[8]{0:T(128)S(1)} %copy-done.2, bf16[128,512]{1,0:T(8,128)(2,1)S(1)} %get-tuple-element.61.refs_0_, bf16[128,512]{1,0:T(8,128)(2,1)S(1)} %collective-permute-done.3.refs_1_, bf16[128,512]{1,0:T(8,128)(2,1)S(1)} %collective-permute-done.4.refs_2_, ...), custom_call_target="tpu_custom_call" | custom-call | flops 2139095040 | tf_op jit(solution)/shard_map/first_product/pallas_call | solution.py:175
  35.7 5.3 %collective-permute-done.1.refs_2_ = bf16[128,768]{1,0:T(8,128)(2,1)S(1)} collective-permute-done((bf16[128,768]{1,0:T(8,128)(2,1)S(1)}, bf16[128,768]{1,0:T(8,128)(2,1)S(1)}, u32[]{:S(2)}, u32[]{:S(2)}) %collective-permute-start.1) | collective-permute-done | bytes 196640 | tf_op jit(solution)/shard_map/ppermute | solution.py:59
  41.0 0.3 collective-permute-done.2.refs_3_
  41.3 1.3 %first_product.6.refs_4_ = f32[544,768]{1,0:T(8,128)S(1)} custom-call(s32[1]{0:T(128)} %bitcast.where_ref, s32[8]{0:T(128)S(1)} %copy-done.2, bf16[128,768]{1,0:T(8,128)(2,1)S(1)} %get-tuple-element.54.refs_0_, bf16[128,768]{1,0:T(8,128)(2,1)S(1)} %collective-permute-done.refs_1_, bf16[128,768]{1,0:T(8,128)(2,1)S(1)} %collective-permute-done.1.refs_2_, ...), custom_call_target="tpu_custom_call" | custom-call | flops 2139095040 | tf_op jit(solution)/shard_map/first_product/pallas_call | solution.py:175
  42.6 2.2 %collective-permute-done.15.refs_5_ = bf16[2,256,384]{2,1,0:T(8,128)(2,1)S(1)} collective-permute-done((bf16[2,256,384]{2,1,0:T(8,128)(2,1)S(1)}, bf16[2,256,384]{2,1,0:T(8,128)(2,1)S(1)}, u32[]{:S(2)}, u32[]{:S(2)}) %collective-permute-start.15) | collective-permute-done | bytes 393248 | tf_op jit(solution)/shard_map/ppermute | solution.py:88
  44.8 1.0 %first_product.7 = (f32[160,768]{1,0:T(8,128)S(1)}, f32[160,768]{1,0:T(8,128)S(1)}, bf16[160,768]{1,0:T(8,128)(2,1)S(1)}, bf16[160,768]{1,0:T(8,128)(2,1)S(1)}) custom-call(s32[1]{0:T(128)} %bitcast.where_ref, s32[8]{0:T(128)S(1)} %copy-done.2, bf16[128,768]{1,0:T(8,128)(2,1)S(1)} %get-tuple-element.54.refs_0_, ...), custom_call_target="tpu_custom_call" | custom-call | flops 1069547520 | tf_op jit(solution)/shard_map/first_product/pallas_call | solution.py:175
  45.8 0.1 collective-permute-start.16
  45.8 1.0 %collective-permute-start.17 = (bf16[160,768]{1,0:T(8,128)(2,1)S(1)}, bf16[160,768]{1,0:T(8,128)(2,1)S(1)}, u32[]{:S(2)}, u32[]{:S(2)}) collective-permute-start(bf16[160,768]{1,0:T(8,128)(2,1)S(1)} %get-tuple-element.79), channel_id=1, source_target_pairs={{0,4},{1,3},{2,6},{3,1},{4,0},{5,7},{6,2},{7,5},{8,12},{9,11},{10,... | collective-permute-start | bytes 737288 | tf_op jit(solution)/shard_map/ppermute | solution.py:59
  46.9 1.5 %collective-permute-start.18 = (bf16[160,768]{1,0:T(8,128)(2,1)S(1)}, bf16[160,768]{1,0:T(8,128)(2,1)S(1)}, u32[]{:S(2)}, u32[]{:S(2)}) collective-permute-start(bf16[160,768]{1,0:T(8,128)(2,1)S(1)} %get-tuple-element.80), channel_id=1, source_target_pairs={{0,5},{1,2},{2,7},{3,0},{4,1},{5,6},{6,3},{7,4},{8,13},{9,10},{10,... | collective-permute-start | bytes 737288 | tf_op jit(solution)/shard_map/ppermute | solution.py:59
  48.4 3.8 %collective-permute-done.17.refs_2_ = bf16[160,768]{1,0:T(8,128)(2,1)S(1)} collective-permute-done((bf16[160,768]{1,0:T(8,128)(2,1)S(1)}, bf16[160,768]{1,0:T(8,128)(2,1)S(1)}, u32[]{:S(2)}, u32[]{:S(2)}) %collective-permute-start.17) | collective-permute-done | bytes 245792 | tf_op jit(solution)/shard_map/ppermute | solution.py:59
  52.1 2.1 %collective-permute-done.18.refs_3_ = bf16[160,768]{1,0:T(8,128)(2,1)S(1)} collective-permute-done((bf16[160,768]{1,0:T(8,128)(2,1)S(1)}, bf16[160,768]{1,0:T(8,128)(2,1)S(1)}, u32[]{:S(2)}, u32[]{:S(2)}) %collective-permute-start.18) | collective-permute-done | bytes 245792 | tf_op jit(solution)/shard_map/ppermute | solution.py:59
  54.2 0.1 add_partners.1
  54.4 2.0 %collective-permute-start.23 = (bf16[256,384]{1,0:T(8,128)(2,1)S(1)}, bf16[256,384]{1,0:T(8,128)(2,1)S(1)}, u32[]{:S(2)}, u32[]{:S(2)}) collective-permute-start(bf16[256,384]{1,0:T(8,128)(2,1)S(1)} %get-tuple-element.82.refs_0_), channel_id=1, source_target_pairs={{0,2},{1,9},{2,10},{3,7},{4,12},{5,1},{6,4},{7,15},{8,0},{9,17},{1... | collective-permute-start | bytes 589832 | tf_op jit(solution)/shard_map/ppermute | solution.py:88
  56.4 1.2 %weights.1.matrix_ref = bf16[384,256]{1,0:T(8,128)(2,1)S(1)} custom-call(s32[1]{0:T(128)} %bitcast.where_ref, bf16[64,384]{1,0:T(8,128)(2,1)S(1)} %get-tuple-element.81.batch_ref), custom_call_target="tpu_custom_call" | custom-call | tf_op jit(solution)/shard_map/weights/pallas_call | solution.py:240
  57.6 0.3 second_product.5
  57.9 2.2 %collective-permute-done.22.refs_0_ = bf16[256,384]{1,0:T(8,128)(2,1)S(1)} collective-permute-done((bf16[256,384]{1,0:T(8,128)(2,1)S(1)}, bf16[256,384]{1,0:T(8,128)(2,1)S(1)}, u32[]{:S(2)}, u32[]{:S(2)}) %collective-permute-start.22) | collective-permute-done | bytes 196640 | tf_op jit(solution)/shard_map/ppermute | solution.py:88
  60.1 1.0 %collective-permute-start.27 = (bf16[256,384]{1,0:T(8,128)(2,1)S(1)}, bf16[256,384]{1,0:T(8,128)(2,1)S(1)}, u32[]{:S(2)}, u32[]{:S(2)}) collective-permute-start(bf16[256,384]{1,0:T(8,128)(2,1)S(1)} %collective-permute-done.22.refs_0_), channel_id=1, source_target_pairs={{0,8},{1,5},{2,0},{3,11},{4,6},{5,13},{6,14},{7,3},{8,16},{9,1},{1... | collective-permute-start | bytes 589832 | tf_op jit(solution)/shard_map/ppermute | solution.py:88
  61.0 0.5 collective-permute-done.23.refs_1_
  61.5 0.8 collective-permute-start.28
  62.3 2.3 %collective-permute-start.20 = (bf16[192,384]{1,0:T(8,128)(2,1)S(1)}, bf16[192,384]{1,0:T(8,128)(2,1)S(1)}, u32[]{:S(2)}, u32[]{:S(2)}) collective-permute-start(bf16[192,384]{1,0:T(8,128)(2,1)S(1)} %get-tuple-element.85), channel_id=1, source_target_pairs={{0,4},{1,3},{2,6},{3,1},{4,0},{5,7},{6,2},{7,5},{8,12},{9,11},{10,... | collective-permute-start | bytes 442376 | tf_op jit(solution)/shard_map/ppermute | solution.py:59
  64.6 0.4 second_product.6
  65.0 0.4 collective-permute-start.25
  65.4 0.5 collective-permute-done.19.refs_1_
  65.9 1.9 %collective-permute-done.20.refs_2_ = bf16[192,384]{1,0:T(8,128)(2,1)S(1)} collective-permute-done((bf16[192,384]{1,0:T(8,128)(2,1)S(1)}, bf16[192,384]{1,0:T(8,128)(2,1)S(1)}, u32[]{:S(2)}, u32[]{:S(2)}) %collective-permute-start.20) | collective-permute-done | bytes 147488 | tf_op jit(solution)/shard_map/ppermute | solution.py:59
  67.7 1.0 %collective-permute-start.32 = (bf16[256,384]{1,0:T(8,128)(2,1)S(1)}, bf16[256,384]{1,0:T(8,128)(2,1)S(1)}, u32[]{:S(2)}, u32[]{:S(2)}) collective-permute-start(bf16[256,384]{1,0:T(8,128)(2,1)S(1)} %collective-permute-done.27.refs_0_), channel_id=1, source_target_pairs={{0,8},{1,5},{2,0},{3,11},{4,6},{5,13},{6,14},{7,3},{8,16},{9,1},{1... | collective-permute-start | bytes 589832 | tf_op jit(solution)/shard_map/ppermute | solution.py:88
  68.7 1.2 %collective-permute-start.33 = (bf16[256,384]{1,0:T(8,128)(2,1)S(1)}, bf16[256,384]{1,0:T(8,128)(2,1)S(1)}, u32[]{:S(2)}, u32[]{:S(2)}) collective-permute-start(bf16[256,384]{1,0:T(8,128)(2,1)S(1)} %collective-permute-done.28.refs_1_), channel_id=1, source_target_pairs={{0,2},{1,9},{2,10},{3,7},{4,12},{5,1},{6,4},{7,15},{8,0},{9,17},{1... | collective-permute-start | bytes 589832 | tf_op jit(solution)/shard_map/ppermute | solution.py:88
  70.0 0.4 second_product.7
  70.3 1.9 %collective-permute-start.30 = (bf16[384,384]{1,0:T(8,128)(2,1)S(1)}, bf16[384,384]{1,0:T(8,128)(2,1)S(1)}, u32[]{:S(2)}, u32[]{:S(2)}) collective-permute-start(bf16[384,384]{1,0:T(8,128)(2,1)S(1)} %get-tuple-element.93), channel_id=1, source_target_pairs={{0,4},{1,3},{2,6},{3,1},{4,0},{5,7},{6,2},{7,5},{8,12},{9,11},{10,... | collective-permute-start | bytes 884744 | tf_op jit(solution)/shard_map/ppermute | solution.py:59
  72.3 1.5 %collective-permute-done.32.refs_0_ = bf16[256,384]{1,0:T(8,128)(2,1)S(1)} collective-permute-done((bf16[256,384]{1,0:T(8,128)(2,1)S(1)}, bf16[256,384]{1,0:T(8,128)(2,1)S(1)}, u32[]{:S(2)}, u32[]{:S(2)}) %collective-permute-start.32) | collective-permute-done | bytes 196640 | tf_op jit(solution)/shard_map/ppermute | solution.py:88
  73.7 0.7 collective-permute-done.33.refs_1_
  74.5 0.4 second_product.8
  74.9 2.6 %collective-permute-start.35 = (bf16[384,384]{1,0:T(8,128)(2,1)S(1)}, bf16[384,384]{1,0:T(8,128)(2,1)S(1)}, u32[]{:S(2)}, u32[]{:S(2)}) collective-permute-start(bf16[384,384]{1,0:T(8,128)(2,1)S(1)} %get-tuple-element.98), channel_id=1, source_target_pairs={{0,4},{1,3},{2,6},{3,1},{4,0},{5,7},{6,2},{7,5},{8,12},{9,11},{10,... | collective-permute-start | bytes 884744 | tf_op jit(solution)/shard_map/ppermute | solution.py:59
  77.4 1.1 %collective-permute-start.37 = (bf16[256,384]{1,0:T(8,128)(2,1)S(1)}, bf16[256,384]{1,0:T(8,128)(2,1)S(1)}, u32[]{:S(2)}, u32[]{:S(2)}) collective-permute-start(bf16[256,384]{1,0:T(8,128)(2,1)S(1)} %collective-permute-done.32.refs_0_), channel_id=1, source_target_pairs={{0,8},{1,5},{2,0},{3,11},{4,6},{5,13},{6,14},{7,3},{8,16},{9,1},{1... | collective-permute-start | bytes 589832 | tf_op jit(solution)/shard_map/ppermute | solution.py:88
  78.7 0.5 collective-permute-start.29
  79.2 0.1 collective-permute-start.26
  79.4 3.7 %collective-permute-done.37.refs_0_ = bf16[256,384]{1,0:T(8,128)(2,1)S(1)} collective-permute-done((bf16[256,384]{1,0:T(8,128)(2,1)S(1)}, bf16[256,384]{1,0:T(8,128)(2,1)S(1)}, u32[]{:S(2)}, u32[]{:S(2)}) %collective-permute-start.37) | collective-permute-done | bytes 196640 | tf_op jit(solution)/shard_map/ppermute | solution.py:88
  83.1 0.3 second_product.9
  83.4 0.6 collective-permute-start.31
  84.0 0.1 collective-permute-start.36
  84.1 0.6 collective-permute-start.38
  84.7 0.4 collective-permute-start.39
  85.0 0.5 collective-permute-start.40
  85.5 0.1 collective-permute-done.38.refs_17_
  85.6 3.4 %collective-permute-done.39.refs_18_ = bf16[96,384]{1,0:T(8,128)(2,1)S(1)} collective-permute-done((bf16[96,384]{1,0:T(8,128)(2,1)S(1)}, bf16[96,384]{1,0:T(8,128)(2,1)S(1)}, u32[]{:S(2)}, u32[]{:S(2)}) %collective-permute-start.39) | collective-permute-done | bytes 73760 | tf_op jit(solution)/shard_map/ppermute | solution.py:59
  89.0 2.6 %place_pairs.1 = bf16[2,12,384,128]{3,2,1,0:T(8,128)(2,1)} custom-call(s32[1]{0:T(128)} %bitcast.where_ref, s32[1,128]{1,0:T(1,128)S(1)} %copy-done, bf16[96,384]{1,0:T(8,128)(2,1)S(1)} %get-tuple-element.83.refs_0_, bf16[96,384]{1,0:T(8,128)(2,1)S(1)} %collective-permute-done.19.refs_1_, bf16[192,384]{1,0:T(8,128)(2,1)S(1)} %collective-permute-done.20.refs_2_, ...), custom_call_target="tpu_custom_call" | custom-call | tf_op jit(solution)/shard_map/place_pairs/pallas_call | solution.py:310
  (42 shorter events, 0.3 us)
Async XLA Ops:
  0.0 28.6 %copy-start.1 = (bf16[2,256,384]{2,1,0:T(8,128)(2,1)S(1)}, bf16[2,256,384]{2,1,0:T(8,128)(2,1)}, u32[]{:S(2)}) copy-start(bf16[2,256,384]{2,1,0:T(8,128)(2,1)} %refs_4_.1) | copy-start | bytes 1179652
  0.0 28.6 %copy-start.2 = (s32[8]{0:T(128)S(1)}, s32[8]{0:T(128)}, u32[]{:S(2)}) copy-start(s32[8]{0:T(128)} %starts_ref.7) | copy-start | bytes 100
  0.0 11.8 %collective-permute-start.9 = (bf16[2,256,384]{2,1,0:T(8,128)(2,1)}, bf16[2,256,384]{2,1,0:T(8,128)(2,1)S(1)}, u32[]{:S(2)}, u32[]{:S(2)}) collective-permute-start(bf16[2,256,384]{2,1,0:T(8,128)(2,1)} %refs_4_.1), channel_id=1, source_target_pairs={{0,8},{1,5},{2,0},{3,11},{4,6},{5,13},{6,14},{7,3},{8,16},{9,1},{1... | collective-permute-start | bytes 1179656 | tf_op jit(solution)/shard_map/ppermute | solution.py:88
  3.0 11.1 %collective-permute-start.10 = (bf16[2,256,384]{2,1,0:T(8,128)(2,1)}, bf16[2,256,384]{2,1,0:T(8,128)(2,1)S(1)}, u32[]{:S(2)}, u32[]{:S(2)}) collective-permute-start(bf16[2,256,384]{2,1,0:T(8,128)(2,1)} %refs_4_.1), channel_id=1, source_target_pairs={{0,2},{1,9},{2,10},{3,7},{4,12},{5,1},{6,4},{7,15},{8,0},{9,17},{1... | collective-permute-start | bytes 1179656 | tf_op jit(solution)/shard_map/ppermute | solution.py:88
  11.8 12.7 %collective-permute-start.11 = (bf16[2,256,384]{2,1,0:T(8,128)(2,1)S(1)}, bf16[2,256,384]{2,1,0:T(8,128)(2,1)S(1)}, u32[]{:S(2)}, u32[]{:S(2)}) collective-permute-start(bf16[2,256,384]{2,1,0:T(8,128)(2,1)S(1)} %collective-permute-done.9.refs_5_), channel_id=1, source_target_pairs={{0,8},{1,5},{2,0},{3,11},{4,6},{5,13},{6,14},{7,3},{8,16},{9,1},{1... | collective-permute-start | bytes 1179656 | tf_op jit(solution)/shard_map/ppermute | solution.py:88
  14.2 14.0 %collective-permute-start.12 = (bf16[2,256,384]{2,1,0:T(8,128)(2,1)S(1)}, bf16[2,256,384]{2,1,0:T(8,128)(2,1)S(1)}, u32[]{:S(2)}, u32[]{:S(2)}) collective-permute-start(bf16[2,256,384]{2,1,0:T(8,128)(2,1)S(1)} %collective-permute-done.10.refs_6_), channel_id=1, source_target_pairs={{0,2},{1,9},{2,10},{3,7},{4,12},{5,1},{6,4},{7,15},{8,0},{9,17},{1... | collective-permute-start | bytes 1179656 | tf_op jit(solution)/shard_map/ppermute | solution.py:88
  15.0 2.2 %collective-permute-start.6 = (bf16[128,768]{1,0:T(8,128)(2,1)S(1)}, bf16[128,768]{1,0:T(8,128)(2,1)S(1)}, u32[]{:S(2)}, u32[]{:S(2)}) collective-permute-start(bf16[128,768]{1,0:T(8,128)(2,1)S(1)} %get-tuple-element.69), channel_id=1, source_target_pairs={{0,1},{1,0},{2,3},{3,2},{4,5},{5,4},{6,7},{7,6},{8,9},{9,8},{10,11... | collective-permute-start | bytes 589832 | tf_op jit(solution)/shard_map/ppermute | solution.py:59
  15.0 7.9 %collective-permute-start.7 = (bf16[128,768]{1,0:T(8,128)(2,1)S(1)}, bf16[128,768]{1,0:T(8,128)(2,1)S(1)}, u32[]{:S(2)}, u32[]{:S(2)}) collective-permute-start(bf16[128,768]{1,0:T(8,128)(2,1)S(1)} %get-tuple-element.70), channel_id=1, source_target_pairs={{0,4},{1,3},{2,6},{3,1},{4,0},{5,7},{6,2},{7,5},{8,12},{9,11},{10,... | collective-permute-start | bytes 589832 | tf_op jit(solution)/shard_map/ppermute | solution.py:59
  17.0 7.5 %collective-permute-start.8 = (bf16[128,768]{1,0:T(8,128)(2,1)S(1)}, bf16[128,768]{1,0:T(8,128)(2,1)S(1)}, u32[]{:S(2)}, u32[]{:S(2)}) collective-permute-start(bf16[128,768]{1,0:T(8,128)(2,1)S(1)} %get-tuple-element.71), channel_id=1, source_target_pairs={{0,3},{1,4},{2,1},{3,6},{4,7},{5,0},{6,5},{7,2},{8,11},{9,12},{10,... | collective-permute-start | bytes 589832 | tf_op jit(solution)/shard_map/ppermute | solution.py:59
  24.5 9.2 %collective-permute-start.13 = (bf16[2,256,384]{2,1,0:T(8,128)(2,1)S(1)}, bf16[2,256,384]{2,1,0:T(8,128)(2,1)S(1)}, u32[]{:S(2)}, u32[]{:S(2)}) collective-permute-start(bf16[2,256,384]{2,1,0:T(8,128)(2,1)S(1)} %collective-permute-done.11.refs_5_), channel_id=1, source_target_pairs={{0,8},{1,5},{2,0},{3,11},{4,6},{5,13},{6,14},{7,3},{8,16},{9,1},{1... | collective-permute-start | bytes 1179656 | tf_op jit(solution)/shard_map/ppermute | solution.py:88
  24.5 5.6 %collective-permute-start.3 = (bf16[128,512]{1,0:T(8,128)(2,1)S(1)}, bf16[128,512]{1,0:T(8,128)(2,1)S(1)}, u32[]{:S(2)}, u32[]{:S(2)}) collective-permute-start(bf16[128,512]{1,0:T(8,128)(2,1)S(1)} %get-tuple-element.63), channel_id=1, source_target_pairs={{0,1},{1,0},{2,3},{3,2},{4,5},{5,4},{6,7},{7,6},{8,9},{9,8},{10,11... | collective-permute-start | bytes 393224 | tf_op jit(solution)/shard_map/ppermute | solution.py:59
  26.8 6.4 %collective-permute-start.4 = (bf16[128,512]{1,0:T(8,128)(2,1)S(1)}, bf16[128,512]{1,0:T(8,128)(2,1)S(1)}, u32[]{:S(2)}, u32[]{:S(2)}) collective-permute-start(bf16[128,512]{1,0:T(8,128)(2,1)S(1)} %get-tuple-element.65), channel_id=1, source_target_pairs={{0,4},{1,3},{2,6},{3,1},{4,0},{5,7},{6,2},{7,5},{8,12},{9,11},{10,... | collective-permute-start | bytes 393224 | tf_op jit(solution)/shard_map/ppermute | solution.py:59
  27.1 6.4 %collective-permute-start.5 = (bf16[128,512]{1,0:T(8,128)(2,1)S(1)}, bf16[128,512]{1,0:T(8,128)(2,1)S(1)}, u32[]{:S(2)}, u32[]{:S(2)}) collective-permute-start(bf16[128,512]{1,0:T(8,128)(2,1)S(1)} %get-tuple-element.67), channel_id=1, source_target_pairs={{0,3},{1,4},{2,1},{3,6},{4,7},{5,0},{6,5},{7,2},{8,11},{9,12},{10,... | collective-permute-start | bytes 393224 | tf_op jit(solution)/shard_map/ppermute | solution.py:59
  28.1 13.2 %collective-permute-start.14 = (bf16[2,256,384]{2,1,0:T(8,128)(2,1)S(1)}, bf16[2,256,384]{2,1,0:T(8,128)(2,1)S(1)}, u32[]{:S(2)}, u32[]{:S(2)}) collective-permute-start(bf16[2,256,384]{2,1,0:T(8,128)(2,1)S(1)} %collective-permute-done.12.refs_6_), channel_id=1, source_target_pairs={{0,2},{1,9},{2,10},{3,7},{4,12},{5,1},{6,4},{7,15},{8,0},{9,17},{1... | collective-permute-start | bytes 1179656 | tf_op jit(solution)/shard_map/ppermute | solution.py:88
  30.1 5.6 %collective-permute-start = (bf16[128,768]{1,0:T(8,128)(2,1)S(1)}, bf16[128,768]{1,0:T(8,128)(2,1)S(1)}, u32[]{:S(2)}, u32[]{:S(2)}) collective-permute-start(bf16[128,768]{1,0:T(8,128)(2,1)S(1)} %get-tuple-element.56), channel_id=1, source_target_pairs={{0,1},{1,0},{2,3},{3,2},{4,5},{5,4},{6,7},{7,6},{8,9},{9,8},{10,11... | collective-permute-start | bytes 589832 | tf_op jit(solution)/shard_map/ppermute | solution.py:59
  33.2 7.8 %collective-permute-start.1 = (bf16[128,768]{1,0:T(8,128)(2,1)S(1)}, bf16[128,768]{1,0:T(8,128)(2,1)S(1)}, u32[]{:S(2)}, u32[]{:S(2)}) collective-permute-start(bf16[128,768]{1,0:T(8,128)(2,1)S(1)} %get-tuple-element.58), channel_id=1, source_target_pairs={{0,4},{1,3},{2,6},{3,1},{4,0},{5,7},{6,2},{7,5},{8,12},{9,11},{10,... | collective-permute-start | bytes 589832 | tf_op jit(solution)/shard_map/ppermute | solution.py:59
  33.4 7.9 %collective-permute-start.2 = (bf16[128,768]{1,0:T(8,128)(2,1)S(1)}, bf16[128,768]{1,0:T(8,128)(2,1)S(1)}, u32[]{:S(2)}, u32[]{:S(2)}) collective-permute-start(bf16[128,768]{1,0:T(8,128)(2,1)S(1)} %get-tuple-element.60), channel_id=1, source_target_pairs={{0,3},{1,4},{2,1},{3,6},{4,7},{5,0},{6,5},{7,2},{8,11},{9,12},{10,... | collective-permute-start | bytes 589832 | tf_op jit(solution)/shard_map/ppermute | solution.py:59
  33.7 11.0 %collective-permute-start.15 = (bf16[2,256,384]{2,1,0:T(8,128)(2,1)S(1)}, bf16[2,256,384]{2,1,0:T(8,128)(2,1)S(1)}, u32[]{:S(2)}, u32[]{:S(2)}) collective-permute-start(bf16[2,256,384]{2,1,0:T(8,128)(2,1)S(1)} %collective-permute-done.13.refs_5_), channel_id=1, source_target_pairs={{0,8},{1,5},{2,0},{3,11},{4,6},{5,13},{6,14},{7,3},{8,16},{9,1},{1... | collective-permute-start | bytes 1179656 | tf_op jit(solution)/shard_map/ppermute | solution.py:88
  45.8 8.4 %collective-permute-start.16 = (f32[160,768]{1,0:T(8,128)S(1)}, f32[160,768]{1,0:T(8,128)S(1)}, u32[]{:S(2)}, u32[]{:S(2)}) collective-permute-start(f32[160,768]{1,0:T(8,128)S(1)} %get-tuple-element.78), channel_id=1, source_target_pairs={{0,1},{1,0},{2,3},{3,2},{4,5},{5,4},{6,7},{7,6},{8,9},{9,8},{10,11... | collective-permute-start | bytes 1474568 | tf_op jit(solution)/shard_map/ppermute | solution.py:59
  45.8 6.3 %collective-permute-start.17 = (bf16[160,768]{1,0:T(8,128)(2,1)S(1)}, bf16[160,768]{1,0:T(8,128)(2,1)S(1)}, u32[]{:S(2)}, u32[]{:S(2)}) collective-permute-start(bf16[160,768]{1,0:T(8,128)(2,1)S(1)} %get-tuple-element.79), channel_id=1, source_target_pairs={{0,4},{1,3},{2,6},{3,1},{4,0},{5,7},{6,2},{7,5},{8,12},{9,11},{10,... | collective-permute-start | bytes 737288 | tf_op jit(solution)/shard_map/ppermute | solution.py:59
  46.9 7.3 %collective-permute-start.18 = (bf16[160,768]{1,0:T(8,128)(2,1)S(1)}, bf16[160,768]{1,0:T(8,128)(2,1)S(1)}, u32[]{:S(2)}, u32[]{:S(2)}) collective-permute-start(bf16[160,768]{1,0:T(8,128)(2,1)S(1)} %get-tuple-element.80), channel_id=1, source_target_pairs={{0,5},{1,2},{2,7},{3,0},{4,1},{5,6},{6,3},{7,4},{8,13},{9,10},{10,... | collective-permute-start | bytes 737288 | tf_op jit(solution)/shard_map/ppermute | solution.py:59
  54.3 5.7 %collective-permute-start.22 = (bf16[256,384]{1,0:T(8,128)(2,1)S(1)}, bf16[256,384]{1,0:T(8,128)(2,1)S(1)}, u32[]{:S(2)}, u32[]{:S(2)}) collective-permute-start(bf16[256,384]{1,0:T(8,128)(2,1)S(1)} %get-tuple-element.82.refs_0_), channel_id=1, source_target_pairs={{0,8},{1,5},{2,0},{3,11},{4,6},{5,13},{6,14},{7,3},{8,16},{9,1},{1... | collective-permute-start | bytes 589832 | tf_op jit(solution)/shard_map/ppermute | solution.py:88
  54.4 7.2 %collective-permute-start.23 = (bf16[256,384]{1,0:T(8,128)(2,1)S(1)}, bf16[256,384]{1,0:T(8,128)(2,1)S(1)}, u32[]{:S(2)}, u32[]{:S(2)}) collective-permute-start(bf16[256,384]{1,0:T(8,128)(2,1)S(1)} %get-tuple-element.82.refs_0_), channel_id=1, source_target_pairs={{0,2},{1,9},{2,10},{3,7},{4,12},{5,1},{6,4},{7,15},{8,0},{9,17},{1... | collective-permute-start | bytes 589832 | tf_op jit(solution)/shard_map/ppermute | solution.py:88
  60.1 7.7 %collective-permute-start.27 = (bf16[256,384]{1,0:T(8,128)(2,1)S(1)}, bf16[256,384]{1,0:T(8,128)(2,1)S(1)}, u32[]{:S(2)}, u32[]{:S(2)}) collective-permute-start(bf16[256,384]{1,0:T(8,128)(2,1)S(1)} %collective-permute-done.22.refs_0_), channel_id=1, source_target_pairs={{0,8},{1,5},{2,0},{3,11},{4,6},{5,13},{6,14},{7,3},{8,16},{9,1},{1... | collective-permute-start | bytes 589832 | tf_op jit(solution)/shard_map/ppermute | solution.py:88
  61.5 7.2 %collective-permute-start.28 = (bf16[256,384]{1,0:T(8,128)(2,1)S(1)}, bf16[256,384]{1,0:T(8,128)(2,1)S(1)}, u32[]{:S(2)}, u32[]{:S(2)}) collective-permute-start(bf16[256,384]{1,0:T(8,128)(2,1)S(1)} %collective-permute-done.23.refs_1_), channel_id=1, source_target_pairs={{0,2},{1,9},{2,10},{3,7},{4,12},{5,1},{6,4},{7,15},{8,0},{9,17},{1... | collective-permute-start | bytes 589832 | tf_op jit(solution)/shard_map/ppermute | solution.py:88
  62.3 5.4 %collective-permute-start.20 = (bf16[192,384]{1,0:T(8,128)(2,1)S(1)}, bf16[192,384]{1,0:T(8,128)(2,1)S(1)}, u32[]{:S(2)}, u32[]{:S(2)}) collective-permute-start(bf16[192,384]{1,0:T(8,128)(2,1)S(1)} %get-tuple-element.85), channel_id=1, source_target_pairs={{0,4},{1,3},{2,6},{3,1},{4,0},{5,7},{6,2},{7,5},{8,12},{9,11},{10,... | collective-permute-start | bytes 442376 | tf_op jit(solution)/shard_map/ppermute | solution.py:59
  64.6 24.4 %copy-start = (s32[1,128]{1,0:T(1,128)S(1)}, s32[1,128]{1,0:T(1,128)}, u32[]{:S(2)}) copy-start(s32[1,128]{1,0:T(1,128)} %pair_ref.1) | copy-start | bytes 1540
  64.6 1.3 %collective-permute-start.19 = (bf16[96,384]{1,0:T(8,128)(2,1)S(1)}, bf16[96,384]{1,0:T(8,128)(2,1)S(1)}, u32[]{:S(2)}, u32[]{:S(2)}) collective-permute-start(bf16[96,384]{1,0:T(8,128)(2,1)S(1)} %get-tuple-element.84), channel_id=1, source_target_pairs={{0,1},{1,0},{2,3},{3,2},{4,5},{5,4},{6,7},{7,6},{8,9},{9,8},{10,11... | collective-permute-start | bytes 221192 | tf_op jit(solution)/shard_map/ppermute | solution.py:59
  65.0 12.4 %collective-permute-start.25 = (bf16[384,384]{1,0:T(8,128)(2,1)S(1)}, bf16[384,384]{1,0:T(8,128)(2,1)S(1)}, u32[]{:S(2)}, u32[]{:S(2)}) collective-permute-start(bf16[384,384]{1,0:T(8,128)(2,1)S(1)} %get-tuple-element.88), channel_id=1, source_target_pairs={{0,4},{1,3},{2,6},{3,1},{4,0},{5,7},{6,2},{7,5},{8,12},{9,11},{10,... | collective-permute-start | bytes 884744 | tf_op jit(solution)/shard_map/ppermute | solution.py:59
  67.7 6.0 %collective-permute-start.32 = (bf16[256,384]{1,0:T(8,128)(2,1)S(1)}, bf16[256,384]{1,0:T(8,128)(2,1)S(1)}, u32[]{:S(2)}, u32[]{:S(2)}) collective-permute-start(bf16[256,384]{1,0:T(8,128)(2,1)S(1)} %collective-permute-done.27.refs_0_), channel_id=1, source_target_pairs={{0,8},{1,5},{2,0},{3,11},{4,6},{5,13},{6,14},{7,3},{8,16},{9,1},{1... | collective-permute-start | bytes 589832 | tf_op jit(solution)/shard_map/ppermute | solution.py:88
  68.7 5.8 %collective-permute-start.33 = (bf16[256,384]{1,0:T(8,128)(2,1)S(1)}, bf16[256,384]{1,0:T(8,128)(2,1)S(1)}, u32[]{:S(2)}, u32[]{:S(2)}) collective-permute-start(bf16[256,384]{1,0:T(8,128)(2,1)S(1)} %collective-permute-done.28.refs_1_), channel_id=1, source_target_pairs={{0,2},{1,9},{2,10},{3,7},{4,12},{5,1},{6,4},{7,15},{8,0},{9,17},{1... | collective-permute-start | bytes 589832 | tf_op jit(solution)/shard_map/ppermute | solution.py:88
  70.0 7.5 %collective-permute-start.24 = (bf16[192,384]{1,0:T(8,128)(2,1)S(1)}, bf16[192,384]{1,0:T(8,128)(2,1)S(1)}, u32[]{:S(2)}, u32[]{:S(2)}) collective-permute-start(bf16[192,384]{1,0:T(8,128)(2,1)S(1)} %get-tuple-element.87), channel_id=1, source_target_pairs={{0,1},{1,0},{2,3},{3,2},{4,5},{5,4},{6,7},{7,6},{8,9},{9,8},{10,11... | collective-permute-start | bytes 442376 | tf_op jit(solution)/shard_map/ppermute | solution.py:59
  70.3 8.9 %collective-permute-start.30 = (bf16[384,384]{1,0:T(8,128)(2,1)S(1)}, bf16[384,384]{1,0:T(8,128)(2,1)S(1)}, u32[]{:S(2)}, u32[]{:S(2)}) collective-permute-start(bf16[384,384]{1,0:T(8,128)(2,1)S(1)} %get-tuple-element.93), channel_id=1, source_target_pairs={{0,4},{1,3},{2,6},{3,1},{4,0},{5,7},{6,2},{7,5},{8,12},{9,11},{10,... | collective-permute-start | bytes 884744 | tf_op jit(solution)/shard_map/ppermute | solution.py:59
  74.9 8.5 %collective-permute-start.35 = (bf16[384,384]{1,0:T(8,128)(2,1)S(1)}, bf16[384,384]{1,0:T(8,128)(2,1)S(1)}, u32[]{:S(2)}, u32[]{:S(2)}) collective-permute-start(bf16[384,384]{1,0:T(8,128)(2,1)S(1)} %get-tuple-element.98), channel_id=1, source_target_pairs={{0,4},{1,3},{2,6},{3,1},{4,0},{5,7},{6,2},{7,5},{8,12},{9,11},{10,... | collective-permute-start | bytes 884744 | tf_op jit(solution)/shard_map/ppermute | solution.py:59
  77.4 5.7 %collective-permute-start.37 = (bf16[256,384]{1,0:T(8,128)(2,1)S(1)}, bf16[256,384]{1,0:T(8,128)(2,1)S(1)}, u32[]{:S(2)}, u32[]{:S(2)}) collective-permute-start(bf16[256,384]{1,0:T(8,128)(2,1)S(1)} %collective-permute-done.32.refs_0_), channel_id=1, source_target_pairs={{0,8},{1,5},{2,0},{3,11},{4,6},{5,13},{6,14},{7,3},{8,16},{9,1},{1... | collective-permute-start | bytes 589832 | tf_op jit(solution)/shard_map/ppermute | solution.py:88
  78.6 5.4 %collective-permute-start.21 = (bf16[96,384]{1,0:T(8,128)(2,1)S(1)}, bf16[96,384]{1,0:T(8,128)(2,1)S(1)}, u32[]{:S(2)}, u32[]{:S(2)}) collective-permute-start(bf16[96,384]{1,0:T(8,128)(2,1)S(1)} %slice.24), channel_id=1, source_target_pairs={{0,1},{1,0},{2,3},{3,2},{4,5},{5,4},{6,7},{7,6},{8,9},{9,8},{10,11... | collective-permute-start | bytes 221192 | tf_op jit(solution)/shard_map/ppermute | solution.py:59
  78.7 5.4 %collective-permute-start.29 = (bf16[192,384]{1,0:T(8,128)(2,1)S(1)}, bf16[192,384]{1,0:T(8,128)(2,1)S(1)}, u32[]{:S(2)}, u32[]{:S(2)}) collective-permute-start(bf16[192,384]{1,0:T(8,128)(2,1)S(1)} %get-tuple-element.92), channel_id=1, source_target_pairs={{0,1},{1,0},{2,3},{3,2},{4,5},{5,4},{6,7},{7,6},{8,9},{9,8},{10,11... | collective-permute-start | bytes 442376 | tf_op jit(solution)/shard_map/ppermute | solution.py:59
  79.2 5.5 %collective-permute-start.26 = (bf16[192,384]{1,0:T(8,128)(2,1)S(1)}, bf16[192,384]{1,0:T(8,128)(2,1)S(1)}, u32[]{:S(2)}, u32[]{:S(2)}) collective-permute-start(bf16[192,384]{1,0:T(8,128)(2,1)S(1)} %slice.25), channel_id=1, source_target_pairs={{0,1},{1,0},{2,3},{3,2},{4,5},{5,4},{6,7},{7,6},{8,9},{9,8},{10,11... | collective-permute-start | bytes 442376 | tf_op jit(solution)/shard_map/ppermute | solution.py:59
  83.1 1.9 %collective-permute-start.34 = (bf16[192,384]{1,0:T(8,128)(2,1)S(1)}, bf16[192,384]{1,0:T(8,128)(2,1)S(1)}, u32[]{:S(2)}, u32[]{:S(2)}) collective-permute-start(bf16[192,384]{1,0:T(8,128)(2,1)S(1)} %get-tuple-element.97), channel_id=1, source_target_pairs={{0,1},{1,0},{2,3},{3,2},{4,5},{5,4},{6,7},{7,6},{8,9},{9,8},{10,11... | collective-permute-start | bytes 442376 | tf_op jit(solution)/shard_map/ppermute | solution.py:59
  83.4 2.1 %collective-permute-start.31 = (bf16[192,384]{1,0:T(8,128)(2,1)S(1)}, bf16[192,384]{1,0:T(8,128)(2,1)S(1)}, u32[]{:S(2)}, u32[]{:S(2)}) collective-permute-start(bf16[192,384]{1,0:T(8,128)(2,1)S(1)} %slice.26), channel_id=1, source_target_pairs={{0,1},{1,0},{2,3},{3,2},{4,5},{5,4},{6,7},{7,6},{8,9},{9,8},{10,11... | collective-permute-start | bytes 442376 | tf_op jit(solution)/shard_map/ppermute | solution.py:59
  84.0 5.0 %collective-permute-start.36 = (bf16[192,384]{1,0:T(8,128)(2,1)S(1)}, bf16[192,384]{1,0:T(8,128)(2,1)S(1)}, u32[]{:S(2)}, u32[]{:S(2)}) collective-permute-start(bf16[192,384]{1,0:T(8,128)(2,1)S(1)} %slice.27), channel_id=1, source_target_pairs={{0,1},{1,0},{2,3},{3,2},{4,5},{5,4},{6,7},{7,6},{8,9},{9,8},{10,11... | collective-permute-start | bytes 442376 | tf_op jit(solution)/shard_map/ppermute | solution.py:59
  84.1 1.5 %collective-permute-start.38 = (bf16[96,384]{1,0:T(8,128)(2,1)S(1)}, bf16[96,384]{1,0:T(8,128)(2,1)S(1)}, u32[]{:S(2)}, u32[]{:S(2)}) collective-permute-start(bf16[96,384]{1,0:T(8,128)(2,1)S(1)} %get-tuple-element.101), channel_id=1, source_target_pairs={{0,1},{1,0},{2,3},{3,2},{4,5},{5,4},{6,7},{7,6},{8,9},{9,8},{10,11... | collective-permute-start | bytes 221192 | tf_op jit(solution)/shard_map/ppermute | solution.py:59
  84.7 4.4 %collective-permute-start.39 = (bf16[96,384]{1,0:T(8,128)(2,1)S(1)}, bf16[96,384]{1,0:T(8,128)(2,1)S(1)}, u32[]{:S(2)}, u32[]{:S(2)}) collective-permute-start(bf16[96,384]{1,0:T(8,128)(2,1)S(1)} %get-tuple-element.104), channel_id=1, source_target_pairs={{0,4},{1,3},{2,6},{3,1},{4,0},{5,7},{6,2},{7,5},{8,12},{9,11},{10,... | collective-permute-start | bytes 221192 | tf_op jit(solution)/shard_map/ppermute | solution.py:59
  85.0 4.0 %collective-permute-start.40 = (bf16[96,384]{1,0:T(8,128)(2,1)S(1)}, bf16[96,384]{1,0:T(8,128)(2,1)S(1)}, u32[]{:S(2)}, u32[]{:S(2)}) collective-permute-start(bf16[96,384]{1,0:T(8,128)(2,1)S(1)} %get-tuple-element.103), channel_id=1, source_target_pairs={{0,5},{1,2},{2,7},{3,0},{4,1},{5,6},{6,3},{7,4},{8,13},{9,10},{10,... | collective-permute-start | bytes 221192 | tf_op jit(solution)/shard_map/ppermute | solution.py:59

commit v6 on v5

--- a/solution.py
+++ b/solution.py
@@ -102,58 +102,66 @@
     return pltpu.with_memory_space_constraint(array, pltpu.HBM)
 
 
-def share_integrals(grid, where, integrals, depth, groups):
-    rows = integrals.shape[0]
-
-    def body(where_ref, ints_ref, *refs):
+def share_integrals(grid, where, batch_starts, moved_to, integrals, depth, groups):
+    rows, batch_rows = integrals.shape[0], batch_starts.shape[0] * SHW
+
+    def body(where_ref, starts_ref, ints_ref, *refs):
         outs, moved = refs[:-1], refs[-1]
+        me = where_ref[0]
         copies = []
-        for k, helper in enumerate(grid.helpers(where_ref[0])):
+        for k, helper in enumerate(grid.helpers(me)):
             for number, group in enumerate(groups):
                 for place, offset in enumerate(group):
                     start = pl.multiple_of(grid.source(helper, offset) * depth, depth)
-                    out = outs[4 * number + k].at[:, pl.ds(place * depth, depth)]
+                    out = outs[4 * number + k].at[pl.ds(0, rows), pl.ds(place * depth, depth)]
                     copies.append(
                         pltpu.make_async_copy(ints_ref.at[:, pl.ds(start, depth)], out, moved.at[len(copies)])
                     )
         for copy in copies:
             copy.start()
-        for copy in copies:
-            copy.wait()
-
-    outs = pl.pallas_call(
-        body,
-        out_shape=[jax.ShapeDtypeStruct((rows, len(group) * depth), BF16) for group in groups for _ in range(4)],
-        in_specs=[pl.BlockSpec(memory_space=pltpu.SMEM), pl.BlockSpec(memory_space=pl.ANY)],
-        out_specs=vmem(4 * len(groups)),
-        scratch_shapes=[pltpu.SemaphoreType.DMA((4 * grid.ring,))],
-        compiler_params=PARAMS,
-        name="share_integrals",
-    )(where, in_hbm(integrals))
-    return [outs[4 * number:4 * number + 4] for number in range(len(groups))]
-
-
-def first_product(grid, where, offsets, ints, begin, batch_starts, moved_to, total, blocks, last):
-    parts, depth, width = blocks[0].shape
-    rows, batch_rows = ints[0].shape[0], batch_starts.shape[0] * SHW
-    high = len(ints) * rows + batch_rows
-    begins = total is None
-
-    def body(where_ref, starts_ref, *refs):
-        ints_refs, refs = refs[: len(ints)], refs[len(ints):]
-        total_ref, refs = (None, refs) if begins else (refs[0], refs[1:])
-        block_refs, outs = refs[: len(blocks)], refs[len(blocks):]
-        sum_ref = outs[-1]
-        me = where_ref[0]
         row = lax.broadcasted_iota(jnp.int32, (batch_rows, depth), 0)
         wanted = row
         for shell in range(batch_starts.shape[0]):
             wanted = jnp.where(row >= shell * SHW, row + (moved_to(starts_ref[shell]) - shell * SHW), wanted)
-        for number, (offset, ref) in enumerate(zip(offsets, block_refs)):
+        for number, group in enumerate(groups):
+            for place, offset in enumerate(group):
+                position = lax.broadcasted_iota(jnp.int32, (batch_rows, depth), 1) + grid.source(me, offset) * depth
+                picks = (wanted == position).astype(F32).astype(BF16)
+                outs[4 * number][rows:, place * depth:(place + 1) * depth] = picks
+        for copy in copies:
+            copy.wait()
+
+    outs = pl.pallas_call(
+        body,
+        out_shape=[
+            jax.ShapeDtypeStruct((rows + batch_rows * (k == 0), len(group) * depth), BF16)
+            for group in groups
+            for k in range(4)
+        ],
+        in_specs=[pl.BlockSpec(memory_space=pltpu.SMEM)] * 2 + [pl.BlockSpec(memory_space=pl.ANY)],
+        out_specs=vmem(4 * len(groups)),
+        scratch_shapes=[pltpu.SemaphoreType.DMA((4 * grid.ring,))],
+        compiler_params=PARAMS,
+        name="share_integrals",
+    )(where, batch_starts, in_hbm(integrals))
+    return [outs[4 * number:4 * number + 4] for number in range(len(groups))]
+
+
+def first_product(ints, begin, total, blocks, last):
+    parts, depth, width = blocks[0].shape
+    rows = ints[1].shape[0]
+    each = ints[0].shape[0]
+    high = each + 3 * rows
+    begins = total is None
+
+    def body(*refs):
+        ints_refs, refs = refs[:4], refs[4:]
+        total_ref, refs = (None, refs) if begins else (refs[0], refs[1:])
+        block_refs, outs = refs[: len(blocks)], refs[len(blocks):]
+        sum_ref = outs[-1]
+        for number, ref in enumerate(block_refs):
             columns = pl.ds((begin + number) * depth, depth)
-            position = lax.broadcasted_iota(jnp.int32, (batch_rows, depth), 1) + grid.source(me, offset) * depth
-            picks = (wanted == position).astype(F32).astype(BF16)
-            left = jnp.concatenate([ints_ref[:, columns] for ints_ref in ints_refs] + [picks], axis=0)
+            left = jnp.concatenate([ints_ref[:, columns] for ints_ref in ints_refs], axis=0)
             for part in range(parts):
                 term = jnp.dot(left, ref[part], preferred_element_type=F32)
                 lanes = pl.ds(part * width, width)
@@ -165,17 +173,18 @@
                     sum_ref[:, lanes] = total_ref[:, lanes] + term
         if last:
             for k, out in enumerate(outs[:-1]):
-                out[:rows, :] = sum_ref[k * rows:(k + 1) * rows, :].astype(out.dtype)
-                out[rows:, :] = sum_ref[len(ints) * rows:, :].astype(out.dtype)
+                start = 0 if k == 0 else each + (k - 1) * rows
+                out[:rows, :] = sum_ref[start:start + rows, :].astype(out.dtype)
+                out[rows:, :] = sum_ref[rows:each, :].astype(out.dtype)
 
     totals = [] if begins else [total]
     whole = jax.ShapeDtypeStruct((high, parts * width), F32)
     kinds = (F32, F32, BF16, BF16)
-    shapes = [jax.ShapeDtypeStruct((rows + batch_rows, parts * width), kind) for kind in kinds] if last else [whole]
+    shapes = [jax.ShapeDtypeStruct((each, parts * width), kind) for kind in kinds] if last else [whole]
     return pl.pallas_call(
         body,
         out_shape=shapes,
-        in_specs=[pl.BlockSpec(memory_space=pltpu.SMEM)] * 2 + vmem(len(ints) + len(totals) + len(blocks)),
+        in_specs=vmem(4 + len(totals) + len(blocks)),
         out_specs=vmem(len(shapes)),
         scratch_shapes=[pltpu.VMEM(whole.shape, F32)] if last else [],
         compiler_params=PARAMS,
@@ -183,7 +192,7 @@
             flops=10 * high * depth * width * parts * len(blocks), bytes_accessed=0, transcendentals=0
         ),
         name="first_product",
-    )(where, batch_starts, *ints, *totals, *blocks)
+    )(*ints, *totals, *blocks)
 
 
 def add_partners(sums, rows, width):
@@ -270,13 +279,39 @@
     )(matrix, *blocks)
 
 
-def place_pairs(grid, where, groups, pair_row, pieces, share):
+def pair_places(grid, where, groups, pair_row, slots):
+    pairs = pair_row.shape[1]
+
+    def body(where_ref, pair_ref, out_ref):
+        row = lax.broadcasted_iota(jnp.int32, (pairs, pairs), 0)
+        lane = lax.broadcasted_iota(jnp.int32, (pairs, pairs), 1)
+        helpers = grid.helpers(where_ref[0])
+        sources = [grid.source(helper, offset) for group in groups for helper in helpers for offset in group]
+        order = row
+        for number, source in enumerate(sources):
+            order = jnp.where(row >= number * slots, row + (source - number) * slots, order)
+        ordered = (order == lane).astype(F32).astype(BF16)
+        paired = (pair_ref[...] == row).astype(F32).astype(BF16)
+        place = lax.dot_general(ordered, paired, (((1,), (1,)), ((), ())), preferred_element_type=F32)
+        out_ref[...] = place.astype(BF16)
+
+    return pl.pallas_call(
+        body,
+        out_shape=jax.ShapeDtypeStruct((pairs, pairs), BF16),
+        in_specs=[pl.BlockSpec(memory_space=pltpu.SMEM)] + vmem(1),
+        out_specs=pl.BlockSpec(memory_space=pltpu.VMEM),
+        compiler_params=PARAMS,
+        name="pair_places",
+    )(where, pair_row)
+
+
+def place_pairs(places, groups, pieces, share):
     width = pieces[0].shape[1]
-    pairs = pair_row.shape[1]
+    pairs = places.shape[0]
     each = 2 * share
-    slots = pairs // (4 * grid.ring)
-
-    def body(where_ref, pair_ref, *refs):
+    slots = pairs // sum(4 * len(group) for group in groups)
+
+    def body(place_ref, *refs):
         piece_refs, (out_ref, held, ready, leaves) = refs[: len(pieces)], refs[-4:]
         start = 0
         for number, ref in enumerate(piece_refs):
@@ -284,16 +319,7 @@
             for tile in range(width // LANES):
                 held[tile, start:start + rows, :] = ref[:rows, tile * LANES:(tile + 1) * LANES].astype(F32)
             start += rows
-        row = lax.broadcasted_iota(jnp.int32, (pairs, pairs), 0)
-        lane = lax.broadcasted_iota(jnp.int32, (pairs, pairs), 1)
-        helpers = grid.helpers(where_ref[0])
-        sources = [grid.source(helper, offset) for group in groups for helper in helpers for offset in group]
-        order = lax.rem(row, slots)
-        for number, source in enumerate(sources):
-            order += jnp.where(lax.div(row, slots) == number, source * slots, 0)
-        ordered = (order == lane).astype(F32).astype(BF16)
-        paired = (pair_ref[...] == row).astype(F32).astype(BF16)
-        place = lax.dot_general(ordered, paired, (((1,), (1,)), ((), ())), preferred_element_type=F32).astype(BF16)
+        place = place_ref[...]
         copies = []
         for number in range(each):
             for tile in range(width // LANES):
@@ -310,7 +336,7 @@
     return pl.pallas_call(
         body,
         out_shape=jax.ShapeDtypeStruct((2, share, width, pairs), BF16),
-        in_specs=[pl.BlockSpec(memory_space=pltpu.SMEM)] + vmem(1 + len(pieces)),
+        in_specs=vmem(1 + len(pieces)),
         out_specs=pl.BlockSpec(memory_space=pl.ANY),
         scratch_shapes=[
             pltpu.VMEM((width // LANES, pairs * each, LANES), F32),
@@ -319,7 +345,7 @@
         ],
         compiler_params=PARAMS,
         name="place_pairs",
-    )(where, pair_row, *pieces)
+    )(places, *pieces)
 
 
 def on_device(n_coef, n_pair, integrals, coefficients, shell_starts, pair_ids):
@@ -346,7 +372,7 @@
     reach = grid.nz
     groups = [[0, -1, 1]] + [[-step, step] for step in range(2, reach)]
     groups[-1].append(-reach)
-    shared = share_integrals(grid, where, flat_ints, depth, groups)
+    shared = share_integrals(grid, where, shell_starts, moved_to, flat_ints, depth, groups)
     ints = []
     result = [None]
 
@@ -364,20 +390,25 @@
         blocks = [held[offset] for offset in offsets]
         number = [offsets[-1] in group for group in groups].index(True)
         begin = groups[number].index(offsets[0])
-        result = first_product(grid, where, offsets, ints[number], begin, shell_starts, moved_to, result[0], blocks, last)
+        result = first_product(ints[number], begin, result[0], blocks, last)
         return ints[-1]
 
     gather_ring(grid, coefficients, multiply)
     kept, *leaving = result
     half_first, batch = add_partners([kept, *grid.exchange(leaving, grid.helped)], rows, occupied)
     matrix = weights(grid, where, batch, slots, share)
+    in_order = [[0, -1, 1]] + [[-step, step] for step in range(2, grid.nz)] + [[-grid.nz]]
+    places = pair_places(grid, where, in_order, pair_ids, slots)
     pieces, groups = [], []
     before = []
 
     def transform(held, group):
+        if group == [0]:
+            return [matrix, places]
+        group = [0, -1, 1] if group == [-1, 1] else group
         kept, aside, across = second_product(matrix, [held[offset] for offset in group])
         half = kept.shape[0]
-        if group == [-grid.nz]:
+        if group == [-grid.nz] or group == [1 - grid.nz, grid.nz - 1]:
             arrived = [kept, *grid.exchange([aside, across[:half], across[half:]], grid.helped)]
         else:
             across = grid.send(across, grid.opposite)
@@ -386,10 +417,12 @@
         groups.append(group)
         nonlocal before
         before, ready = arrived, before
-        return [[kept,*ready[:3]],[kept,*ready[:3]],[kept,*ready[:3]]][len(groups) - 1] if len(groups) < 4 else []
+        gates = [[kept,*ready[:3]],[kept,*ready[:2]]]
+        return gates[len(groups) - 1] if len(groups) <= len(gates) else []
 
     gather_ring(grid, half_first, transform)
-    return place_pairs(grid, where, groups, pair_ids, pieces, share)
+    assert groups == in_order
+    return place_pairs(places, groups, pieces, share)
 
 
 def solution(mesh):

time: 91.9 us -> 88.4 us (0.962)
  waiting for transfers between devices: 44.9 us -> 40.6 us
  starting transfers between devices: 33.8 us -> 35.7 us
  Pallas kernels: 12.6 us -> 11.1 us
    ppermute x14, waiting for transfers between devices: 17.7 us -> 15.3 us  [gather_ring(): held[way * step] = lax.ppermute(block, 'pair', around[way])]
    ppermute x27 -> x24, waiting for transfers between devices: 27.3 us -> 25.3 us  [send(): lax.ppermute(block, 'pair', [(device, int(target(device))) for device in...]
    ppermute x27 -> x24, starting transfers between devices: 19.3 us -> 20.5 us  [send(): lax.ppermute(block, 'pair', [(device, int(target(device))) for device in...]
    pallas_call x5 -> x6, Pallas kernels: 7.06 us -> 5.99 us  [the longest x4 2.99 us: first_product(): pl.pallas_call(body, out_shape=shapes, in_specs=vmem(4 + len(totals) + le...]
  transfers between devices with their start and end apart: 41 -> 38, of which waited for: 18 -> 18; matrix products, arithmetic and copies ran while one was open for 0% -> 0% of each run, Pallas kernels for 10% -> 9%
where the time goes in v6:
time: 88.4 us; the launch traced here: 88.2 us
  waiting for transfers between devices  40.6 us (46%)
  starting transfers between devices  35.7 us (40%)
  Pallas kernels  11.1 us (13%)
    ppermute x24, waiting for transfers between devices, send(): lax.ppermute(block, 'pair', [(device, int(target(device))) for device in...  25.3 us
    ppermute x24, starting transfers between devices, send(): lax.ppermute(block, 'pair', [(device, int(target(device))) for device in...  20.5 us
    ppermute x14, waiting for transfers between devices, gather_ring(): held[way * step] = lax.ppermute(block, 'pair', around[way])  15.3 us
    ppermute x14, starting transfers between devices, gather_ring(): held[way * step] = lax.ppermute(block, 'pair', around[way])  15.1 us
    pallas_call x4, Pallas kernels, first_product(): pl.pallas_call(body, out_shape=shapes, in_specs=vmem(4 + len(totals) + le...  2.99 us
    pallas_call x1, Pallas kernels, share_integrals(): pl.pallas_call(body, out_shape=[jax.ShapeDtypeStruct((rows + batch_rows *...  2.52 us
    pallas_call x1, Pallas kernels, place_pairs(): pl.pallas_call(body, out_shape=jax.ShapeDtypeStruct((2, share, width, pai...  2.29 us
  transfers between devices with their start and end apart: 38, of which 18 were waited for; matrix products, arithmetic and copies ran while one was open for 0% of the time, Pallas kernels for 9%

profile of v6, /device:TPU:0, one launch (start us, length us, event | category | flops | bytes accessed | tf_op | source)
XLA Modules:
  0.0 88.2 jit_solution(13054900771401831611)
XLA Ops:
  0.0 3.0 %collective-permute-start.9 = (bf16[2,256,384]{2,1,0:T(8,128)(2,1)}, bf16[2,256,384]{2,1,0:T(8,128)(2,1)S(1)}, u32[]{:S(2)}, u32[]{:S(2)}) collective-permute-start(bf16[2,256,384]{2,1,0:T(8,128)(2,1)} %refs_4_.1), channel_id=1, source_target_pairs={{0,8},{1,5},{2,0},{3,11},{4,6},{5,13},{6,14},{7,3},{8,16},{9,1},{1... | collective-permute-start | bytes 1179656 | tf_op jit(solution)/shard_map/ppermute | solution.py:88
  3.0 0.7 copy-done.1
  3.7 2.5 %share_integrals.1 = (bf16[160,768]{1,0:T(8,128)(2,1)S(1)}, bf16[128,768]{1,0:T(8,128)(2,1)S(1)}, bf16[128,768]{1,0:T(8,128)(2,1)S(1)}, bf16[128,768]{1,0:T(8,12...) custom-call(s32[1]{0:T(128)} %bitcast.where_ref, ...), custom_call_target="tpu_custom_call" | custom-call | tf_op jit(solution)/shard_map/share_integrals/pallas_call | solution.py:134
  6.2 5.5 %collective-permute-done.9.refs_5_ = bf16[2,256,384]{2,1,0:T(8,128)(2,1)S(1)} collective-permute-done((bf16[2,256,384]{2,1,0:T(8,128)(2,1)}, bf16[2,256,384]{2,1,0:T(8,128)(2,1)S(1)}, u32[]{:S(2)}, u32[]{:S(2)}) %collective-permute-start.9) | collective-permute-done | bytes 393248 | tf_op jit(solution)/shard_map/ppermute | solution.py:88
  11.7 2.4 %collective-permute-start.11 = (bf16[2,256,384]{2,1,0:T(8,128)(2,1)S(1)}, bf16[2,256,384]{2,1,0:T(8,128)(2,1)S(1)}, u32[]{:S(2)}, u32[]{:S(2)}) collective-permute-start(bf16[2,256,384]{2,1,0:T(8,128)(2,1)S(1)} %collective-permute-done.9.refs_5_), channel_id=1, source_target_pairs={{0,8},{1,5},{2,0},{3,11},{4,6},{5,13},{6,14},{7,3},{8,16},{9,1},{1... | collective-permute-start | bytes 1179656 | tf_op jit(solution)/shard_map/ppermute | solution.py:88
  14.1 0.9 collective-permute-start.12
  15.0 2.1 %collective-permute-start.7 = (bf16[128,768]{1,0:T(8,128)(2,1)S(1)}, bf16[128,768]{1,0:T(8,128)(2,1)S(1)}, u32[]{:S(2)}, u32[]{:S(2)}) collective-permute-start(bf16[128,768]{1,0:T(8,128)(2,1)S(1)} %get-tuple-element.67), channel_id=1, source_target_pairs={{0,4},{1,3},{2,6},{3,1},{4,0},{5,7},{6,2},{7,5},{8,12},{9,11},{10,... | collective-permute-start | bytes 589832 | tf_op jit(solution)/shard_map/ppermute | solution.py:59
  17.0 0.1 collective-permute-start.8
  17.2 5.7 %collective-permute-done.7.refs_2_ = bf16[128,768]{1,0:T(8,128)(2,1)S(1)} collective-permute-done((bf16[128,768]{1,0:T(8,128)(2,1)S(1)}, bf16[128,768]{1,0:T(8,128)(2,1)S(1)}, u32[]{:S(2)}, u32[]{:S(2)}) %collective-permute-start.7) | collective-permute-done | bytes 196640 | tf_op jit(solution)/shard_map/ppermute | solution.py:59
  22.9 1.6 %collective-permute-done.8.refs_3_ = bf16[128,768]{1,0:T(8,128)(2,1)S(1)} collective-permute-done((bf16[128,768]{1,0:T(8,128)(2,1)S(1)}, bf16[128,768]{1,0:T(8,128)(2,1)S(1)}, u32[]{:S(2)}, u32[]{:S(2)}) %collective-permute-start.8) | collective-permute-done | bytes 196640 | tf_op jit(solution)/shard_map/ppermute | solution.py:59
  24.5 2.3 %collective-permute-start.3 = (bf16[128,512]{1,0:T(8,128)(2,1)S(1)}, bf16[128,512]{1,0:T(8,128)(2,1)S(1)}, u32[]{:S(2)}, u32[]{:S(2)}) collective-permute-start(bf16[128,512]{1,0:T(8,128)(2,1)S(1)} %get-tuple-element.60), channel_id=1, source_target_pairs={{0,1},{1,0},{2,3},{3,2},{4,5},{5,4},{6,7},{7,6},{8,9},{9,8},{10,11... | collective-permute-start | bytes 393224 | tf_op jit(solution)/shard_map/ppermute | solution.py:59
  26.8 0.3 collective-permute-start.4
  27.1 1.1 %collective-permute-start.5 = (bf16[128,512]{1,0:T(8,128)(2,1)S(1)}, bf16[128,512]{1,0:T(8,128)(2,1)S(1)}, u32[]{:S(2)}, u32[]{:S(2)}) collective-permute-start(bf16[128,512]{1,0:T(8,128)(2,1)S(1)} %get-tuple-element.64), channel_id=1, source_target_pairs={{0,3},{1,4},{2,1},{3,6},{4,7},{5,0},{6,5},{7,2},{8,11},{9,12},{10,... | collective-permute-start | bytes 393224 | tf_op jit(solution)/shard_map/ppermute | solution.py:59
  28.1 0.4 collective-permute-start.14
  28.6 1.0 %first_product.4.refs_4_ = f32[544,768]{1,0:T(8,128)S(1)} custom-call(bf16[160,768]{1,0:T(8,128)(2,1)S(1)} %get-tuple-element.65.refs_0_, bf16[128,768]{1,0:T(8,128)(2,1)S(1)} %collective-permute-done.6.refs_1_, bf16[128,768]{1,0:T(8,128)(2,1)S(1)} %collective-permute-done.7.refs_2_, bf16[128,768]{1,0:T(8,128)(2,1)S(1)} %collective-permute-done.8.refs_3_, ...), custom_call_target="tpu_custom_call" | custom-call | flops 3208642560 | tf_op jit(solution)/shard_map/first_product/pallas_call | solution.py:184
  29.6 0.5 collective-permute-start
  30.1 3.1 %collective-permute-done.4.refs_2_ = bf16[128,512]{1,0:T(8,128)(2,1)S(1)} collective-permute-done((bf16[128,512]{1,0:T(8,128)(2,1)S(1)}, bf16[128,512]{1,0:T(8,128)(2,1)S(1)}, u32[]{:S(2)}, u32[]{:S(2)}) %collective-permute-start.4) | collective-permute-done | bytes 131104 | tf_op jit(solution)/shard_map/ppermute | solution.py:59
  33.2 0.3 collective-permute-start.1
  33.4 0.3 collective-permute-start.2
  33.7 0.7 collective-permute-start.15
  34.4 0.7 first_product.5.refs_4_
  35.2 5.8 %collective-permute-done.1.refs_2_ = bf16[128,768]{1,0:T(8,128)(2,1)S(1)} collective-permute-done((bf16[128,768]{1,0:T(8,128)(2,1)S(1)}, bf16[128,768]{1,0:T(8,128)(2,1)S(1)}, u32[]{:S(2)}, u32[]{:S(2)}) %collective-permute-start.1) | collective-permute-done | bytes 196640 | tf_op jit(solution)/shard_map/ppermute | solution.py:59
  41.0 0.3 collective-permute-done.2.refs_3_
  41.3 0.7 first_product.6.refs_4_
  42.1 2.7 %collective-permute-done.15.refs_5_ = bf16[2,256,384]{2,1,0:T(8,128)(2,1)S(1)} collective-permute-done((bf16[2,256,384]{2,1,0:T(8,128)(2,1)S(1)}, bf16[2,256,384]{2,1,0:T(8,128)(2,1)S(1)}, u32[]{:S(2)}, u32[]{:S(2)}) %collective-permute-start.15) | collective-permute-done | bytes 393248 | tf_op jit(solution)/shard_map/ppermute | solution.py:88
  44.8 0.5 first_product.7
  45.2 0.1 collective-permute-start.16
  45.3 1.0 %collective-permute-start.17 = (bf16[160,768]{1,0:T(8,128)(2,1)S(1)}, bf16[160,768]{1,0:T(8,128)(2,1)S(1)}, u32[]{:S(2)}, u32[]{:S(2)}) collective-permute-start(bf16[160,768]{1,0:T(8,128)(2,1)S(1)} %get-tuple-element.76), channel_id=1, source_target_pairs={{0,4},{1,3},{2,6},{3,1},{4,0},{5,7},{6,2},{7,5},{8,12},{9,11},{10,... | collective-permute-start | bytes 737288 | tf_op jit(solution)/shard_map/ppermute | solution.py:59
  46.3 1.5 %collective-permute-start.18 = (bf16[160,768]{1,0:T(8,128)(2,1)S(1)}, bf16[160,768]{1,0:T(8,128)(2,1)S(1)}, u32[]{:S(2)}, u32[]{:S(2)}) collective-permute-start(bf16[160,768]{1,0:T(8,128)(2,1)S(1)} %get-tuple-element.77), channel_id=1, source_target_pairs={{0,5},{1,2},{2,7},{3,0},{4,1},{5,6},{6,3},{7,4},{8,13},{9,10},{10,... | collective-permute-start | bytes 737288 | tf_op jit(solution)/shard_map/ppermute | solution.py:59
  47.8 3.8 %collective-permute-done.17.refs_2_ = bf16[160,768]{1,0:T(8,128)(2,1)S(1)} collective-permute-done((bf16[160,768]{1,0:T(8,128)(2,1)S(1)}, bf16[160,768]{1,0:T(8,128)(2,1)S(1)}, u32[]{:S(2)}, u32[]{:S(2)}) %collective-permute-start.17) | collective-permute-done | bytes 245792 | tf_op jit(solution)/shard_map/ppermute | solution.py:59
  51.6 2.1 %collective-permute-done.18.refs_3_ = bf16[160,768]{1,0:T(8,128)(2,1)S(1)} collective-permute-done((bf16[160,768]{1,0:T(8,128)(2,1)S(1)}, bf16[160,768]{1,0:T(8,128)(2,1)S(1)}, u32[]{:S(2)}, u32[]{:S(2)}) %collective-permute-start.18) | collective-permute-done | bytes 245792 | tf_op jit(solution)/shard_map/ppermute | solution.py:59
  53.7 0.1 add_partners.1
  53.8 0.1 collective-permute-start.19
  53.8 2.0 %collective-permute-start.20 = (bf16[256,384]{1,0:T(8,128)(2,1)S(1)}, bf16[256,384]{1,0:T(8,128)(2,1)S(1)}, u32[]{:S(2)}, u32[]{:S(2)}) collective-permute-start(bf16[256,384]{1,0:T(8,128)(2,1)S(1)} %get-tuple-element.79.refs_0_), channel_id=1, source_target_pairs={{0,2},{1,9},{2,10},{3,7},{4,12},{5,1},{6,4},{7,15},{8,0},{9,17},{1... | collective-permute-start | bytes 589832 | tf_op jit(solution)/shard_map/ppermute | solution.py:88
  55.8 0.5 pair_places.1.place_ref
  56.3 1.2 %weights.1.matrix_ref = bf16[384,256]{1,0:T(8,128)(2,1)S(1)} custom-call(s32[1]{0:T(128)} %bitcast.where_ref, bf16[64,384]{1,0:T(8,128)(2,1)S(1)} %get-tuple-element.78.batch_ref), custom_call_target="tpu_custom_call" | custom-call | tf_op jit(solution)/shard_map/weights/pallas_call | solution.py:249
  57.6 1.9 %collective-permute-done.19.refs_1_ = bf16[256,384]{1,0:T(8,128)(2,1)S(1)} collective-permute-done((bf16[256,384]{1,0:T(8,128)(2,1)S(1)}, bf16[256,384]{1,0:T(8,128)(2,1)S(1)}, u32[]{:S(2)}, u32[]{:S(2)}) %collective-permute-start.19) | collective-permute-done | bytes 196640 | tf_op jit(solution)/shard_map/ppermute | solution.py:88
  59.5 1.0 %collective-permute-start.24 = (bf16[256,384]{1,0:T(8,128)(2,1)S(1)}, bf16[256,384]{1,0:T(8,128)(2,1)S(1)}, u32[]{:S(2)}, u32[]{:S(2)}) collective-permute-start(bf16[256,384]{1,0:T(8,128)(2,1)S(1)} %collective-permute-done.19.refs_1_), channel_id=1, source_target_pairs={{0,8},{1,5},{2,0},{3,11},{4,6},{5,13},{6,14},{7,3},{8,16},{9,1},{1... | collective-permute-start | bytes 589832 | tf_op jit(solution)/shard_map/ppermute | solution.py:88
  60.4 0.5 collective-permute-done.20.refs_2_
  61.0 0.8 collective-permute-start.25
  61.8 0.5 second_product.4
  62.2 0.2 collective-permute-start.21
  62.5 2.2 %collective-permute-start.22 = (bf16[576,384]{1,0:T(8,128)(2,1)S(1)}, bf16[576,384]{1,0:T(8,128)(2,1)S(1)}, u32[]{:S(2)}, u32[]{:S(2)}) collective-permute-start(bf16[576,384]{1,0:T(8,128)(2,1)S(1)} %get-tuple-element.82), channel_id=1, source_target_pairs={{0,4},{1,3},{2,6},{3,1},{4,0},{5,7},{6,2},{7,5},{8,12},{9,11},{10,... | collective-permute-start | bytes 1327112 | tf_op jit(solution)/shard_map/ppermute | solution.py:59
  64.7 0.7 collective-permute-done.24.refs_0_
  65.4 2.1 %collective-permute-start.29 = (bf16[256,384]{1,0:T(8,128)(2,1)S(1)}, bf16[256,384]{1,0:T(8,128)(2,1)S(1)}, u32[]{:S(2)}, u32[]{:S(2)}) collective-permute-start(bf16[256,384]{1,0:T(8,128)(2,1)S(1)} %collective-permute-done.24.refs_0_), channel_id=1, source_target_pairs={{0,8},{1,5},{2,0},{3,11},{4,6},{5,13},{6,14},{7,3},{8,16},{9,1},{1... | collective-permute-start | bytes 589832 | tf_op jit(solution)/shard_map/ppermute | solution.py:88
  67.5 0.7 collective-permute-start.30
  68.1 0.4 second_product.5
  68.5 2.7 %collective-permute-start.27 = (bf16[384,384]{1,0:T(8,128)(2,1)S(1)}, bf16[384,384]{1,0:T(8,128)(2,1)S(1)}, u32[]{:S(2)}, u32[]{:S(2)}) collective-permute-start(bf16[384,384]{1,0:T(8,128)(2,1)S(1)} %get-tuple-element.87), channel_id=1, source_target_pairs={{0,4},{1,3},{2,6},{3,1},{4,0},{5,7},{6,2},{7,5},{8,12},{9,11},{10,... | collective-permute-start | bytes 884744 | tf_op jit(solution)/shard_map/ppermute | solution.py:59
  71.2 2.8 %collective-permute-done.29.refs_0_ = bf16[256,384]{1,0:T(8,128)(2,1)S(1)} collective-permute-done((bf16[256,384]{1,0:T(8,128)(2,1)S(1)}, bf16[256,384]{1,0:T(8,128)(2,1)S(1)}, u32[]{:S(2)}, u32[]{:S(2)}) %collective-permute-start.29) | collective-permute-done | bytes 196640 | tf_op jit(solution)/shard_map/ppermute | solution.py:88
  73.9 1.2 %collective-permute-start.34 = (bf16[256,384]{1,0:T(8,128)(2,1)S(1)}, bf16[256,384]{1,0:T(8,128)(2,1)S(1)}, u32[]{:S(2)}, u32[]{:S(2)}) collective-permute-start(bf16[256,384]{1,0:T(8,128)(2,1)S(1)} %collective-permute-done.29.refs_0_), channel_id=1, source_target_pairs={{0,8},{1,5},{2,0},{3,11},{4,6},{5,13},{6,14},{7,3},{8,16},{9,1},{1... | collective-permute-start | bytes 589832 | tf_op jit(solution)/shard_map/ppermute | solution.py:88
  75.2 0.4 second_product.6
  75.6 1.5 %collective-permute-start.32 = (bf16[192,384]{1,0:T(8,128)(2,1)S(1)}, bf16[192,384]{1,0:T(8,128)(2,1)S(1)}, u32[]{:S(2)}, u32[]{:S(2)}) collective-permute-start(bf16[192,384]{1,0:T(8,128)(2,1)S(1)} %get-tuple-element.98), channel_id=1, source_target_pairs={{0,4},{1,3},{2,6},{3,1},{4,0},{5,7},{6,2},{7,5},{8,12},{9,11},{10,... | collective-permute-start | bytes 442376 | tf_op jit(solution)/shard_map/ppermute | solution.py:59
  77.1 0.8 collective-permute-done.27.refs_6_
  77.9 0.7 collective-permute-start.31
  78.6 1.1 %collective-permute-done.34.refs_0_ = bf16[256,384]{1,0:T(8,128)(2,1)S(1)} collective-permute-done((bf16[256,384]{1,0:T(8,128)(2,1)S(1)}, bf16[256,384]{1,0:T(8,128)(2,1)S(1)}, u32[]{:S(2)}, u32[]{:S(2)}) %collective-permute-start.34) | collective-permute-done | bytes 196640 | tf_op jit(solution)/shard_map/ppermute | solution.py:88
  79.7 0.3 second_product.7
  80.0 0.6 collective-permute-start.28
  80.6 0.2 collective-permute-done.32.refs_10_
  80.8 1.4 %collective-permute-start.36 = (bf16[96,384]{1,0:T(8,128)(2,1)S(1)}, bf16[96,384]{1,0:T(8,128)(2,1)S(1)}, u32[]{:S(2)}, u32[]{:S(2)}) collective-permute-start(bf16[96,384]{1,0:T(8,128)(2,1)S(1)} %get-tuple-element.100), channel_id=1, source_target_pairs={{0,4},{1,3},{2,6},{3,1},{4,0},{5,7},{6,2},{7,5},{8,12},{9,11},{10,... | collective-permute-start | bytes 221192 | tf_op jit(solution)/shard_map/ppermute | solution.py:59
  82.2 1.2 %collective-permute-start.37 = (bf16[96,384]{1,0:T(8,128)(2,1)S(1)}, bf16[96,384]{1,0:T(8,128)(2,1)S(1)}, u32[]{:S(2)}, u32[]{:S(2)}) collective-permute-start(bf16[96,384]{1,0:T(8,128)(2,1)S(1)} %get-tuple-element.99), channel_id=1, source_target_pairs={{0,5},{1,2},{2,7},{3,0},{4,1},{5,6},{6,3},{7,4},{8,13},{9,10},{10,... | collective-permute-start | bytes 221192 | tf_op jit(solution)/shard_map/ppermute | solution.py:59
  83.4 0.8 collective-permute-start.35
  84.1 1.0 %collective-permute-done.36.refs_14_ = bf16[96,384]{1,0:T(8,128)(2,1)S(1)} collective-permute-done((bf16[96,384]{1,0:T(8,128)(2,1)S(1)}, bf16[96,384]{1,0:T(8,128)(2,1)S(1)}, u32[]{:S(2)}, u32[]{:S(2)}) %collective-permute-start.36) | collective-permute-done | bytes 73760 | tf_op jit(solution)/shard_map/ppermute | solution.py:59
  85.1 0.8 collective-permute-done.37.refs_15_
  86.0 2.3 %place_pairs.1 = bf16[2,12,384,128]{3,2,1,0:T(8,128)(2,1)} custom-call(bf16[128,128]{1,0:T(8,128)(2,1)S(1)} %pair_places.1.place_ref, bf16[288,384]{1,0:T(8,128)(2,1)S(1)} %get-tuple-element.80.refs_0_, bf16[288,384]{1,0:T(8,128)(2,1)S(1)} %collective-permute-done.21.refs_1_, bf16[576,384]{1,0:T(8,128)(2,1)S(1)} %collective-permute-done.22.refs_2_, ...), custom_call_target="tpu_custom_call" | custom-call | tf_op jit(solution)/shard_map/place_pairs/pallas_call | solution.py:336
  (35 shorter events, 0.2 us)
Async XLA Ops:
  0.0 11.7 %collective-permute-start.9 = (bf16[2,256,384]{2,1,0:T(8,128)(2,1)}, bf16[2,256,384]{2,1,0:T(8,128)(2,1)S(1)}, u32[]{:S(2)}, u32[]{:S(2)}) collective-permute-start(bf16[2,256,384]{2,1,0:T(8,128)(2,1)} %refs_4_.1), channel_id=1, source_target_pairs={{0,8},{1,5},{2,0},{3,11},{4,6},{5,13},{6,14},{7,3},{8,16},{9,1},{1... | collective-permute-start | bytes 1179656 | tf_op jit(solution)/shard_map/ppermute | solution.py:88
  3.0 11.1 %collective-permute-start.10 = (bf16[2,256,384]{2,1,0:T(8,128)(2,1)}, bf16[2,256,384]{2,1,0:T(8,128)(2,1)S(1)}, u32[]{:S(2)}, u32[]{:S(2)}) collective-permute-start(bf16[2,256,384]{2,1,0:T(8,128)(2,1)} %refs_4_.1), channel_id=1, source_target_pairs={{0,2},{1,9},{2,10},{3,7},{4,12},{5,1},{6,4},{7,15},{8,0},{9,17},{1... | collective-permute-start | bytes 1179656 | tf_op jit(solution)/shard_map/ppermute | solution.py:88
  3.0 0.7 copy-start.1
  3.7 24.9 %copy-start.2 = (bf16[2,256,384]{2,1,0:T(8,128)(2,1)S(1)}, bf16[2,256,384]{2,1,0:T(8,128)(2,1)}, u32[]{:S(2)}) copy-start(bf16[2,256,384]{2,1,0:T(8,128)(2,1)} %refs_4_.1) | copy-start | bytes 1179652
  11.7 12.8 %collective-permute-start.11 = (bf16[2,256,384]{2,1,0:T(8,128)(2,1)S(1)}, bf16[2,256,384]{2,1,0:T(8,128)(2,1)S(1)}, u32[]{:S(2)}, u32[]{:S(2)}) collective-permute-start(bf16[2,256,384]{2,1,0:T(8,128)(2,1)S(1)} %collective-permute-done.9.refs_5_), channel_id=1, source_target_pairs={{0,8},{1,5},{2,0},{3,11},{4,6},{5,13},{6,14},{7,3},{8,16},{9,1},{1... | collective-permute-start | bytes 1179656 | tf_op jit(solution)/shard_map/ppermute | solution.py:88
  14.1 14.0 %collective-permute-start.12 = (bf16[2,256,384]{2,1,0:T(8,128)(2,1)S(1)}, bf16[2,256,384]{2,1,0:T(8,128)(2,1)S(1)}, u32[]{:S(2)}, u32[]{:S(2)}) collective-permute-start(bf16[2,256,384]{2,1,0:T(8,128)(2,1)S(1)} %collective-permute-done.10.refs_6_), channel_id=1, source_target_pairs={{0,2},{1,9},{2,10},{3,7},{4,12},{5,1},{6,4},{7,15},{8,0},{9,17},{1... | collective-permute-start | bytes 1179656 | tf_op jit(solution)/shard_map/ppermute | solution.py:88
  15.0 2.2 %collective-permute-start.6 = (bf16[128,768]{1,0:T(8,128)(2,1)S(1)}, bf16[128,768]{1,0:T(8,128)(2,1)S(1)}, u32[]{:S(2)}, u32[]{:S(2)}) collective-permute-start(bf16[128,768]{1,0:T(8,128)(2,1)S(1)} %get-tuple-element.66), channel_id=1, source_target_pairs={{0,1},{1,0},{2,3},{3,2},{4,5},{5,4},{6,7},{7,6},{8,9},{9,8},{10,11... | collective-permute-start | bytes 589832 | tf_op jit(solution)/shard_map/ppermute | solution.py:59
  15.0 7.9 %collective-permute-start.7 = (bf16[128,768]{1,0:T(8,128)(2,1)S(1)}, bf16[128,768]{1,0:T(8,128)(2,1)S(1)}, u32[]{:S(2)}, u32[]{:S(2)}) collective-permute-start(bf16[128,768]{1,0:T(8,128)(2,1)S(1)} %get-tuple-element.67), channel_id=1, source_target_pairs={{0,4},{1,3},{2,6},{3,1},{4,0},{5,7},{6,2},{7,5},{8,12},{9,11},{10,... | collective-permute-start | bytes 589832 | tf_op jit(solution)/shard_map/ppermute | solution.py:59
  17.0 7.5 %collective-permute-start.8 = (bf16[128,768]{1,0:T(8,128)(2,1)S(1)}, bf16[128,768]{1,0:T(8,128)(2,1)S(1)}, u32[]{:S(2)}, u32[]{:S(2)}) collective-permute-start(bf16[128,768]{1,0:T(8,128)(2,1)S(1)} %get-tuple-element.68), channel_id=1, source_target_pairs={{0,3},{1,4},{2,1},{3,6},{4,7},{5,0},{6,5},{7,2},{8,11},{9,12},{10,... | collective-permute-start | bytes 589832 | tf_op jit(solution)/shard_map/ppermute | solution.py:59
  24.5 9.2 %collective-permute-start.13 = (bf16[2,256,384]{2,1,0:T(8,128)(2,1)S(1)}, bf16[2,256,384]{2,1,0:T(8,128)(2,1)S(1)}, u32[]{:S(2)}, u32[]{:S(2)}) collective-permute-start(bf16[2,256,384]{2,1,0:T(8,128)(2,1)S(1)} %collective-permute-done.11.refs_5_), channel_id=1, source_target_pairs={{0,8},{1,5},{2,0},{3,11},{4,6},{5,13},{6,14},{7,3},{8,16},{9,1},{1... | collective-permute-start | bytes 1179656 | tf_op jit(solution)/shard_map/ppermute | solution.py:88
  24.5 5.1 %collective-permute-start.3 = (bf16[128,512]{1,0:T(8,128)(2,1)S(1)}, bf16[128,512]{1,0:T(8,128)(2,1)S(1)}, u32[]{:S(2)}, u32[]{:S(2)}) collective-permute-start(bf16[128,512]{1,0:T(8,128)(2,1)S(1)} %get-tuple-element.60), channel_id=1, source_target_pairs={{0,1},{1,0},{2,3},{3,2},{4,5},{5,4},{6,7},{7,6},{8,9},{9,8},{10,11... | collective-permute-start | bytes 393224 | tf_op jit(solution)/shard_map/ppermute | solution.py:59
  26.8 6.4 %collective-permute-start.4 = (bf16[128,512]{1,0:T(8,128)(2,1)S(1)}, bf16[128,512]{1,0:T(8,128)(2,1)S(1)}, u32[]{:S(2)}, u32[]{:S(2)}) collective-permute-start(bf16[128,512]{1,0:T(8,128)(2,1)S(1)} %get-tuple-element.62), channel_id=1, source_target_pairs={{0,4},{1,3},{2,6},{3,1},{4,0},{5,7},{6,2},{7,5},{8,12},{9,11},{10,... | collective-permute-start | bytes 393224 | tf_op jit(solution)/shard_map/ppermute | solution.py:59
  27.1 6.4 %collective-permute-start.5 = (bf16[128,512]{1,0:T(8,128)(2,1)S(1)}, bf16[128,512]{1,0:T(8,128)(2,1)S(1)}, u32[]{:S(2)}, u32[]{:S(2)}) collective-permute-start(bf16[128,512]{1,0:T(8,128)(2,1)S(1)} %get-tuple-element.64), channel_id=1, source_target_pairs={{0,3},{1,4},{2,1},{3,6},{4,7},{5,0},{6,5},{7,2},{8,11},{9,12},{10,... | collective-permute-start | bytes 393224 | tf_op jit(solution)/shard_map/ppermute | solution.py:59
  28.1 13.2 %collective-permute-start.14 = (bf16[2,256,384]{2,1,0:T(8,128)(2,1)S(1)}, bf16[2,256,384]{2,1,0:T(8,128)(2,1)S(1)}, u32[]{:S(2)}, u32[]{:S(2)}) collective-permute-start(bf16[2,256,384]{2,1,0:T(8,128)(2,1)S(1)} %collective-permute-done.12.refs_6_), channel_id=1, source_target_pairs={{0,2},{1,9},{2,10},{3,7},{4,12},{5,1},{6,4},{7,15},{8,0},{9,17},{1... | collective-permute-start | bytes 1179656 | tf_op jit(solution)/shard_map/ppermute | solution.py:88
  29.6 5.5 %collective-permute-start = (bf16[128,768]{1,0:T(8,128)(2,1)S(1)}, bf16[128,768]{1,0:T(8,128)(2,1)S(1)}, u32[]{:S(2)}, u32[]{:S(2)}) collective-permute-start(bf16[128,768]{1,0:T(8,128)(2,1)S(1)} %get-tuple-element.53), channel_id=1, source_target_pairs={{0,1},{1,0},{2,3},{3,2},{4,5},{5,4},{6,7},{7,6},{8,9},{9,8},{10,11... | collective-permute-start | bytes 589832 | tf_op jit(solution)/shard_map/ppermute | solution.py:59
  33.2 7.8 %collective-permute-start.1 = (bf16[128,768]{1,0:T(8,128)(2,1)S(1)}, bf16[128,768]{1,0:T(8,128)(2,1)S(1)}, u32[]{:S(2)}, u32[]{:S(2)}) collective-permute-start(bf16[128,768]{1,0:T(8,128)(2,1)S(1)} %get-tuple-element.55), channel_id=1, source_target_pairs={{0,4},{1,3},{2,6},{3,1},{4,0},{5,7},{6,2},{7,5},{8,12},{9,11},{10,... | collective-permute-start | bytes 589832 | tf_op jit(solution)/shard_map/ppermute | solution.py:59
  33.4 7.9 %collective-permute-start.2 = (bf16[128,768]{1,0:T(8,128)(2,1)S(1)}, bf16[128,768]{1,0:T(8,128)(2,1)S(1)}, u32[]{:S(2)}, u32[]{:S(2)}) collective-permute-start(bf16[128,768]{1,0:T(8,128)(2,1)S(1)} %get-tuple-element.57), channel_id=1, source_target_pairs={{0,3},{1,4},{2,1},{3,6},{4,7},{5,0},{6,5},{7,2},{8,11},{9,12},{10,... | collective-permute-start | bytes 589832 | tf_op jit(solution)/shard_map/ppermute | solution.py:59
  33.7 11.0 %collective-permute-start.15 = (bf16[2,256,384]{2,1,0:T(8,128)(2,1)S(1)}, bf16[2,256,384]{2,1,0:T(8,128)(2,1)S(1)}, u32[]{:S(2)}, u32[]{:S(2)}) collective-permute-start(bf16[2,256,384]{2,1,0:T(8,128)(2,1)S(1)} %collective-permute-done.13.refs_5_), channel_id=1, source_target_pairs={{0,8},{1,5},{2,0},{3,11},{4,6},{5,13},{6,14},{7,3},{8,16},{9,1},{1... | collective-permute-start | bytes 1179656 | tf_op jit(solution)/shard_map/ppermute | solution.py:88
  42.1 13.8 %copy-start = (s32[1,128]{1,0:T(1,128)S(1)}, s32[1,128]{1,0:T(1,128)}, u32[]{:S(2)}) copy-start(s32[1,128]{1,0:T(1,128)} %pair_ref.1) | copy-start | bytes 1540
  45.2 8.4 %collective-permute-start.16 = (f32[160,768]{1,0:T(8,128)S(1)}, f32[160,768]{1,0:T(8,128)S(1)}, u32[]{:S(2)}, u32[]{:S(2)}) collective-permute-start(f32[160,768]{1,0:T(8,128)S(1)} %get-tuple-element.75), channel_id=1, source_target_pairs={{0,1},{1,0},{2,3},{3,2},{4,5},{5,4},{6,7},{7,6},{8,9},{9,8},{10,11... | collective-permute-start | bytes 1474568 | tf_op jit(solution)/shard_map/ppermute | solution.py:59
  45.3 6.3 %collective-permute-start.17 = (bf16[160,768]{1,0:T(8,128)(2,1)S(1)}, bf16[160,768]{1,0:T(8,128)(2,1)S(1)}, u32[]{:S(2)}, u32[]{:S(2)}) collective-permute-start(bf16[160,768]{1,0:T(8,128)(2,1)S(1)} %get-tuple-element.76), channel_id=1, source_target_pairs={{0,4},{1,3},{2,6},{3,1},{4,0},{5,7},{6,2},{7,5},{8,12},{9,11},{10,... | collective-permute-start | bytes 737288 | tf_op jit(solution)/shard_map/ppermute | solution.py:59
  46.3 7.3 %collective-permute-start.18 = (bf16[160,768]{1,0:T(8,128)(2,1)S(1)}, bf16[160,768]{1,0:T(8,128)(2,1)S(1)}, u32[]{:S(2)}, u32[]{:S(2)}) collective-permute-start(bf16[160,768]{1,0:T(8,128)(2,1)S(1)} %get-tuple-element.77), channel_id=1, source_target_pairs={{0,5},{1,2},{2,7},{3,0},{4,1},{5,6},{6,3},{7,4},{8,13},{9,10},{10,... | collective-permute-start | bytes 737288 | tf_op jit(solution)/shard_map/ppermute | solution.py:59
  53.8 5.7 %collective-permute-start.19 = (bf16[256,384]{1,0:T(8,128)(2,1)S(1)}, bf16[256,384]{1,0:T(8,128)(2,1)S(1)}, u32[]{:S(2)}, u32[]{:S(2)}) collective-permute-start(bf16[256,384]{1,0:T(8,128)(2,1)S(1)} %get-tuple-element.79.refs_0_), channel_id=1, source_target_pairs={{0,8},{1,5},{2,0},{3,11},{4,6},{5,13},{6,14},{7,3},{8,16},{9,1},{1... | collective-permute-start | bytes 589832 | tf_op jit(solution)/shard_map/ppermute | solution.py:88
  53.8 7.2 %collective-permute-start.20 = (bf16[256,384]{1,0:T(8,128)(2,1)S(1)}, bf16[256,384]{1,0:T(8,128)(2,1)S(1)}, u32[]{:S(2)}, u32[]{:S(2)}) collective-permute-start(bf16[256,384]{1,0:T(8,128)(2,1)S(1)} %get-tuple-element.79.refs_0_), channel_id=1, source_target_pairs={{0,2},{1,9},{2,10},{3,7},{4,12},{5,1},{6,4},{7,15},{8,0},{9,17},{1... | collective-permute-start | bytes 589832 | tf_op jit(solution)/shard_map/ppermute | solution.py:88
  59.5 5.9 %collective-permute-start.24 = (bf16[256,384]{1,0:T(8,128)(2,1)S(1)}, bf16[256,384]{1,0:T(8,128)(2,1)S(1)}, u32[]{:S(2)}, u32[]{:S(2)}) collective-permute-start(bf16[256,384]{1,0:T(8,128)(2,1)S(1)} %collective-permute-done.19.refs_1_), channel_id=1, source_target_pairs={{0,8},{1,5},{2,0},{3,11},{4,6},{5,13},{6,14},{7,3},{8,16},{9,1},{1... | collective-permute-start | bytes 589832 | tf_op jit(solution)/shard_map/ppermute | solution.py:88
  61.0 6.5 %collective-permute-start.25 = (bf16[256,384]{1,0:T(8,128)(2,1)S(1)}, bf16[256,384]{1,0:T(8,128)(2,1)S(1)}, u32[]{:S(2)}, u32[]{:S(2)}) collective-permute-start(bf16[256,384]{1,0:T(8,128)(2,1)S(1)} %collective-permute-done.20.refs_2_), channel_id=1, source_target_pairs={{0,2},{1,9},{2,10},{3,7},{4,12},{5,1},{6,4},{7,15},{8,0},{9,17},{1... | collective-permute-start | bytes 589832 | tf_op jit(solution)/shard_map/ppermute | solution.py:88
  62.2 8.9 %collective-permute-start.21 = (bf16[288,384]{1,0:T(8,128)(2,1)S(1)}, bf16[288,384]{1,0:T(8,128)(2,1)S(1)}, u32[]{:S(2)}, u32[]{:S(2)}) collective-permute-start(bf16[288,384]{1,0:T(8,128)(2,1)S(1)} %get-tuple-element.81), channel_id=1, source_target_pairs={{0,1},{1,0},{2,3},{3,2},{4,5},{5,4},{6,7},{7,6},{8,9},{9,8},{10,11... | collective-permute-start | bytes 663560 | tf_op jit(solution)/shard_map/ppermute | solution.py:59
  62.5 14.5 %collective-permute-start.22 = (bf16[576,384]{1,0:T(8,128)(2,1)S(1)}, bf16[576,384]{1,0:T(8,128)(2,1)S(1)}, u32[]{:S(2)}, u32[]{:S(2)}) collective-permute-start(bf16[576,384]{1,0:T(8,128)(2,1)S(1)} %get-tuple-element.82), channel_id=1, source_target_pairs={{0,4},{1,3},{2,6},{3,1},{4,0},{5,7},{6,2},{7,5},{8,12},{9,11},{10,... | collective-permute-start | bytes 1327112 | tf_op jit(solution)/shard_map/ppermute | solution.py:59
  65.4 8.5 %collective-permute-start.29 = (bf16[256,384]{1,0:T(8,128)(2,1)S(1)}, bf16[256,384]{1,0:T(8,128)(2,1)S(1)}, u32[]{:S(2)}, u32[]{:S(2)}) collective-permute-start(bf16[256,384]{1,0:T(8,128)(2,1)S(1)} %collective-permute-done.24.refs_0_), channel_id=1, source_target_pairs={{0,8},{1,5},{2,0},{3,11},{4,6},{5,13},{6,14},{7,3},{8,16},{9,1},{1... | collective-permute-start | bytes 589832 | tf_op jit(solution)/shard_map/ppermute | solution.py:88
  67.5 7.7 %collective-permute-start.30 = (bf16[256,384]{1,0:T(8,128)(2,1)S(1)}, bf16[256,384]{1,0:T(8,128)(2,1)S(1)}, u32[]{:S(2)}, u32[]{:S(2)}) collective-permute-start(bf16[256,384]{1,0:T(8,128)(2,1)S(1)} %collective-permute-done.25.refs_1_), channel_id=1, source_target_pairs={{0,2},{1,9},{2,10},{3,7},{4,12},{5,1},{6,4},{7,15},{8,0},{9,17},{1... | collective-permute-start | bytes 589832 | tf_op jit(solution)/shard_map/ppermute | solution.py:88
  68.5 9.4 %collective-permute-start.27 = (bf16[384,384]{1,0:T(8,128)(2,1)S(1)}, bf16[384,384]{1,0:T(8,128)(2,1)S(1)}, u32[]{:S(2)}, u32[]{:S(2)}) collective-permute-start(bf16[384,384]{1,0:T(8,128)(2,1)S(1)} %get-tuple-element.87), channel_id=1, source_target_pairs={{0,4},{1,3},{2,6},{3,1},{4,0},{5,7},{6,2},{7,5},{8,12},{9,11},{10,... | collective-permute-start | bytes 884744 | tf_op jit(solution)/shard_map/ppermute | solution.py:59
  71.2 8.8 %collective-permute-start.26 = (bf16[192,384]{1,0:T(8,128)(2,1)S(1)}, bf16[192,384]{1,0:T(8,128)(2,1)S(1)}, u32[]{:S(2)}, u32[]{:S(2)}) collective-permute-start(bf16[192,384]{1,0:T(8,128)(2,1)S(1)} %get-tuple-element.86), channel_id=1, source_target_pairs={{0,1},{1,0},{2,3},{3,2},{4,5},{5,4},{6,7},{7,6},{8,9},{9,8},{10,11... | collective-permute-start | bytes 442376 | tf_op jit(solution)/shard_map/ppermute | solution.py:59
  73.9 5.8 %collective-permute-start.34 = (bf16[256,384]{1,0:T(8,128)(2,1)S(1)}, bf16[256,384]{1,0:T(8,128)(2,1)S(1)}, u32[]{:S(2)}, u32[]{:S(2)}) collective-permute-start(bf16[256,384]{1,0:T(8,128)(2,1)S(1)} %collective-permute-done.29.refs_0_), channel_id=1, source_target_pairs={{0,8},{1,5},{2,0},{3,11},{4,6},{5,13},{6,14},{7,3},{8,16},{9,1},{1... | collective-permute-start | bytes 589832 | tf_op jit(solution)/shard_map/ppermute | solution.py:88
  75.6 5.2 %collective-permute-start.32 = (bf16[192,384]{1,0:T(8,128)(2,1)S(1)}, bf16[192,384]{1,0:T(8,128)(2,1)S(1)}, u32[]{:S(2)}, u32[]{:S(2)}) collective-permute-start(bf16[192,384]{1,0:T(8,128)(2,1)S(1)} %get-tuple-element.98), channel_id=1, source_target_pairs={{0,4},{1,3},{2,6},{3,1},{4,0},{5,7},{6,2},{7,5},{8,12},{9,11},{10,... | collective-permute-start | bytes 442376 | tf_op jit(solution)/shard_map/ppermute | solution.py:59
  77.0 5.1 %collective-permute-start.33 = (bf16[192,384]{1,0:T(8,128)(2,1)S(1)}, bf16[192,384]{1,0:T(8,128)(2,1)S(1)}, u32[]{:S(2)}, u32[]{:S(2)}) collective-permute-start(bf16[192,384]{1,0:T(8,128)(2,1)S(1)} %get-tuple-element.97), channel_id=1, source_target_pairs={{0,5},{1,2},{2,7},{3,0},{4,1},{5,6},{6,3},{7,4},{8,13},{9,10},{10,... | collective-permute-start | bytes 442376 | tf_op jit(solution)/shard_map/ppermute | solution.py:59
  77.9 5.5 %collective-permute-start.31 = (bf16[192,384]{1,0:T(8,128)(2,1)S(1)}, bf16[192,384]{1,0:T(8,128)(2,1)S(1)}, u32[]{:S(2)}, u32[]{:S(2)}) collective-permute-start(bf16[192,384]{1,0:T(8,128)(2,1)S(1)} %get-tuple-element.91), channel_id=1, source_target_pairs={{0,1},{1,0},{2,3},{3,2},{4,5},{5,4},{6,7},{7,6},{8,9},{9,8},{10,11... | collective-permute-start | bytes 442376 | tf_op jit(solution)/shard_map/ppermute | solution.py:59
  79.7 4.4 %collective-permute-start.23 = (bf16[288,384]{1,0:T(8,128)(2,1)S(1)}, bf16[288,384]{1,0:T(8,128)(2,1)S(1)}, u32[]{:S(2)}, u32[]{:S(2)}) collective-permute-start(bf16[288,384]{1,0:T(8,128)(2,1)S(1)} %slice.24), channel_id=1, source_target_pairs={{0,1},{1,0},{2,3},{3,2},{4,5},{5,4},{6,7},{7,6},{8,9},{9,8},{10,11... | collective-permute-start | bytes 663560 | tf_op jit(solution)/shard_map/ppermute | solution.py:59
  80.0 4.2 %collective-permute-start.28 = (bf16[192,384]{1,0:T(8,128)(2,1)S(1)}, bf16[192,384]{1,0:T(8,128)(2,1)S(1)}, u32[]{:S(2)}, u32[]{:S(2)}) collective-permute-start(bf16[192,384]{1,0:T(8,128)(2,1)S(1)} %slice.25), channel_id=1, source_target_pairs={{0,1},{1,0},{2,3},{3,2},{4,5},{5,4},{6,7},{7,6},{8,9},{9,8},{10,11... | collective-permute-start | bytes 442376 | tf_op jit(solution)/shard_map/ppermute | solution.py:59
  80.8 4.4 %collective-permute-start.36 = (bf16[96,384]{1,0:T(8,128)(2,1)S(1)}, bf16[96,384]{1,0:T(8,128)(2,1)S(1)}, u32[]{:S(2)}, u32[]{:S(2)}) collective-permute-start(bf16[96,384]{1,0:T(8,128)(2,1)S(1)} %get-tuple-element.100), channel_id=1, source_target_pairs={{0,4},{1,3},{2,6},{3,1},{4,0},{5,7},{6,2},{7,5},{8,12},{9,11},{10,... | collective-permute-start | bytes 221192 | tf_op jit(solution)/shard_map/ppermute | solution.py:59
  82.2 3.8 %collective-permute-start.37 = (bf16[96,384]{1,0:T(8,128)(2,1)S(1)}, bf16[96,384]{1,0:T(8,128)(2,1)S(1)}, u32[]{:S(2)}, u32[]{:S(2)}) collective-permute-start(bf16[96,384]{1,0:T(8,128)(2,1)S(1)} %get-tuple-element.99), channel_id=1, source_target_pairs={{0,5},{1,2},{2,7},{3,0},{4,1},{5,6},{6,3},{7,4},{8,13},{9,10},{10,... | collective-permute-start | bytes 221192 | tf_op jit(solution)/shard_map/ppermute | solution.py:59
  83.4 2.6 %collective-permute-start.35 = (bf16[96,384]{1,0:T(8,128)(2,1)S(1)}, bf16[96,384]{1,0:T(8,128)(2,1)S(1)}, u32[]{:S(2)}, u32[]{:S(2)}) collective-permute-start(bf16[96,384]{1,0:T(8,128)(2,1)S(1)} %get-tuple-element.95), channel_id=1, source_target_pairs={{0,1},{1,0},{2,3},{3,2},{4,5},{5,4},{6,7},{7,6},{8,9},{9,8},{10,11... | collective-permute-start | bytes 221192 | tf_op jit(solution)/shard_map/ppermute | solution.py:59

commit v7 on v6

--- a/solution.py
+++ b/solution.py
@@ -15,7 +15,7 @@
 
 class Grid:
     def __init__(self, n_pair):
-        assert n_pair % 8 == 0
+        assert n_pair % 8 == 0 and n_pair > 8
         self.nz = n_pair // 8
         self.ring = 2 * self.nz
 
@@ -339,7 +339,7 @@
         in_specs=vmem(1 + len(pieces)),
         out_specs=pl.BlockSpec(memory_space=pl.ANY),
         scratch_shapes=[
-            pltpu.VMEM((width // LANES, pairs * each, LANES), F32),
+            pltpu.VMEM((width // LANES, (pairs + 1) * each, LANES), F32),
             pltpu.VMEM((each, width, pairs), BF16),
             pltpu.SemaphoreType.DMA((each,)),
         ],
@@ -417,8 +417,7 @@
         groups.append(group)
         nonlocal before
         before, ready = arrived, before
-        gates = [[kept,*ready[:3]],[kept,*ready[:2]]]
-        return gates[len(groups) - 1] if len(groups) <= len(gates) else []
+        return [kept, *ready[:2]]
 
     gather_ring(grid, half_first, transform)
     assert groups == in_order

time: 88.4 us -> 88.4 us (level)
  no operation moved by 1% of the time
where the time goes in v7:
time: 88.4 us; the launch traced here: 88.2 us
  waiting for transfers between devices  40.6 us (46%)
  starting transfers between devices  35.7 us (40%)
  Pallas kernels  11.1 us (13%)
    ppermute x24, waiting for transfers between devices, send(): lax.ppermute(block, 'pair', [(device, int(target(device))) for device in...  25.3 us
    ppermute x24, starting transfers between devices, send(): lax.ppermute(block, 'pair', [(device, int(target(device))) for device in...  20.5 us
    ppermute x14, waiting for transfers between devices, gather_ring(): held[way * step] = lax.ppermute(block, 'pair', around[way])  15.3 us
    ppermute x14, starting transfers between devices, gather_ring(): held[way * step] = lax.ppermute(block, 'pair', around[way])  15.1 us
    pallas_call x4, Pallas kernels, first_product(): pl.pallas_call(body, out_shape=shapes, in_specs=vmem(4 + len(totals) + le...  2.99 us
    pallas_call x1, Pallas kernels, share_integrals(): pl.pallas_call(body, out_shape=[jax.ShapeDtypeStruct((rows + batch_rows *...  2.52 us
    pallas_call x1, Pallas kernels, place_pairs(): pl.pallas_call(body, out_shape=jax.ShapeDtypeStruct((2, share, width, pai...  2.29 us
  transfers between devices with their start and end apart: 38, of which 18 were waited for; matrix products, arithmetic and copies ran while one was open for 0% of the time, Pallas kernels for 9%

profile of v7, /device:TPU:0, one launch (start us, length us, event | category | flops | bytes accessed | tf_op | source)
XLA Modules:
  0.0 88.2 jit_solution(6515816586620111132)
XLA Ops:
  0.0 3.0 %collective-permute-start.9 = (bf16[2,256,384]{2,1,0:T(8,128)(2,1)}, bf16[2,256,384]{2,1,0:T(8,128)(2,1)S(1)}, u32[]{:S(2)}, u32[]{:S(2)}) collective-permute-start(bf16[2,256,384]{2,1,0:T(8,128)(2,1)} %refs_4_.1), channel_id=1, source_target_pairs={{0,8},{1,5},{2,0},{3,11},{4,6},{5,13},{6,14},{7,3},{8,16},{9,1},{1... | collective-permute-start | bytes 1179656 | tf_op jit(solution)/shard_map/ppermute | solution.py:88
  3.0 0.7 copy-done.1
  3.7 2.5 %share_integrals.1 = (bf16[160,768]{1,0:T(8,128)(2,1)S(1)}, bf16[128,768]{1,0:T(8,128)(2,1)S(1)}, bf16[128,768]{1,0:T(8,128)(2,1)S(1)}, bf16[128,768]{1,0:T(8,12...) custom-call(s32[1]{0:T(128)} %bitcast.where_ref, ...), custom_call_target="tpu_custom_call" | custom-call | tf_op jit(solution)/shard_map/share_integrals/pallas_call | solution.py:134
  6.2 5.5 %collective-permute-done.9.refs_5_ = bf16[2,256,384]{2,1,0:T(8,128)(2,1)S(1)} collective-permute-done((bf16[2,256,384]{2,1,0:T(8,128)(2,1)}, bf16[2,256,384]{2,1,0:T(8,128)(2,1)S(1)}, u32[]{:S(2)}, u32[]{:S(2)}) %collective-permute-start.9) | collective-permute-done | bytes 393248 | tf_op jit(solution)/shard_map/ppermute | solution.py:88
  11.7 2.4 %collective-permute-start.11 = (bf16[2,256,384]{2,1,0:T(8,128)(2,1)S(1)}, bf16[2,256,384]{2,1,0:T(8,128)(2,1)S(1)}, u32[]{:S(2)}, u32[]{:S(2)}) collective-permute-start(bf16[2,256,384]{2,1,0:T(8,128)(2,1)S(1)} %collective-permute-done.9.refs_5_), channel_id=1, source_target_pairs={{0,8},{1,5},{2,0},{3,11},{4,6},{5,13},{6,14},{7,3},{8,16},{9,1},{1... | collective-permute-start | bytes 1179656 | tf_op jit(solution)/shard_map/ppermute | solution.py:88
  14.1 0.9 collective-permute-start.12
  15.0 2.1 %collective-permute-start.7 = (bf16[128,768]{1,0:T(8,128)(2,1)S(1)}, bf16[128,768]{1,0:T(8,128)(2,1)S(1)}, u32[]{:S(2)}, u32[]{:S(2)}) collective-permute-start(bf16[128,768]{1,0:T(8,128)(2,1)S(1)} %get-tuple-element.67), channel_id=1, source_target_pairs={{0,4},{1,3},{2,6},{3,1},{4,0},{5,7},{6,2},{7,5},{8,12},{9,11},{10,... | collective-permute-start | bytes 589832 | tf_op jit(solution)/shard_map/ppermute | solution.py:59
  17.0 0.1 collective-permute-start.8
  17.2 5.7 %collective-permute-done.7.refs_2_ = bf16[128,768]{1,0:T(8,128)(2,1)S(1)} collective-permute-done((bf16[128,768]{1,0:T(8,128)(2,1)S(1)}, bf16[128,768]{1,0:T(8,128)(2,1)S(1)}, u32[]{:S(2)}, u32[]{:S(2)}) %collective-permute-start.7) | collective-permute-done | bytes 196640 | tf_op jit(solution)/shard_map/ppermute | solution.py:59
  22.9 1.6 %collective-permute-done.8.refs_3_ = bf16[128,768]{1,0:T(8,128)(2,1)S(1)} collective-permute-done((bf16[128,768]{1,0:T(8,128)(2,1)S(1)}, bf16[128,768]{1,0:T(8,128)(2,1)S(1)}, u32[]{:S(2)}, u32[]{:S(2)}) %collective-permute-start.8) | collective-permute-done | bytes 196640 | tf_op jit(solution)/shard_map/ppermute | solution.py:59
  24.5 2.3 %collective-permute-start.3 = (bf16[128,512]{1,0:T(8,128)(2,1)S(1)}, bf16[128,512]{1,0:T(8,128)(2,1)S(1)}, u32[]{:S(2)}, u32[]{:S(2)}) collective-permute-start(bf16[128,512]{1,0:T(8,128)(2,1)S(1)} %get-tuple-element.60), channel_id=1, source_target_pairs={{0,1},{1,0},{2,3},{3,2},{4,5},{5,4},{6,7},{7,6},{8,9},{9,8},{10,11... | collective-permute-start | bytes 393224 | tf_op jit(solution)/shard_map/ppermute | solution.py:59
  26.8 0.3 collective-permute-start.4
  27.1 1.1 %collective-permute-start.5 = (bf16[128,512]{1,0:T(8,128)(2,1)S(1)}, bf16[128,512]{1,0:T(8,128)(2,1)S(1)}, u32[]{:S(2)}, u32[]{:S(2)}) collective-permute-start(bf16[128,512]{1,0:T(8,128)(2,1)S(1)} %get-tuple-element.64), channel_id=1, source_target_pairs={{0,3},{1,4},{2,1},{3,6},{4,7},{5,0},{6,5},{7,2},{8,11},{9,12},{10,... | collective-permute-start | bytes 393224 | tf_op jit(solution)/shard_map/ppermute | solution.py:59
  28.1 0.4 collective-permute-start.14
  28.6 1.0 %first_product.4.refs_4_ = f32[544,768]{1,0:T(8,128)S(1)} custom-call(bf16[160,768]{1,0:T(8,128)(2,1)S(1)} %get-tuple-element.65.refs_0_, bf16[128,768]{1,0:T(8,128)(2,1)S(1)} %collective-permute-done.6.refs_1_, bf16[128,768]{1,0:T(8,128)(2,1)S(1)} %collective-permute-done.7.refs_2_, bf16[128,768]{1,0:T(8,128)(2,1)S(1)} %collective-permute-done.8.refs_3_, ...), custom_call_target="tpu_custom_call" | custom-call | flops 3208642560 | tf_op jit(solution)/shard_map/first_product/pallas_call | solution.py:184
  29.6 0.5 collective-permute-start
  30.1 3.1 %collective-permute-done.4.refs_2_ = bf16[128,512]{1,0:T(8,128)(2,1)S(1)} collective-permute-done((bf16[128,512]{1,0:T(8,128)(2,1)S(1)}, bf16[128,512]{1,0:T(8,128)(2,1)S(1)}, u32[]{:S(2)}, u32[]{:S(2)}) %collective-permute-start.4) | collective-permute-done | bytes 131104 | tf_op jit(solution)/shard_map/ppermute | solution.py:59
  33.2 0.3 collective-permute-start.1
  33.4 0.3 collective-permute-start.2
  33.7 0.7 collective-permute-start.15
  34.4 0.7 first_product.5.refs_4_
  35.2 5.8 %collective-permute-done.1.refs_2_ = bf16[128,768]{1,0:T(8,128)(2,1)S(1)} collective-permute-done((bf16[128,768]{1,0:T(8,128)(2,1)S(1)}, bf16[128,768]{1,0:T(8,128)(2,1)S(1)}, u32[]{:S(2)}, u32[]{:S(2)}) %collective-permute-start.1) | collective-permute-done | bytes 196640 | tf_op jit(solution)/shard_map/ppermute | solution.py:59
  41.0 0.3 collective-permute-done.2.refs_3_
  41.3 0.7 first_product.6.refs_4_
  42.1 2.7 %collective-permute-done.15.refs_5_ = bf16[2,256,384]{2,1,0:T(8,128)(2,1)S(1)} collective-permute-done((bf16[2,256,384]{2,1,0:T(8,128)(2,1)S(1)}, bf16[2,256,384]{2,1,0:T(8,128)(2,1)S(1)}, u32[]{:S(2)}, u32[]{:S(2)}) %collective-permute-start.15) | collective-permute-done | bytes 393248 | tf_op jit(solution)/shard_map/ppermute | solution.py:88
  44.8 0.5 first_product.7
  45.2 0.1 collective-permute-start.16
  45.3 1.0 %collective-permute-start.17 = (bf16[160,768]{1,0:T(8,128)(2,1)S(1)}, bf16[160,768]{1,0:T(8,128)(2,1)S(1)}, u32[]{:S(2)}, u32[]{:S(2)}) collective-permute-start(bf16[160,768]{1,0:T(8,128)(2,1)S(1)} %get-tuple-element.76), channel_id=1, source_target_pairs={{0,4},{1,3},{2,6},{3,1},{4,0},{5,7},{6,2},{7,5},{8,12},{9,11},{10,... | collective-permute-start | bytes 737288 | tf_op jit(solution)/shard_map/ppermute | solution.py:59
  46.3 1.5 %collective-permute-start.18 = (bf16[160,768]{1,0:T(8,128)(2,1)S(1)}, bf16[160,768]{1,0:T(8,128)(2,1)S(1)}, u32[]{:S(2)}, u32[]{:S(2)}) collective-permute-start(bf16[160,768]{1,0:T(8,128)(2,1)S(1)} %get-tuple-element.77), channel_id=1, source_target_pairs={{0,5},{1,2},{2,7},{3,0},{4,1},{5,6},{6,3},{7,4},{8,13},{9,10},{10,... | collective-permute-start | bytes 737288 | tf_op jit(solution)/shard_map/ppermute | solution.py:59
  47.8 3.8 %collective-permute-done.17.refs_2_ = bf16[160,768]{1,0:T(8,128)(2,1)S(1)} collective-permute-done((bf16[160,768]{1,0:T(8,128)(2,1)S(1)}, bf16[160,768]{1,0:T(8,128)(2,1)S(1)}, u32[]{:S(2)}, u32[]{:S(2)}) %collective-permute-start.17) | collective-permute-done | bytes 245792 | tf_op jit(solution)/shard_map/ppermute | solution.py:59
  51.6 2.1 %collective-permute-done.18.refs_3_ = bf16[160,768]{1,0:T(8,128)(2,1)S(1)} collective-permute-done((bf16[160,768]{1,0:T(8,128)(2,1)S(1)}, bf16[160,768]{1,0:T(8,128)(2,1)S(1)}, u32[]{:S(2)}, u32[]{:S(2)}) %collective-permute-start.18) | collective-permute-done | bytes 245792 | tf_op jit(solution)/shard_map/ppermute | solution.py:59
  53.7 0.1 add_partners.1
  53.8 0.1 collective-permute-start.19
  53.8 2.0 %collective-permute-start.20 = (bf16[256,384]{1,0:T(8,128)(2,1)S(1)}, bf16[256,384]{1,0:T(8,128)(2,1)S(1)}, u32[]{:S(2)}, u32[]{:S(2)}) collective-permute-start(bf16[256,384]{1,0:T(8,128)(2,1)S(1)} %get-tuple-element.79.refs_0_), channel_id=1, source_target_pairs={{0,2},{1,9},{2,10},{3,7},{4,12},{5,1},{6,4},{7,15},{8,0},{9,17},{1... | collective-permute-start | bytes 589832 | tf_op jit(solution)/shard_map/ppermute | solution.py:88
  55.8 0.5 pair_places.1.place_ref
  56.3 1.2 %weights.1.matrix_ref = bf16[384,256]{1,0:T(8,128)(2,1)S(1)} custom-call(s32[1]{0:T(128)} %bitcast.where_ref, bf16[64,384]{1,0:T(8,128)(2,1)S(1)} %get-tuple-element.78.batch_ref), custom_call_target="tpu_custom_call" | custom-call | tf_op jit(solution)/shard_map/weights/pallas_call | solution.py:249
  57.6 1.9 %collective-permute-done.19.refs_1_ = bf16[256,384]{1,0:T(8,128)(2,1)S(1)} collective-permute-done((bf16[256,384]{1,0:T(8,128)(2,1)S(1)}, bf16[256,384]{1,0:T(8,128)(2,1)S(1)}, u32[]{:S(2)}, u32[]{:S(2)}) %collective-permute-start.19) | collective-permute-done | bytes 196640 | tf_op jit(solution)/shard_map/ppermute | solution.py:88
  59.5 1.0 %collective-permute-start.24 = (bf16[256,384]{1,0:T(8,128)(2,1)S(1)}, bf16[256,384]{1,0:T(8,128)(2,1)S(1)}, u32[]{:S(2)}, u32[]{:S(2)}) collective-permute-start(bf16[256,384]{1,0:T(8,128)(2,1)S(1)} %collective-permute-done.19.refs_1_), channel_id=1, source_target_pairs={{0,8},{1,5},{2,0},{3,11},{4,6},{5,13},{6,14},{7,3},{8,16},{9,1},{1... | collective-permute-start | bytes 589832 | tf_op jit(solution)/shard_map/ppermute | solution.py:88
  60.4 0.5 collective-permute-done.20.refs_2_
  61.0 0.8 collective-permute-start.25
  61.8 0.5 second_product.4
  62.2 0.2 collective-permute-start.21
  62.5 2.2 %collective-permute-start.22 = (bf16[576,384]{1,0:T(8,128)(2,1)S(1)}, bf16[576,384]{1,0:T(8,128)(2,1)S(1)}, u32[]{:S(2)}, u32[]{:S(2)}) collective-permute-start(bf16[576,384]{1,0:T(8,128)(2,1)S(1)} %get-tuple-element.82), channel_id=1, source_target_pairs={{0,4},{1,3},{2,6},{3,1},{4,0},{5,7},{6,2},{7,5},{8,12},{9,11},{10,... | collective-permute-start | bytes 1327112 | tf_op jit(solution)/shard_map/ppermute | solution.py:59
  64.7 0.7 collective-permute-done.24.refs_0_
  65.4 2.1 %collective-permute-start.29 = (bf16[256,384]{1,0:T(8,128)(2,1)S(1)}, bf16[256,384]{1,0:T(8,128)(2,1)S(1)}, u32[]{:S(2)}, u32[]{:S(2)}) collective-permute-start(bf16[256,384]{1,0:T(8,128)(2,1)S(1)} %collective-permute-done.24.refs_0_), channel_id=1, source_target_pairs={{0,8},{1,5},{2,0},{3,11},{4,6},{5,13},{6,14},{7,3},{8,16},{9,1},{1... | collective-permute-start | bytes 589832 | tf_op jit(solution)/shard_map/ppermute | solution.py:88
  67.5 0.7 collective-permute-start.30
  68.1 0.4 second_product.5
  68.5 2.7 %collective-permute-start.27 = (bf16[384,384]{1,0:T(8,128)(2,1)S(1)}, bf16[384,384]{1,0:T(8,128)(2,1)S(1)}, u32[]{:S(2)}, u32[]{:S(2)}) collective-permute-start(bf16[384,384]{1,0:T(8,128)(2,1)S(1)} %get-tuple-element.87), channel_id=1, source_target_pairs={{0,4},{1,3},{2,6},{3,1},{4,0},{5,7},{6,2},{7,5},{8,12},{9,11},{10,... | collective-permute-start | bytes 884744 | tf_op jit(solution)/shard_map/ppermute | solution.py:59
  71.2 2.8 %collective-permute-done.29.refs_0_ = bf16[256,384]{1,0:T(8,128)(2,1)S(1)} collective-permute-done((bf16[256,384]{1,0:T(8,128)(2,1)S(1)}, bf16[256,384]{1,0:T(8,128)(2,1)S(1)}, u32[]{:S(2)}, u32[]{:S(2)}) %collective-permute-start.29) | collective-permute-done | bytes 196640 | tf_op jit(solution)/shard_map/ppermute | solution.py:88
  73.9 1.2 %collective-permute-start.34 = (bf16[256,384]{1,0:T(8,128)(2,1)S(1)}, bf16[256,384]{1,0:T(8,128)(2,1)S(1)}, u32[]{:S(2)}, u32[]{:S(2)}) collective-permute-start(bf16[256,384]{1,0:T(8,128)(2,1)S(1)} %collective-permute-done.29.refs_0_), channel_id=1, source_target_pairs={{0,8},{1,5},{2,0},{3,11},{4,6},{5,13},{6,14},{7,3},{8,16},{9,1},{1... | collective-permute-start | bytes 589832 | tf_op jit(solution)/shard_map/ppermute | solution.py:88
  75.2 0.4 second_product.6
  75.6 1.5 %collective-permute-start.32 = (bf16[192,384]{1,0:T(8,128)(2,1)S(1)}, bf16[192,384]{1,0:T(8,128)(2,1)S(1)}, u32[]{:S(2)}, u32[]{:S(2)}) collective-permute-start(bf16[192,384]{1,0:T(8,128)(2,1)S(1)} %get-tuple-element.98), channel_id=1, source_target_pairs={{0,4},{1,3},{2,6},{3,1},{4,0},{5,7},{6,2},{7,5},{8,12},{9,11},{10,... | collective-permute-start | bytes 442376 | tf_op jit(solution)/shard_map/ppermute | solution.py:59
  77.1 0.8 collective-permute-done.27.refs_6_
  77.9 0.7 collective-permute-start.31
  78.6 1.1 %collective-permute-done.34.refs_0_ = bf16[256,384]{1,0:T(8,128)(2,1)S(1)} collective-permute-done((bf16[256,384]{1,0:T(8,128)(2,1)S(1)}, bf16[256,384]{1,0:T(8,128)(2,1)S(1)}, u32[]{:S(2)}, u32[]{:S(2)}) %collective-permute-start.34) | collective-permute-done | bytes 196640 | tf_op jit(solution)/shard_map/ppermute | solution.py:88
  79.7 0.3 second_product.7
  80.0 0.6 collective-permute-start.28
  80.6 0.2 collective-permute-done.32.refs_10_
  80.8 1.4 %collective-permute-start.36 = (bf16[96,384]{1,0:T(8,128)(2,1)S(1)}, bf16[96,384]{1,0:T(8,128)(2,1)S(1)}, u32[]{:S(2)}, u32[]{:S(2)}) collective-permute-start(bf16[96,384]{1,0:T(8,128)(2,1)S(1)} %get-tuple-element.100), channel_id=1, source_target_pairs={{0,4},{1,3},{2,6},{3,1},{4,0},{5,7},{6,2},{7,5},{8,12},{9,11},{10,... | collective-permute-start | bytes 221192 | tf_op jit(solution)/shard_map/ppermute | solution.py:59
  82.2 1.2 %collective-permute-start.37 = (bf16[96,384]{1,0:T(8,128)(2,1)S(1)}, bf16[96,384]{1,0:T(8,128)(2,1)S(1)}, u32[]{:S(2)}, u32[]{:S(2)}) collective-permute-start(bf16[96,384]{1,0:T(8,128)(2,1)S(1)} %get-tuple-element.99), channel_id=1, source_target_pairs={{0,5},{1,2},{2,7},{3,0},{4,1},{5,6},{6,3},{7,4},{8,13},{9,10},{10,... | collective-permute-start | bytes 221192 | tf_op jit(solution)/shard_map/ppermute | solution.py:59
  83.4 0.8 collective-permute-start.35
  84.1 1.0 %collective-permute-done.36.refs_14_ = bf16[96,384]{1,0:T(8,128)(2,1)S(1)} collective-permute-done((bf16[96,384]{1,0:T(8,128)(2,1)S(1)}, bf16[96,384]{1,0:T(8,128)(2,1)S(1)}, u32[]{:S(2)}, u32[]{:S(2)}) %collective-permute-start.36) | collective-permute-done | bytes 73760 | tf_op jit(solution)/shard_map/ppermute | solution.py:59
  85.1 0.8 collective-permute-done.37.refs_15_
  86.0 2.3 %place_pairs.1 = bf16[2,12,384,128]{3,2,1,0:T(8,128)(2,1)} custom-call(bf16[128,128]{1,0:T(8,128)(2,1)S(1)} %pair_places.1.place_ref, bf16[288,384]{1,0:T(8,128)(2,1)S(1)} %get-tuple-element.80.refs_0_, bf16[288,384]{1,0:T(8,128)(2,1)S(1)} %collective-permute-done.21.refs_1_, bf16[576,384]{1,0:T(8,128)(2,1)S(1)} %collective-permute-done.22.refs_2_, ...), custom_call_target="tpu_custom_call" | custom-call | tf_op jit(solution)/shard_map/place_pairs/pallas_call | solution.py:336
  (35 shorter events, 0.2 us)
Async XLA Ops:
  0.0 11.7 %collective-permute-start.9 = (bf16[2,256,384]{2,1,0:T(8,128)(2,1)}, bf16[2,256,384]{2,1,0:T(8,128)(2,1)S(1)}, u32[]{:S(2)}, u32[]{:S(2)}) collective-permute-start(bf16[2,256,384]{2,1,0:T(8,128)(2,1)} %refs_4_.1), channel_id=1, source_target_pairs={{0,8},{1,5},{2,0},{3,11},{4,6},{5,13},{6,14},{7,3},{8,16},{9,1},{1... | collective-permute-start | bytes 1179656 | tf_op jit(solution)/shard_map/ppermute | solution.py:88
  3.0 11.1 %collective-permute-start.10 = (bf16[2,256,384]{2,1,0:T(8,128)(2,1)}, bf16[2,256,384]{2,1,0:T(8,128)(2,1)S(1)}, u32[]{:S(2)}, u32[]{:S(2)}) collective-permute-start(bf16[2,256,384]{2,1,0:T(8,128)(2,1)} %refs_4_.1), channel_id=1, source_target_pairs={{0,2},{1,9},{2,10},{3,7},{4,12},{5,1},{6,4},{7,15},{8,0},{9,17},{1... | collective-permute-start | bytes 1179656 | tf_op jit(solution)/shard_map/ppermute | solution.py:88
  3.0 0.7 copy-start.1
  3.7 24.9 %copy-start.2 = (bf16[2,256,384]{2,1,0:T(8,128)(2,1)S(1)}, bf16[2,256,384]{2,1,0:T(8,128)(2,1)}, u32[]{:S(2)}) copy-start(bf16[2,256,384]{2,1,0:T(8,128)(2,1)} %refs_4_.1) | copy-start | bytes 1179652
  11.7 12.8 %collective-permute-start.11 = (bf16[2,256,384]{2,1,0:T(8,128)(2,1)S(1)}, bf16[2,256,384]{2,1,0:T(8,128)(2,1)S(1)}, u32[]{:S(2)}, u32[]{:S(2)}) collective-permute-start(bf16[2,256,384]{2,1,0:T(8,128)(2,1)S(1)} %collective-permute-done.9.refs_5_), channel_id=1, source_target_pairs={{0,8},{1,5},{2,0},{3,11},{4,6},{5,13},{6,14},{7,3},{8,16},{9,1},{1... | collective-permute-start | bytes 1179656 | tf_op jit(solution)/shard_map/ppermute | solution.py:88
  14.1 14.0 %collective-permute-start.12 = (bf16[2,256,384]{2,1,0:T(8,128)(2,1)S(1)}, bf16[2,256,384]{2,1,0:T(8,128)(2,1)S(1)}, u32[]{:S(2)}, u32[]{:S(2)}) collective-permute-start(bf16[2,256,384]{2,1,0:T(8,128)(2,1)S(1)} %collective-permute-done.10.refs_6_), channel_id=1, source_target_pairs={{0,2},{1,9},{2,10},{3,7},{4,12},{5,1},{6,4},{7,15},{8,0},{9,17},{1... | collective-permute-start | bytes 1179656 | tf_op jit(solution)/shard_map/ppermute | solution.py:88
  15.0 2.2 %collective-permute-start.6 = (bf16[128,768]{1,0:T(8,128)(2,1)S(1)}, bf16[128,768]{1,0:T(8,128)(2,1)S(1)}, u32[]{:S(2)}, u32[]{:S(2)}) collective-permute-start(bf16[128,768]{1,0:T(8,128)(2,1)S(1)} %get-tuple-element.66), channel_id=1, source_target_pairs={{0,1},{1,0},{2,3},{3,2},{4,5},{5,4},{6,7},{7,6},{8,9},{9,8},{10,11... | collective-permute-start | bytes 589832 | tf_op jit(solution)/shard_map/ppermute | solution.py:59
  15.0 7.9 %collective-permute-start.7 = (bf16[128,768]{1,0:T(8,128)(2,1)S(1)}, bf16[128,768]{1,0:T(8,128)(2,1)S(1)}, u32[]{:S(2)}, u32[]{:S(2)}) collective-permute-start(bf16[128,768]{1,0:T(8,128)(2,1)S(1)} %get-tuple-element.67), channel_id=1, source_target_pairs={{0,4},{1,3},{2,6},{3,1},{4,0},{5,7},{6,2},{7,5},{8,12},{9,11},{10,... | collective-permute-start | bytes 589832 | tf_op jit(solution)/shard_map/ppermute | solution.py:59
  17.0 7.5 %collective-permute-start.8 = (bf16[128,768]{1,0:T(8,128)(2,1)S(1)}, bf16[128,768]{1,0:T(8,128)(2,1)S(1)}, u32[]{:S(2)}, u32[]{:S(2)}) collective-permute-start(bf16[128,768]{1,0:T(8,128)(2,1)S(1)} %get-tuple-element.68), channel_id=1, source_target_pairs={{0,3},{1,4},{2,1},{3,6},{4,7},{5,0},{6,5},{7,2},{8,11},{9,12},{10,... | collective-permute-start | bytes 589832 | tf_op jit(solution)/shard_map/ppermute | solution.py:59
  24.5 9.2 %collective-permute-start.13 = (bf16[2,256,384]{2,1,0:T(8,128)(2,1)S(1)}, bf16[2,256,384]{2,1,0:T(8,128)(2,1)S(1)}, u32[]{:S(2)}, u32[]{:S(2)}) collective-permute-start(bf16[2,256,384]{2,1,0:T(8,128)(2,1)S(1)} %collective-permute-done.11.refs_5_), channel_id=1, source_target_pairs={{0,8},{1,5},{2,0},{3,11},{4,6},{5,13},{6,14},{7,3},{8,16},{9,1},{1... | collective-permute-start | bytes 1179656 | tf_op jit(solution)/shard_map/ppermute | solution.py:88
  24.5 5.1 %collective-permute-start.3 = (bf16[128,512]{1,0:T(8,128)(2,1)S(1)}, bf16[128,512]{1,0:T(8,128)(2,1)S(1)}, u32[]{:S(2)}, u32[]{:S(2)}) collective-permute-start(bf16[128,512]{1,0:T(8,128)(2,1)S(1)} %get-tuple-element.60), channel_id=1, source_target_pairs={{0,1},{1,0},{2,3},{3,2},{4,5},{5,4},{6,7},{7,6},{8,9},{9,8},{10,11... | collective-permute-start | bytes 393224 | tf_op jit(solution)/shard_map/ppermute | solution.py:59
  26.8 6.4 %collective-permute-start.4 = (bf16[128,512]{1,0:T(8,128)(2,1)S(1)}, bf16[128,512]{1,0:T(8,128)(2,1)S(1)}, u32[]{:S(2)}, u32[]{:S(2)}) collective-permute-start(bf16[128,512]{1,0:T(8,128)(2,1)S(1)} %get-tuple-element.62), channel_id=1, source_target_pairs={{0,4},{1,3},{2,6},{3,1},{4,0},{5,7},{6,2},{7,5},{8,12},{9,11},{10,... | collective-permute-start | bytes 393224 | tf_op jit(solution)/shard_map/ppermute | solution.py:59
  27.1 6.4 %collective-permute-start.5 = (bf16[128,512]{1,0:T(8,128)(2,1)S(1)}, bf16[128,512]{1,0:T(8,128)(2,1)S(1)}, u32[]{:S(2)}, u32[]{:S(2)}) collective-permute-start(bf16[128,512]{1,0:T(8,128)(2,1)S(1)} %get-tuple-element.64), channel_id=1, source_target_pairs={{0,3},{1,4},{2,1},{3,6},{4,7},{5,0},{6,5},{7,2},{8,11},{9,12},{10,... | collective-permute-start | bytes 393224 | tf_op jit(solution)/shard_map/ppermute | solution.py:59
  28.1 13.2 %collective-permute-start.14 = (bf16[2,256,384]{2,1,0:T(8,128)(2,1)S(1)}, bf16[2,256,384]{2,1,0:T(8,128)(2,1)S(1)}, u32[]{:S(2)}, u32[]{:S(2)}) collective-permute-start(bf16[2,256,384]{2,1,0:T(8,128)(2,1)S(1)} %collective-permute-done.12.refs_6_), channel_id=1, source_target_pairs={{0,2},{1,9},{2,10},{3,7},{4,12},{5,1},{6,4},{7,15},{8,0},{9,17},{1... | collective-permute-start | bytes 1179656 | tf_op jit(solution)/shard_map/ppermute | solution.py:88
  29.6 5.5 %collective-permute-start = (bf16[128,768]{1,0:T(8,128)(2,1)S(1)}, bf16[128,768]{1,0:T(8,128)(2,1)S(1)}, u32[]{:S(2)}, u32[]{:S(2)}) collective-permute-start(bf16[128,768]{1,0:T(8,128)(2,1)S(1)} %get-tuple-element.53), channel_id=1, source_target_pairs={{0,1},{1,0},{2,3},{3,2},{4,5},{5,4},{6,7},{7,6},{8,9},{9,8},{10,11... | collective-permute-start | bytes 589832 | tf_op jit(solution)/shard_map/ppermute | solution.py:59
  33.2 7.8 %collective-permute-start.1 = (bf16[128,768]{1,0:T(8,128)(2,1)S(1)}, bf16[128,768]{1,0:T(8,128)(2,1)S(1)}, u32[]{:S(2)}, u32[]{:S(2)}) collective-permute-start(bf16[128,768]{1,0:T(8,128)(2,1)S(1)} %get-tuple-element.55), channel_id=1, source_target_pairs={{0,4},{1,3},{2,6},{3,1},{4,0},{5,7},{6,2},{7,5},{8,12},{9,11},{10,... | collective-permute-start | bytes 589832 | tf_op jit(solution)/shard_map/ppermute | solution.py:59
  33.4 7.9 %collective-permute-start.2 = (bf16[128,768]{1,0:T(8,128)(2,1)S(1)}, bf16[128,768]{1,0:T(8,128)(2,1)S(1)}, u32[]{:S(2)}, u32[]{:S(2)}) collective-permute-start(bf16[128,768]{1,0:T(8,128)(2,1)S(1)} %get-tuple-element.57), channel_id=1, source_target_pairs={{0,3},{1,4},{2,1},{3,6},{4,7},{5,0},{6,5},{7,2},{8,11},{9,12},{10,... | collective-permute-start | bytes 589832 | tf_op jit(solution)/shard_map/ppermute | solution.py:59
  33.7 11.0 %collective-permute-start.15 = (bf16[2,256,384]{2,1,0:T(8,128)(2,1)S(1)}, bf16[2,256,384]{2,1,0:T(8,128)(2,1)S(1)}, u32[]{:S(2)}, u32[]{:S(2)}) collective-permute-start(bf16[2,256,384]{2,1,0:T(8,128)(2,1)S(1)} %collective-permute-done.13.refs_5_), channel_id=1, source_target_pairs={{0,8},{1,5},{2,0},{3,11},{4,6},{5,13},{6,14},{7,3},{8,16},{9,1},{1... | collective-permute-start | bytes 1179656 | tf_op jit(solution)/shard_map/ppermute | solution.py:88
  42.1 13.8 %copy-start = (s32[1,128]{1,0:T(1,128)S(1)}, s32[1,128]{1,0:T(1,128)}, u32[]{:S(2)}) copy-start(s32[1,128]{1,0:T(1,128)} %pair_ref.1) | copy-start | bytes 1540
  45.2 8.4 %collective-permute-start.16 = (f32[160,768]{1,0:T(8,128)S(1)}, f32[160,768]{1,0:T(8,128)S(1)}, u32[]{:S(2)}, u32[]{:S(2)}) collective-permute-start(f32[160,768]{1,0:T(8,128)S(1)} %get-tuple-element.75), channel_id=1, source_target_pairs={{0,1},{1,0},{2,3},{3,2},{4,5},{5,4},{6,7},{7,6},{8,9},{9,8},{10,11... | collective-permute-start | bytes 1474568 | tf_op jit(solution)/shard_map/ppermute | solution.py:59
  45.3 6.3 %collective-permute-start.17 = (bf16[160,768]{1,0:T(8,128)(2,1)S(1)}, bf16[160,768]{1,0:T(8,128)(2,1)S(1)}, u32[]{:S(2)}, u32[]{:S(2)}) collective-permute-start(bf16[160,768]{1,0:T(8,128)(2,1)S(1)} %get-tuple-element.76), channel_id=1, source_target_pairs={{0,4},{1,3},{2,6},{3,1},{4,0},{5,7},{6,2},{7,5},{8,12},{9,11},{10,... | collective-permute-start | bytes 737288 | tf_op jit(solution)/shard_map/ppermute | solution.py:59
  46.3 7.3 %collective-permute-start.18 = (bf16[160,768]{1,0:T(8,128)(2,1)S(1)}, bf16[160,768]{1,0:T(8,128)(2,1)S(1)}, u32[]{:S(2)}, u32[]{:S(2)}) collective-permute-start(bf16[160,768]{1,0:T(8,128)(2,1)S(1)} %get-tuple-element.77), channel_id=1, source_target_pairs={{0,5},{1,2},{2,7},{3,0},{4,1},{5,6},{6,3},{7,4},{8,13},{9,10},{10,... | collective-permute-start | bytes 737288 | tf_op jit(solution)/shard_map/ppermute | solution.py:59
  53.8 5.7 %collective-permute-start.19 = (bf16[256,384]{1,0:T(8,128)(2,1)S(1)}, bf16[256,384]{1,0:T(8,128)(2,1)S(1)}, u32[]{:S(2)}, u32[]{:S(2)}) collective-permute-start(bf16[256,384]{1,0:T(8,128)(2,1)S(1)} %get-tuple-element.79.refs_0_), channel_id=1, source_target_pairs={{0,8},{1,5},{2,0},{3,11},{4,6},{5,13},{6,14},{7,3},{8,16},{9,1},{1... | collective-permute-start | bytes 589832 | tf_op jit(solution)/shard_map/ppermute | solution.py:88
  53.8 7.2 %collective-permute-start.20 = (bf16[256,384]{1,0:T(8,128)(2,1)S(1)}, bf16[256,384]{1,0:T(8,128)(2,1)S(1)}, u32[]{:S(2)}, u32[]{:S(2)}) collective-permute-start(bf16[256,384]{1,0:T(8,128)(2,1)S(1)} %get-tuple-element.79.refs_0_), channel_id=1, source_target_pairs={{0,2},{1,9},{2,10},{3,7},{4,12},{5,1},{6,4},{7,15},{8,0},{9,17},{1... | collective-permute-start | bytes 589832 | tf_op jit(solution)/shard_map/ppermute | solution.py:88
  59.5 5.9 %collective-permute-start.24 = (bf16[256,384]{1,0:T(8,128)(2,1)S(1)}, bf16[256,384]{1,0:T(8,128)(2,1)S(1)}, u32[]{:S(2)}, u32[]{:S(2)}) collective-permute-start(bf16[256,384]{1,0:T(8,128)(2,1)S(1)} %collective-permute-done.19.refs_1_), channel_id=1, source_target_pairs={{0,8},{1,5},{2,0},{3,11},{4,6},{5,13},{6,14},{7,3},{8,16},{9,1},{1... | collective-permute-start | bytes 589832 | tf_op jit(solution)/shard_map/ppermute | solution.py:88
  61.0 6.5 %collective-permute-start.25 = (bf16[256,384]{1,0:T(8,128)(2,1)S(1)}, bf16[256,384]{1,0:T(8,128)(2,1)S(1)}, u32[]{:S(2)}, u32[]{:S(2)}) collective-permute-start(bf16[256,384]{1,0:T(8,128)(2,1)S(1)} %collective-permute-done.20.refs_2_), channel_id=1, source_target_pairs={{0,2},{1,9},{2,10},{3,7},{4,12},{5,1},{6,4},{7,15},{8,0},{9,17},{1... | collective-permute-start | bytes 589832 | tf_op jit(solution)/shard_map/ppermute | solution.py:88
  62.2 8.9 %collective-permute-start.21 = (bf16[288,384]{1,0:T(8,128)(2,1)S(1)}, bf16[288,384]{1,0:T(8,128)(2,1)S(1)}, u32[]{:S(2)}, u32[]{:S(2)}) collective-permute-start(bf16[288,384]{1,0:T(8,128)(2,1)S(1)} %get-tuple-element.81), channel_id=1, source_target_pairs={{0,1},{1,0},{2,3},{3,2},{4,5},{5,4},{6,7},{7,6},{8,9},{9,8},{10,11... | collective-permute-start | bytes 663560 | tf_op jit(solution)/shard_map/ppermute | solution.py:59
  62.5 14.5 %collective-permute-start.22 = (bf16[576,384]{1,0:T(8,128)(2,1)S(1)}, bf16[576,384]{1,0:T(8,128)(2,1)S(1)}, u32[]{:S(2)}, u32[]{:S(2)}) collective-permute-start(bf16[576,384]{1,0:T(8,128)(2,1)S(1)} %get-tuple-element.82), channel_id=1, source_target_pairs={{0,4},{1,3},{2,6},{3,1},{4,0},{5,7},{6,2},{7,5},{8,12},{9,11},{10,... | collective-permute-start | bytes 1327112 | tf_op jit(solution)/shard_map/ppermute | solution.py:59
  65.4 8.5 %collective-permute-start.29 = (bf16[256,384]{1,0:T(8,128)(2,1)S(1)}, bf16[256,384]{1,0:T(8,128)(2,1)S(1)}, u32[]{:S(2)}, u32[]{:S(2)}) collective-permute-start(bf16[256,384]{1,0:T(8,128)(2,1)S(1)} %collective-permute-done.24.refs_0_), channel_id=1, source_target_pairs={{0,8},{1,5},{2,0},{3,11},{4,6},{5,13},{6,14},{7,3},{8,16},{9,1},{1... | collective-permute-start | bytes 589832 | tf_op jit(solution)/shard_map/ppermute | solution.py:88
  67.5 7.7 %collective-permute-start.30 = (bf16[256,384]{1,0:T(8,128)(2,1)S(1)}, bf16[256,384]{1,0:T(8,128)(2,1)S(1)}, u32[]{:S(2)}, u32[]{:S(2)}) collective-permute-start(bf16[256,384]{1,0:T(8,128)(2,1)S(1)} %collective-permute-done.25.refs_1_), channel_id=1, source_target_pairs={{0,2},{1,9},{2,10},{3,7},{4,12},{5,1},{6,4},{7,15},{8,0},{9,17},{1... | collective-permute-start | bytes 589832 | tf_op jit(solution)/shard_map/ppermute | solution.py:88
  68.5 9.4 %collective-permute-start.27 = (bf16[384,384]{1,0:T(8,128)(2,1)S(1)}, bf16[384,384]{1,0:T(8,128)(2,1)S(1)}, u32[]{:S(2)}, u32[]{:S(2)}) collective-permute-start(bf16[384,384]{1,0:T(8,128)(2,1)S(1)} %get-tuple-element.87), channel_id=1, source_target_pairs={{0,4},{1,3},{2,6},{3,1},{4,0},{5,7},{6,2},{7,5},{8,12},{9,11},{10,... | collective-permute-start | bytes 884744 | tf_op jit(solution)/shard_map/ppermute | solution.py:59
  71.2 8.8 %collective-permute-start.26 = (bf16[192,384]{1,0:T(8,128)(2,1)S(1)}, bf16[192,384]{1,0:T(8,128)(2,1)S(1)}, u32[]{:S(2)}, u32[]{:S(2)}) collective-permute-start(bf16[192,384]{1,0:T(8,128)(2,1)S(1)} %get-tuple-element.86), channel_id=1, source_target_pairs={{0,1},{1,0},{2,3},{3,2},{4,5},{5,4},{6,7},{7,6},{8,9},{9,8},{10,11... | collective-permute-start | bytes 442376 | tf_op jit(solution)/shard_map/ppermute | solution.py:59
  73.9 5.8 %collective-permute-start.34 = (bf16[256,384]{1,0:T(8,128)(2,1)S(1)}, bf16[256,384]{1,0:T(8,128)(2,1)S(1)}, u32[]{:S(2)}, u32[]{:S(2)}) collective-permute-start(bf16[256,384]{1,0:T(8,128)(2,1)S(1)} %collective-permute-done.29.refs_0_), channel_id=1, source_target_pairs={{0,8},{1,5},{2,0},{3,11},{4,6},{5,13},{6,14},{7,3},{8,16},{9,1},{1... | collective-permute-start | bytes 589832 | tf_op jit(solution)/shard_map/ppermute | solution.py:88
  75.6 5.2 %collective-permute-start.32 = (bf16[192,384]{1,0:T(8,128)(2,1)S(1)}, bf16[192,384]{1,0:T(8,128)(2,1)S(1)}, u32[]{:S(2)}, u32[]{:S(2)}) collective-permute-start(bf16[192,384]{1,0:T(8,128)(2,1)S(1)} %get-tuple-element.98), channel_id=1, source_target_pairs={{0,4},{1,3},{2,6},{3,1},{4,0},{5,7},{6,2},{7,5},{8,12},{9,11},{10,... | collective-permute-start | bytes 442376 | tf_op jit(solution)/shard_map/ppermute | solution.py:59
  77.0 5.1 %collective-permute-start.33 = (bf16[192,384]{1,0:T(8,128)(2,1)S(1)}, bf16[192,384]{1,0:T(8,128)(2,1)S(1)}, u32[]{:S(2)}, u32[]{:S(2)}) collective-permute-start(bf16[192,384]{1,0:T(8,128)(2,1)S(1)} %get-tuple-element.97), channel_id=1, source_target_pairs={{0,5},{1,2},{2,7},{3,0},{4,1},{5,6},{6,3},{7,4},{8,13},{9,10},{10,... | collective-permute-start | bytes 442376 | tf_op jit(solution)/shard_map/ppermute | solution.py:59
  77.9 5.5 %collective-permute-start.31 = (bf16[192,384]{1,0:T(8,128)(2,1)S(1)}, bf16[192,384]{1,0:T(8,128)(2,1)S(1)}, u32[]{:S(2)}, u32[]{:S(2)}) collective-permute-start(bf16[192,384]{1,0:T(8,128)(2,1)S(1)} %get-tuple-element.91), channel_id=1, source_target_pairs={{0,1},{1,0},{2,3},{3,2},{4,5},{5,4},{6,7},{7,6},{8,9},{9,8},{10,11... | collective-permute-start | bytes 442376 | tf_op jit(solution)/shard_map/ppermute | solution.py:59
  79.7 4.4 %collective-permute-start.23 = (bf16[288,384]{1,0:T(8,128)(2,1)S(1)}, bf16[288,384]{1,0:T(8,128)(2,1)S(1)}, u32[]{:S(2)}, u32[]{:S(2)}) collective-permute-start(bf16[288,384]{1,0:T(8,128)(2,1)S(1)} %slice.24), channel_id=1, source_target_pairs={{0,1},{1,0},{2,3},{3,2},{4,5},{5,4},{6,7},{7,6},{8,9},{9,8},{10,11... | collective-permute-start | bytes 663560 | tf_op jit(solution)/shard_map/ppermute | solution.py:59
  80.0 4.2 %collective-permute-start.28 = (bf16[192,384]{1,0:T(8,128)(2,1)S(1)}, bf16[192,384]{1,0:T(8,128)(2,1)S(1)}, u32[]{:S(2)}, u32[]{:S(2)}) collective-permute-start(bf16[192,384]{1,0:T(8,128)(2,1)S(1)} %slice.25), channel_id=1, source_target_pairs={{0,1},{1,0},{2,3},{3,2},{4,5},{5,4},{6,7},{7,6},{8,9},{9,8},{10,11... | collective-permute-start | bytes 442376 | tf_op jit(solution)/shard_map/ppermute | solution.py:59
  80.8 4.4 %collective-permute-start.36 = (bf16[96,384]{1,0:T(8,128)(2,1)S(1)}, bf16[96,384]{1,0:T(8,128)(2,1)S(1)}, u32[]{:S(2)}, u32[]{:S(2)}) collective-permute-start(bf16[96,384]{1,0:T(8,128)(2,1)S(1)} %get-tuple-element.100), channel_id=1, source_target_pairs={{0,4},{1,3},{2,6},{3,1},{4,0},{5,7},{6,2},{7,5},{8,12},{9,11},{10,... | collective-permute-start | bytes 221192 | tf_op jit(solution)/shard_map/ppermute | solution.py:59
  82.2 3.8 %collective-permute-start.37 = (bf16[96,384]{1,0:T(8,128)(2,1)S(1)}, bf16[96,384]{1,0:T(8,128)(2,1)S(1)}, u32[]{:S(2)}, u32[]{:S(2)}) collective-permute-start(bf16[96,384]{1,0:T(8,128)(2,1)S(1)} %get-tuple-element.99), channel_id=1, source_target_pairs={{0,5},{1,2},{2,7},{3,0},{4,1},{5,6},{6,3},{7,4},{8,13},{9,10},{10,... | collective-permute-start | bytes 221192 | tf_op jit(solution)/shard_map/ppermute | solution.py:59
  83.4 2.6 %collective-permute-start.35 = (bf16[96,384]{1,0:T(8,128)(2,1)S(1)}, bf16[96,384]{1,0:T(8,128)(2,1)S(1)}, u32[]{:S(2)}, u32[]{:S(2)}) collective-permute-start(bf16[96,384]{1,0:T(8,128)(2,1)S(1)} %get-tuple-element.95), channel_id=1, source_target_pairs={{0,1},{1,0},{2,3},{3,2},{4,5},{5,4},{6,7},{7,6},{8,9},{9,8},{10,11... | collective-permute-start | bytes 221192 | tf_op jit(solution)/shard_map/ppermute | solution.py:59

commit v8 on v7

--- a/solution.py
+++ b/solution.py
@@ -305,17 +305,39 @@
     )(where, pair_row)
 
 
+def widen(pieces, high):
+    tiles = pieces[0].shape[1] // LANES
+
+    def body(*refs):
+        for number, ref in enumerate(refs[:-1]):
+            for tile in range(tiles):
+                lanes = pl.ds(tile * LANES, LANES)
+                refs[-1][tile, number * high:(number + 1) * high, :] = ref[:high, lanes].astype(F32)
+
+    return pl.pallas_call(
+        body,
+        out_shape=jax.ShapeDtypeStruct((tiles, len(pieces) * high + high, LANES), F32),
+        in_specs=vmem(len(pieces)),
+        out_specs=pl.BlockSpec(memory_space=pltpu.VMEM),
+        compiler_params=PARAMS,
+        name="widen",
+    )(*pieces)
+
+
 def place_pairs(places, groups, pieces, share):
     width = pieces[0].shape[1]
     pairs = places.shape[0]
     each = 2 * share
+    early = pieces[0].shape[0] * 4
+    wide, pieces = widen(pieces[:4], pieces[0].shape[0]), pieces[4:]
+    before = early // each
     slots = pairs // sum(4 * len(group) for group in groups)
 
-    def body(place_ref, *refs):
+    def body(place_ref, wide_ref, *refs):
         piece_refs, (out_ref, held, ready, leaves) = refs[: len(pieces)], refs[-4:]
         start = 0
         for number, ref in enumerate(piece_refs):
-            rows = len(groups[number // 4]) * slots * each
+            rows = len(groups[1 + number // 4]) * slots * each
             for tile in range(width // LANES):
                 held[tile, start:start + rows, :] = ref[:rows, tile * LANES:(tile + 1) * LANES].astype(F32)
             start += rows
@@ -323,7 +345,9 @@
         copies = []
         for number in range(each):
             for tile in range(width // LANES):
-                rows = held[tile, pl.ds(number, pairs, stride=each), :].astype(BF16)
+                first = wide_ref[tile, pl.ds(number, before, stride=each), :]
+                later = held[tile, pl.ds(number, pairs - before, stride=each), :]
+                rows = jnp.concatenate([first, later], axis=0).astype(BF16)
                 placed = lax.dot_general(rows, place, (((0,), (0,)), ((), ())), preferred_element_type=F32)
                 ready[number, tile * LANES:(tile + 1) * LANES, :] = placed.astype(BF16)
             copies.append(
@@ -336,16 +360,16 @@
     return pl.pallas_call(
         body,
         out_shape=jax.ShapeDtypeStruct((2, share, width, pairs), BF16),
-        in_specs=vmem(1 + len(pieces)),
+        in_specs=vmem(2 + len(pieces)),
         out_specs=pl.BlockSpec(memory_space=pl.ANY),
         scratch_shapes=[
-            pltpu.VMEM((width // LANES, (pairs + 1) * each, LANES), F32),
+            pltpu.VMEM((width // LANES, (pairs - before + 1) * each, LANES), F32),
             pltpu.VMEM((each, width, pairs), BF16),
             pltpu.SemaphoreType.DMA((each,)),
         ],
         compiler_params=PARAMS,
         name="place_pairs",
-    )(places, *pieces)
+    )(places, wide, *pieces)
 
 
 def on_device(n_coef, n_pair, integrals, coefficients, shell_starts, pair_ids):
@@ -382,8 +406,6 @@
             return [shared[0][0]]
         if len(ints) < len(groups):
             kept, *leaving = shared[len(ints)]
-            if ints:
-                leaving = [after(block, held[0]) for block in leaving]
             ints.append([kept, *grid.exchange(leaving, grid.helpers)])
         last = offsets == [-reach]
         offsets = [0, *offsets] if offsets == [-1, 1] else offsets

time: 88.4 us -> 88.3 us (level)
  no operation moved by 1% of the time
where the time goes in v8:
time: 88.3 us; the launch traced here: 88.1 us
  waiting for transfers between devices  40.5 us (46%)
  starting transfers between devices  35.7 us (40%)
  Pallas kernels  11.1 us (13%)
    ppermute x24, waiting for transfers between devices, send(): lax.ppermute(block, 'pair', [(device, int(target(device))) for device in...  25.1 us
    ppermute x24, starting transfers between devices, send(): lax.ppermute(block, 'pair', [(device, int(target(device))) for device in...  20.5 us
    ppermute x14, waiting for transfers between devices, gather_ring(): held[way * step] = lax.ppermute(block, 'pair', around[way])  15.3 us
    ppermute x14, starting transfers between devices, gather_ring(): held[way * step] = lax.ppermute(block, 'pair', around[way])  15.1 us
    pallas_call x4, Pallas kernels, first_product(): pl.pallas_call(body, out_shape=shapes, in_specs=vmem(4 + len(totals) + le...  2.99 us
    pallas_call x1, Pallas kernels, share_integrals(): pl.pallas_call(body, out_shape=[jax.ShapeDtypeStruct((rows + batch_rows *...  2.52 us
    pallas_call x1, Pallas kernels, place_pairs(): pl.pallas_call(body, out_shape=jax.ShapeDtypeStruct((2, share, width, pai...  2.2 us
  transfers between devices with their start and end apart: 38, of which 18 were waited for; matrix products, arithmetic and copies ran while one was open for 0% of the time, Pallas kernels for 9%

profile of v8, /device:TPU:0, one launch (start us, length us, event | category | flops | bytes accessed | tf_op | source)
XLA Modules:
  0.0 88.1 jit_solution(15447119566108197005)
XLA Ops:
  0.0 3.0 %collective-permute-start.9 = (bf16[2,256,384]{2,1,0:T(8,128)(2,1)}, bf16[2,256,384]{2,1,0:T(8,128)(2,1)S(1)}, u32[]{:S(2)}, u32[]{:S(2)}) collective-permute-start(bf16[2,256,384]{2,1,0:T(8,128)(2,1)} %refs_4_.1), channel_id=1, source_target_pairs={{0,8},{1,5},{2,0},{3,11},{4,6},{5,13},{6,14},{7,3},{8,16},{9,1},{1... | collective-permute-start | bytes 1179656 | tf_op jit(solution)/shard_map/ppermute | solution.py:88
  3.0 0.7 copy-done.1
  3.7 2.5 %share_integrals.1 = (bf16[160,768]{1,0:T(8,128)(2,1)S(1)}, bf16[128,768]{1,0:T(8,128)(2,1)S(1)}, bf16[128,768]{1,0:T(8,128)(2,1)S(1)}, bf16[128,768]{1,0:T(8,12...) custom-call(s32[1]{0:T(128)} %bitcast.where_ref, ...), custom_call_target="tpu_custom_call" | custom-call | tf_op jit(solution)/shard_map/share_integrals/pallas_call | solution.py:134
  6.2 5.5 %collective-permute-done.9.refs_5_ = bf16[2,256,384]{2,1,0:T(8,128)(2,1)S(1)} collective-permute-done((bf16[2,256,384]{2,1,0:T(8,128)(2,1)}, bf16[2,256,384]{2,1,0:T(8,128)(2,1)S(1)}, u32[]{:S(2)}, u32[]{:S(2)}) %collective-permute-start.9) | collective-permute-done | bytes 393248 | tf_op jit(solution)/shard_map/ppermute | solution.py:88
  11.7 2.4 %collective-permute-start.11 = (bf16[2,256,384]{2,1,0:T(8,128)(2,1)S(1)}, bf16[2,256,384]{2,1,0:T(8,128)(2,1)S(1)}, u32[]{:S(2)}, u32[]{:S(2)}) collective-permute-start(bf16[2,256,384]{2,1,0:T(8,128)(2,1)S(1)} %collective-permute-done.9.refs_5_), channel_id=1, source_target_pairs={{0,8},{1,5},{2,0},{3,11},{4,6},{5,13},{6,14},{7,3},{8,16},{9,1},{1... | collective-permute-start | bytes 1179656 | tf_op jit(solution)/shard_map/ppermute | solution.py:88
  14.1 0.9 collective-permute-start.12
  15.0 2.1 %collective-permute-start.7 = (bf16[128,768]{1,0:T(8,128)(2,1)S(1)}, bf16[128,768]{1,0:T(8,128)(2,1)S(1)}, u32[]{:S(2)}, u32[]{:S(2)}) collective-permute-start(bf16[128,768]{1,0:T(8,128)(2,1)S(1)} %get-tuple-element.55), channel_id=1, source_target_pairs={{0,4},{1,3},{2,6},{3,1},{4,0},{5,7},{6,2},{7,5},{8,12},{9,11},{10,... | collective-permute-start | bytes 589832 | tf_op jit(solution)/shard_map/ppermute | solution.py:59
  17.0 0.1 collective-permute-start.8
  17.2 5.7 %collective-permute-done.7.refs_2_ = bf16[128,768]{1,0:T(8,128)(2,1)S(1)} collective-permute-done((bf16[128,768]{1,0:T(8,128)(2,1)S(1)}, bf16[128,768]{1,0:T(8,128)(2,1)S(1)}, u32[]{:S(2)}, u32[]{:S(2)}) %collective-permute-start.7) | collective-permute-done | bytes 196640 | tf_op jit(solution)/shard_map/ppermute | solution.py:59
  22.9 1.6 %collective-permute-done.8.refs_3_ = bf16[128,768]{1,0:T(8,128)(2,1)S(1)} collective-permute-done((bf16[128,768]{1,0:T(8,128)(2,1)S(1)}, bf16[128,768]{1,0:T(8,128)(2,1)S(1)}, u32[]{:S(2)}, u32[]{:S(2)}) %collective-permute-start.8) | collective-permute-done | bytes 196640 | tf_op jit(solution)/shard_map/ppermute | solution.py:59
  24.5 2.3 %collective-permute-start.3 = (bf16[128,512]{1,0:T(8,128)(2,1)S(1)}, bf16[128,512]{1,0:T(8,128)(2,1)S(1)}, u32[]{:S(2)}, u32[]{:S(2)}) collective-permute-start(bf16[128,512]{1,0:T(8,128)(2,1)S(1)} %get-tuple-element.50), channel_id=1, source_target_pairs={{0,1},{1,0},{2,3},{3,2},{4,5},{5,4},{6,7},{7,6},{8,9},{9,8},{10,11... | collective-permute-start | bytes 393224 | tf_op jit(solution)/shard_map/ppermute | solution.py:59
  26.8 0.3 collective-permute-start.4
  27.1 1.1 %collective-permute-start.5 = (bf16[128,512]{1,0:T(8,128)(2,1)S(1)}, bf16[128,512]{1,0:T(8,128)(2,1)S(1)}, u32[]{:S(2)}, u32[]{:S(2)}) collective-permute-start(bf16[128,512]{1,0:T(8,128)(2,1)S(1)} %get-tuple-element.52), channel_id=1, source_target_pairs={{0,3},{1,4},{2,1},{3,6},{4,7},{5,0},{6,5},{7,2},{8,11},{9,12},{10,... | collective-permute-start | bytes 393224 | tf_op jit(solution)/shard_map/ppermute | solution.py:59
  28.1 0.4 collective-permute-start.14
  28.6 1.0 %first_product.4.refs_4_ = f32[544,768]{1,0:T(8,128)S(1)} custom-call(bf16[160,768]{1,0:T(8,128)(2,1)S(1)} %get-tuple-element.53.refs_0_, bf16[128,768]{1,0:T(8,128)(2,1)S(1)} %collective-permute-done.6.refs_1_, bf16[128,768]{1,0:T(8,128)(2,1)S(1)} %collective-permute-done.7.refs_2_, bf16[128,768]{1,0:T(8,128)(2,1)S(1)} %collective-permute-done.8.refs_3_, ...), custom_call_target="tpu_custom_call" | custom-call | flops 3208642560 | tf_op jit(solution)/shard_map/first_product/pallas_call | solution.py:184
  29.6 0.5 collective-permute-start
  30.1 3.1 %collective-permute-done.4.refs_2_ = bf16[128,512]{1,0:T(8,128)(2,1)S(1)} collective-permute-done((bf16[128,512]{1,0:T(8,128)(2,1)S(1)}, bf16[128,512]{1,0:T(8,128)(2,1)S(1)}, u32[]{:S(2)}, u32[]{:S(2)}) %collective-permute-start.4) | collective-permute-done | bytes 131104 | tf_op jit(solution)/shard_map/ppermute | solution.py:59
  33.2 0.3 collective-permute-start.1
  33.4 0.3 collective-permute-start.2
  33.7 0.7 collective-permute-start.15
  34.4 0.7 first_product.5.refs_4_
  35.2 5.8 %collective-permute-done.1.refs_2_ = bf16[128,768]{1,0:T(8,128)(2,1)S(1)} collective-permute-done((bf16[128,768]{1,0:T(8,128)(2,1)S(1)}, bf16[128,768]{1,0:T(8,128)(2,1)S(1)}, u32[]{:S(2)}, u32[]{:S(2)}) %collective-permute-start.1) | collective-permute-done | bytes 196640 | tf_op jit(solution)/shard_map/ppermute | solution.py:59
  41.0 0.3 collective-permute-done.2.refs_3_
  41.3 0.7 first_product.6.refs_4_
  42.1 2.7 %collective-permute-done.15.refs_5_ = bf16[2,256,384]{2,1,0:T(8,128)(2,1)S(1)} collective-permute-done((bf16[2,256,384]{2,1,0:T(8,128)(2,1)S(1)}, bf16[2,256,384]{2,1,0:T(8,128)(2,1)S(1)}, u32[]{:S(2)}, u32[]{:S(2)}) %collective-permute-start.15) | collective-permute-done | bytes 393248 | tf_op jit(solution)/shard_map/ppermute | solution.py:88
  44.8 0.5 first_product.7
  45.2 0.1 collective-permute-start.16
  45.3 1.0 %collective-permute-start.17 = (bf16[160,768]{1,0:T(8,128)(2,1)S(1)}, bf16[160,768]{1,0:T(8,128)(2,1)S(1)}, u32[]{:S(2)}, u32[]{:S(2)}) collective-permute-start(bf16[160,768]{1,0:T(8,128)(2,1)S(1)} %get-tuple-element.64), channel_id=1, source_target_pairs={{0,4},{1,3},{2,6},{3,1},{4,0},{5,7},{6,2},{7,5},{8,12},{9,11},{10,... | collective-permute-start | bytes 737288 | tf_op jit(solution)/shard_map/ppermute | solution.py:59
  46.3 1.5 %collective-permute-start.18 = (bf16[160,768]{1,0:T(8,128)(2,1)S(1)}, bf16[160,768]{1,0:T(8,128)(2,1)S(1)}, u32[]{:S(2)}, u32[]{:S(2)}) collective-permute-start(bf16[160,768]{1,0:T(8,128)(2,1)S(1)} %get-tuple-element.65), channel_id=1, source_target_pairs={{0,5},{1,2},{2,7},{3,0},{4,1},{5,6},{6,3},{7,4},{8,13},{9,10},{10,... | collective-permute-start | bytes 737288 | tf_op jit(solution)/shard_map/ppermute | solution.py:59
  47.8 3.8 %collective-permute-done.17.refs_2_ = bf16[160,768]{1,0:T(8,128)(2,1)S(1)} collective-permute-done((bf16[160,768]{1,0:T(8,128)(2,1)S(1)}, bf16[160,768]{1,0:T(8,128)(2,1)S(1)}, u32[]{:S(2)}, u32[]{:S(2)}) %collective-permute-start.17) | collective-permute-done | bytes 245792 | tf_op jit(solution)/shard_map/ppermute | solution.py:59
  51.6 2.1 %collective-permute-done.18.refs_3_ = bf16[160,768]{1,0:T(8,128)(2,1)S(1)} collective-permute-done((bf16[160,768]{1,0:T(8,128)(2,1)S(1)}, bf16[160,768]{1,0:T(8,128)(2,1)S(1)}, u32[]{:S(2)}, u32[]{:S(2)}) %collective-permute-start.18) | collective-permute-done | bytes 245792 | tf_op jit(solution)/shard_map/ppermute | solution.py:59
  53.7 0.1 add_partners.1
  53.8 2.0 %collective-permute-start.20 = (bf16[256,384]{1,0:T(8,128)(2,1)S(1)}, bf16[256,384]{1,0:T(8,128)(2,1)S(1)}, u32[]{:S(2)}, u32[]{:S(2)}) collective-permute-start(bf16[256,384]{1,0:T(8,128)(2,1)S(1)} %get-tuple-element.67.refs_0_), channel_id=1, source_target_pairs={{0,2},{1,9},{2,10},{3,7},{4,12},{5,1},{6,4},{7,15},{8,0},{9,17},{1... | collective-permute-start | bytes 589832 | tf_op jit(solution)/shard_map/ppermute | solution.py:88
  55.8 0.5 pair_places.1.place_ref
  56.3 1.2 %weights.1.matrix_ref = bf16[384,256]{1,0:T(8,128)(2,1)S(1)} custom-call(s32[1]{0:T(128)} %bitcast.where_ref, bf16[64,384]{1,0:T(8,128)(2,1)S(1)} %get-tuple-element.66.batch_ref), custom_call_target="tpu_custom_call" | custom-call | tf_op jit(solution)/shard_map/weights/pallas_call | solution.py:249
  57.6 1.9 %collective-permute-done.19.refs_1_ = bf16[256,384]{1,0:T(8,128)(2,1)S(1)} collective-permute-done((bf16[256,384]{1,0:T(8,128)(2,1)S(1)}, bf16[256,384]{1,0:T(8,128)(2,1)S(1)}, u32[]{:S(2)}, u32[]{:S(2)}) %collective-permute-start.19) | collective-permute-done | bytes 196640 | tf_op jit(solution)/shard_map/ppermute | solution.py:88
  59.5 1.0 %collective-permute-start.24 = (bf16[256,384]{1,0:T(8,128)(2,1)S(1)}, bf16[256,384]{1,0:T(8,128)(2,1)S(1)}, u32[]{:S(2)}, u32[]{:S(2)}) collective-permute-start(bf16[256,384]{1,0:T(8,128)(2,1)S(1)} %collective-permute-done.19.refs_1_), channel_id=1, source_target_pairs={{0,8},{1,5},{2,0},{3,11},{4,6},{5,13},{6,14},{7,3},{8,16},{9,1},{1... | collective-permute-start | bytes 589832 | tf_op jit(solution)/shard_map/ppermute | solution.py:88
  60.4 0.5 collective-permute-done.20.refs_2_
  61.0 0.8 collective-permute-start.25
  61.8 0.5 second_product.4
  62.2 0.2 collective-permute-start.21
  62.5 2.2 %collective-permute-start.22 = (bf16[576,384]{1,0:T(8,128)(2,1)S(1)}, bf16[576,384]{1,0:T(8,128)(2,1)S(1)}, u32[]{:S(2)}, u32[]{:S(2)}) collective-permute-start(bf16[576,384]{1,0:T(8,128)(2,1)S(1)} %get-tuple-element.70), channel_id=1, source_target_pairs={{0,4},{1,3},{2,6},{3,1},{4,0},{5,7},{6,2},{7,5},{8,12},{9,11},{10,... | collective-permute-start | bytes 1327112 | tf_op jit(solution)/shard_map/ppermute | solution.py:59
  64.7 0.7 collective-permute-done.24.refs_0_
  65.4 2.1 %collective-permute-start.29 = (bf16[256,384]{1,0:T(8,128)(2,1)S(1)}, bf16[256,384]{1,0:T(8,128)(2,1)S(1)}, u32[]{:S(2)}, u32[]{:S(2)}) collective-permute-start(bf16[256,384]{1,0:T(8,128)(2,1)S(1)} %collective-permute-done.24.refs_0_), channel_id=1, source_target_pairs={{0,8},{1,5},{2,0},{3,11},{4,6},{5,13},{6,14},{7,3},{8,16},{9,1},{1... | collective-permute-start | bytes 589832 | tf_op jit(solution)/shard_map/ppermute | solution.py:88
  67.5 0.7 collective-permute-start.30
  68.1 0.4 second_product.5
  68.5 2.7 %collective-permute-start.27 = (bf16[384,384]{1,0:T(8,128)(2,1)S(1)}, bf16[384,384]{1,0:T(8,128)(2,1)S(1)}, u32[]{:S(2)}, u32[]{:S(2)}) collective-permute-start(bf16[384,384]{1,0:T(8,128)(2,1)S(1)} %get-tuple-element.75), channel_id=1, source_target_pairs={{0,4},{1,3},{2,6},{3,1},{4,0},{5,7},{6,2},{7,5},{8,12},{9,11},{10,... | collective-permute-start | bytes 884744 | tf_op jit(solution)/shard_map/ppermute | solution.py:59
  71.2 2.8 %collective-permute-done.29.refs_0_ = bf16[256,384]{1,0:T(8,128)(2,1)S(1)} collective-permute-done((bf16[256,384]{1,0:T(8,128)(2,1)S(1)}, bf16[256,384]{1,0:T(8,128)(2,1)S(1)}, u32[]{:S(2)}, u32[]{:S(2)}) %collective-permute-start.29) | collective-permute-done | bytes 196640 | tf_op jit(solution)/shard_map/ppermute | solution.py:88
  73.9 1.2 %collective-permute-start.34 = (bf16[256,384]{1,0:T(8,128)(2,1)S(1)}, bf16[256,384]{1,0:T(8,128)(2,1)S(1)}, u32[]{:S(2)}, u32[]{:S(2)}) collective-permute-start(bf16[256,384]{1,0:T(8,128)(2,1)S(1)} %collective-permute-done.29.refs_0_), channel_id=1, source_target_pairs={{0,8},{1,5},{2,0},{3,11},{4,6},{5,13},{6,14},{7,3},{8,16},{9,1},{1... | collective-permute-start | bytes 589832 | tf_op jit(solution)/shard_map/ppermute | solution.py:88
  75.2 0.4 second_product.6
  75.6 1.5 %collective-permute-start.32 = (bf16[192,384]{1,0:T(8,128)(2,1)S(1)}, bf16[192,384]{1,0:T(8,128)(2,1)S(1)}, u32[]{:S(2)}, u32[]{:S(2)}) collective-permute-start(bf16[192,384]{1,0:T(8,128)(2,1)S(1)} %get-tuple-element.86), channel_id=1, source_target_pairs={{0,4},{1,3},{2,6},{3,1},{4,0},{5,7},{6,2},{7,5},{8,12},{9,11},{10,... | collective-permute-start | bytes 442376 | tf_op jit(solution)/shard_map/ppermute | solution.py:59
  77.1 0.8 collective-permute-done.27.refs_2_
  77.9 0.7 collective-permute-start.31
  78.6 1.1 %collective-permute-done.34.refs_0_ = bf16[256,384]{1,0:T(8,128)(2,1)S(1)} collective-permute-done((bf16[256,384]{1,0:T(8,128)(2,1)S(1)}, bf16[256,384]{1,0:T(8,128)(2,1)S(1)}, u32[]{:S(2)}, u32[]{:S(2)}) %collective-permute-start.34) | collective-permute-done | bytes 196640 | tf_op jit(solution)/shard_map/ppermute | solution.py:88
  79.7 0.3 second_product.7
  80.0 0.6 collective-permute-start.28
  80.6 0.2 collective-permute-done.32.refs_6_
  80.8 1.4 %collective-permute-start.36 = (bf16[96,384]{1,0:T(8,128)(2,1)S(1)}, bf16[96,384]{1,0:T(8,128)(2,1)S(1)}, u32[]{:S(2)}, u32[]{:S(2)}) collective-permute-start(bf16[96,384]{1,0:T(8,128)(2,1)S(1)} %get-tuple-element.88), channel_id=1, source_target_pairs={{0,4},{1,3},{2,6},{3,1},{4,0},{5,7},{6,2},{7,5},{8,12},{9,11},{10,... | collective-permute-start | bytes 221192 | tf_op jit(solution)/shard_map/ppermute | solution.py:59
  82.2 1.2 %collective-permute-start.37 = (bf16[96,384]{1,0:T(8,128)(2,1)S(1)}, bf16[96,384]{1,0:T(8,128)(2,1)S(1)}, u32[]{:S(2)}, u32[]{:S(2)}) collective-permute-start(bf16[96,384]{1,0:T(8,128)(2,1)S(1)} %get-tuple-element.87), channel_id=1, source_target_pairs={{0,5},{1,2},{2,7},{3,0},{4,1},{5,6},{6,3},{7,4},{8,13},{9,10},{10,... | collective-permute-start | bytes 221192 | tf_op jit(solution)/shard_map/ppermute | solution.py:59
  83.4 0.8 collective-permute-start.35
  84.1 0.1 widen.1.wide_ref
  84.3 0.9 collective-permute-done.36.refs_10_
  85.1 0.8 collective-permute-done.37.refs_11_
  86.0 2.2 %place_pairs.1 = bf16[2,12,384,128]{3,2,1,0:T(8,128)(2,1)} custom-call(bf16[128,128]{1,0:T(8,128)(2,1)S(1)} %pair_places.1.place_ref, f32[3,1440,128]{2,1,0:T(8,128)S(1)} %widen.1.wide_ref, bf16[192,384]{1,0:T(8,128)(2,1)S(1)} %get-tuple-element.73.refs_0_, bf16[192,384]{1,0:T(8,128)(2,1)S(1)} %collective-permute-done.26.refs_1_, ...), custom_call_target="tpu_custom_call" | custom-call | tf_op jit(solution)/shard_map/place_pairs/pallas_call | solution.py:360
  (36 shorter events, 0.2 us)
Async XLA Ops:
  0.0 11.7 %collective-permute-start.9 = (bf16[2,256,384]{2,1,0:T(8,128)(2,1)}, bf16[2,256,384]{2,1,0:T(8,128)(2,1)S(1)}, u32[]{:S(2)}, u32[]{:S(2)}) collective-permute-start(bf16[2,256,384]{2,1,0:T(8,128)(2,1)} %refs_4_.1), channel_id=1, source_target_pairs={{0,8},{1,5},{2,0},{3,11},{4,6},{5,13},{6,14},{7,3},{8,16},{9,1},{1... | collective-permute-start | bytes 1179656 | tf_op jit(solution)/shard_map/ppermute | solution.py:88
  3.0 11.1 %collective-permute-start.10 = (bf16[2,256,384]{2,1,0:T(8,128)(2,1)}, bf16[2,256,384]{2,1,0:T(8,128)(2,1)S(1)}, u32[]{:S(2)}, u32[]{:S(2)}) collective-permute-start(bf16[2,256,384]{2,1,0:T(8,128)(2,1)} %refs_4_.1), channel_id=1, source_target_pairs={{0,2},{1,9},{2,10},{3,7},{4,12},{5,1},{6,4},{7,15},{8,0},{9,17},{1... | collective-permute-start | bytes 1179656 | tf_op jit(solution)/shard_map/ppermute | solution.py:88
  3.0 0.7 copy-start.1
  3.7 24.9 %copy-start.2 = (bf16[2,256,384]{2,1,0:T(8,128)(2,1)S(1)}, bf16[2,256,384]{2,1,0:T(8,128)(2,1)}, u32[]{:S(2)}) copy-start(bf16[2,256,384]{2,1,0:T(8,128)(2,1)} %refs_4_.1) | copy-start | bytes 1179652
  11.7 12.8 %collective-permute-start.11 = (bf16[2,256,384]{2,1,0:T(8,128)(2,1)S(1)}, bf16[2,256,384]{2,1,0:T(8,128)(2,1)S(1)}, u32[]{:S(2)}, u32[]{:S(2)}) collective-permute-start(bf16[2,256,384]{2,1,0:T(8,128)(2,1)S(1)} %collective-permute-done.9.refs_5_), channel_id=1, source_target_pairs={{0,8},{1,5},{2,0},{3,11},{4,6},{5,13},{6,14},{7,3},{8,16},{9,1},{1... | collective-permute-start | bytes 1179656 | tf_op jit(solution)/shard_map/ppermute | solution.py:88
  14.1 14.0 %collective-permute-start.12 = (bf16[2,256,384]{2,1,0:T(8,128)(2,1)S(1)}, bf16[2,256,384]{2,1,0:T(8,128)(2,1)S(1)}, u32[]{:S(2)}, u32[]{:S(2)}) collective-permute-start(bf16[2,256,384]{2,1,0:T(8,128)(2,1)S(1)} %collective-permute-done.10.refs_6_), channel_id=1, source_target_pairs={{0,2},{1,9},{2,10},{3,7},{4,12},{5,1},{6,4},{7,15},{8,0},{9,17},{1... | collective-permute-start | bytes 1179656 | tf_op jit(solution)/shard_map/ppermute | solution.py:88
  15.0 2.2 %collective-permute-start.6 = (bf16[128,768]{1,0:T(8,128)(2,1)S(1)}, bf16[128,768]{1,0:T(8,128)(2,1)S(1)}, u32[]{:S(2)}, u32[]{:S(2)}) collective-permute-start(bf16[128,768]{1,0:T(8,128)(2,1)S(1)} %get-tuple-element.54), channel_id=1, source_target_pairs={{0,1},{1,0},{2,3},{3,2},{4,5},{5,4},{6,7},{7,6},{8,9},{9,8},{10,11... | collective-permute-start | bytes 589832 | tf_op jit(solution)/shard_map/ppermute | solution.py:59
  15.0 7.9 %collective-permute-start.7 = (bf16[128,768]{1,0:T(8,128)(2,1)S(1)}, bf16[128,768]{1,0:T(8,128)(2,1)S(1)}, u32[]{:S(2)}, u32[]{:S(2)}) collective-permute-start(bf16[128,768]{1,0:T(8,128)(2,1)S(1)} %get-tuple-element.55), channel_id=1, source_target_pairs={{0,4},{1,3},{2,6},{3,1},{4,0},{5,7},{6,2},{7,5},{8,12},{9,11},{10,... | collective-permute-start | bytes 589832 | tf_op jit(solution)/shard_map/ppermute | solution.py:59
  17.0 7.5 %collective-permute-start.8 = (bf16[128,768]{1,0:T(8,128)(2,1)S(1)}, bf16[128,768]{1,0:T(8,128)(2,1)S(1)}, u32[]{:S(2)}, u32[]{:S(2)}) collective-permute-start(bf16[128,768]{1,0:T(8,128)(2,1)S(1)} %get-tuple-element.56), channel_id=1, source_target_pairs={{0,3},{1,4},{2,1},{3,6},{4,7},{5,0},{6,5},{7,2},{8,11},{9,12},{10,... | collective-permute-start | bytes 589832 | tf_op jit(solution)/shard_map/ppermute | solution.py:59
  24.5 9.2 %collective-permute-start.13 = (bf16[2,256,384]{2,1,0:T(8,128)(2,1)S(1)}, bf16[2,256,384]{2,1,0:T(8,128)(2,1)S(1)}, u32[]{:S(2)}, u32[]{:S(2)}) collective-permute-start(bf16[2,256,384]{2,1,0:T(8,128)(2,1)S(1)} %collective-permute-done.11.refs_5_), channel_id=1, source_target_pairs={{0,8},{1,5},{2,0},{3,11},{4,6},{5,13},{6,14},{7,3},{8,16},{9,1},{1... | collective-permute-start | bytes 1179656 | tf_op jit(solution)/shard_map/ppermute | solution.py:88
  24.5 5.1 %collective-permute-start.3 = (bf16[128,512]{1,0:T(8,128)(2,1)S(1)}, bf16[128,512]{1,0:T(8,128)(2,1)S(1)}, u32[]{:S(2)}, u32[]{:S(2)}) collective-permute-start(bf16[128,512]{1,0:T(8,128)(2,1)S(1)} %get-tuple-element.50), channel_id=1, source_target_pairs={{0,1},{1,0},{2,3},{3,2},{4,5},{5,4},{6,7},{7,6},{8,9},{9,8},{10,11... | collective-permute-start | bytes 393224 | tf_op jit(solution)/shard_map/ppermute | solution.py:59
  26.8 6.4 %collective-permute-start.4 = (bf16[128,512]{1,0:T(8,128)(2,1)S(1)}, bf16[128,512]{1,0:T(8,128)(2,1)S(1)}, u32[]{:S(2)}, u32[]{:S(2)}) collective-permute-start(bf16[128,512]{1,0:T(8,128)(2,1)S(1)} %get-tuple-element.51), channel_id=1, source_target_pairs={{0,4},{1,3},{2,6},{3,1},{4,0},{5,7},{6,2},{7,5},{8,12},{9,11},{10,... | collective-permute-start | bytes 393224 | tf_op jit(solution)/shard_map/ppermute | solution.py:59
  27.1 6.4 %collective-permute-start.5 = (bf16[128,512]{1,0:T(8,128)(2,1)S(1)}, bf16[128,512]{1,0:T(8,128)(2,1)S(1)}, u32[]{:S(2)}, u32[]{:S(2)}) collective-permute-start(bf16[128,512]{1,0:T(8,128)(2,1)S(1)} %get-tuple-element.52), channel_id=1, source_target_pairs={{0,3},{1,4},{2,1},{3,6},{4,7},{5,0},{6,5},{7,2},{8,11},{9,12},{10,... | collective-permute-start | bytes 393224 | tf_op jit(solution)/shard_map/ppermute | solution.py:59
  28.1 13.2 %collective-permute-start.14 = (bf16[2,256,384]{2,1,0:T(8,128)(2,1)S(1)}, bf16[2,256,384]{2,1,0:T(8,128)(2,1)S(1)}, u32[]{:S(2)}, u32[]{:S(2)}) collective-permute-start(bf16[2,256,384]{2,1,0:T(8,128)(2,1)S(1)} %collective-permute-done.12.refs_6_), channel_id=1, source_target_pairs={{0,2},{1,9},{2,10},{3,7},{4,12},{5,1},{6,4},{7,15},{8,0},{9,17},{1... | collective-permute-start | bytes 1179656 | tf_op jit(solution)/shard_map/ppermute | solution.py:88
  29.6 5.5 %collective-permute-start = (bf16[128,768]{1,0:T(8,128)(2,1)S(1)}, bf16[128,768]{1,0:T(8,128)(2,1)S(1)}, u32[]{:S(2)}, u32[]{:S(2)}) collective-permute-start(bf16[128,768]{1,0:T(8,128)(2,1)S(1)} %get-tuple-element.46), channel_id=1, source_target_pairs={{0,1},{1,0},{2,3},{3,2},{4,5},{5,4},{6,7},{7,6},{8,9},{9,8},{10,11... | collective-permute-start | bytes 589832 | tf_op jit(solution)/shard_map/ppermute | solution.py:59
  33.2 7.8 %collective-permute-start.1 = (bf16[128,768]{1,0:T(8,128)(2,1)S(1)}, bf16[128,768]{1,0:T(8,128)(2,1)S(1)}, u32[]{:S(2)}, u32[]{:S(2)}) collective-permute-start(bf16[128,768]{1,0:T(8,128)(2,1)S(1)} %get-tuple-element.47), channel_id=1, source_target_pairs={{0,4},{1,3},{2,6},{3,1},{4,0},{5,7},{6,2},{7,5},{8,12},{9,11},{10,... | collective-permute-start | bytes 589832 | tf_op jit(solution)/shard_map/ppermute | solution.py:59
  33.4 7.9 %collective-permute-start.2 = (bf16[128,768]{1,0:T(8,128)(2,1)S(1)}, bf16[128,768]{1,0:T(8,128)(2,1)S(1)}, u32[]{:S(2)}, u32[]{:S(2)}) collective-permute-start(bf16[128,768]{1,0:T(8,128)(2,1)S(1)} %get-tuple-element.48), channel_id=1, source_target_pairs={{0,3},{1,4},{2,1},{3,6},{4,7},{5,0},{6,5},{7,2},{8,11},{9,12},{10,... | collective-permute-start | bytes 589832 | tf_op jit(solution)/shard_map/ppermute | solution.py:59
  33.7 11.0 %collective-permute-start.15 = (bf16[2,256,384]{2,1,0:T(8,128)(2,1)S(1)}, bf16[2,256,384]{2,1,0:T(8,128)(2,1)S(1)}, u32[]{:S(2)}, u32[]{:S(2)}) collective-permute-start(bf16[2,256,384]{2,1,0:T(8,128)(2,1)S(1)} %collective-permute-done.13.refs_5_), channel_id=1, source_target_pairs={{0,8},{1,5},{2,0},{3,11},{4,6},{5,13},{6,14},{7,3},{8,16},{9,1},{1... | collective-permute-start | bytes 1179656 | tf_op jit(solution)/shard_map/ppermute | solution.py:88
  42.1 13.8 %copy-start = (s32[1,128]{1,0:T(1,128)S(1)}, s32[1,128]{1,0:T(1,128)}, u32[]{:S(2)}) copy-start(s32[1,128]{1,0:T(1,128)} %pair_ref.1) | copy-start | bytes 1540
  45.2 8.4 %collective-permute-start.16 = (f32[160,768]{1,0:T(8,128)S(1)}, f32[160,768]{1,0:T(8,128)S(1)}, u32[]{:S(2)}, u32[]{:S(2)}) collective-permute-start(f32[160,768]{1,0:T(8,128)S(1)} %get-tuple-element.63), channel_id=1, source_target_pairs={{0,1},{1,0},{2,3},{3,2},{4,5},{5,4},{6,7},{7,6},{8,9},{9,8},{10,11... | collective-permute-start | bytes 1474568 | tf_op jit(solution)/shard_map/ppermute | solution.py:59
  45.3 6.3 %collective-permute-start.17 = (bf16[160,768]{1,0:T(8,128)(2,1)S(1)}, bf16[160,768]{1,0:T(8,128)(2,1)S(1)}, u32[]{:S(2)}, u32[]{:S(2)}) collective-permute-start(bf16[160,768]{1,0:T(8,128)(2,1)S(1)} %get-tuple-element.64), channel_id=1, source_target_pairs={{0,4},{1,3},{2,6},{3,1},{4,0},{5,7},{6,2},{7,5},{8,12},{9,11},{10,... | collective-permute-start | bytes 737288 | tf_op jit(solution)/shard_map/ppermute | solution.py:59
  46.3 7.3 %collective-permute-start.18 = (bf16[160,768]{1,0:T(8,128)(2,1)S(1)}, bf16[160,768]{1,0:T(8,128)(2,1)S(1)}, u32[]{:S(2)}, u32[]{:S(2)}) collective-permute-start(bf16[160,768]{1,0:T(8,128)(2,1)S(1)} %get-tuple-element.65), channel_id=1, source_target_pairs={{0,5},{1,2},{2,7},{3,0},{4,1},{5,6},{6,3},{7,4},{8,13},{9,10},{10,... | collective-permute-start | bytes 737288 | tf_op jit(solution)/shard_map/ppermute | solution.py:59
  53.8 5.7 %collective-permute-start.19 = (bf16[256,384]{1,0:T(8,128)(2,1)S(1)}, bf16[256,384]{1,0:T(8,128)(2,1)S(1)}, u32[]{:S(2)}, u32[]{:S(2)}) collective-permute-start(bf16[256,384]{1,0:T(8,128)(2,1)S(1)} %get-tuple-element.67.refs_0_), channel_id=1, source_target_pairs={{0,8},{1,5},{2,0},{3,11},{4,6},{5,13},{6,14},{7,3},{8,16},{9,1},{1... | collective-permute-start | bytes 589832 | tf_op jit(solution)/shard_map/ppermute | solution.py:88
  53.8 7.2 %collective-permute-start.20 = (bf16[256,384]{1,0:T(8,128)(2,1)S(1)}, bf16[256,384]{1,0:T(8,128)(2,1)S(1)}, u32[]{:S(2)}, u32[]{:S(2)}) collective-permute-start(bf16[256,384]{1,0:T(8,128)(2,1)S(1)} %get-tuple-element.67.refs_0_), channel_id=1, source_target_pairs={{0,2},{1,9},{2,10},{3,7},{4,12},{5,1},{6,4},{7,15},{8,0},{9,17},{1... | collective-permute-start | bytes 589832 | tf_op jit(solution)/shard_map/ppermute | solution.py:88
  59.5 5.9 %collective-permute-start.24 = (bf16[256,384]{1,0:T(8,128)(2,1)S(1)}, bf16[256,384]{1,0:T(8,128)(2,1)S(1)}, u32[]{:S(2)}, u32[]{:S(2)}) collective-permute-start(bf16[256,384]{1,0:T(8,128)(2,1)S(1)} %collective-permute-done.19.refs_1_), channel_id=1, source_target_pairs={{0,8},{1,5},{2,0},{3,11},{4,6},{5,13},{6,14},{7,3},{8,16},{9,1},{1... | collective-permute-start | bytes 589832 | tf_op jit(solution)/shard_map/ppermute | solution.py:88
  61.0 6.5 %collective-permute-start.25 = (bf16[256,384]{1,0:T(8,128)(2,1)S(1)}, bf16[256,384]{1,0:T(8,128)(2,1)S(1)}, u32[]{:S(2)}, u32[]{:S(2)}) collective-permute-start(bf16[256,384]{1,0:T(8,128)(2,1)S(1)} %collective-permute-done.20.refs_2_), channel_id=1, source_target_pairs={{0,2},{1,9},{2,10},{3,7},{4,12},{5,1},{6,4},{7,15},{8,0},{9,17},{1... | collective-permute-start | bytes 589832 | tf_op jit(solution)/shard_map/ppermute | solution.py:88
  62.2 8.9 %collective-permute-start.21 = (bf16[288,384]{1,0:T(8,128)(2,1)S(1)}, bf16[288,384]{1,0:T(8,128)(2,1)S(1)}, u32[]{:S(2)}, u32[]{:S(2)}) collective-permute-start(bf16[288,384]{1,0:T(8,128)(2,1)S(1)} %get-tuple-element.69), channel_id=1, source_target_pairs={{0,1},{1,0},{2,3},{3,2},{4,5},{5,4},{6,7},{7,6},{8,9},{9,8},{10,11... | collective-permute-start | bytes 663560 | tf_op jit(solution)/shard_map/ppermute | solution.py:59
  62.5 14.5 %collective-permute-start.22 = (bf16[576,384]{1,0:T(8,128)(2,1)S(1)}, bf16[576,384]{1,0:T(8,128)(2,1)S(1)}, u32[]{:S(2)}, u32[]{:S(2)}) collective-permute-start(bf16[576,384]{1,0:T(8,128)(2,1)S(1)} %get-tuple-element.70), channel_id=1, source_target_pairs={{0,4},{1,3},{2,6},{3,1},{4,0},{5,7},{6,2},{7,5},{8,12},{9,11},{10,... | collective-permute-start | bytes 1327112 | tf_op jit(solution)/shard_map/ppermute | solution.py:59
  65.4 8.5 %collective-permute-start.29 = (bf16[256,384]{1,0:T(8,128)(2,1)S(1)}, bf16[256,384]{1,0:T(8,128)(2,1)S(1)}, u32[]{:S(2)}, u32[]{:S(2)}) collective-permute-start(bf16[256,384]{1,0:T(8,128)(2,1)S(1)} %collective-permute-done.24.refs_0_), channel_id=1, source_target_pairs={{0,8},{1,5},{2,0},{3,11},{4,6},{5,13},{6,14},{7,3},{8,16},{9,1},{1... | collective-permute-start | bytes 589832 | tf_op jit(solution)/shard_map/ppermute | solution.py:88
  67.5 7.7 %collective-permute-start.30 = (bf16[256,384]{1,0:T(8,128)(2,1)S(1)}, bf16[256,384]{1,0:T(8,128)(2,1)S(1)}, u32[]{:S(2)}, u32[]{:S(2)}) collective-permute-start(bf16[256,384]{1,0:T(8,128)(2,1)S(1)} %collective-permute-done.25.refs_1_), channel_id=1, source_target_pairs={{0,2},{1,9},{2,10},{3,7},{4,12},{5,1},{6,4},{7,15},{8,0},{9,17},{1... | collective-permute-start | bytes 589832 | tf_op jit(solution)/shard_map/ppermute | solution.py:88
  68.5 9.4 %collective-permute-start.27 = (bf16[384,384]{1,0:T(8,128)(2,1)S(1)}, bf16[384,384]{1,0:T(8,128)(2,1)S(1)}, u32[]{:S(2)}, u32[]{:S(2)}) collective-permute-start(bf16[384,384]{1,0:T(8,128)(2,1)S(1)} %get-tuple-element.75), channel_id=1, source_target_pairs={{0,4},{1,3},{2,6},{3,1},{4,0},{5,7},{6,2},{7,5},{8,12},{9,11},{10,... | collective-permute-start | bytes 884744 | tf_op jit(solution)/shard_map/ppermute | solution.py:59
  71.2 8.8 %collective-permute-start.26 = (bf16[192,384]{1,0:T(8,128)(2,1)S(1)}, bf16[192,384]{1,0:T(8,128)(2,1)S(1)}, u32[]{:S(2)}, u32[]{:S(2)}) collective-permute-start(bf16[192,384]{1,0:T(8,128)(2,1)S(1)} %get-tuple-element.74), channel_id=1, source_target_pairs={{0,1},{1,0},{2,3},{3,2},{4,5},{5,4},{6,7},{7,6},{8,9},{9,8},{10,11... | collective-permute-start | bytes 442376 | tf_op jit(solution)/shard_map/ppermute | solution.py:59
  73.9 5.8 %collective-permute-start.34 = (bf16[256,384]{1,0:T(8,128)(2,1)S(1)}, bf16[256,384]{1,0:T(8,128)(2,1)S(1)}, u32[]{:S(2)}, u32[]{:S(2)}) collective-permute-start(bf16[256,384]{1,0:T(8,128)(2,1)S(1)} %collective-permute-done.29.refs_0_), channel_id=1, source_target_pairs={{0,8},{1,5},{2,0},{3,11},{4,6},{5,13},{6,14},{7,3},{8,16},{9,1},{1... | collective-permute-start | bytes 589832 | tf_op jit(solution)/shard_map/ppermute | solution.py:88
  75.6 5.2 %collective-permute-start.32 = (bf16[192,384]{1,0:T(8,128)(2,1)S(1)}, bf16[192,384]{1,0:T(8,128)(2,1)S(1)}, u32[]{:S(2)}, u32[]{:S(2)}) collective-permute-start(bf16[192,384]{1,0:T(8,128)(2,1)S(1)} %get-tuple-element.86), channel_id=1, source_target_pairs={{0,4},{1,3},{2,6},{3,1},{4,0},{5,7},{6,2},{7,5},{8,12},{9,11},{10,... | collective-permute-start | bytes 442376 | tf_op jit(solution)/shard_map/ppermute | solution.py:59
  77.0 5.1 %collective-permute-start.33 = (bf16[192,384]{1,0:T(8,128)(2,1)S(1)}, bf16[192,384]{1,0:T(8,128)(2,1)S(1)}, u32[]{:S(2)}, u32[]{:S(2)}) collective-permute-start(bf16[192,384]{1,0:T(8,128)(2,1)S(1)} %get-tuple-element.85), channel_id=1, source_target_pairs={{0,5},{1,2},{2,7},{3,0},{4,1},{5,6},{6,3},{7,4},{8,13},{9,10},{10,... | collective-permute-start | bytes 442376 | tf_op jit(solution)/shard_map/ppermute | solution.py:59
  77.9 6.4 %collective-permute-start.31 = (bf16[192,384]{1,0:T(8,128)(2,1)S(1)}, bf16[192,384]{1,0:T(8,128)(2,1)S(1)}, u32[]{:S(2)}, u32[]{:S(2)}) collective-permute-start(bf16[192,384]{1,0:T(8,128)(2,1)S(1)} %get-tuple-element.79), channel_id=1, source_target_pairs={{0,1},{1,0},{2,3},{3,2},{4,5},{5,4},{6,7},{7,6},{8,9},{9,8},{10,11... | collective-permute-start | bytes 442376 | tf_op jit(solution)/shard_map/ppermute | solution.py:59
  79.7 3.7 %collective-permute-start.23 = (bf16[288,384]{1,0:T(8,128)(2,1)S(1)}, bf16[288,384]{1,0:T(8,128)(2,1)S(1)}, u32[]{:S(2)}, u32[]{:S(2)}) collective-permute-start(bf16[288,384]{1,0:T(8,128)(2,1)S(1)} %slice.24), channel_id=1, source_target_pairs={{0,1},{1,0},{2,3},{3,2},{4,5},{5,4},{6,7},{7,6},{8,9},{9,8},{10,11... | collective-permute-start | bytes 663560 | tf_op jit(solution)/shard_map/ppermute | solution.py:59
  80.0 4.3 %collective-permute-start.28 = (bf16[192,384]{1,0:T(8,128)(2,1)S(1)}, bf16[192,384]{1,0:T(8,128)(2,1)S(1)}, u32[]{:S(2)}, u32[]{:S(2)}) collective-permute-start(bf16[192,384]{1,0:T(8,128)(2,1)S(1)} %slice.25), channel_id=1, source_target_pairs={{0,1},{1,0},{2,3},{3,2},{4,5},{5,4},{6,7},{7,6},{8,9},{9,8},{10,11... | collective-permute-start | bytes 442376 | tf_op jit(solution)/shard_map/ppermute | solution.py:59
  80.8 4.4 %collective-permute-start.36 = (bf16[96,384]{1,0:T(8,128)(2,1)S(1)}, bf16[96,384]{1,0:T(8,128)(2,1)S(1)}, u32[]{:S(2)}, u32[]{:S(2)}) collective-permute-start(bf16[96,384]{1,0:T(8,128)(2,1)S(1)} %get-tuple-element.88), channel_id=1, source_target_pairs={{0,4},{1,3},{2,6},{3,1},{4,0},{5,7},{6,2},{7,5},{8,12},{9,11},{10,... | collective-permute-start | bytes 221192 | tf_op jit(solution)/shard_map/ppermute | solution.py:59
  82.2 3.8 %collective-permute-start.37 = (bf16[96,384]{1,0:T(8,128)(2,1)S(1)}, bf16[96,384]{1,0:T(8,128)(2,1)S(1)}, u32[]{:S(2)}, u32[]{:S(2)}) collective-permute-start(bf16[96,384]{1,0:T(8,128)(2,1)S(1)} %get-tuple-element.87), channel_id=1, source_target_pairs={{0,5},{1,2},{2,7},{3,0},{4,1},{5,6},{6,3},{7,4},{8,13},{9,10},{10,... | collective-permute-start | bytes 221192 | tf_op jit(solution)/shard_map/ppermute | solution.py:59
  83.4 2.6 %collective-permute-start.35 = (bf16[96,384]{1,0:T(8,128)(2,1)S(1)}, bf16[96,384]{1,0:T(8,128)(2,1)S(1)}, u32[]{:S(2)}, u32[]{:S(2)}) collective-permute-start(bf16[96,384]{1,0:T(8,128)(2,1)S(1)} %get-tuple-element.83), channel_id=1, source_target_pairs={{0,1},{1,0},{2,3},{3,2},{4,5},{5,4},{6,7},{7,6},{8,9},{9,8},{10,11... | collective-permute-start | bytes 221192 | tf_op jit(solution)/shard_map/ppermute | solution.py:59

commit v9 on v8

--- a/solution.py
+++ b/solution.py
@@ -82,7 +82,7 @@
     around = {-1: grid.around(1), 1: grid.around(-1)}
     held, gates = {0: own}, [[]]
     for step in range(1, grid.nz + 1):
-        ways = (-1, 1) if step < grid.nz else (-1,)
+        ways = (1, -1) if step < grid.nz else (-1,)
         for way in ways:
             block = after(held[way * (step - 1)], *gates[step - 1])
             held[way * step] = lax.ppermute(block, "pair", around[way])

time: 88.3 us -> 88.3 us (level)
  no operation moved by 1% of the time
where the time goes in v9:
time: 88.3 us; the launch traced here: 88.1 us
  waiting for transfers between devices  40.5 us (46%)
  starting transfers between devices  35.7 us (40%)
  Pallas kernels  11.1 us (13%)
    ppermute x24, waiting for transfers between devices, send(): lax.ppermute(block, 'pair', [(device, int(target(device))) for device in...  25.1 us
    ppermute x24, starting transfers between devices, send(): lax.ppermute(block, 'pair', [(device, int(target(device))) for device in...  20.5 us
    ppermute x14, waiting for transfers between devices, gather_ring(): held[way * step] = lax.ppermute(block, 'pair', around[way])  15.3 us
    ppermute x14, starting transfers between devices, gather_ring(): held[way * step] = lax.ppermute(block, 'pair', around[way])  15.1 us
    pallas_call x4, Pallas kernels, first_product(): pl.pallas_call(body, out_shape=shapes, in_specs=vmem(4 + len(totals) + le...  2.99 us
    pallas_call x1, Pallas kernels, share_integrals(): pl.pallas_call(body, out_shape=[jax.ShapeDtypeStruct((rows + batch_rows *...  2.52 us
    pallas_call x1, Pallas kernels, place_pairs(): pl.pallas_call(body, out_shape=jax.ShapeDtypeStruct((2, share, width, pai...  2.2 us
  transfers between devices with their start and end apart: 38, of which 18 were waited for; matrix products, arithmetic and copies ran while one was open for 0% of the time, Pallas kernels for 9%

profile of v9, /device:TPU:0, one launch (start us, length us, event | category | flops | bytes accessed | tf_op | source)
XLA Modules:
  0.0 88.1 jit_solution(15447119566108197005)
XLA Ops:
  0.0 3.0 %collective-permute-start.9 = (bf16[2,256,384]{2,1,0:T(8,128)(2,1)}, bf16[2,256,384]{2,1,0:T(8,128)(2,1)S(1)}, u32[]{:S(2)}, u32[]{:S(2)}) collective-permute-start(bf16[2,256,384]{2,1,0:T(8,128)(2,1)} %refs_4_.1), channel_id=1, source_target_pairs={{0,8},{1,5},{2,0},{3,11},{4,6},{5,13},{6,14},{7,3},{8,16},{9,1},{1... | collective-permute-start | bytes 1179656 | tf_op jit(solution)/shard_map/ppermute | solution.py:88
  3.0 0.7 copy-done.1
  3.7 2.5 %share_integrals.1 = (bf16[160,768]{1,0:T(8,128)(2,1)S(1)}, bf16[128,768]{1,0:T(8,128)(2,1)S(1)}, bf16[128,768]{1,0:T(8,128)(2,1)S(1)}, bf16[128,768]{1,0:T(8,12...) custom-call(s32[1]{0:T(128)} %bitcast.where_ref, ...), custom_call_target="tpu_custom_call" | custom-call | tf_op jit(solution)/shard_map/share_integrals/pallas_call | solution.py:134
  6.2 5.5 %collective-permute-done.9.refs_5_ = bf16[2,256,384]{2,1,0:T(8,128)(2,1)S(1)} collective-permute-done((bf16[2,256,384]{2,1,0:T(8,128)(2,1)}, bf16[2,256,384]{2,1,0:T(8,128)(2,1)S(1)}, u32[]{:S(2)}, u32[]{:S(2)}) %collective-permute-start.9) | collective-permute-done | bytes 393248 | tf_op jit(solution)/shard_map/ppermute | solution.py:88
  11.7 2.4 %collective-permute-start.11 = (bf16[2,256,384]{2,1,0:T(8,128)(2,1)S(1)}, bf16[2,256,384]{2,1,0:T(8,128)(2,1)S(1)}, u32[]{:S(2)}, u32[]{:S(2)}) collective-permute-start(bf16[2,256,384]{2,1,0:T(8,128)(2,1)S(1)} %collective-permute-done.9.refs_5_), channel_id=1, source_target_pairs={{0,8},{1,5},{2,0},{3,11},{4,6},{5,13},{6,14},{7,3},{8,16},{9,1},{1... | collective-permute-start | bytes 1179656 | tf_op jit(solution)/shard_map/ppermute | solution.py:88
  14.1 0.9 collective-permute-start.12
  15.0 2.1 %collective-permute-start.7 = (bf16[128,768]{1,0:T(8,128)(2,1)S(1)}, bf16[128,768]{1,0:T(8,128)(2,1)S(1)}, u32[]{:S(2)}, u32[]{:S(2)}) collective-permute-start(bf16[128,768]{1,0:T(8,128)(2,1)S(1)} %get-tuple-element.55), channel_id=1, source_target_pairs={{0,4},{1,3},{2,6},{3,1},{4,0},{5,7},{6,2},{7,5},{8,12},{9,11},{10,... | collective-permute-start | bytes 589832 | tf_op jit(solution)/shard_map/ppermute | solution.py:59
  17.0 0.1 collective-permute-start.8
  17.2 5.7 %collective-permute-done.7.refs_2_ = bf16[128,768]{1,0:T(8,128)(2,1)S(1)} collective-permute-done((bf16[128,768]{1,0:T(8,128)(2,1)S(1)}, bf16[128,768]{1,0:T(8,128)(2,1)S(1)}, u32[]{:S(2)}, u32[]{:S(2)}) %collective-permute-start.7) | collective-permute-done | bytes 196640 | tf_op jit(solution)/shard_map/ppermute | solution.py:59
  22.9 1.6 %collective-permute-done.8.refs_3_ = bf16[128,768]{1,0:T(8,128)(2,1)S(1)} collective-permute-done((bf16[128,768]{1,0:T(8,128)(2,1)S(1)}, bf16[128,768]{1,0:T(8,128)(2,1)S(1)}, u32[]{:S(2)}, u32[]{:S(2)}) %collective-permute-start.8) | collective-permute-done | bytes 196640 | tf_op jit(solution)/shard_map/ppermute | solution.py:59
  24.5 2.3 %collective-permute-start.3 = (bf16[128,512]{1,0:T(8,128)(2,1)S(1)}, bf16[128,512]{1,0:T(8,128)(2,1)S(1)}, u32[]{:S(2)}, u32[]{:S(2)}) collective-permute-start(bf16[128,512]{1,0:T(8,128)(2,1)S(1)} %get-tuple-element.50), channel_id=1, source_target_pairs={{0,1},{1,0},{2,3},{3,2},{4,5},{5,4},{6,7},{7,6},{8,9},{9,8},{10,11... | collective-permute-start | bytes 393224 | tf_op jit(solution)/shard_map/ppermute | solution.py:59
  26.8 0.3 collective-permute-start.4
  27.1 1.1 %collective-permute-start.5 = (bf16[128,512]{1,0:T(8,128)(2,1)S(1)}, bf16[128,512]{1,0:T(8,128)(2,1)S(1)}, u32[]{:S(2)}, u32[]{:S(2)}) collective-permute-start(bf16[128,512]{1,0:T(8,128)(2,1)S(1)} %get-tuple-element.52), channel_id=1, source_target_pairs={{0,3},{1,4},{2,1},{3,6},{4,7},{5,0},{6,5},{7,2},{8,11},{9,12},{10,... | collective-permute-start | bytes 393224 | tf_op jit(solution)/shard_map/ppermute | solution.py:59
  28.1 0.4 collective-permute-start.14
  28.6 1.0 %first_product.4.refs_4_ = f32[544,768]{1,0:T(8,128)S(1)} custom-call(bf16[160,768]{1,0:T(8,128)(2,1)S(1)} %get-tuple-element.53.refs_0_, bf16[128,768]{1,0:T(8,128)(2,1)S(1)} %collective-permute-done.6.refs_1_, bf16[128,768]{1,0:T(8,128)(2,1)S(1)} %collective-permute-done.7.refs_2_, bf16[128,768]{1,0:T(8,128)(2,1)S(1)} %collective-permute-done.8.refs_3_, ...), custom_call_target="tpu_custom_call" | custom-call | flops 3208642560 | tf_op jit(solution)/shard_map/first_product/pallas_call | solution.py:184
  29.6 0.5 collective-permute-start
  30.1 3.1 %collective-permute-done.4.refs_2_ = bf16[128,512]{1,0:T(8,128)(2,1)S(1)} collective-permute-done((bf16[128,512]{1,0:T(8,128)(2,1)S(1)}, bf16[128,512]{1,0:T(8,128)(2,1)S(1)}, u32[]{:S(2)}, u32[]{:S(2)}) %collective-permute-start.4) | collective-permute-done | bytes 131104 | tf_op jit(solution)/shard_map/ppermute | solution.py:59
  33.2 0.3 collective-permute-start.1
  33.4 0.3 collective-permute-start.2
  33.7 0.7 collective-permute-start.15
  34.4 0.7 first_product.5.refs_4_
  35.2 5.8 %collective-permute-done.1.refs_2_ = bf16[128,768]{1,0:T(8,128)(2,1)S(1)} collective-permute-done((bf16[128,768]{1,0:T(8,128)(2,1)S(1)}, bf16[128,768]{1,0:T(8,128)(2,1)S(1)}, u32[]{:S(2)}, u32[]{:S(2)}) %collective-permute-start.1) | collective-permute-done | bytes 196640 | tf_op jit(solution)/shard_map/ppermute | solution.py:59
  41.0 0.3 collective-permute-done.2.refs_3_
  41.3 0.7 first_product.6.refs_4_
  42.1 2.7 %collective-permute-done.15.refs_5_ = bf16[2,256,384]{2,1,0:T(8,128)(2,1)S(1)} collective-permute-done((bf16[2,256,384]{2,1,0:T(8,128)(2,1)S(1)}, bf16[2,256,384]{2,1,0:T(8,128)(2,1)S(1)}, u32[]{:S(2)}, u32[]{:S(2)}) %collective-permute-start.15) | collective-permute-done | bytes 393248 | tf_op jit(solution)/shard_map/ppermute | solution.py:88
  44.8 0.5 first_product.7
  45.2 0.1 collective-permute-start.16
  45.3 1.0 %collective-permute-start.17 = (bf16[160,768]{1,0:T(8,128)(2,1)S(1)}, bf16[160,768]{1,0:T(8,128)(2,1)S(1)}, u32[]{:S(2)}, u32[]{:S(2)}) collective-permute-start(bf16[160,768]{1,0:T(8,128)(2,1)S(1)} %get-tuple-element.64), channel_id=1, source_target_pairs={{0,4},{1,3},{2,6},{3,1},{4,0},{5,7},{6,2},{7,5},{8,12},{9,11},{10,... | collective-permute-start | bytes 737288 | tf_op jit(solution)/shard_map/ppermute | solution.py:59
  46.3 1.5 %collective-permute-start.18 = (bf16[160,768]{1,0:T(8,128)(2,1)S(1)}, bf16[160,768]{1,0:T(8,128)(2,1)S(1)}, u32[]{:S(2)}, u32[]{:S(2)}) collective-permute-start(bf16[160,768]{1,0:T(8,128)(2,1)S(1)} %get-tuple-element.65), channel_id=1, source_target_pairs={{0,5},{1,2},{2,7},{3,0},{4,1},{5,6},{6,3},{7,4},{8,13},{9,10},{10,... | collective-permute-start | bytes 737288 | tf_op jit(solution)/shard_map/ppermute | solution.py:59
  47.8 3.8 %collective-permute-done.17.refs_2_ = bf16[160,768]{1,0:T(8,128)(2,1)S(1)} collective-permute-done((bf16[160,768]{1,0:T(8,128)(2,1)S(1)}, bf16[160,768]{1,0:T(8,128)(2,1)S(1)}, u32[]{:S(2)}, u32[]{:S(2)}) %collective-permute-start.17) | collective-permute-done | bytes 245792 | tf_op jit(solution)/shard_map/ppermute | solution.py:59
  51.6 2.1 %collective-permute-done.18.refs_3_ = bf16[160,768]{1,0:T(8,128)(2,1)S(1)} collective-permute-done((bf16[160,768]{1,0:T(8,128)(2,1)S(1)}, bf16[160,768]{1,0:T(8,128)(2,1)S(1)}, u32[]{:S(2)}, u32[]{:S(2)}) %collective-permute-start.18) | collective-permute-done | bytes 245792 | tf_op jit(solution)/shard_map/ppermute | solution.py:59
  53.7 0.1 add_partners.1
  53.8 2.0 %collective-permute-start.20 = (bf16[256,384]{1,0:T(8,128)(2,1)S(1)}, bf16[256,384]{1,0:T(8,128)(2,1)S(1)}, u32[]{:S(2)}, u32[]{:S(2)}) collective-permute-start(bf16[256,384]{1,0:T(8,128)(2,1)S(1)} %get-tuple-element.67.refs_0_), channel_id=1, source_target_pairs={{0,2},{1,9},{2,10},{3,7},{4,12},{5,1},{6,4},{7,15},{8,0},{9,17},{1... | collective-permute-start | bytes 589832 | tf_op jit(solution)/shard_map/ppermute | solution.py:88
  55.8 0.5 pair_places.1.place_ref
  56.3 1.2 %weights.1.matrix_ref = bf16[384,256]{1,0:T(8,128)(2,1)S(1)} custom-call(s32[1]{0:T(128)} %bitcast.where_ref, bf16[64,384]{1,0:T(8,128)(2,1)S(1)} %get-tuple-element.66.batch_ref), custom_call_target="tpu_custom_call" | custom-call | tf_op jit(solution)/shard_map/weights/pallas_call | solution.py:249
  57.6 1.9 %collective-permute-done.19.refs_1_ = bf16[256,384]{1,0:T(8,128)(2,1)S(1)} collective-permute-done((bf16[256,384]{1,0:T(8,128)(2,1)S(1)}, bf16[256,384]{1,0:T(8,128)(2,1)S(1)}, u32[]{:S(2)}, u32[]{:S(2)}) %collective-permute-start.19) | collective-permute-done | bytes 196640 | tf_op jit(solution)/shard_map/ppermute | solution.py:88
  59.5 1.0 %collective-permute-start.24 = (bf16[256,384]{1,0:T(8,128)(2,1)S(1)}, bf16[256,384]{1,0:T(8,128)(2,1)S(1)}, u32[]{:S(2)}, u32[]{:S(2)}) collective-permute-start(bf16[256,384]{1,0:T(8,128)(2,1)S(1)} %collective-permute-done.19.refs_1_), channel_id=1, source_target_pairs={{0,8},{1,5},{2,0},{3,11},{4,6},{5,13},{6,14},{7,3},{8,16},{9,1},{1... | collective-permute-start | bytes 589832 | tf_op jit(solution)/shard_map/ppermute | solution.py:88
  60.4 0.5 collective-permute-done.20.refs_2_
  61.0 0.8 collective-permute-start.25
  61.8 0.5 second_product.4
  62.2 0.2 collective-permute-start.21
  62.5 2.2 %collective-permute-start.22 = (bf16[576,384]{1,0:T(8,128)(2,1)S(1)}, bf16[576,384]{1,0:T(8,128)(2,1)S(1)}, u32[]{:S(2)}, u32[]{:S(2)}) collective-permute-start(bf16[576,384]{1,0:T(8,128)(2,1)S(1)} %get-tuple-element.70), channel_id=1, source_target_pairs={{0,4},{1,3},{2,6},{3,1},{4,0},{5,7},{6,2},{7,5},{8,12},{9,11},{10,... | collective-permute-start | bytes 1327112 | tf_op jit(solution)/shard_map/ppermute | solution.py:59
  64.7 0.7 collective-permute-done.24.refs_0_
  65.4 2.1 %collective-permute-start.29 = (bf16[256,384]{1,0:T(8,128)(2,1)S(1)}, bf16[256,384]{1,0:T(8,128)(2,1)S(1)}, u32[]{:S(2)}, u32[]{:S(2)}) collective-permute-start(bf16[256,384]{1,0:T(8,128)(2,1)S(1)} %collective-permute-done.24.refs_0_), channel_id=1, source_target_pairs={{0,8},{1,5},{2,0},{3,11},{4,6},{5,13},{6,14},{7,3},{8,16},{9,1},{1... | collective-permute-start | bytes 589832 | tf_op jit(solution)/shard_map/ppermute | solution.py:88
  67.5 0.7 collective-permute-start.30
  68.1 0.4 second_product.5
  68.5 2.7 %collective-permute-start.27 = (bf16[384,384]{1,0:T(8,128)(2,1)S(1)}, bf16[384,384]{1,0:T(8,128)(2,1)S(1)}, u32[]{:S(2)}, u32[]{:S(2)}) collective-permute-start(bf16[384,384]{1,0:T(8,128)(2,1)S(1)} %get-tuple-element.75), channel_id=1, source_target_pairs={{0,4},{1,3},{2,6},{3,1},{4,0},{5,7},{6,2},{7,5},{8,12},{9,11},{10,... | collective-permute-start | bytes 884744 | tf_op jit(solution)/shard_map/ppermute | solution.py:59
  71.2 2.8 %collective-permute-done.29.refs_0_ = bf16[256,384]{1,0:T(8,128)(2,1)S(1)} collective-permute-done((bf16[256,384]{1,0:T(8,128)(2,1)S(1)}, bf16[256,384]{1,0:T(8,128)(2,1)S(1)}, u32[]{:S(2)}, u32[]{:S(2)}) %collective-permute-start.29) | collective-permute-done | bytes 196640 | tf_op jit(solution)/shard_map/ppermute | solution.py:88
  73.9 1.2 %collective-permute-start.34 = (bf16[256,384]{1,0:T(8,128)(2,1)S(1)}, bf16[256,384]{1,0:T(8,128)(2,1)S(1)}, u32[]{:S(2)}, u32[]{:S(2)}) collective-permute-start(bf16[256,384]{1,0:T(8,128)(2,1)S(1)} %collective-permute-done.29.refs_0_), channel_id=1, source_target_pairs={{0,8},{1,5},{2,0},{3,11},{4,6},{5,13},{6,14},{7,3},{8,16},{9,1},{1... | collective-permute-start | bytes 589832 | tf_op jit(solution)/shard_map/ppermute | solution.py:88
  75.2 0.4 second_product.6
  75.6 1.5 %collective-permute-start.32 = (bf16[192,384]{1,0:T(8,128)(2,1)S(1)}, bf16[192,384]{1,0:T(8,128)(2,1)S(1)}, u32[]{:S(2)}, u32[]{:S(2)}) collective-permute-start(bf16[192,384]{1,0:T(8,128)(2,1)S(1)} %get-tuple-element.86), channel_id=1, source_target_pairs={{0,4},{1,3},{2,6},{3,1},{4,0},{5,7},{6,2},{7,5},{8,12},{9,11},{10,... | collective-permute-start | bytes 442376 | tf_op jit(solution)/shard_map/ppermute | solution.py:59
  77.1 0.8 collective-permute-done.27.refs_2_
  77.9 0.7 collective-permute-start.31
  78.6 1.1 %collective-permute-done.34.refs_0_ = bf16[256,384]{1,0:T(8,128)(2,1)S(1)} collective-permute-done((bf16[256,384]{1,0:T(8,128)(2,1)S(1)}, bf16[256,384]{1,0:T(8,128)(2,1)S(1)}, u32[]{:S(2)}, u32[]{:S(2)}) %collective-permute-start.34) | collective-permute-done | bytes 196640 | tf_op jit(solution)/shard_map/ppermute | solution.py:88
  79.7 0.3 second_product.7
  80.0 0.6 collective-permute-start.28
  80.6 0.2 collective-permute-done.32.refs_6_
  80.8 1.4 %collective-permute-start.36 = (bf16[96,384]{1,0:T(8,128)(2,1)S(1)}, bf16[96,384]{1,0:T(8,128)(2,1)S(1)}, u32[]{:S(2)}, u32[]{:S(2)}) collective-permute-start(bf16[96,384]{1,0:T(8,128)(2,1)S(1)} %get-tuple-element.88), channel_id=1, source_target_pairs={{0,4},{1,3},{2,6},{3,1},{4,0},{5,7},{6,2},{7,5},{8,12},{9,11},{10,... | collective-permute-start | bytes 221192 | tf_op jit(solution)/shard_map/ppermute | solution.py:59
  82.2 1.2 %collective-permute-start.37 = (bf16[96,384]{1,0:T(8,128)(2,1)S(1)}, bf16[96,384]{1,0:T(8,128)(2,1)S(1)}, u32[]{:S(2)}, u32[]{:S(2)}) collective-permute-start(bf16[96,384]{1,0:T(8,128)(2,1)S(1)} %get-tuple-element.87), channel_id=1, source_target_pairs={{0,5},{1,2},{2,7},{3,0},{4,1},{5,6},{6,3},{7,4},{8,13},{9,10},{10,... | collective-permute-start | bytes 221192 | tf_op jit(solution)/shard_map/ppermute | solution.py:59
  83.4 0.8 collective-permute-start.35
  84.1 0.1 widen.1.wide_ref
  84.3 0.9 collective-permute-done.36.refs_10_
  85.1 0.8 collective-permute-done.37.refs_11_
  86.0 2.2 %place_pairs.1 = bf16[2,12,384,128]{3,2,1,0:T(8,128)(2,1)} custom-call(bf16[128,128]{1,0:T(8,128)(2,1)S(1)} %pair_places.1.place_ref, f32[3,1440,128]{2,1,0:T(8,128)S(1)} %widen.1.wide_ref, bf16[192,384]{1,0:T(8,128)(2,1)S(1)} %get-tuple-element.73.refs_0_, bf16[192,384]{1,0:T(8,128)(2,1)S(1)} %collective-permute-done.26.refs_1_, ...), custom_call_target="tpu_custom_call" | custom-call | tf_op jit(solution)/shard_map/place_pairs/pallas_call | solution.py:360
  (36 shorter events, 0.2 us)
Async XLA Ops:
  0.0 11.7 %collective-permute-start.9 = (bf16[2,256,384]{2,1,0:T(8,128)(2,1)}, bf16[2,256,384]{2,1,0:T(8,128)(2,1)S(1)}, u32[]{:S(2)}, u32[]{:S(2)}) collective-permute-start(bf16[2,256,384]{2,1,0:T(8,128)(2,1)} %refs_4_.1), channel_id=1, source_target_pairs={{0,8},{1,5},{2,0},{3,11},{4,6},{5,13},{6,14},{7,3},{8,16},{9,1},{1... | collective-permute-start | bytes 1179656 | tf_op jit(solution)/shard_map/ppermute | solution.py:88
  3.0 11.1 %collective-permute-start.10 = (bf16[2,256,384]{2,1,0:T(8,128)(2,1)}, bf16[2,256,384]{2,1,0:T(8,128)(2,1)S(1)}, u32[]{:S(2)}, u32[]{:S(2)}) collective-permute-start(bf16[2,256,384]{2,1,0:T(8,128)(2,1)} %refs_4_.1), channel_id=1, source_target_pairs={{0,2},{1,9},{2,10},{3,7},{4,12},{5,1},{6,4},{7,15},{8,0},{9,17},{1... | collective-permute-start | bytes 1179656 | tf_op jit(solution)/shard_map/ppermute | solution.py:88
  3.0 0.7 copy-start.1
  3.7 24.9 %copy-start.2 = (bf16[2,256,384]{2,1,0:T(8,128)(2,1)S(1)}, bf16[2,256,384]{2,1,0:T(8,128)(2,1)}, u32[]{:S(2)}) copy-start(bf16[2,256,384]{2,1,0:T(8,128)(2,1)} %refs_4_.1) | copy-start | bytes 1179652
  11.7 12.8 %collective-permute-start.11 = (bf16[2,256,384]{2,1,0:T(8,128)(2,1)S(1)}, bf16[2,256,384]{2,1,0:T(8,128)(2,1)S(1)}, u32[]{:S(2)}, u32[]{:S(2)}) collective-permute-start(bf16[2,256,384]{2,1,0:T(8,128)(2,1)S(1)} %collective-permute-done.9.refs_5_), channel_id=1, source_target_pairs={{0,8},{1,5},{2,0},{3,11},{4,6},{5,13},{6,14},{7,3},{8,16},{9,1},{1... | collective-permute-start | bytes 1179656 | tf_op jit(solution)/shard_map/ppermute | solution.py:88
  14.1 14.0 %collective-permute-start.12 = (bf16[2,256,384]{2,1,0:T(8,128)(2,1)S(1)}, bf16[2,256,384]{2,1,0:T(8,128)(2,1)S(1)}, u32[]{:S(2)}, u32[]{:S(2)}) collective-permute-start(bf16[2,256,384]{2,1,0:T(8,128)(2,1)S(1)} %collective-permute-done.10.refs_6_), channel_id=1, source_target_pairs={{0,2},{1,9},{2,10},{3,7},{4,12},{5,1},{6,4},{7,15},{8,0},{9,17},{1... | collective-permute-start | bytes 1179656 | tf_op jit(solution)/shard_map/ppermute | solution.py:88
  15.0 2.2 %collective-permute-start.6 = (bf16[128,768]{1,0:T(8,128)(2,1)S(1)}, bf16[128,768]{1,0:T(8,128)(2,1)S(1)}, u32[]{:S(2)}, u32[]{:S(2)}) collective-permute-start(bf16[128,768]{1,0:T(8,128)(2,1)S(1)} %get-tuple-element.54), channel_id=1, source_target_pairs={{0,1},{1,0},{2,3},{3,2},{4,5},{5,4},{6,7},{7,6},{8,9},{9,8},{10,11... | collective-permute-start | bytes 589832 | tf_op jit(solution)/shard_map/ppermute | solution.py:59
  15.0 7.9 %collective-permute-start.7 = (bf16[128,768]{1,0:T(8,128)(2,1)S(1)}, bf16[128,768]{1,0:T(8,128)(2,1)S(1)}, u32[]{:S(2)}, u32[]{:S(2)}) collective-permute-start(bf16[128,768]{1,0:T(8,128)(2,1)S(1)} %get-tuple-element.55), channel_id=1, source_target_pairs={{0,4},{1,3},{2,6},{3,1},{4,0},{5,7},{6,2},{7,5},{8,12},{9,11},{10,... | collective-permute-start | bytes 589832 | tf_op jit(solution)/shard_map/ppermute | solution.py:59
  17.0 7.5 %collective-permute-start.8 = (bf16[128,768]{1,0:T(8,128)(2,1)S(1)}, bf16[128,768]{1,0:T(8,128)(2,1)S(1)}, u32[]{:S(2)}, u32[]{:S(2)}) collective-permute-start(bf16[128,768]{1,0:T(8,128)(2,1)S(1)} %get-tuple-element.56), channel_id=1, source_target_pairs={{0,3},{1,4},{2,1},{3,6},{4,7},{5,0},{6,5},{7,2},{8,11},{9,12},{10,... | collective-permute-start | bytes 589832 | tf_op jit(solution)/shard_map/ppermute | solution.py:59
  24.5 9.2 %collective-permute-start.13 = (bf16[2,256,384]{2,1,0:T(8,128)(2,1)S(1)}, bf16[2,256,384]{2,1,0:T(8,128)(2,1)S(1)}, u32[]{:S(2)}, u32[]{:S(2)}) collective-permute-start(bf16[2,256,384]{2,1,0:T(8,128)(2,1)S(1)} %collective-permute-done.11.refs_5_), channel_id=1, source_target_pairs={{0,8},{1,5},{2,0},{3,11},{4,6},{5,13},{6,14},{7,3},{8,16},{9,1},{1... | collective-permute-start | bytes 1179656 | tf_op jit(solution)/shard_map/ppermute | solution.py:88
  24.5 5.1 %collective-permute-start.3 = (bf16[128,512]{1,0:T(8,128)(2,1)S(1)}, bf16[128,512]{1,0:T(8,128)(2,1)S(1)}, u32[]{:S(2)}, u32[]{:S(2)}) collective-permute-start(bf16[128,512]{1,0:T(8,128)(2,1)S(1)} %get-tuple-element.50), channel_id=1, source_target_pairs={{0,1},{1,0},{2,3},{3,2},{4,5},{5,4},{6,7},{7,6},{8,9},{9,8},{10,11... | collective-permute-start | bytes 393224 | tf_op jit(solution)/shard_map/ppermute | solution.py:59
  26.8 6.4 %collective-permute-start.4 = (bf16[128,512]{1,0:T(8,128)(2,1)S(1)}, bf16[128,512]{1,0:T(8,128)(2,1)S(1)}, u32[]{:S(2)}, u32[]{:S(2)}) collective-permute-start(bf16[128,512]{1,0:T(8,128)(2,1)S(1)} %get-tuple-element.51), channel_id=1, source_target_pairs={{0,4},{1,3},{2,6},{3,1},{4,0},{5,7},{6,2},{7,5},{8,12},{9,11},{10,... | collective-permute-start | bytes 393224 | tf_op jit(solution)/shard_map/ppermute | solution.py:59
  27.1 6.4 %collective-permute-start.5 = (bf16[128,512]{1,0:T(8,128)(2,1)S(1)}, bf16[128,512]{1,0:T(8,128)(2,1)S(1)}, u32[]{:S(2)}, u32[]{:S(2)}) collective-permute-start(bf16[128,512]{1,0:T(8,128)(2,1)S(1)} %get-tuple-element.52), channel_id=1, source_target_pairs={{0,3},{1,4},{2,1},{3,6},{4,7},{5,0},{6,5},{7,2},{8,11},{9,12},{10,... | collective-permute-start | bytes 393224 | tf_op jit(solution)/shard_map/ppermute | solution.py:59
  28.1 13.2 %collective-permute-start.14 = (bf16[2,256,384]{2,1,0:T(8,128)(2,1)S(1)}, bf16[2,256,384]{2,1,0:T(8,128)(2,1)S(1)}, u32[]{:S(2)}, u32[]{:S(2)}) collective-permute-start(bf16[2,256,384]{2,1,0:T(8,128)(2,1)S(1)} %collective-permute-done.12.refs_6_), channel_id=1, source_target_pairs={{0,2},{1,9},{2,10},{3,7},{4,12},{5,1},{6,4},{7,15},{8,0},{9,17},{1... | collective-permute-start | bytes 1179656 | tf_op jit(solution)/shard_map/ppermute | solution.py:88
  29.6 5.5 %collective-permute-start = (bf16[128,768]{1,0:T(8,128)(2,1)S(1)}, bf16[128,768]{1,0:T(8,128)(2,1)S(1)}, u32[]{:S(2)}, u32[]{:S(2)}) collective-permute-start(bf16[128,768]{1,0:T(8,128)(2,1)S(1)} %get-tuple-element.46), channel_id=1, source_target_pairs={{0,1},{1,0},{2,3},{3,2},{4,5},{5,4},{6,7},{7,6},{8,9},{9,8},{10,11... | collective-permute-start | bytes 589832 | tf_op jit(solution)/shard_map/ppermute | solution.py:59
  33.2 7.8 %collective-permute-start.1 = (bf16[128,768]{1,0:T(8,128)(2,1)S(1)}, bf16[128,768]{1,0:T(8,128)(2,1)S(1)}, u32[]{:S(2)}, u32[]{:S(2)}) collective-permute-start(bf16[128,768]{1,0:T(8,128)(2,1)S(1)} %get-tuple-element.47), channel_id=1, source_target_pairs={{0,4},{1,3},{2,6},{3,1},{4,0},{5,7},{6,2},{7,5},{8,12},{9,11},{10,... | collective-permute-start | bytes 589832 | tf_op jit(solution)/shard_map/ppermute | solution.py:59
  33.4 7.9 %collective-permute-start.2 = (bf16[128,768]{1,0:T(8,128)(2,1)S(1)}, bf16[128,768]{1,0:T(8,128)(2,1)S(1)}, u32[]{:S(2)}, u32[]{:S(2)}) collective-permute-start(bf16[128,768]{1,0:T(8,128)(2,1)S(1)} %get-tuple-element.48), channel_id=1, source_target_pairs={{0,3},{1,4},{2,1},{3,6},{4,7},{5,0},{6,5},{7,2},{8,11},{9,12},{10,... | collective-permute-start | bytes 589832 | tf_op jit(solution)/shard_map/ppermute | solution.py:59
  33.7 11.0 %collective-permute-start.15 = (bf16[2,256,384]{2,1,0:T(8,128)(2,1)S(1)}, bf16[2,256,384]{2,1,0:T(8,128)(2,1)S(1)}, u32[]{:S(2)}, u32[]{:S(2)}) collective-permute-start(bf16[2,256,384]{2,1,0:T(8,128)(2,1)S(1)} %collective-permute-done.13.refs_5_), channel_id=1, source_target_pairs={{0,8},{1,5},{2,0},{3,11},{4,6},{5,13},{6,14},{7,3},{8,16},{9,1},{1... | collective-permute-start | bytes 1179656 | tf_op jit(solution)/shard_map/ppermute | solution.py:88
  42.1 13.8 %copy-start = (s32[1,128]{1,0:T(1,128)S(1)}, s32[1,128]{1,0:T(1,128)}, u32[]{:S(2)}) copy-start(s32[1,128]{1,0:T(1,128)} %pair_ref.1) | copy-start | bytes 1540
  45.2 8.4 %collective-permute-start.16 = (f32[160,768]{1,0:T(8,128)S(1)}, f32[160,768]{1,0:T(8,128)S(1)}, u32[]{:S(2)}, u32[]{:S(2)}) collective-permute-start(f32[160,768]{1,0:T(8,128)S(1)} %get-tuple-element.63), channel_id=1, source_target_pairs={{0,1},{1,0},{2,3},{3,2},{4,5},{5,4},{6,7},{7,6},{8,9},{9,8},{10,11... | collective-permute-start | bytes 1474568 | tf_op jit(solution)/shard_map/ppermute | solution.py:59
  45.3 6.3 %collective-permute-start.17 = (bf16[160,768]{1,0:T(8,128)(2,1)S(1)}, bf16[160,768]{1,0:T(8,128)(2,1)S(1)}, u32[]{:S(2)}, u32[]{:S(2)}) collective-permute-start(bf16[160,768]{1,0:T(8,128)(2,1)S(1)} %get-tuple-element.64), channel_id=1, source_target_pairs={{0,4},{1,3},{2,6},{3,1},{4,0},{5,7},{6,2},{7,5},{8,12},{9,11},{10,... | collective-permute-start | bytes 737288 | tf_op jit(solution)/shard_map/ppermute | solution.py:59
  46.3 7.3 %collective-permute-start.18 = (bf16[160,768]{1,0:T(8,128)(2,1)S(1)}, bf16[160,768]{1,0:T(8,128)(2,1)S(1)}, u32[]{:S(2)}, u32[]{:S(2)}) collective-permute-start(bf16[160,768]{1,0:T(8,128)(2,1)S(1)} %get-tuple-element.65), channel_id=1, source_target_pairs={{0,5},{1,2},{2,7},{3,0},{4,1},{5,6},{6,3},{7,4},{8,13},{9,10},{10,... | collective-permute-start | bytes 737288 | tf_op jit(solution)/shard_map/ppermute | solution.py:59
  53.8 5.7 %collective-permute-start.19 = (bf16[256,384]{1,0:T(8,128)(2,1)S(1)}, bf16[256,384]{1,0:T(8,128)(2,1)S(1)}, u32[]{:S(2)}, u32[]{:S(2)}) collective-permute-start(bf16[256,384]{1,0:T(8,128)(2,1)S(1)} %get-tuple-element.67.refs_0_), channel_id=1, source_target_pairs={{0,8},{1,5},{2,0},{3,11},{4,6},{5,13},{6,14},{7,3},{8,16},{9,1},{1... | collective-permute-start | bytes 589832 | tf_op jit(solution)/shard_map/ppermute | solution.py:88
  53.8 7.2 %collective-permute-start.20 = (bf16[256,384]{1,0:T(8,128)(2,1)S(1)}, bf16[256,384]{1,0:T(8,128)(2,1)S(1)}, u32[]{:S(2)}, u32[]{:S(2)}) collective-permute-start(bf16[256,384]{1,0:T(8,128)(2,1)S(1)} %get-tuple-element.67.refs_0_), channel_id=1, source_target_pairs={{0,2},{1,9},{2,10},{3,7},{4,12},{5,1},{6,4},{7,15},{8,0},{9,17},{1... | collective-permute-start | bytes 589832 | tf_op jit(solution)/shard_map/ppermute | solution.py:88
  59.5 5.9 %collective-permute-start.24 = (bf16[256,384]{1,0:T(8,128)(2,1)S(1)}, bf16[256,384]{1,0:T(8,128)(2,1)S(1)}, u32[]{:S(2)}, u32[]{:S(2)}) collective-permute-start(bf16[256,384]{1,0:T(8,128)(2,1)S(1)} %collective-permute-done.19.refs_1_), channel_id=1, source_target_pairs={{0,8},{1,5},{2,0},{3,11},{4,6},{5,13},{6,14},{7,3},{8,16},{9,1},{1... | collective-permute-start | bytes 589832 | tf_op jit(solution)/shard_map/ppermute | solution.py:88
  61.0 6.5 %collective-permute-start.25 = (bf16[256,384]{1,0:T(8,128)(2,1)S(1)}, bf16[256,384]{1,0:T(8,128)(2,1)S(1)}, u32[]{:S(2)}, u32[]{:S(2)}) collective-permute-start(bf16[256,384]{1,0:T(8,128)(2,1)S(1)} %collective-permute-done.20.refs_2_), channel_id=1, source_target_pairs={{0,2},{1,9},{2,10},{3,7},{4,12},{5,1},{6,4},{7,15},{8,0},{9,17},{1... | collective-permute-start | bytes 589832 | tf_op jit(solution)/shard_map/ppermute | solution.py:88
  62.2 8.9 %collective-permute-start.21 = (bf16[288,384]{1,0:T(8,128)(2,1)S(1)}, bf16[288,384]{1,0:T(8,128)(2,1)S(1)}, u32[]{:S(2)}, u32[]{:S(2)}) collective-permute-start(bf16[288,384]{1,0:T(8,128)(2,1)S(1)} %get-tuple-element.69), channel_id=1, source_target_pairs={{0,1},{1,0},{2,3},{3,2},{4,5},{5,4},{6,7},{7,6},{8,9},{9,8},{10,11... | collective-permute-start | bytes 663560 | tf_op jit(solution)/shard_map/ppermute | solution.py:59
  62.5 14.5 %collective-permute-start.22 = (bf16[576,384]{1,0:T(8,128)(2,1)S(1)}, bf16[576,384]{1,0:T(8,128)(2,1)S(1)}, u32[]{:S(2)}, u32[]{:S(2)}) collective-permute-start(bf16[576,384]{1,0:T(8,128)(2,1)S(1)} %get-tuple-element.70), channel_id=1, source_target_pairs={{0,4},{1,3},{2,6},{3,1},{4,0},{5,7},{6,2},{7,5},{8,12},{9,11},{10,... | collective-permute-start | bytes 1327112 | tf_op jit(solution)/shard_map/ppermute | solution.py:59
  65.4 8.5 %collective-permute-start.29 = (bf16[256,384]{1,0:T(8,128)(2,1)S(1)}, bf16[256,384]{1,0:T(8,128)(2,1)S(1)}, u32[]{:S(2)}, u32[]{:S(2)}) collective-permute-start(bf16[256,384]{1,0:T(8,128)(2,1)S(1)} %collective-permute-done.24.refs_0_), channel_id=1, source_target_pairs={{0,8},{1,5},{2,0},{3,11},{4,6},{5,13},{6,14},{7,3},{8,16},{9,1},{1... | collective-permute-start | bytes 589832 | tf_op jit(solution)/shard_map/ppermute | solution.py:88
  67.5 7.7 %collective-permute-start.30 = (bf16[256,384]{1,0:T(8,128)(2,1)S(1)}, bf16[256,384]{1,0:T(8,128)(2,1)S(1)}, u32[]{:S(2)}, u32[]{:S(2)}) collective-permute-start(bf16[256,384]{1,0:T(8,128)(2,1)S(1)} %collective-permute-done.25.refs_1_), channel_id=1, source_target_pairs={{0,2},{1,9},{2,10},{3,7},{4,12},{5,1},{6,4},{7,15},{8,0},{9,17},{1... | collective-permute-start | bytes 589832 | tf_op jit(solution)/shard_map/ppermute | solution.py:88
  68.5 9.4 %collective-permute-start.27 = (bf16[384,384]{1,0:T(8,128)(2,1)S(1)}, bf16[384,384]{1,0:T(8,128)(2,1)S(1)}, u32[]{:S(2)}, u32[]{:S(2)}) collective-permute-start(bf16[384,384]{1,0:T(8,128)(2,1)S(1)} %get-tuple-element.75), channel_id=1, source_target_pairs={{0,4},{1,3},{2,6},{3,1},{4,0},{5,7},{6,2},{7,5},{8,12},{9,11},{10,... | collective-permute-start | bytes 884744 | tf_op jit(solution)/shard_map/ppermute | solution.py:59
  71.2 8.8 %collective-permute-start.26 = (bf16[192,384]{1,0:T(8,128)(2,1)S(1)}, bf16[192,384]{1,0:T(8,128)(2,1)S(1)}, u32[]{:S(2)}, u32[]{:S(2)}) collective-permute-start(bf16[192,384]{1,0:T(8,128)(2,1)S(1)} %get-tuple-element.74), channel_id=1, source_target_pairs={{0,1},{1,0},{2,3},{3,2},{4,5},{5,4},{6,7},{7,6},{8,9},{9,8},{10,11... | collective-permute-start | bytes 442376 | tf_op jit(solution)/shard_map/ppermute | solution.py:59
  73.9 5.8 %collective-permute-start.34 = (bf16[256,384]{1,0:T(8,128)(2,1)S(1)}, bf16[256,384]{1,0:T(8,128)(2,1)S(1)}, u32[]{:S(2)}, u32[]{:S(2)}) collective-permute-start(bf16[256,384]{1,0:T(8,128)(2,1)S(1)} %collective-permute-done.29.refs_0_), channel_id=1, source_target_pairs={{0,8},{1,5},{2,0},{3,11},{4,6},{5,13},{6,14},{7,3},{8,16},{9,1},{1... | collective-permute-start | bytes 589832 | tf_op jit(solution)/shard_map/ppermute | solution.py:88
  75.6 5.2 %collective-permute-start.32 = (bf16[192,384]{1,0:T(8,128)(2,1)S(1)}, bf16[192,384]{1,0:T(8,128)(2,1)S(1)}, u32[]{:S(2)}, u32[]{:S(2)}) collective-permute-start(bf16[192,384]{1,0:T(8,128)(2,1)S(1)} %get-tuple-element.86), channel_id=1, source_target_pairs={{0,4},{1,3},{2,6},{3,1},{4,0},{5,7},{6,2},{7,5},{8,12},{9,11},{10,... | collective-permute-start | bytes 442376 | tf_op jit(solution)/shard_map/ppermute | solution.py:59
  77.0 5.1 %collective-permute-start.33 = (bf16[192,384]{1,0:T(8,128)(2,1)S(1)}, bf16[192,384]{1,0:T(8,128)(2,1)S(1)}, u32[]{:S(2)}, u32[]{:S(2)}) collective-permute-start(bf16[192,384]{1,0:T(8,128)(2,1)S(1)} %get-tuple-element.85), channel_id=1, source_target_pairs={{0,5},{1,2},{2,7},{3,0},{4,1},{5,6},{6,3},{7,4},{8,13},{9,10},{10,... | collective-permute-start | bytes 442376 | tf_op jit(solution)/shard_map/ppermute | solution.py:59
  77.9 6.4 %collective-permute-start.31 = (bf16[192,384]{1,0:T(8,128)(2,1)S(1)}, bf16[192,384]{1,0:T(8,128)(2,1)S(1)}, u32[]{:S(2)}, u32[]{:S(2)}) collective-permute-start(bf16[192,384]{1,0:T(8,128)(2,1)S(1)} %get-tuple-element.79), channel_id=1, source_target_pairs={{0,1},{1,0},{2,3},{3,2},{4,5},{5,4},{6,7},{7,6},{8,9},{9,8},{10,11... | collective-permute-start | bytes 442376 | tf_op jit(solution)/shard_map/ppermute | solution.py:59
  79.7 3.7 %collective-permute-start.23 = (bf16[288,384]{1,0:T(8,128)(2,1)S(1)}, bf16[288,384]{1,0:T(8,128)(2,1)S(1)}, u32[]{:S(2)}, u32[]{:S(2)}) collective-permute-start(bf16[288,384]{1,0:T(8,128)(2,1)S(1)} %slice.24), channel_id=1, source_target_pairs={{0,1},{1,0},{2,3},{3,2},{4,5},{5,4},{6,7},{7,6},{8,9},{9,8},{10,11... | collective-permute-start | bytes 663560 | tf_op jit(solution)/shard_map/ppermute | solution.py:59
  80.0 4.3 %collective-permute-start.28 = (bf16[192,384]{1,0:T(8,128)(2,1)S(1)}, bf16[192,384]{1,0:T(8,128)(2,1)S(1)}, u32[]{:S(2)}, u32[]{:S(2)}) collective-permute-start(bf16[192,384]{1,0:T(8,128)(2,1)S(1)} %slice.25), channel_id=1, source_target_pairs={{0,1},{1,0},{2,3},{3,2},{4,5},{5,4},{6,7},{7,6},{8,9},{9,8},{10,11... | collective-permute-start | bytes 442376 | tf_op jit(solution)/shard_map/ppermute | solution.py:59
  80.8 4.4 %collective-permute-start.36 = (bf16[96,384]{1,0:T(8,128)(2,1)S(1)}, bf16[96,384]{1,0:T(8,128)(2,1)S(1)}, u32[]{:S(2)}, u32[]{:S(2)}) collective-permute-start(bf16[96,384]{1,0:T(8,128)(2,1)S(1)} %get-tuple-element.88), channel_id=1, source_target_pairs={{0,4},{1,3},{2,6},{3,1},{4,0},{5,7},{6,2},{7,5},{8,12},{9,11},{10,... | collective-permute-start | bytes 221192 | tf_op jit(solution)/shard_map/ppermute | solution.py:59
  82.2 3.8 %collective-permute-start.37 = (bf16[96,384]{1,0:T(8,128)(2,1)S(1)}, bf16[96,384]{1,0:T(8,128)(2,1)S(1)}, u32[]{:S(2)}, u32[]{:S(2)}) collective-permute-start(bf16[96,384]{1,0:T(8,128)(2,1)S(1)} %get-tuple-element.87), channel_id=1, source_target_pairs={{0,5},{1,2},{2,7},{3,0},{4,1},{5,6},{6,3},{7,4},{8,13},{9,10},{10,... | collective-permute-start | bytes 221192 | tf_op jit(solution)/shard_map/ppermute | solution.py:59
  83.4 2.6 %collective-permute-start.35 = (bf16[96,384]{1,0:T(8,128)(2,1)S(1)}, bf16[96,384]{1,0:T(8,128)(2,1)S(1)}, u32[]{:S(2)}, u32[]{:S(2)}) collective-permute-start(bf16[96,384]{1,0:T(8,128)(2,1)S(1)} %get-tuple-element.83), channel_id=1, source_target_pairs={{0,1},{1,0},{2,3},{3,2},{4,5},{5,4},{6,7},{7,6},{8,9},{9,8},{10,11... | collective-permute-start | bytes 221192 | tf_op jit(solution)/shard_map/ppermute | solution.py:59
